TPU v7x, 32 devices: a whole 2x2x4 slice. The times are simulated.
32 devices in a mesh: layers: 2 (over y), fa: 4 (over z), fb: 4 (over x, core).
Axes of the slice: x: 2, y: 2, z: 4, core: 2. Of those that a mesh axis runs over, the one named last changes fastest.
Arguments:
- a_acts: bfloat16 [512, 14336], P(('layers', 'fa', 'fb')), parts along dimension 0, may hold values from -60 to 60, as said below
- b_acts: bfloat16 [512, 14336], P(('layers', 'fa', 'fb')), parts along dimension 0, may hold values from -60 to 60, as said below
Outputs:
- correlation: float32 [28672, 14336], P(('layers', 'fa'), 'fb'), parts along dimension 0
There are 2 independent parts, one for each index of `layers`. A program takes and returns all parts, laid end to end along the dimension named above; each array names one. Nothing has to cross between parts.
Inputs may be any that keep to these rules, and one draw needn't show every extreme that they name: `a_acts`: activations with per-feature offsets and scales. `b_acts`: activations with per-feature offsets and scales.
All inputs are finite; a program needn't handle non-finite values.
Results may differ from a plain program's by a relative error of at most 0.004.
Values may be sent and summed in bfloat16 or wider, within the bound.
No kernel may reach another device: no remote copies, remote signals or barrier semaphores. Data moves between devices by JAX's collectives and lax.ppermute only.
A program may use at most 128 MiB of HBM per device.

v0:
```python
import jax
import jax.numpy as jnp
from jax import lax
from jax.sharding import PartitionSpec as P


def standardize(acts):
    values = acts.astype(jnp.float32)
    mean = jnp.mean(values, axis=0)
    centred = values - mean
    var = jnp.mean(centred * centred, axis=0)
    return (centred * lax.rsqrt(var + 1e-05)).astype(jnp.bfloat16)


def swap_groups(rows, outer, inner, tok_count):
    width = rows.shape[1]
    grouped = rows.reshape(outer, inner, tok_count, width)
    return jnp.transpose(grouped, (1, 0, 2, 3)).reshape(outer * inner * tok_count, width)


def per_device(a_acts, b_acts):
    n_fa = lax.axis_size("fa")
    n_fb = lax.axis_size("fb")
    tok_count = a_acts.shape[0]
    a_group = lax.all_gather(a_acts, "fb", axis=0, tiled=True)
    a_whole = lax.all_to_all(a_group, "fa", split_axis=1, concat_axis=0, tiled=True)
    b_group = lax.all_gather(b_acts, "fa", axis=0, tiled=True)
    b_whole = lax.all_to_all(b_group, "fb", split_axis=1, concat_axis=0, tiled=True)
    b_whole = swap_groups(b_whole, n_fb, n_fa, tok_count)
    std_a = standardize(a_whole)
    std_b = standardize(b_whole)
    product = lax.dot_general(
        std_a, std_b, (((0,), (0,)), ((), ())), preferred_element_type=jnp.float32
    )
    return product / std_a.shape[0]


def solution(mesh):
    placed = (P(("layers", "fa", "fb"), None), P(("layers", "fa", "fb"), None))
    return jax.shard_map(
        per_device, mesh=mesh, in_specs=placed, out_specs=P(("layers", "fa"), "fb"), check_vma=False
    )
```

profile of v0, /device:TPU:0, one launch (start us, length us, event | category | flops | bytes accessed | tf_op | source)
XLA Modules:
  0.0 172.0 jit_solution(16237016325270978743)
XLA Ops:
  6.5 0.0 all-gather.5.cloned.1.call-start
  6.5 0.7 all-gather.5.cloned.1.call-update
  7.3 0.0 all-gather.3.cloned.1.call-start
  7.3 0.7 all-gather.3.cloned.1.call-update
  8.0 45.0 %all-gather.5.cloned.1.call-done = bf16[64,14336]{1,0:T(8,128)(2,1)} async-done(((bf16[16,14336]{1,0:T(8,128)(2,1)}), bf16[64,14336]{1,0:T(8,128)(2,1)}) %all-gather.5.cloned.1.call-update) | async-done | bytes 1835024 | tf_op jit(solution)/shard_map/all_gather | solution.py:27
  53.1 2.9 %copy.15 = bf16[8,4,8,3584]{3,2,0,1:T(8,128)(2,1)} copy(bf16[8,4,8,3584]{3,2,1,0:T(8,128)(2,1)} %bitcast.26) | data formatting | bytes 3670016 | tf_op jit(solution)/shard_map/all_to_all | solution.py:28
  55.9 3.6 %all-to-all-start.1 = ((bf16[64,4,3584]{2,0,1:T(8,128)(2,1)}), bf16[64,4,3584]{2,0,1:T(8,128)(2,1)S(1)}, u32[]{:S(2)}, u32[]{:S(2)}) async-start(bf16[64,4,3584]{2,0,1:T(8,128)(2,1)} %bitcast.23), calls=%async_computation.1 | async-start | bytes 3670016 | tf_op jit(solution)/shard_map/all_to_all | solution.py:28
  59.5 24.8 %all-gather.3.cloned.1.call-done = bf16[64,14336]{1,0:T(8,128)(2,1)} async-done(((bf16[16,14336]{1,0:T(8,128)(2,1)}), bf16[64,14336]{1,0:T(8,128)(2,1)}) %all-gather.3.cloned.1.call-update) | async-done | bytes 1835024 | tf_op jit(solution)/shard_map/all_gather | solution.py:25
  84.4 2.9 %copy.16 = bf16[8,4,8,3584]{3,2,0,1:T(8,128)(2,1)} copy(bf16[8,4,8,3584]{3,2,1,0:T(8,128)(2,1)} %bitcast.25) | data formatting | bytes 3670016 | tf_op jit(solution)/shard_map/all_to_all | solution.py:26
  87.3 5.0 %all-to-all-done.1 = bf16[64,4,3584]{2,0,1:T(8,128)(2,1)S(1)} async-done(((bf16[64,4,3584]{2,0,1:T(8,128)(2,1)}), bf16[64,4,3584]{2,0,1:T(8,128)(2,1)S(1)}, u32[]{:S(2)}, u32[]{:S(2)}) %all-to-all-start.1) | async-done | bytes 1835040 | tf_op jit(solution)/shard_map/all_to_all | solution.py:28
  92.2 0.0 copy-start
  92.2 1.3 copy-done
  93.5 3.6 %all-to-all-start = ((bf16[64,4,3584]{2,0,1:T(8,128)(2,1)}), bf16[64,4,3584]{2,0,1:T(8,128)(2,1)S(1)}, u32[]{:S(2)}, u32[]{:S(2)}) async-start(bf16[64,4,3584]{2,0,1:T(8,128)(2,1)} %bitcast.22), calls=%async_computation | async-start | bytes 3670016 | tf_op jit(solution)/shard_map/all_to_all | solution.py:26
  97.1 0.0 copy-start.1
  97.1 2.1 %convert_element_type.42 = f32[64,4,3584]{2,0,1:T(8,128)S(1)} convert(bf16[64,4,3584]{2,0,1:T(8,128)(2,1)} %copy-done) | non-fusion elementwise | flops 917504 | bytes 5505024 | tf_op jit(solution)/shard_map/convert_element_type | solution.py:8
  99.2 0.0 copy-done.1
  99.2 0.3 convert_reduce_fusion.1
  99.5 0.4 multiply_reduce_fusion
  99.9 0.5 fusion.4
  100.4 1.3 copy.10
  101.7 38.0 %all-to-all-done = bf16[64,4,3584]{2,0,1:T(8,128)(2,1)S(1)} async-done(((bf16[64,4,3584]{2,0,1:T(8,128)(2,1)}), bf16[64,4,3584]{2,0,1:T(8,128)(2,1)S(1)}, u32[]{:S(2)}, u32[]{:S(2)}) %all-to-all-start) | async-done | bytes 1835040 | tf_op jit(solution)/shard_map/all_to_all | solution.py:26
  139.7 0.3 convert_reduce_fusion
  140.0 0.5 fusion.2
  140.5 1.7 fusion.3
  142.2 22.9 %convolution_multiply_fusion = f32[3584,3584]{1,0:T(8,128)} fusion(bf16[256,3584]{1,0:T(8,128)(2,1)} %bitcast.21, bf16[256,3584]{1,0:T(8,128)(2,1)} %bitcast.24), kind=kOutput, calls=%fused_computation | convolution fusion | flops 6589513728 | bytes 55050240 | tf_op jit(solution)/shard_map/dot_general | solution.py:32
  (4 shorter events, 0.0 us)
Async XLA Ops:
  6.5 46.5 %all-gather.5.cloned.1.call-start = ((), (), s32[]{:S(2)}) async-start(), calls=%async_computation.3 | async-start | bytes 2293760 | tf_op jit(solution)/shard_map/all_gather | solution.py:27
  7.3 77.1 %all-gather.3.cloned.1.call-start = ((), (), s32[]{:S(2)}) async-start(), calls=%async_computation.2 | async-start | bytes 2293760 | tf_op jit(solution)/shard_map/all_gather | solution.py:25
  55.9 36.3 %all-to-all-start.1 = ((bf16[64,4,3584]{2,0,1:T(8,128)(2,1)}), bf16[64,4,3584]{2,0,1:T(8,128)(2,1)S(1)}, u32[]{:S(2)}, u32[]{:S(2)}) async-start(bf16[64,4,3584]{2,0,1:T(8,128)(2,1)} %bitcast.23), calls=%async_computation.1 | async-start | bytes 3670016 | tf_op jit(solution)/shard_map/all_to_all | solution.py:28
  92.2 1.3 copy-start
  93.5 46.2 %all-to-all-start = ((bf16[64,4,3584]{2,0,1:T(8,128)(2,1)}), bf16[64,4,3584]{2,0,1:T(8,128)(2,1)S(1)}, u32[]{:S(2)}, u32[]{:S(2)}) async-start(bf16[64,4,3584]{2,0,1:T(8,128)(2,1)} %bitcast.22), calls=%async_computation | async-start | bytes 3670016 | tf_op jit(solution)/shard_map/all_to_all | solution.py:26
  97.1 2.1 %copy-start.1 = (bf16[64,4,3584]{2,0,1:T(8,128)(2,1)S(1)}, bf16[64,4,3584]{2,0,1:T(8,128)(2,1)}, u32[]{:S(2)}) copy-start(bf16[64,4,3584]{2,0,1:T(8,128)(2,1)} %copy-done) | copy-start | bytes 5505028
Sparse Core Ops, SparseCore 0:
  8.9 44.0 all-gather.4
  54.6 29.7 all-gather.2
where the time goes:
time: 172 us
  waiting for transfers between devices  114 us (66%)
  matrix products  22.9 us (13%)
  between operations  13.5 us (8%)
  local copies, waits for them, and re-layouts  8.38 us (5%)
  starting transfers between devices  7.21 us (4%)
  other arithmetic  5.73 us (3%)
    all_gather x1, waiting for transfers between devices, per_device(): b_group = lax.all_gather(b_acts, 'fa', axis=0, tiled=True)  45 us
    all_to_all x1, waiting for transfers between devices, per_device(): lax.all_to_all(a_group, 'fa', split_axis=1, concat_axis=0, tiled=True)  38 us
    all_gather x1, waiting for transfers between devices, per_device(): a_group = lax.all_gather(a_acts, 'fb', axis=0, tiled=True)  24.8 us
    dot_general x1, matrix products, per_device(): lax.dot_general(std_a, std_b, (((0,), (0,)), ((), ())), preferred_element...  22.9 us
    all_to_all x1, waiting for transfers between devices, per_device(): lax.all_to_all(b_group, 'fb', split_axis=1, concat_axis=0, tiled=True)  4.97 us
    all_to_all x1, starting transfers between devices, per_device(): lax.all_to_all(a_group, 'fa', split_axis=1, concat_axis=0, tiled=True)  3.59 us
    all_to_all x1, starting transfers between devices, per_device(): lax.all_to_all(b_group, 'fb', split_axis=1, concat_axis=0, tiled=True)  3.58 us
  transfers between devices with their start and end apart: 4, of which 4 were waited for; matrix products, arithmetic and copies ran while one was open for 6% of the time, Pallas kernels for 0%

commit v1 on v0

v1 whole, which is shorter than its diff:
```python
import functools

import jax
import jax.numpy as jnp
from jax import lax
from jax.experimental import pallas as pl
from jax.experimental.pallas import tpu as pltpu
from jax.sharding import PartitionSpec as P

EPS = 1e-05
VMEM = 48 * 1024 * 1024


def block_of(size, limit):
    tiles = size // 128
    best = 1
    for count in range(1, tiles + 1):
        if tiles % count == 0 and count * 128 <= limit:
            best = count
    return best * 128


def chunks_of(size, limit):
    tiles = size // 128
    return max(count for count in range(1, limit + 1) if tiles % count == 0)


def standardize(values):
    count = values.shape[0]
    mean = jnp.sum(values, axis=0, keepdims=True) / count
    centred = values - mean
    var = jnp.sum(centred * centred, axis=0, keepdims=True) / count
    return (centred * lax.rsqrt(var + EPS)).astype(jnp.bfloat16)


def slice_kernel(n_fa, n_fb, a_ref, b_ref, *refs):
    outs, sems = refs[:-1], refs[-1]
    width_a = a_ref.shape[1] // n_fa
    width_b = b_ref.shape[1] // n_fb
    fa = lax.axis_index("fa")
    fb = lax.axis_index("fb")
    copies = []
    for step in range(n_fa):
        start = pl.multiple_of(lax.rem(fa + step, n_fa) * width_a, 128)
        copies.append((a_ref.at[:, pl.ds(start, width_a)], outs[step]))
    for step in range(n_fb):
        start = pl.multiple_of(lax.rem(fb + step, n_fb) * width_b, 128)
        copies.append((b_ref.at[:, pl.ds(start, width_b)], outs[n_fa + step]))
    started = []
    for place, (src, dst) in enumerate(copies):
        copy = pltpu.make_async_copy(src, dst, sems.at[place])
        copy.start()
        started.append(copy)
    for copy in started:
        copy.wait()


def cut_panels(a_acts, b_acts, n_fa, n_fb):
    tok, width_a = a_acts.shape[0], a_acts.shape[1] // n_fa
    width_b = b_acts.shape[1] // n_fb
    shapes = [jax.ShapeDtypeStruct((tok, width_a), a_acts.dtype)] * n_fa
    shapes += [jax.ShapeDtypeStruct((tok, width_b), b_acts.dtype)] * n_fb
    outs = pl.pallas_call(
        functools.partial(slice_kernel, n_fa, n_fb),
        out_shape=shapes,
        in_specs=[pl.BlockSpec(memory_space=pl.ANY)] * 2,
        out_specs=[pl.BlockSpec(memory_space=pl.ANY)] * len(shapes),
        scratch_shapes=[pltpu.SemaphoreType.DMA((len(shapes),))],
        name="cut_panels",
    )(a_acts, b_acts)
    return outs[:n_fa], outs[n_fa:]


def standardize_a_kernel(*refs):
    groups, out = refs[:-1], refs[-1]
    values = jnp.concatenate([ref[...].astype(jnp.float32) for ref in groups], axis=0)
    out[...] = standardize(values).T


def standardize_a(groups):
    rows, width = groups[0].shape
    block = block_of(width, 512)
    total = rows * len(groups)
    return pl.pallas_call(
        standardize_a_kernel,
        out_shape=jax.ShapeDtypeStruct((width, total), jnp.bfloat16),
        grid=(width // block,),
        in_specs=[pl.BlockSpec((rows, block), lambda i: (0, i))] * len(groups),
        out_specs=pl.BlockSpec((block, total), lambda i: (i, 0)),
        compiler_params=pltpu.CompilerParams(vmem_limit_bytes=VMEM),
        cost_estimate=pl.CostEstimate(
            flops=10 * width * total, bytes_accessed=4 * width * total, transcendentals=0
        ),
        name="standardize_a",
    )(*groups)


def product_kernel(n_fa, n_fb, aliased, a_ref, *refs):
    groups = refs[:n_fa]
    out, std = refs[-2], refs[-1]
    tok = groups[0].shape[0] // n_fb

    @pl.when(pl.program_id(0) == 0)
    def _():
        pieces = []
        for j in range(n_fb):
            for i in range(n_fa):
                pieces.append(groups[i][pl.ds(j * tok, tok), :].astype(jnp.float32))
        std[...] = standardize(jnp.concatenate(pieces, axis=0))

    product = jnp.dot(a_ref[...], std[...], preferred_element_type=jnp.float32)
    out[...] = product / std.shape[0]


def product_chunk(std_a, groups, n_fa, n_fb, chunk, n_chunks, buffer):
    height, total = std_a.shape
    rows, width = groups[0].shape
    block = block_of(height, 512)
    in_specs = [pl.BlockSpec((block, total), lambda i: (i, 0))]
    in_specs += [pl.BlockSpec((rows, width), lambda i: (0, 0))] * n_fa
    args = [std_a, *groups]
    aliases = {}
    if buffer is not None:
        aliases = {len(args): 0}
        in_specs.append(pl.BlockSpec(memory_space=pl.ANY))
        args.append(buffer)
    return pl.pallas_call(
        functools.partial(product_kernel, n_fa, n_fb, buffer is not None),
        out_shape=jax.ShapeDtypeStruct((height, width * n_chunks), jnp.float32),
        grid=(height // block,),
        in_specs=in_specs,
        out_specs=pl.BlockSpec((block, width), lambda i: (i, chunk)),
        scratch_shapes=[pltpu.VMEM((total, width), jnp.bfloat16)],
        input_output_aliases=aliases,
        compiler_params=pltpu.CompilerParams(vmem_limit_bytes=VMEM),
        cost_estimate=pl.CostEstimate(
            flops=2 * height * width * total, bytes_accessed=4 * height * width, transcendentals=0
        ),
        name="product_chunk",
    )(*args)


def shifted(x, axis, step):
    size = lax.axis_size(axis)
    return lax.ppermute(x, axis, [(i, (i + step) % size) for i in range(size)])


def per_device(a_acts, b_acts):
    n_fa = lax.axis_size("fa")
    n_fb = lax.axis_size("fb")
    panels_a, panels_b = cut_panels(a_acts, b_acts, n_fa, n_fb)
    own_a = [panels_a[0]] + [shifted(panels_a[s], "fa", s) for s in range(1, n_fa)]
    own_b = [panels_b[0]] + [shifted(panels_b[s], "fb", s) for s in range(1, n_fb)]
    group_a = jnp.concatenate(own_a, axis=0)
    group_b = jnp.concatenate(own_b, axis=0)
    width = group_b.shape[1]
    n_chunks = chunks_of(width, 4)
    step = width // n_chunks
    all_a = [group_a] + [shifted(group_a, "fb", s) for s in range(1, n_fb)]
    std_a = standardize_a(all_a)
    buffer = None
    for chunk in range(n_chunks):
        part = group_b[:, chunk * step : (chunk + 1) * step]
        groups = [part] + [shifted(part, "fa", s) for s in range(1, n_fa)]
        buffer = product_chunk(std_a, groups, n_fa, n_fb, chunk, n_chunks, buffer)
    return buffer


def solution(mesh):
    placed = (P(("layers", "fa", "fb"), None), P(("layers", "fa", "fb"), None))
    return jax.shard_map(
        per_device, mesh=mesh, in_specs=placed, out_specs=P(("layers", "fa"), "fb"), check_vma=False
    )
```

time: 172 us -> 108 us (0.63)
  waiting for transfers between devices: 114 us -> 11.6 us
  Pallas kernels: 0 us -> 58.8 us
  starting transfers between devices: 7.21 us -> 34.9 us
  matrix products: 22.9 us -> 0 us
  between operations: 13.5 us -> 0.13 us
  local copies, waits for them, and re-layouts: 8.38 us -> 1.91 us
  other arithmetic: 5.73 us -> 0 us
    all_gather x2 -> x0, waiting for transfers between devices: 69.9 us -> none  [the longest x1 45 us: per_device(): b_group = lax.all_gather(b_acts, 'fa', axis=0, tiled=True)]
    pallas_call x0 -> x6, Pallas kernels: none -> 58.8 us  [the longest x1 29 us: cut_panels(): pl.pallas_call(functools.partial(slice_kernel, n_fa, n_fb), out_shape=sha...]
    all_to_all x2 -> x0, waiting for transfers between devices: 43 us -> none  [the longest x1 38 us: per_device(): lax.all_to_all(a_group, 'fa', split_axis=1, concat_axis=0, tiled=True)]
    ppermute x0 -> x21, starting transfers between devices: none -> 34.9 us  [shifted(): return lax.ppermute(x, axis, [(i, (i + step) % size) for i in range(size)])]
    dot_general x1 -> x0, matrix products: 22.9 us -> none  [per_device(): lax.dot_general(std_a, std_b, (((0,), (0,)), ((), ())), preferred_element...]
    ppermute x0 -> x21, waiting for transfers between devices: none -> 11.6 us  [shifted(): return lax.ppermute(x, axis, [(i, (i + step) % size) for i in range(size)])]
    all_to_all x2 -> x0, starting transfers between devices: 7.17 us -> none  [the longest x1 3.59 us: per_device(): lax.all_to_all(a_group, 'fa', split_axis=1, concat_axis=0, tiled=True)]
    all_to_all x2 -> x0, local copies, waits for them, and re-layouts: 5.76 us -> none  [the longest x1 2.89 us: per_device(): lax.all_to_all(b_group, 'fb', split_axis=1, concat_axis=0, tiled=True)]
  transfers between devices with their start and end apart: 4 -> 21, of which waited for: 4 -> 3; matrix products, arithmetic and copies ran while one was open for 6% -> 2% of each run, Pallas kernels for 0% -> 21%
where the time goes in v1:
time: 108 us; the launch traced here: 107 us
  Pallas kernels  58.8 us (54%)
  starting transfers between devices  34.9 us (32%)
  waiting for transfers between devices  11.6 us (11%)
  local copies, waits for them, and re-layouts  1.91 us (2%)
    ppermute x21, starting transfers between devices, shifted(): return lax.ppermute(x, axis, [(i, (i + step) % size) for i in range(size)])  34.9 us
    pallas_call x1, Pallas kernels, cut_panels(): pl.pallas_call(functools.partial(slice_kernel, n_fa, n_fb), out_shape=sha...  29 us
    pallas_call x4, Pallas kernels, product_chunk(): pl.pallas_call(functools.partial(product_kernel, n_fa, n_fb, buffer is no...  27.8 us
    ppermute x21, waiting for transfers between devices, shifted(): return lax.ppermute(x, axis, [(i, (i + step) % size) for i in range(size)])  11.6 us
  transfers between devices with their start and end apart: 21, of which 3 were waited for; matrix products, arithmetic and copies ran while one was open for 2% of the time, Pallas kernels for 21%

profile of v1, /device:TPU:0, one launch (start us, length us, event | category | flops | bytes accessed | tf_op | source)
XLA Modules:
  0.0 107.4 jit_solution(12439988585690509062)
XLA Ops:
  0.0 29.0 %cut_panels.1 = (bf16[16,3584]{1,0:T(8,128)(2,1)}, bf16[16,3584]{1,0:T(8,128)(2,1)}, bf16[16,3584]{1,0:T(8,128)(2,1)}, bf16[16,3584]{1,0:T(8,128)(2,1)}, bf16[16...) custom-call(bf16[16,14336]{1,0:T(8,128)(2,1)} %a_ref.1, ...), custom_call_target="tpu_custom_call" | custom-call | tf_op jit(solution)/shard_map/cut_panels/pallas_call | solution.py:63
  29.0 3.1 %collective-permute-start = (bf16[16,3584]{1,0:T(8,128)(2,1)}, bf16[16,3584]{1,0:T(8,128)(2,1)S(1)}, u32[]{:S(2)}, u32[]{:S(2)}) collective-permute-start(bf16[16,3584]{1,0:T(8,128)(2,1)} %get-tuple-element.14), channel_id=1, source_target_pairs={{0,4},{4,8},{8,12},{12,0},{1,5},{5,9},{9,13},{13,1},{2,6},{6,10},{... | collective-permute-start | bytes 344072 | tf_op jit(solution)/shard_map/ppermute | solution.py:145
  32.0 2.6 %collective-permute-start.1 = (bf16[16,3584]{1,0:T(8,128)(2,1)}, bf16[16,3584]{1,0:T(8,128)(2,1)S(1)}, u32[]{:S(2)}, u32[]{:S(2)}) collective-permute-start(bf16[16,3584]{1,0:T(8,128)(2,1)} %get-tuple-element.15), channel_id=1, source_target_pairs={{0,8},{4,12},{8,0},{12,4},{1,9},{5,13},{9,1},{13,5},{2,10},{6,14},... | collective-permute-start | bytes 344072 | tf_op jit(solution)/shard_map/ppermute | solution.py:145
  34.6 1.3 %collective-permute-start.2 = (bf16[16,3584]{1,0:T(8,128)(2,1)}, bf16[16,3584]{1,0:T(8,128)(2,1)S(1)}, u32[]{:S(2)}, u32[]{:S(2)}) collective-permute-start(bf16[16,3584]{1,0:T(8,128)(2,1)} %get-tuple-element.16), channel_id=1, source_target_pairs={{0,12},{4,0},{8,4},{12,8},{1,13},{5,1},{9,5},{13,9},{2,14},{6,2},{... | collective-permute-start | bytes 344072 | tf_op jit(solution)/shard_map/ppermute | solution.py:145
  36.0 0.0 collective-permute-start.6
  36.0 1.5 %collective-permute-start.7 = (bf16[16,3584]{1,0:T(8,128)(2,1)}, bf16[16,3584]{1,0:T(8,128)(2,1)S(1)}, u32[]{:S(2)}, u32[]{:S(2)}) collective-permute-start(bf16[16,3584]{1,0:T(8,128)(2,1)} %get-tuple-element.19), channel_id=1, source_target_pairs={{0,2},{1,3},{2,0},{3,1},{4,6},{5,7},{6,4},{7,5},{8,10},{9,11},{10,... | collective-permute-start | bytes 344072 | tf_op jit(solution)/shard_map/ppermute | solution.py:145
  37.5 0.9 constant_dynamic-update-slice_fusion.3
  38.4 0.9 constant_dynamic-update-slice_fusion.7
  39.3 0.0 collective-permute-done
  39.3 1.5 %collective-permute-start.8 = (bf16[16,3584]{1,0:T(8,128)(2,1)}, bf16[16,3584]{1,0:T(8,128)(2,1)S(1)}, u32[]{:S(2)}, u32[]{:S(2)}) collective-permute-start(bf16[16,3584]{1,0:T(8,128)(2,1)} %get-tuple-element.20), channel_id=1, source_target_pairs={{0,3},{1,0},{2,1},{3,2},{4,7},{5,4},{6,5},{7,6},{8,11},{9,8},{10,9... | collective-permute-start | bytes 344072 | tf_op jit(solution)/shard_map/ppermute | solution.py:145
  40.8 1.6 %collective-permute-done.1 = bf16[16,3584]{1,0:T(8,128)(2,1)S(1)} collective-permute-done((bf16[16,3584]{1,0:T(8,128)(2,1)}, bf16[16,3584]{1,0:T(8,128)(2,1)S(1)}, u32[]{:S(2)}, u32[]{:S(2)}) %collective-permute-start.1) | collective-permute-done | bytes 114720 | tf_op jit(solution)/shard_map/ppermute | solution.py:145
  42.5 0.0 collective-permute-done.2
  42.5 0.1 collective-permute-start.3
  42.5 1.6 %collective-permute-start.4 = (bf16[64,3584]{1,0:T(8,128)(2,1)S(1)}, bf16[64,3584]{1,0:T(8,128)(2,1)S(1)}, u32[]{:S(2)}, u32[]{:S(2)}) collective-permute-start(bf16[64,3584]{1,0:T(8,128)(2,1)S(1)} %constant_dynamic-update-slice_fusion.refs_0_), channel_id=1, source_target_pairs={{0,2},{1,3},{2,0},{3,1},{4,6},{5,7},{6,4},{7,5},{8,10},{9,11},{10,... | collective-permute-start | bytes 1376264 | tf_op jit(solution)/shard_map/ppermute | solution.py:145
  44.1 0.0 collective-permute-done.6
  44.1 1.4 %collective-permute-start.5 = (bf16[64,3584]{1,0:T(8,128)(2,1)S(1)}, bf16[64,3584]{1,0:T(8,128)(2,1)S(1)}, u32[]{:S(2)}, u32[]{:S(2)}) collective-permute-start(bf16[64,3584]{1,0:T(8,128)(2,1)S(1)} %constant_dynamic-update-slice_fusion.refs_0_), channel_id=1, source_target_pairs={{0,3},{1,0},{2,1},{3,2},{4,7},{5,4},{6,5},{7,6},{8,11},{9,8},{10,9... | collective-permute-start | bytes 1376264 | tf_op jit(solution)/shard_map/ppermute | solution.py:145
  45.5 0.0 collective-permute-done.7
  45.6 0.0 collective-permute-done.8
  45.7 3.0 %collective-permute-start.18 = (bf16[64,896]{1,0:T(8,128)(2,1)S(1)}, bf16[64,896]{1,0:T(8,128)(2,1)S(1)}, u32[]{:S(2)}, u32[]{:S(2)}) collective-permute-start(bf16[64,896]{1,0:T(8,128)(2,1)S(1)} %get-tuple-element.21.refs_0_), channel_id=1, source_target_pairs={{0,4},{4,8},{8,12},{12,0},{1,5},{5,9},{9,13},{13,1},{2,6},{6,10},{... | collective-permute-start | bytes 344072 | tf_op jit(solution)/shard_map/ppermute | solution.py:145
  48.6 1.6 %collective-permute-start.19 = (bf16[64,896]{1,0:T(8,128)(2,1)S(1)}, bf16[64,896]{1,0:T(8,128)(2,1)S(1)}, u32[]{:S(2)}, u32[]{:S(2)}) collective-permute-start(bf16[64,896]{1,0:T(8,128)(2,1)S(1)} %get-tuple-element.21.refs_0_), channel_id=1, source_target_pairs={{0,8},{4,12},{8,0},{12,4},{1,9},{5,13},{9,1},{13,5},{2,10},{6,14},... | collective-permute-start | bytes 344072 | tf_op jit(solution)/shard_map/ppermute | solution.py:145
  50.2 4.5 %collective-permute-done.3.refs_1_ = bf16[64,3584]{1,0:T(8,128)(2,1)S(1)} collective-permute-done((bf16[64,3584]{1,0:T(8,128)(2,1)S(1)}, bf16[64,3584]{1,0:T(8,128)(2,1)S(1)}, u32[]{:S(2)}, u32[]{:S(2)}) %collective-permute-start.3) | collective-permute-done | bytes 458784 | tf_op jit(solution)/shard_map/ppermute | solution.py:145
  54.7 4.0 %collective-permute-start.20 = (bf16[64,896]{1,0:T(8,128)(2,1)S(1)}, bf16[64,896]{1,0:T(8,128)(2,1)S(1)}, u32[]{:S(2)}, u32[]{:S(2)}) collective-permute-start(bf16[64,896]{1,0:T(8,128)(2,1)S(1)} %get-tuple-element.21.refs_0_), channel_id=1, source_target_pairs={{0,12},{4,0},{8,4},{12,8},{1,13},{5,1},{9,5},{13,9},{2,14},{6,2},{... | collective-permute-start | bytes 344072 | tf_op jit(solution)/shard_map/ppermute | solution.py:145
  58.7 0.0 collective-permute-done.4.refs_2_
  58.7 0.1 collective-permute-start.15
  58.9 5.4 %collective-permute-done.5.refs_3_ = bf16[64,3584]{1,0:T(8,128)(2,1)S(1)} collective-permute-done((bf16[64,3584]{1,0:T(8,128)(2,1)S(1)}, bf16[64,3584]{1,0:T(8,128)(2,1)S(1)}, u32[]{:S(2)}, u32[]{:S(2)}) %collective-permute-start.5) | collective-permute-done | bytes 458784 | tf_op jit(solution)/shard_map/ppermute | solution.py:145
  64.2 2.2 %collective-permute-start.16 = (bf16[64,896]{1,0:T(8,128)(2,1)S(1)}, bf16[64,896]{1,0:T(8,128)(2,1)S(1)}, u32[]{:S(2)}, u32[]{:S(2)}) collective-permute-start(bf16[64,896]{1,0:T(8,128)(2,1)S(1)} %get-tuple-element.22.refs_0_), channel_id=1, source_target_pairs={{0,8},{4,12},{8,0},{12,4},{1,9},{5,13},{9,1},{13,5},{2,10},{6,14},... | collective-permute-start | bytes 344072 | tf_op jit(solution)/shard_map/ppermute | solution.py:145
  66.4 2.1 %standardize_a.1.a_ref = bf16[3584,256]{1,0:T(8,128)(2,1)S(1)} custom-call(bf16[64,3584]{1,0:T(8,128)(2,1)S(1)} %constant_dynamic-update-slice_fusion.refs_0_, bf16[64,3584]{1,0:T(8,128)(2,1)S(1)} %collective-permute-done.3.refs_1_, bf16[64,3584]{1,0:T(8,128)(2,1)S(1)} %collective-permute-done.4.refs_2_, bf16[64,3584]{1,0:T(8,128)(2,1)S(1)} %collective-permute-done.5.refs_3_), custom_call_target="tpu_custom_call" | custom-call | flops 9175040 | bytes 3670016 | tf_op jit(solution)/shard_map/standardize_a/pallas_call | solution.py:84
  68.5 0.0 collective-permute-done.18.refs_1_
  68.5 3.1 %collective-permute-start.17 = (bf16[64,896]{1,0:T(8,128)(2,1)S(1)}, bf16[64,896]{1,0:T(8,128)(2,1)S(1)}, u32[]{:S(2)}, u32[]{:S(2)}) collective-permute-start(bf16[64,896]{1,0:T(8,128)(2,1)S(1)} %get-tuple-element.22.refs_0_), channel_id=1, source_target_pairs={{0,12},{4,0},{8,4},{12,8},{1,13},{5,1},{9,5},{13,9},{2,14},{6,2},{... | collective-permute-start | bytes 344072 | tf_op jit(solution)/shard_map/ppermute | solution.py:145
  71.7 0.0 collective-permute-done.19.refs_2_
  71.7 0.0 collective-permute-start.12
  71.7 0.0 collective-permute-done.20.refs_3_
  71.7 0.8 collective-permute-start.13
  72.5 6.9 %product_chunk.4.refs_4_ = f32[3584,3584]{1,0:T(8,128)} custom-call(bf16[3584,256]{1,0:T(8,128)(2,1)S(1)} %standardize_a.1.a_ref, bf16[64,896]{1,0:T(8,128)(2,1)S(1)} %get-tuple-element.21.refs_0_, bf16[64,896]{1,0:T(8,128)(2,1)S(1)} %collective-permute-done.18.refs_1_, bf16[64,896]{1,0:T(8,128)(2,1)S(1)} %collective-permute-done.19.refs_2_, ...), custom_call_target="tpu_custom_call" | custom-call | flops 1644167168 | bytes 12845056 | tf_op jit(solution)/shard_map/product_chunk/pallas_call | solution.py:127
  79.4 0.0 collective-permute-done.15.refs_1_
  79.4 3.0 %collective-permute-start.14 = (bf16[64,896]{1,0:T(8,128)(2,1)S(1)}, bf16[64,896]{1,0:T(8,128)(2,1)S(1)}, u32[]{:S(2)}, u32[]{:S(2)}) collective-permute-start(bf16[64,896]{1,0:T(8,128)(2,1)S(1)} %get-tuple-element.23.refs_0_), channel_id=1, source_target_pairs={{0,12},{4,0},{8,4},{12,8},{1,13},{5,1},{9,5},{13,9},{2,14},{6,2},{... | collective-permute-start | bytes 344072 | tf_op jit(solution)/shard_map/ppermute | solution.py:145
  82.5 0.0 collective-permute-done.16.refs_2_
  82.5 2.0 %collective-permute-start.10 = (bf16[64,896]{1,0:T(8,128)(2,1)S(1)}, bf16[64,896]{1,0:T(8,128)(2,1)S(1)}, u32[]{:S(2)}, u32[]{:S(2)}) collective-permute-start(bf16[64,896]{1,0:T(8,128)(2,1)S(1)} %get-tuple-element.24.refs_0_), channel_id=1, source_target_pairs={{0,8},{4,12},{8,0},{12,4},{1,9},{5,13},{9,1},{13,5},{2,10},{6,14},... | collective-permute-start | bytes 344072 | tf_op jit(solution)/shard_map/ppermute | solution.py:145
  84.5 0.0 collective-permute-done.17.refs_3_
  84.5 1.0 collective-permute-start.11
  85.5 6.9 %product_chunk.5.refs_4_ = f32[3584,3584]{1,0:T(8,128)} custom-call(bf16[3584,256]{1,0:T(8,128)(2,1)S(1)} %standardize_a.1.a_ref, bf16[64,896]{1,0:T(8,128)(2,1)S(1)} %get-tuple-element.22.refs_0_, bf16[64,896]{1,0:T(8,128)(2,1)S(1)} %collective-permute-done.15.refs_1_, ...), custom_call_target="tpu_custom_call", output_to_operand_aliasing={{}: (5, {})} | custom-call | flops 1644167168 | bytes 12845056 | tf_op jit(solution)/shard_map/product_chunk/pallas_call | solution.py:127
  92.4 0.0 collective-permute-done.12.refs_1_
  92.4 1.1 collective-permute-start.9
  93.4 0.0 collective-permute-done.13.refs_2_
  93.5 0.0 collective-permute-done.14.refs_3_
  93.5 6.9 %product_chunk.6.refs_4_ = f32[3584,3584]{1,0:T(8,128)} custom-call(bf16[3584,256]{1,0:T(8,128)(2,1)S(1)} %standardize_a.1.a_ref, bf16[64,896]{1,0:T(8,128)(2,1)S(1)} %get-tuple-element.23.refs_0_, bf16[64,896]{1,0:T(8,128)(2,1)S(1)} %collective-permute-done.12.refs_1_, ...), custom_call_target="tpu_custom_call", output_to_operand_aliasing={{}: (5, {})} | custom-call | flops 1644167168 | bytes 12845056 | tf_op jit(solution)/shard_map/product_chunk/pallas_call | solution.py:127
  100.4 0.0 collective-permute-done.10.refs_2_
  100.4 0.0 collective-permute-done.11.refs_3_
  100.4 0.0 collective-permute-done.9.refs_1_
  100.4 7.0 %product_chunk.7 = f32[3584,3584]{1,0:T(8,128)} custom-call(bf16[3584,256]{1,0:T(8,128)(2,1)S(1)} %standardize_a.1.a_ref, bf16[64,896]{1,0:T(8,128)(2,1)S(1)} %get-tuple-element.24.refs_0_, bf16[64,896]{1,0:T(8,128)(2,1)S(1)} %collective-permute-done.9.refs_1_, bf16[64,896]{1,0:T(8,128)(2,1)S(1)} %collective-permute-done.10.refs_2_, ...), custom_call_target="tpu_custom_call", output_to_operand_aliasing={{}: (5, {})} | custom-call | flops 1644167168 | bytes 12845056 | tf_op jit(solution)/shard_map/product_chunk/pallas_call | solution.py:127
  (7 shorter events, 0.1 us)
Async XLA Ops:
  29.0 10.4 %collective-permute-start = (bf16[16,3584]{1,0:T(8,128)(2,1)}, bf16[16,3584]{1,0:T(8,128)(2,1)S(1)}, u32[]{:S(2)}, u32[]{:S(2)}) collective-permute-start(bf16[16,3584]{1,0:T(8,128)(2,1)} %get-tuple-element.14), channel_id=1, source_target_pairs={{0,4},{4,8},{8,12},{12,0},{1,5},{5,9},{9,13},{13,1},{2,6},{6,10},{... | collective-permute-start | bytes 344072 | tf_op jit(solution)/shard_map/ppermute | solution.py:145
  32.0 10.4 %collective-permute-start.1 = (bf16[16,3584]{1,0:T(8,128)(2,1)}, bf16[16,3584]{1,0:T(8,128)(2,1)S(1)}, u32[]{:S(2)}, u32[]{:S(2)}) collective-permute-start(bf16[16,3584]{1,0:T(8,128)(2,1)} %get-tuple-element.15), channel_id=1, source_target_pairs={{0,8},{4,12},{8,0},{12,4},{1,9},{5,13},{9,1},{13,5},{2,10},{6,14},... | collective-permute-start | bytes 344072 | tf_op jit(solution)/shard_map/ppermute | solution.py:145
  34.6 7.8 %collective-permute-start.2 = (bf16[16,3584]{1,0:T(8,128)(2,1)}, bf16[16,3584]{1,0:T(8,128)(2,1)S(1)}, u32[]{:S(2)}, u32[]{:S(2)}) collective-permute-start(bf16[16,3584]{1,0:T(8,128)(2,1)} %get-tuple-element.16), channel_id=1, source_target_pairs={{0,12},{4,0},{8,4},{12,8},{1,13},{5,1},{9,5},{13,9},{2,14},{6,2},{... | collective-permute-start | bytes 344072 | tf_op jit(solution)/shard_map/ppermute | solution.py:145
  36.0 8.2 %collective-permute-start.6 = (bf16[16,3584]{1,0:T(8,128)(2,1)}, bf16[16,3584]{1,0:T(8,128)(2,1)S(1)}, u32[]{:S(2)}, u32[]{:S(2)}) collective-permute-start(bf16[16,3584]{1,0:T(8,128)(2,1)} %get-tuple-element.18), channel_id=1, source_target_pairs={{0,1},{1,2},{2,3},{3,0},{4,5},{5,6},{6,7},{7,4},{8,9},{9,10},{10,1... | collective-permute-start | bytes 344072 | tf_op jit(solution)/shard_map/ppermute | solution.py:145
  36.0 9.6 %collective-permute-start.7 = (bf16[16,3584]{1,0:T(8,128)(2,1)}, bf16[16,3584]{1,0:T(8,128)(2,1)S(1)}, u32[]{:S(2)}, u32[]{:S(2)}) collective-permute-start(bf16[16,3584]{1,0:T(8,128)(2,1)} %get-tuple-element.19), channel_id=1, source_target_pairs={{0,2},{1,3},{2,0},{3,1},{4,6},{5,7},{6,4},{7,5},{8,10},{9,11},{10,... | collective-permute-start | bytes 344072 | tf_op jit(solution)/shard_map/ppermute | solution.py:145
  39.3 6.2 %collective-permute-start.8 = (bf16[16,3584]{1,0:T(8,128)(2,1)}, bf16[16,3584]{1,0:T(8,128)(2,1)S(1)}, u32[]{:S(2)}, u32[]{:S(2)}) collective-permute-start(bf16[16,3584]{1,0:T(8,128)(2,1)} %get-tuple-element.20), channel_id=1, source_target_pairs={{0,3},{1,0},{2,1},{3,2},{4,7},{5,4},{6,5},{7,6},{8,11},{9,8},{10,9... | collective-permute-start | bytes 344072 | tf_op jit(solution)/shard_map/ppermute | solution.py:145
  42.5 12.3 %collective-permute-start.3 = (bf16[64,3584]{1,0:T(8,128)(2,1)S(1)}, bf16[64,3584]{1,0:T(8,128)(2,1)S(1)}, u32[]{:S(2)}, u32[]{:S(2)}) collective-permute-start(bf16[64,3584]{1,0:T(8,128)(2,1)S(1)} %constant_dynamic-update-slice_fusion.refs_0_), channel_id=1, source_target_pairs={{0,1},{1,2},{2,3},{3,0},{4,5},{5,6},{6,7},{7,4},{8,9},{9,10},{10,1... | collective-permute-start | bytes 1376264 | tf_op jit(solution)/shard_map/ppermute | solution.py:145
  42.5 16.2 %collective-permute-start.4 = (bf16[64,3584]{1,0:T(8,128)(2,1)S(1)}, bf16[64,3584]{1,0:T(8,128)(2,1)S(1)}, u32[]{:S(2)}, u32[]{:S(2)}) collective-permute-start(bf16[64,3584]{1,0:T(8,128)(2,1)S(1)} %constant_dynamic-update-slice_fusion.refs_0_), channel_id=1, source_target_pairs={{0,2},{1,3},{2,0},{3,1},{4,6},{5,7},{6,4},{7,5},{8,10},{9,11},{10,... | collective-permute-start | bytes 1376264 | tf_op jit(solution)/shard_map/ppermute | solution.py:145
  44.1 20.1 %collective-permute-start.5 = (bf16[64,3584]{1,0:T(8,128)(2,1)S(1)}, bf16[64,3584]{1,0:T(8,128)(2,1)S(1)}, u32[]{:S(2)}, u32[]{:S(2)}) collective-permute-start(bf16[64,3584]{1,0:T(8,128)(2,1)S(1)} %constant_dynamic-update-slice_fusion.refs_0_), channel_id=1, source_target_pairs={{0,3},{1,0},{2,1},{3,2},{4,7},{5,4},{6,5},{7,6},{8,11},{9,8},{10,9... | collective-permute-start | bytes 1376264 | tf_op jit(solution)/shard_map/ppermute | solution.py:145
  45.7 22.9 %collective-permute-start.18 = (bf16[64,896]{1,0:T(8,128)(2,1)S(1)}, bf16[64,896]{1,0:T(8,128)(2,1)S(1)}, u32[]{:S(2)}, u32[]{:S(2)}) collective-permute-start(bf16[64,896]{1,0:T(8,128)(2,1)S(1)} %get-tuple-element.21.refs_0_), channel_id=1, source_target_pairs={{0,4},{4,8},{8,12},{12,0},{1,5},{5,9},{9,13},{13,1},{2,6},{6,10},{... | collective-permute-start | bytes 344072 | tf_op jit(solution)/shard_map/ppermute | solution.py:145
  48.6 23.1 %collective-permute-start.19 = (bf16[64,896]{1,0:T(8,128)(2,1)S(1)}, bf16[64,896]{1,0:T(8,128)(2,1)S(1)}, u32[]{:S(2)}, u32[]{:S(2)}) collective-permute-start(bf16[64,896]{1,0:T(8,128)(2,1)S(1)} %get-tuple-element.21.refs_0_), channel_id=1, source_target_pairs={{0,8},{4,12},{8,0},{12,4},{1,9},{5,13},{9,1},{13,5},{2,10},{6,14},... | collective-permute-start | bytes 344072 | tf_op jit(solution)/shard_map/ppermute | solution.py:145
  54.7 16.9 %collective-permute-start.20 = (bf16[64,896]{1,0:T(8,128)(2,1)S(1)}, bf16[64,896]{1,0:T(8,128)(2,1)S(1)}, u32[]{:S(2)}, u32[]{:S(2)}) collective-permute-start(bf16[64,896]{1,0:T(8,128)(2,1)S(1)} %get-tuple-element.21.refs_0_), channel_id=1, source_target_pairs={{0,12},{4,0},{8,4},{12,8},{1,13},{5,1},{9,5},{13,9},{2,14},{6,2},{... | collective-permute-start | bytes 344072 | tf_op jit(solution)/shard_map/ppermute | solution.py:145
  58.7 20.7 %collective-permute-start.15 = (bf16[64,896]{1,0:T(8,128)(2,1)S(1)}, bf16[64,896]{1,0:T(8,128)(2,1)S(1)}, u32[]{:S(2)}, u32[]{:S(2)}) collective-permute-start(bf16[64,896]{1,0:T(8,128)(2,1)S(1)} %get-tuple-element.22.refs_0_), channel_id=1, source_target_pairs={{0,4},{4,8},{8,12},{12,0},{1,5},{5,9},{9,13},{13,1},{2,6},{6,10},{... | collective-permute-start | bytes 344072 | tf_op jit(solution)/shard_map/ppermute | solution.py:145
  64.2 18.2 %collective-permute-start.16 = (bf16[64,896]{1,0:T(8,128)(2,1)S(1)}, bf16[64,896]{1,0:T(8,128)(2,1)S(1)}, u32[]{:S(2)}, u32[]{:S(2)}) collective-permute-start(bf16[64,896]{1,0:T(8,128)(2,1)S(1)} %get-tuple-element.22.refs_0_), channel_id=1, source_target_pairs={{0,8},{4,12},{8,0},{12,4},{1,9},{5,13},{9,1},{13,5},{2,10},{6,14},... | collective-permute-start | bytes 344072 | tf_op jit(solution)/shard_map/ppermute | solution.py:145
  68.5 15.9 %collective-permute-start.17 = (bf16[64,896]{1,0:T(8,128)(2,1)S(1)}, bf16[64,896]{1,0:T(8,128)(2,1)S(1)}, u32[]{:S(2)}, u32[]{:S(2)}) collective-permute-start(bf16[64,896]{1,0:T(8,128)(2,1)S(1)} %get-tuple-element.22.refs_0_), channel_id=1, source_target_pairs={{0,12},{4,0},{8,4},{12,8},{1,13},{5,1},{9,5},{13,9},{2,14},{6,2},{... | collective-permute-start | bytes 344072 | tf_op jit(solution)/shard_map/ppermute | solution.py:145
  71.7 20.7 %collective-permute-start.12 = (bf16[64,896]{1,0:T(8,128)(2,1)S(1)}, bf16[64,896]{1,0:T(8,128)(2,1)S(1)}, u32[]{:S(2)}, u32[]{:S(2)}) collective-permute-start(bf16[64,896]{1,0:T(8,128)(2,1)S(1)} %get-tuple-element.23.refs_0_), channel_id=1, source_target_pairs={{0,4},{4,8},{8,12},{12,0},{1,5},{5,9},{9,13},{13,1},{2,6},{6,10},{... | collective-permute-start | bytes 344072 | tf_op jit(solution)/shard_map/ppermute | solution.py:145
  71.7 21.8 %collective-permute-start.13 = (bf16[64,896]{1,0:T(8,128)(2,1)S(1)}, bf16[64,896]{1,0:T(8,128)(2,1)S(1)}, u32[]{:S(2)}, u32[]{:S(2)}) collective-permute-start(bf16[64,896]{1,0:T(8,128)(2,1)S(1)} %get-tuple-element.23.refs_0_), channel_id=1, source_target_pairs={{0,8},{4,12},{8,0},{12,4},{1,9},{5,13},{9,1},{13,5},{2,10},{6,14},... | collective-permute-start | bytes 344072 | tf_op jit(solution)/shard_map/ppermute | solution.py:145
  79.4 14.0 %collective-permute-start.14 = (bf16[64,896]{1,0:T(8,128)(2,1)S(1)}, bf16[64,896]{1,0:T(8,128)(2,1)S(1)}, u32[]{:S(2)}, u32[]{:S(2)}) collective-permute-start(bf16[64,896]{1,0:T(8,128)(2,1)S(1)} %get-tuple-element.23.refs_0_), channel_id=1, source_target_pairs={{0,12},{4,0},{8,4},{12,8},{1,13},{5,1},{9,5},{13,9},{2,14},{6,2},{... | collective-permute-start | bytes 344072 | tf_op jit(solution)/shard_map/ppermute | solution.py:145
  82.5 17.9 %collective-permute-start.10 = (bf16[64,896]{1,0:T(8,128)(2,1)S(1)}, bf16[64,896]{1,0:T(8,128)(2,1)S(1)}, u32[]{:S(2)}, u32[]{:S(2)}) collective-permute-start(bf16[64,896]{1,0:T(8,128)(2,1)S(1)} %get-tuple-element.24.refs_0_), channel_id=1, source_target_pairs={{0,8},{4,12},{8,0},{12,4},{1,9},{5,13},{9,1},{13,5},{2,10},{6,14},... | collective-permute-start | bytes 344072 | tf_op jit(solution)/shard_map/ppermute | solution.py:145
  84.5 15.9 %collective-permute-start.11 = (bf16[64,896]{1,0:T(8,128)(2,1)S(1)}, bf16[64,896]{1,0:T(8,128)(2,1)S(1)}, u32[]{:S(2)}, u32[]{:S(2)}) collective-permute-start(bf16[64,896]{1,0:T(8,128)(2,1)S(1)} %get-tuple-element.24.refs_0_), channel_id=1, source_target_pairs={{0,12},{4,0},{8,4},{12,8},{1,13},{5,1},{9,5},{13,9},{2,14},{6,2},{... | collective-permute-start | bytes 344072 | tf_op jit(solution)/shard_map/ppermute | solution.py:145
  92.4 8.0 %collective-permute-start.9 = (bf16[64,896]{1,0:T(8,128)(2,1)S(1)}, bf16[64,896]{1,0:T(8,128)(2,1)S(1)}, u32[]{:S(2)}, u32[]{:S(2)}) collective-permute-start(bf16[64,896]{1,0:T(8,128)(2,1)S(1)} %get-tuple-element.24.refs_0_), channel_id=1, source_target_pairs={{0,4},{4,8},{8,12},{12,0},{1,5},{5,9},{9,13},{13,1},{2,6},{6,10},{... | collective-permute-start | bytes 344072 | tf_op jit(solution)/shard_map/ppermute | solution.py:145

commit v2 on v1

v2 whole, which is shorter than its diff:
```python
import functools

import jax
import jax.numpy as jnp
from jax import lax
from jax.experimental import pallas as pl
from jax.experimental.pallas import tpu as pltpu
from jax.sharding import PartitionSpec as P

EPS = 1e-05
VMEM = 48 * 1024 * 1024


def block_of(size, limit):
    tiles = size // 128
    best = 1
    for count in range(1, tiles + 1):
        if tiles % count == 0 and count * 128 <= limit:
            best = count
    return best * 128


def chunks_of(size, limit):
    tiles = size // 128
    return max(count for count in range(1, limit + 1) if tiles % count == 0)


def over_count(values, count):
    if count & (count - 1) == 0:
        return values * (1.0 / count)
    return values / count


def standardize(values):
    count = values.shape[0]
    mean = over_count(jnp.sum(values, axis=0, keepdims=True), count)
    centred = values - mean
    var = over_count(jnp.sum(centred * centred, axis=0, keepdims=True), count)
    return (centred * lax.rsqrt(var + EPS)).astype(jnp.bfloat16)


def cut_kernel(n_fa, n_fb, a_ref, b_ref, a_out, b_out):
    tok = a_ref.shape[0]
    width_a, width_b = a_out.shape[1], b_out.shape[1]
    for i in range(n_fa):
        a_out[pl.ds(i * tok, tok), :] = a_ref[:, pl.ds(i * width_a, width_a)]
    for j in range(n_fb):
        b_out[pl.ds(j * tok, tok), :] = b_ref[:, pl.ds(j * width_b, width_b)]


def cut_panels(a_acts, b_acts, n_fa, n_fb):
    tok, width = a_acts.shape
    return pl.pallas_call(
        functools.partial(cut_kernel, n_fa, n_fb),
        out_shape=[
            jax.ShapeDtypeStruct((tok * n_fa, width // n_fa), a_acts.dtype),
            jax.ShapeDtypeStruct((tok * n_fb, width // n_fb), b_acts.dtype),
        ],
        compiler_params=pltpu.CompilerParams(vmem_limit_bytes=VMEM),
        name="cut_panels",
    )(a_acts, b_acts)


def standardize_a_kernel(n_fa, n_fb, *refs):
    groups, out, rows = refs[:n_fb], refs[-2], refs[-1]
    tok = groups[0].shape[0] // n_fa
    fb = lax.axis_index("fb")
    for step, (even, odd) in enumerate(zip(groups[0::2], groups[1::2])):
        for core, ref in enumerate((even, odd)):
            source = lax.rem(fb + n_fb - 2 * step, n_fb)
            if core:
                source = source + 1 - 2 * lax.rem(source, 2)
            for i in range(n_fa):
                place = pl.multiple_of((source + i * n_fb) * tok, tok)
                rows[pl.ds(place, tok), :] = ref[pl.ds(i * tok, tok), :].astype(jnp.float32)
    out[...] = standardize(rows[...]).T


def standardize_a(groups, n_fa, n_fb):
    rows, width = groups[0].shape
    block = block_of(width, 512)
    total = rows * n_fb
    return pl.pallas_call(
        functools.partial(standardize_a_kernel, n_fa, n_fb),
        out_shape=jax.ShapeDtypeStruct((width, total), jnp.bfloat16),
        grid=(width // block,),
        in_specs=[pl.BlockSpec((rows, block), lambda i: (0, i))] * n_fb,
        out_specs=pl.BlockSpec((block, total), lambda i: (i, 0)),
        scratch_shapes=[pltpu.VMEM((total, block), jnp.float32)],
        compiler_params=pltpu.CompilerParams(vmem_limit_bytes=VMEM),
        cost_estimate=pl.CostEstimate(
            flops=10 * width * total, bytes_accessed=4 * width * total, transcendentals=0
        ),
        name="standardize_a",
    )(*groups)


def product_kernel(n_fa, a_ref, *refs):
    groups = refs[:n_fa]
    out, rows, std = refs[-3], refs[-2], refs[-1]
    size = groups[0].shape[0]
    total = std.shape[0]

    @pl.when(pl.program_id(0) == 0)
    def _():
        fa = lax.axis_index("fa")
        for step in range(n_fa):
            place = pl.multiple_of(lax.rem(fa + n_fa - step, n_fa) * size, size)
            rows[pl.ds(place, size), :] = groups[step][...].astype(jnp.float32)
        std[...] = standardize(rows[...])

    product = jnp.dot(a_ref[...], std[...], preferred_element_type=jnp.float32)
    out[...] = over_count(product, total)


def product_chunk(std_a, groups, n_fa, chunk, n_chunks, buffer):
    height, total = std_a.shape
    rows, width = groups[0].shape
    block = block_of(height, 512)
    in_specs = [pl.BlockSpec((block, total), lambda i: (i, 0))]
    in_specs += [pl.BlockSpec((rows, width), lambda i: (0, 0))] * n_fa
    args = [std_a, *groups]
    aliases = {}
    if buffer is not None:
        aliases = {len(args): 0}
        in_specs.append(pl.BlockSpec(memory_space=pl.ANY))
        args.append(buffer)
    return pl.pallas_call(
        functools.partial(product_kernel, n_fa),
        out_shape=jax.ShapeDtypeStruct((height, width * n_chunks), jnp.float32),
        grid=(height // block,),
        in_specs=in_specs,
        out_specs=pl.BlockSpec((block, width), lambda i: (i, chunk)),
        scratch_shapes=[pltpu.VMEM((total, width), jnp.float32), pltpu.VMEM((total, width), jnp.bfloat16)],
        input_output_aliases=aliases,
        compiler_params=pltpu.CompilerParams(vmem_limit_bytes=VMEM),
        cost_estimate=pl.CostEstimate(
            flops=2 * height * width * total, bytes_accessed=4 * height * width, transcendentals=0
        ),
        name="product_chunk",
    )(*args)


def shifted(x, axis, step):
    size = lax.axis_size(axis)
    return lax.ppermute(x, axis, [(i, (i + step) % size) for i in range(size)])


def swapped(x, axis):
    return lax.ppermute(x, axis, [(i, i ^ 1) for i in range(lax.axis_size(axis))])


def per_device(a_acts, b_acts):
    n_fa = lax.axis_size("fa")
    n_fb = lax.axis_size("fb")
    panels_a, panels_b = cut_panels(a_acts, b_acts, n_fa, n_fb)
    group_a = lax.all_to_all(panels_a, "fa", split_axis=0, concat_axis=0, tiled=True)
    group_b = lax.all_to_all(panels_b, "fb", split_axis=0, concat_axis=0, tiled=True)
    width = group_b.shape[1]
    n_chunks = chunks_of(width, 4)
    step = width // n_chunks
    same_core = [group_a] + [shifted(group_a, "fb", 2 * s) for s in range(1, n_fb // 2)]
    all_a = []
    for block in same_core:
        all_a += [block, swapped(block, "fb")]
    std_a = standardize_a(all_a, n_fa, n_fb)
    buffer = None
    for chunk in range(n_chunks):
        part = group_b[:, chunk * step : (chunk + 1) * step]
        groups = [part] + [shifted(part, "fa", s) for s in range(1, n_fa)]
        buffer = product_chunk(std_a, groups, n_fa, chunk, n_chunks, buffer)
    return buffer


def solution(mesh):
    placed = (P(("layers", "fa", "fb"), None), P(("layers", "fa", "fb"), None))
    return jax.shard_map(
        per_device, mesh=mesh, in_specs=placed, out_specs=P(("layers", "fa"), "fb"), check_vma=False
    )
```

time: 108 us -> 91.6 us (0.85)
  Pallas kernels: 58.8 us -> 31.3 us
  blocking collectives: 0 us -> 19.2 us
  starting transfers between devices: 34.9 us -> 27.7 us
    pallas_call x6, Pallas kernels: 58.8 us -> 31.3 us  [the longest x4 28.2 us: product_chunk(): pl.pallas_call(functools.partial(product_kernel, n_fa), out_shape=jax.Sha...]
    all_to_all x0 -> x1, blocking collectives: none -> 19.2 us  [per_device(): lax.all_to_all(panels_a, 'fa', split_axis=0, concat_axis=0, tiled=True)]
    ppermute x21 -> x13, starting transfers between devices: 34.9 us -> 23.8 us  [shifted(): return lax.ppermute(x, axis, [(i, (i + step) % size) for i in range(size)])]
    ppermute x21 -> x13, waiting for transfers between devices: 11.6 us -> 8.05 us  [shifted(): return lax.ppermute(x, axis, [(i, (i + step) % size) for i in range(size)])]
    all_to_all x0 -> x1, starting transfers between devices: none -> 3.47 us  [per_device(): lax.all_to_all(panels_b, 'fb', split_axis=0, concat_axis=0, tiled=True)]
    all_to_all x0 -> x1, waiting for transfers between devices: none -> 2.88 us  [per_device(): lax.all_to_all(panels_b, 'fb', split_axis=0, concat_axis=0, tiled=True)]
  transfers between devices with their start and end apart: 21 -> 16, of which waited for: 3 -> 2; matrix products, arithmetic and copies ran while one was open for 2% -> 0% of each run, Pallas kernels for 21% -> 26%
where the time goes in v2:
time: 91.6 us; the launch traced here: 91.3 us
  Pallas kernels  31.3 us (34%)
  starting transfers between devices  27.7 us (30%)
  blocking collectives  19.2 us (21%)
  waiting for transfers between devices  10.9 us (12%)
  local copies, waits for them, and re-layouts  2.08 us (2%)
    pallas_call x4, Pallas kernels, product_chunk(): pl.pallas_call(functools.partial(product_kernel, n_fa), out_shape=jax.Sha...  28.2 us
    ppermute x13, starting transfers between devices, shifted(): return lax.ppermute(x, axis, [(i, (i + step) % size) for i in range(size)])  23.8 us
    all_to_all x1, blocking collectives, per_device(): lax.all_to_all(panels_a, 'fa', split_axis=0, concat_axis=0, tiled=True)  19.2 us
    ppermute x13, waiting for transfers between devices, shifted(): return lax.ppermute(x, axis, [(i, (i + step) % size) for i in range(size)])  8.05 us
    all_to_all x1, starting transfers between devices, per_device(): lax.all_to_all(panels_b, 'fb', split_axis=0, concat_axis=0, tiled=True)  3.47 us
    all_to_all x1, waiting for transfers between devices, per_device(): lax.all_to_all(panels_b, 'fb', split_axis=0, concat_axis=0, tiled=True)  2.88 us
    pallas_call x1, Pallas kernels, standardize_a(): pl.pallas_call(functools.partial(standardize_a_kernel, n_fa, n_fb), out_s...  2.3 us
    unnamed x4, local copies, waits for them, and re-layouts  2.04 us
  transfers between devices with their start and end apart: 16, of which 2 were waited for; matrix products, arithmetic and copies ran while one was open for 0% of the time, Pallas kernels for 26%

profile of v2, /device:TPU:0, one launch (start us, length us, event | category | flops | bytes accessed | tf_op | source)
XLA Modules:
  0.0 91.3 jit_solution(14723474409727946561)
XLA Ops:
  0.0 0.0 copy-start
  0.0 1.0 %copy-done = bf16[16,14336]{1,0:T(8,128)(2,1)S(1)} copy-done((bf16[16,14336]{1,0:T(8,128)(2,1)S(1)}, bf16[16,14336]{1,0:T(8,128)(2,1)}, u32[]{:S(2)}) %copy-start) | copy-done | bytes 458776
  1.0 0.0 copy-start.1
  1.0 1.0 %copy-done.1 = bf16[16,14336]{1,0:T(8,128)(2,1)S(1)} copy-done((bf16[16,14336]{1,0:T(8,128)(2,1)S(1)}, bf16[16,14336]{1,0:T(8,128)(2,1)}, u32[]{:S(2)}) %copy-start.1) | copy-done | bytes 458776
  2.0 0.8 cut_panels.1
  2.9 19.2 %all_to_all.23 = bf16[4,16,3584]{2,1,0:T(8,128)(2,1)S(1)} all-to-all(bf16[4,16,3584]{2,1,0:T(8,128)(2,1)S(1)} %bitcast.7), channel_id=1, replica_groups=mesh['layers'=2,'fa'=4,'fb'=4] {'fa'}, dimensions={0} | all-to-all | bytes 917504 | tf_op jit(solution)/shard_map/all_to_all | solution.py:157
  22.1 1.5 %collective-permute-start.1 = (bf16[64,3584]{1,0:T(8,128)(2,1)S(1)}, bf16[64,3584]{1,0:T(8,128)(2,1)S(1)}, u32[]{:S(2)}, u32[]{:S(2)}) collective-permute-start(bf16[64,3584]{1,0:T(8,128)(2,1)S(1)} %bitcast.4), channel_id=1, source_target_pairs={{0,2},{1,3},{2,0},{3,1},{4,6},{5,7},{6,4},{7,5},{8,10},{9,11},{10,... | collective-permute-start | bytes 1376264 | tf_op jit(solution)/shard_map/ppermute | solution.py:146
  23.5 3.5 %all-to-all-start.1 = ((bf16[4,16,3584]{2,1,0:T(8,128)(2,1)}), bf16[4,16,3584]{2,1,0:T(8,128)(2,1)S(1)}, u32[]{:S(2)}, u32[]{:S(2)}) async-start(bf16[4,16,3584]{2,1,0:T(8,128)(2,1)} %bitcast.2), calls=%async_computation.1 | async-start | bytes 917504 | tf_op jit(solution)/shard_map/all_to_all | solution.py:158
  27.0 0.5 collective-permute-start
  27.5 8.0 %collective-permute-done.1.refs_2_ = bf16[64,3584]{1,0:T(8,128)(2,1)S(1)} collective-permute-done((bf16[64,3584]{1,0:T(8,128)(2,1)S(1)}, bf16[64,3584]{1,0:T(8,128)(2,1)S(1)}, u32[]{:S(2)}, u32[]{:S(2)}) %collective-permute-start.1) | collective-permute-done | bytes 458784 | tf_op jit(solution)/shard_map/ppermute | solution.py:146
  35.5 0.0 collective-permute-start.2
  35.5 2.9 %all-to-all-done.1 = bf16[4,16,3584]{2,1,0:T(8,128)(2,1)S(1)} async-done(((bf16[4,16,3584]{2,1,0:T(8,128)(2,1)}), bf16[4,16,3584]{2,1,0:T(8,128)(2,1)S(1)}, u32[]{:S(2)}, u32[]{:S(2)}) %all-to-all-start.1) | async-done | bytes 458784 | tf_op jit(solution)/shard_map/all_to_all | solution.py:158
  38.4 0.2 collective-permute-start.12
  38.6 2.0 %collective-permute-start.13 = (bf16[64,896]{1,0:T(8,128)(2,1)S(1)}, bf16[64,896]{1,0:T(8,128)(2,1)S(1)}, u32[]{:S(2)}, u32[]{:S(2)}) collective-permute-start(bf16[64,896]{1,0:T(8,128)(2,1)S(1)} %get-tuple-element.9.refs_0_), channel_id=1, source_target_pairs={{0,8},{4,12},{8,0},{12,4},{1,9},{5,13},{9,1},{13,5},{2,10},{6,14},... | collective-permute-start | bytes 344072 | tf_op jit(solution)/shard_map/ppermute | solution.py:146
  40.6 1.7 %collective-permute-start.14 = (bf16[64,896]{1,0:T(8,128)(2,1)S(1)}, bf16[64,896]{1,0:T(8,128)(2,1)S(1)}, u32[]{:S(2)}, u32[]{:S(2)}) collective-permute-start(bf16[64,896]{1,0:T(8,128)(2,1)S(1)} %get-tuple-element.9.refs_0_), channel_id=1, source_target_pairs={{0,12},{4,0},{8,4},{12,8},{1,13},{5,1},{9,5},{13,9},{2,14},{6,2},{... | collective-permute-start | bytes 344072 | tf_op jit(solution)/shard_map/ppermute | solution.py:146
  42.3 0.0 collective-permute-done.refs_1_
  42.3 2.0 %collective-permute-start.10 = (bf16[64,896]{1,0:T(8,128)(2,1)S(1)}, bf16[64,896]{1,0:T(8,128)(2,1)S(1)}, u32[]{:S(2)}, u32[]{:S(2)}) collective-permute-start(bf16[64,896]{1,0:T(8,128)(2,1)S(1)} %get-tuple-element.10.refs_0_), channel_id=1, source_target_pairs={{0,8},{4,12},{8,0},{12,4},{1,9},{5,13},{9,1},{13,5},{2,10},{6,14},... | collective-permute-start | bytes 344072 | tf_op jit(solution)/shard_map/ppermute | solution.py:146
  44.4 0.0 collective-permute-done.2.refs_3_
  44.4 0.9 collective-permute-start.11
  45.3 2.3 %standardize_a.1.a_ref = bf16[3584,256]{1,0:T(8,128)(2,1)S(1)} custom-call(bf16[64,3584]{1,0:T(8,128)(2,1)S(1)} %bitcast.6, bf16[64,3584]{1,0:T(8,128)(2,1)S(1)} %collective-permute-done.refs_1_, bf16[64,3584]{1,0:T(8,128)(2,1)S(1)} %collective-permute-done.1.refs_2_, bf16[64,3584]{1,0:T(8,128)(2,1)S(1)} %collective-permute-done.2.refs_3_), custom_call_target="tpu_custom_call" | custom-call | flops 9175040 | bytes 3670016 | tf_op jit(solution)/shard_map/standardize_a/pallas_call | solution.py:83
  47.6 0.0 collective-permute-done.12.refs_1_
  47.6 3.9 %collective-permute-start.9 = (bf16[64,896]{1,0:T(8,128)(2,1)S(1)}, bf16[64,896]{1,0:T(8,128)(2,1)S(1)}, u32[]{:S(2)}, u32[]{:S(2)}) collective-permute-start(bf16[64,896]{1,0:T(8,128)(2,1)S(1)} %get-tuple-element.10.refs_0_), channel_id=1, source_target_pairs={{0,4},{4,8},{8,12},{12,0},{1,5},{5,9},{9,13},{13,1},{2,6},{6,10},{... | collective-permute-start | bytes 344072 | tf_op jit(solution)/shard_map/ppermute | solution.py:146
  51.5 0.0 collective-permute-done.13.refs_2_
  51.5 3.6 %collective-permute-start.6 = (bf16[64,896]{1,0:T(8,128)(2,1)S(1)}, bf16[64,896]{1,0:T(8,128)(2,1)S(1)}, u32[]{:S(2)}, u32[]{:S(2)}) collective-permute-start(bf16[64,896]{1,0:T(8,128)(2,1)S(1)} %get-tuple-element.11.refs_0_), channel_id=1, source_target_pairs={{0,4},{4,8},{8,12},{12,0},{1,5},{5,9},{9,13},{13,1},{2,6},{6,10},{... | collective-permute-start | bytes 344072 | tf_op jit(solution)/shard_map/ppermute | solution.py:146
  55.2 0.0 collective-permute-done.14.refs_3_
  55.2 3.4 %collective-permute-start.7 = (bf16[64,896]{1,0:T(8,128)(2,1)S(1)}, bf16[64,896]{1,0:T(8,128)(2,1)S(1)}, u32[]{:S(2)}, u32[]{:S(2)}) collective-permute-start(bf16[64,896]{1,0:T(8,128)(2,1)S(1)} %get-tuple-element.11.refs_0_), channel_id=1, source_target_pairs={{0,8},{4,12},{8,0},{12,4},{1,9},{5,13},{9,1},{13,5},{2,10},{6,14},... | collective-permute-start | bytes 344072 | tf_op jit(solution)/shard_map/ppermute | solution.py:146
  58.6 7.0 %product_chunk.4.refs_4_ = f32[3584,3584]{1,0:T(8,128)} custom-call(bf16[3584,256]{1,0:T(8,128)(2,1)S(1)} %standardize_a.1.a_ref, bf16[64,896]{1,0:T(8,128)(2,1)S(1)} %get-tuple-element.9.refs_0_, bf16[64,896]{1,0:T(8,128)(2,1)S(1)} %collective-permute-done.12.refs_1_, bf16[64,896]{1,0:T(8,128)(2,1)S(1)} %collective-permute-done.13.refs_2_, ...), custom_call_target="tpu_custom_call" | custom-call | flops 1644167168 | bytes 12845056 | tf_op jit(solution)/shard_map/product_chunk/pallas_call | solution.py:128
  65.6 0.0 collective-permute-done.10.refs_2_
  65.7 0.0 collective-permute-start.8
  65.7 0.0 collective-permute-done.11.refs_3_
  65.7 2.0 %collective-permute-start.3 = (bf16[64,896]{1,0:T(8,128)(2,1)S(1)}, bf16[64,896]{1,0:T(8,128)(2,1)S(1)}, u32[]{:S(2)}, u32[]{:S(2)}) collective-permute-start(bf16[64,896]{1,0:T(8,128)(2,1)S(1)} %get-tuple-element.12.refs_0_), channel_id=1, source_target_pairs={{0,4},{4,8},{8,12},{12,0},{1,5},{5,9},{9,13},{13,1},{2,6},{6,10},{... | collective-permute-start | bytes 344072 | tf_op jit(solution)/shard_map/ppermute | solution.py:146
  67.7 0.0 collective-permute-done.9.refs_1_
  67.7 0.0 collective-permute-start.4
  67.7 7.0 %product_chunk.5.refs_4_ = f32[3584,3584]{1,0:T(8,128)} custom-call(bf16[3584,256]{1,0:T(8,128)(2,1)S(1)} %standardize_a.1.a_ref, bf16[64,896]{1,0:T(8,128)(2,1)S(1)} %get-tuple-element.10.refs_0_, bf16[64,896]{1,0:T(8,128)(2,1)S(1)} %collective-permute-done.9.refs_1_, ...), custom_call_target="tpu_custom_call", output_to_operand_aliasing={{}: (5, {})} | custom-call | flops 1644167168 | bytes 12845056 | tf_op jit(solution)/shard_map/product_chunk/pallas_call | solution.py:128
  74.7 0.0 collective-permute-done.6.refs_1_
  74.7 2.4 %collective-permute-start.5 = (bf16[64,896]{1,0:T(8,128)(2,1)S(1)}, bf16[64,896]{1,0:T(8,128)(2,1)S(1)}, u32[]{:S(2)}, u32[]{:S(2)}) collective-permute-start(bf16[64,896]{1,0:T(8,128)(2,1)S(1)} %get-tuple-element.12.refs_0_), channel_id=1, source_target_pairs={{0,12},{4,0},{8,4},{12,8},{1,13},{5,1},{9,5},{13,9},{2,14},{6,2},{... | collective-permute-start | bytes 344072 | tf_op jit(solution)/shard_map/ppermute | solution.py:146
  77.2 0.0 collective-permute-done.7.refs_2_
  77.2 0.0 collective-permute-done.8.refs_3_
  77.2 7.0 %product_chunk.6.refs_4_ = f32[3584,3584]{1,0:T(8,128)} custom-call(bf16[3584,256]{1,0:T(8,128)(2,1)S(1)} %standardize_a.1.a_ref, bf16[64,896]{1,0:T(8,128)(2,1)S(1)} %get-tuple-element.11.refs_0_, bf16[64,896]{1,0:T(8,128)(2,1)S(1)} %collective-permute-done.6.refs_1_, ...), custom_call_target="tpu_custom_call", output_to_operand_aliasing={{}: (5, {})} | custom-call | flops 1644167168 | bytes 12845056 | tf_op jit(solution)/shard_map/product_chunk/pallas_call | solution.py:128
  84.2 0.0 collective-permute-done.3.refs_1_
  84.2 0.0 collective-permute-done.4.refs_2_
  84.2 0.0 collective-permute-done.5.refs_3_
  84.2 7.1 %product_chunk.7 = f32[3584,3584]{1,0:T(8,128)} custom-call(bf16[3584,256]{1,0:T(8,128)(2,1)S(1)} %standardize_a.1.a_ref, bf16[64,896]{1,0:T(8,128)(2,1)S(1)} %get-tuple-element.12.refs_0_, bf16[64,896]{1,0:T(8,128)(2,1)S(1)} %collective-permute-done.3.refs_1_, bf16[64,896]{1,0:T(8,128)(2,1)S(1)} %collective-permute-done.4.refs_2_, ...), custom_call_target="tpu_custom_call", output_to_operand_aliasing={{}: (5, {})} | custom-call | flops 1644167168 | bytes 12845056 | tf_op jit(solution)/shard_map/product_chunk/pallas_call | solution.py:128
  (1 shorter events, 0.0 us)
Async XLA Ops:
  0.0 1.0 %copy-start = (bf16[16,14336]{1,0:T(8,128)(2,1)S(1)}, bf16[16,14336]{1,0:T(8,128)(2,1)}, u32[]{:S(2)}) copy-start(bf16[16,14336]{1,0:T(8,128)(2,1)} %a_ref.1) | copy-start | bytes 1376260
  1.0 1.0 %copy-start.1 = (bf16[16,14336]{1,0:T(8,128)(2,1)S(1)}, bf16[16,14336]{1,0:T(8,128)(2,1)}, u32[]{:S(2)}) copy-start(bf16[16,14336]{1,0:T(8,128)(2,1)} %b_ref.1) | copy-start | bytes 1376260
  22.1 13.5 %collective-permute-start.1 = (bf16[64,3584]{1,0:T(8,128)(2,1)S(1)}, bf16[64,3584]{1,0:T(8,128)(2,1)S(1)}, u32[]{:S(2)}, u32[]{:S(2)}) collective-permute-start(bf16[64,3584]{1,0:T(8,128)(2,1)S(1)} %bitcast.4), channel_id=1, source_target_pairs={{0,2},{1,3},{2,0},{3,1},{4,6},{5,7},{6,4},{7,5},{8,10},{9,11},{10,... | collective-permute-start | bytes 1376264 | tf_op jit(solution)/shard_map/ppermute | solution.py:146
  23.5 14.8 %all-to-all-start.1 = ((bf16[4,16,3584]{2,1,0:T(8,128)(2,1)}), bf16[4,16,3584]{2,1,0:T(8,128)(2,1)S(1)}, u32[]{:S(2)}, u32[]{:S(2)}) async-start(bf16[4,16,3584]{2,1,0:T(8,128)(2,1)} %bitcast.2), calls=%async_computation.1 | async-start | bytes 917504 | tf_op jit(solution)/shard_map/all_to_all | solution.py:158
  27.0 15.3 %collective-permute-start = (bf16[64,3584]{1,0:T(8,128)(2,1)S(1)}, bf16[64,3584]{1,0:T(8,128)(2,1)S(1)}, u32[]{:S(2)}, u32[]{:S(2)}) collective-permute-start(bf16[64,3584]{1,0:T(8,128)(2,1)S(1)} %bitcast.5), channel_id=1, source_target_pairs={{0,1},{1,0},{2,3},{3,2},{4,5},{5,4},{6,7},{7,6},{8,9},{9,8},{10,11... | collective-permute-start | bytes 1376264 | tf_op jit(solution)/shard_map/ppermute | solution.py:150
  35.5 8.8 %collective-permute-start.2 = (bf16[64,3584]{1,0:T(8,128)(2,1)S(1)}, bf16[64,3584]{1,0:T(8,128)(2,1)S(1)}, u32[]{:S(2)}, u32[]{:S(2)}) collective-permute-start(bf16[64,3584]{1,0:T(8,128)(2,1)S(1)} %collective-permute-done.1.refs_2_), channel_id=1, source_target_pairs={{0,1},{1,0},{2,3},{3,2},{4,5},{5,4},{6,7},{7,6},{8,9},{9,8},{10,11... | collective-permute-start | bytes 1376264 | tf_op jit(solution)/shard_map/ppermute | solution.py:150
  38.4 9.1 %collective-permute-start.12 = (bf16[64,896]{1,0:T(8,128)(2,1)S(1)}, bf16[64,896]{1,0:T(8,128)(2,1)S(1)}, u32[]{:S(2)}, u32[]{:S(2)}) collective-permute-start(bf16[64,896]{1,0:T(8,128)(2,1)S(1)} %get-tuple-element.9.refs_0_), channel_id=1, source_target_pairs={{0,4},{4,8},{8,12},{12,0},{1,5},{5,9},{9,13},{13,1},{2,6},{6,10},{... | collective-permute-start | bytes 344072 | tf_op jit(solution)/shard_map/ppermute | solution.py:146
  38.6 12.9 %collective-permute-start.13 = (bf16[64,896]{1,0:T(8,128)(2,1)S(1)}, bf16[64,896]{1,0:T(8,128)(2,1)S(1)}, u32[]{:S(2)}, u32[]{:S(2)}) collective-permute-start(bf16[64,896]{1,0:T(8,128)(2,1)S(1)} %get-tuple-element.9.refs_0_), channel_id=1, source_target_pairs={{0,8},{4,12},{8,0},{12,4},{1,9},{5,13},{9,1},{13,5},{2,10},{6,14},... | collective-permute-start | bytes 344072 | tf_op jit(solution)/shard_map/ppermute | solution.py:146
  40.6 14.6 %collective-permute-start.14 = (bf16[64,896]{1,0:T(8,128)(2,1)S(1)}, bf16[64,896]{1,0:T(8,128)(2,1)S(1)}, u32[]{:S(2)}, u32[]{:S(2)}) collective-permute-start(bf16[64,896]{1,0:T(8,128)(2,1)S(1)} %get-tuple-element.9.refs_0_), channel_id=1, source_target_pairs={{0,12},{4,0},{8,4},{12,8},{1,13},{5,1},{9,5},{13,9},{2,14},{6,2},{... | collective-permute-start | bytes 344072 | tf_op jit(solution)/shard_map/ppermute | solution.py:146
  42.3 23.3 %collective-permute-start.10 = (bf16[64,896]{1,0:T(8,128)(2,1)S(1)}, bf16[64,896]{1,0:T(8,128)(2,1)S(1)}, u32[]{:S(2)}, u32[]{:S(2)}) collective-permute-start(bf16[64,896]{1,0:T(8,128)(2,1)S(1)} %get-tuple-element.10.refs_0_), channel_id=1, source_target_pairs={{0,8},{4,12},{8,0},{12,4},{1,9},{5,13},{9,1},{13,5},{2,10},{6,14},... | collective-permute-start | bytes 344072 | tf_op jit(solution)/shard_map/ppermute | solution.py:146
  44.4 21.3 %collective-permute-start.11 = (bf16[64,896]{1,0:T(8,128)(2,1)S(1)}, bf16[64,896]{1,0:T(8,128)(2,1)S(1)}, u32[]{:S(2)}, u32[]{:S(2)}) collective-permute-start(bf16[64,896]{1,0:T(8,128)(2,1)S(1)} %get-tuple-element.10.refs_0_), channel_id=1, source_target_pairs={{0,12},{4,0},{8,4},{12,8},{1,13},{5,1},{9,5},{13,9},{2,14},{6,2},{... | collective-permute-start | bytes 344072 | tf_op jit(solution)/shard_map/ppermute | solution.py:146
  47.6 20.1 %collective-permute-start.9 = (bf16[64,896]{1,0:T(8,128)(2,1)S(1)}, bf16[64,896]{1,0:T(8,128)(2,1)S(1)}, u32[]{:S(2)}, u32[]{:S(2)}) collective-permute-start(bf16[64,896]{1,0:T(8,128)(2,1)S(1)} %get-tuple-element.10.refs_0_), channel_id=1, source_target_pairs={{0,4},{4,8},{8,12},{12,0},{1,5},{5,9},{9,13},{13,1},{2,6},{6,10},{... | collective-permute-start | bytes 344072 | tf_op jit(solution)/shard_map/ppermute | solution.py:146
  51.5 23.2 %collective-permute-start.6 = (bf16[64,896]{1,0:T(8,128)(2,1)S(1)}, bf16[64,896]{1,0:T(8,128)(2,1)S(1)}, u32[]{:S(2)}, u32[]{:S(2)}) collective-permute-start(bf16[64,896]{1,0:T(8,128)(2,1)S(1)} %get-tuple-element.11.refs_0_), channel_id=1, source_target_pairs={{0,4},{4,8},{8,12},{12,0},{1,5},{5,9},{9,13},{13,1},{2,6},{6,10},{... | collective-permute-start | bytes 344072 | tf_op jit(solution)/shard_map/ppermute | solution.py:146
  55.2 22.0 %collective-permute-start.7 = (bf16[64,896]{1,0:T(8,128)(2,1)S(1)}, bf16[64,896]{1,0:T(8,128)(2,1)S(1)}, u32[]{:S(2)}, u32[]{:S(2)}) collective-permute-start(bf16[64,896]{1,0:T(8,128)(2,1)S(1)} %get-tuple-element.11.refs_0_), channel_id=1, source_target_pairs={{0,8},{4,12},{8,0},{12,4},{1,9},{5,13},{9,1},{13,5},{2,10},{6,14},... | collective-permute-start | bytes 344072 | tf_op jit(solution)/shard_map/ppermute | solution.py:146
  65.7 11.5 %collective-permute-start.8 = (bf16[64,896]{1,0:T(8,128)(2,1)S(1)}, bf16[64,896]{1,0:T(8,128)(2,1)S(1)}, u32[]{:S(2)}, u32[]{:S(2)}) collective-permute-start(bf16[64,896]{1,0:T(8,128)(2,1)S(1)} %get-tuple-element.11.refs_0_), channel_id=1, source_target_pairs={{0,12},{4,0},{8,4},{12,8},{1,13},{5,1},{9,5},{13,9},{2,14},{6,2},{... | collective-permute-start | bytes 344072 | tf_op jit(solution)/shard_map/ppermute | solution.py:146
  65.7 18.5 %collective-permute-start.3 = (bf16[64,896]{1,0:T(8,128)(2,1)S(1)}, bf16[64,896]{1,0:T(8,128)(2,1)S(1)}, u32[]{:S(2)}, u32[]{:S(2)}) collective-permute-start(bf16[64,896]{1,0:T(8,128)(2,1)S(1)} %get-tuple-element.12.refs_0_), channel_id=1, source_target_pairs={{0,4},{4,8},{8,12},{12,0},{1,5},{5,9},{9,13},{13,1},{2,6},{6,10},{... | collective-permute-start | bytes 344072 | tf_op jit(solution)/shard_map/ppermute | solution.py:146
  67.7 16.5 %collective-permute-start.4 = (bf16[64,896]{1,0:T(8,128)(2,1)S(1)}, bf16[64,896]{1,0:T(8,128)(2,1)S(1)}, u32[]{:S(2)}, u32[]{:S(2)}) collective-permute-start(bf16[64,896]{1,0:T(8,128)(2,1)S(1)} %get-tuple-element.12.refs_0_), channel_id=1, source_target_pairs={{0,8},{4,12},{8,0},{12,4},{1,9},{5,13},{9,1},{13,5},{2,10},{6,14},... | collective-permute-start | bytes 344072 | tf_op jit(solution)/shard_map/ppermute | solution.py:146
  74.7 9.5 %collective-permute-start.5 = (bf16[64,896]{1,0:T(8,128)(2,1)S(1)}, bf16[64,896]{1,0:T(8,128)(2,1)S(1)}, u32[]{:S(2)}, u32[]{:S(2)}) collective-permute-start(bf16[64,896]{1,0:T(8,128)(2,1)S(1)} %get-tuple-element.12.refs_0_), channel_id=1, source_target_pairs={{0,12},{4,0},{8,4},{12,8},{1,13},{5,1},{9,5},{13,9},{2,14},{6,2},{... | collective-permute-start | bytes 344072 | tf_op jit(solution)/shard_map/ppermute | solution.py:146

commit v3 on v1

v3 whole, which is shorter than its diff:
```python
import functools

import jax
import jax.numpy as jnp
from jax import lax
from jax.experimental import pallas as pl
from jax.experimental.pallas import tpu as pltpu
from jax.sharding import PartitionSpec as P

EPS = 1e-05
VMEM = 48 * 1024 * 1024


def block_of(size, limit):
    tiles = size // 128
    best = 1
    for count in range(1, tiles + 1):
        if tiles % count == 0 and count * 128 <= limit:
            best = count
    return best * 128


def chunk_widths(width, shares):
    unit = 256 if width % 256 == 0 else 128
    tiles = width // unit
    ends = [round(tiles * sum(shares[: k + 1]) / sum(shares)) for k in range(len(shares))]
    counts = [end - start for start, end in zip([0] + ends, ends)]
    return [count * unit for count in counts if count > 0]


def over_count(values, count):
    if count & (count - 1) == 0:
        return values * (1.0 / count)
    return values / count


def standardize(values):
    count = values.shape[0]
    mean = over_count(jnp.sum(values, axis=0, keepdims=True), count)
    centred = values - mean
    var = over_count(jnp.sum(centred * centred, axis=0, keepdims=True), count)
    return (centred * lax.rsqrt(var + EPS)).astype(jnp.bfloat16)


def cut_kernel(n_fa, n_fb, a_ref, b_ref, *refs):
    outs, sems = refs[:-1], refs[-1]
    width_a = a_ref.shape[1] // n_fa
    width_b = b_ref.shape[1] // n_fb
    fa = lax.axis_index("fa")
    fb = lax.axis_index("fb")
    copies = []
    for step in range(n_fa):
        start = pl.multiple_of(lax.rem(fa + step, n_fa) * width_a, 128)
        copies.append((a_ref.at[:, pl.ds(start, width_a)], outs[step]))
    for step in range(n_fb):
        start = pl.multiple_of(lax.rem(fb + step, n_fb) * width_b, 128)
        copies.append((b_ref.at[:, pl.ds(start, width_b)], outs[n_fa + step]))
    started = []
    for place, (src, dst) in enumerate(copies):
        copy = pltpu.make_async_copy(src, dst, sems.at[place])
        copy.start()
        started.append(copy)
    for copy in started:
        copy.wait()


def cut_panels(a_acts, b_acts, n_fa, n_fb):
    tok, width = a_acts.shape
    shapes = [jax.ShapeDtypeStruct((tok, width // n_fa), a_acts.dtype)] * n_fa
    shapes += [jax.ShapeDtypeStruct((tok, width // n_fb), b_acts.dtype)] * n_fb
    outs = pl.pallas_call(
        functools.partial(cut_kernel, n_fa, n_fb),
        out_shape=shapes,
        in_specs=[pl.BlockSpec(memory_space=pl.ANY)] * 2,
        out_specs=[pl.BlockSpec(memory_space=pltpu.VMEM)] * len(shapes),
        scratch_shapes=[pltpu.SemaphoreType.DMA((len(shapes),))],
        compiler_params=pltpu.CompilerParams(vmem_limit_bytes=VMEM),
        name="cut_panels",
    )(a_acts, b_acts)
    return outs[:n_fa], outs[n_fa:]


def join_kernel(n_in, n_out, *refs):
    tok = refs[0].shape[0]
    column = 0
    for out in refs[-n_out:]:
        width = out.shape[1]
        for i in range(n_in):
            out[pl.ds(i * tok, tok), :] = refs[i][:, pl.ds(column, width)]
        column += width


def join_rows(pieces, widths, after=()):
    rows = pieces[0].shape[0] * len(pieces)
    return pl.pallas_call(
        functools.partial(join_kernel, len(pieces), len(widths)),
        out_shape=[jax.ShapeDtypeStruct((rows, width), pieces[0].dtype) for width in widths],
        in_specs=[pl.BlockSpec(memory_space=pltpu.VMEM)] * len(pieces)
        + [pl.BlockSpec(memory_space=pl.ANY)] * len(after),
        out_specs=[pl.BlockSpec(memory_space=pltpu.VMEM)] * len(widths),
        compiler_params=pltpu.CompilerParams(vmem_limit_bytes=VMEM),
        name="join_rows",
    )(*pieces, *after)


def standardize_a_kernel(n_fa, n_fb, *refs):
    groups, out, rows = refs[:n_fb], refs[-2], refs[-1]
    tok = groups[0].shape[0] // n_fa
    odd = lax.rem(lax.axis_index("fb"), 2)
    for place, ref in enumerate(groups):
        back = place if place % 2 == 0 else lax.rem(place - 2 + 2 * odd + n_fb, n_fb)
        for i in range(n_fa):
            row = (i * n_fb + back) * tok
            if place % 2:
                row = pl.multiple_of(row, tok)
            rows[pl.ds(row, tok), :] = ref[pl.ds(i * tok, tok), :].astype(jnp.float32)
    out[...] = standardize(rows[...]).T


def standardize_a(groups, n_fa, n_fb):
    rows, width = groups[0].shape
    block = block_of(width, 512)
    total = rows * n_fb
    return pl.pallas_call(
        functools.partial(standardize_a_kernel, n_fa, n_fb),
        out_shape=jax.ShapeDtypeStruct((width, total), jnp.bfloat16),
        grid=(width // block,),
        in_specs=[pl.BlockSpec((rows, block), lambda i: (0, i))] * n_fb,
        out_specs=pl.BlockSpec((block, total), lambda i: (i, 0)),
        scratch_shapes=[pltpu.VMEM((total, block), jnp.float32)],
        compiler_params=pltpu.CompilerParams(vmem_limit_bytes=VMEM),
        cost_estimate=pl.CostEstimate(
            flops=10 * width * total, bytes_accessed=4 * width * total, transcendentals=0
        ),
        name="standardize_a",
    )(*groups)


def product_kernel(n_fa, column, a_ref, *refs):
    groups = refs[:n_fa]
    out, std, slots, sems = refs[-4:]
    total, width = std.shape
    n_slots, block = slots.shape[0], slots.shape[1]
    steps = a_ref.shape[0] // block

    @pl.loop(0, width // 128)
    def _(strip):
        columns = pl.ds(pl.multiple_of(strip * 128, 128), 128)
        values = jnp.concatenate([ref[:, columns].astype(jnp.float32) for ref in groups], axis=0)
        std[:, columns] = standardize(values)

    def copy_of(step):
        slot = lax.rem(step, n_slots)
        place = pl.multiple_of(step * block, block)
        return pltpu.make_async_copy(
            slots.at[slot], out.at[pl.ds(place, block), pl.ds(column, width)], sems.at[slot]
        )

    @pl.loop(0, steps)
    def _(step):
        @pl.when(step >= n_slots)
        def _():
            copy_of(step - n_slots).wait()

        place = pl.multiple_of(step * block, block)
        product = jnp.dot(a_ref[pl.ds(place, block), :], std[...], preferred_element_type=jnp.float32)
        slots[lax.rem(step, n_slots)] = over_count(product, total)
        copy_of(step).start()

    @pl.loop(max(steps - n_slots, 0), steps)
    def _(step):
        copy_of(step).wait()


def product_chunk(std_a, groups, column, full_width, buffer):
    height, total = std_a.shape
    width = groups[0].shape[1]
    block = block_of(height, 512)
    in_specs = [pl.BlockSpec(memory_space=pltpu.VMEM)] * (1 + len(groups))
    args = [std_a, *groups]
    aliases = {}
    if buffer is not None:
        aliases = {len(args): 0}
        in_specs.append(pl.BlockSpec(memory_space=pl.ANY))
        args.append(buffer)
    return pl.pallas_call(
        functools.partial(product_kernel, len(groups), column),
        out_shape=jax.ShapeDtypeStruct((height, full_width), jnp.float32),
        in_specs=in_specs,
        out_specs=pl.BlockSpec(memory_space=pl.ANY),
        scratch_shapes=[
            pltpu.VMEM((total, width), jnp.bfloat16),
            pltpu.VMEM((4, block, width), jnp.float32),
            pltpu.SemaphoreType.DMA((4,)),
        ],
        input_output_aliases=aliases,
        compiler_params=pltpu.CompilerParams(vmem_limit_bytes=VMEM),
        cost_estimate=pl.CostEstimate(
            flops=2 * height * width * total, bytes_accessed=4 * height * width, transcendentals=0
        ),
        name="product_chunk",
    )(*args)


def shifted(x, axis, step):
    size = lax.axis_size(axis)
    return lax.ppermute(x, axis, [(i, (i + step) % size) for i in range(size)])


def swapped(x, axis):
    return lax.ppermute(x, axis, [(i, i ^ 1) for i in range(lax.axis_size(axis))])


def per_device(a_acts, b_acts):
    n_fa = lax.axis_size("fa")
    n_fb = lax.axis_size("fb")
    panels_a, panels_b = cut_panels(a_acts, b_acts, n_fa, n_fb)
    own_a = [panels_a[0]] + [shifted(panels_a[s], "fa", s) for s in range(1, n_fa)]
    own_b = [panels_b[0]] + [shifted(panels_b[s], "fb", s) for s in range(1, n_fb)]
    full_width = panels_b[0].shape[1]
    widths = chunk_widths(full_width, (6, 5, 3))
    parts_b = join_rows(own_b, widths)
    group_a = join_rows(own_a, [panels_a[0].shape[1]], parts_b[-1:])[0]
    same_core = [group_a] + [shifted(group_a, "fb", 2 * s) for s in range(1, n_fb // 2)]
    all_a = []
    for block in same_core:
        all_a += [block, swapped(block, "fb")]
    std_a = standardize_a(all_a, n_fa, n_fb)
    buffer = None
    column = 0
    for part in parts_b:
        groups = [part] + [shifted(part, "fa", s) for s in range(1, n_fa)]
        buffer = product_chunk(std_a, groups, column, full_width, buffer)
        column += part.shape[1]
    return buffer


def solution(mesh):
    placed = (P(("layers", "fa", "fb"), None), P(("layers", "fa", "fb"), None))
    return jax.shard_map(
        per_device, mesh=mesh, in_specs=placed, out_specs=P(("layers", "fa"), "fb"), check_vma=False
    )
```

time: 108 us -> 85 us (0.79)
  Pallas kernels: 58.8 us -> 25.5 us
  waiting for transfers between devices: 11.6 us -> 23.4 us
  starting transfers between devices: 34.9 us -> 33.8 us
    pallas_call x6 -> x7, Pallas kernels: 58.8 us -> 25.5 us  [the longest x3 22.4 us: product_chunk(): pl.pallas_call(functools.partial(product_kernel, len(groups), column), ou...]
    ppermute x21 -> x16, waiting for transfers between devices: 11.6 us -> 23.4 us  [shifted(): return lax.ppermute(x, axis, [(i, (i + step) % size) for i in range(size)])]
    ppermute x21 -> x16, starting transfers between devices: 34.9 us -> 33.8 us  [shifted(): return lax.ppermute(x, axis, [(i, (i + step) % size) for i in range(size)])]
  transfers between devices with their start and end apart: 21 -> 18, of which waited for: 3 -> 5; matrix products, arithmetic and copies ran while one was open for 2% -> 0% of each run, Pallas kernels for 21% -> 23%
where the time goes in v3:
time: 85 us; the launch traced here: 84.8 us
  starting transfers between devices  33.8 us (40%)
  Pallas kernels  25.5 us (30%)
  waiting for transfers between devices  23.4 us (28%)
  local copies, waits for them, and re-layouts  2.04 us (2%)
    ppermute x16, starting transfers between devices, shifted(): return lax.ppermute(x, axis, [(i, (i + step) % size) for i in range(size)])  33.8 us
    ppermute x16, waiting for transfers between devices, shifted(): return lax.ppermute(x, axis, [(i, (i + step) % size) for i in range(size)])  23.4 us
    pallas_call x3, Pallas kernels, product_chunk(): pl.pallas_call(functools.partial(product_kernel, len(groups), column), ou...  22.4 us
    pallas_call x1, Pallas kernels, standardize_a(): pl.pallas_call(functools.partial(standardize_a_kernel, n_fa, n_fb), out_s...  2.26 us
    unnamed x4, local copies, waits for them, and re-layouts  2.04 us
  transfers between devices with their start and end apart: 18, of which 5 were waited for; matrix products, arithmetic and copies ran while one was open for 0% of the time, Pallas kernels for 23%

profile of v3, /device:TPU:0, one launch (start us, length us, event | category | flops | bytes accessed | tf_op | source)
XLA Modules:
  0.0 84.8 jit_solution(17461755243116688431)
XLA Ops:
  0.0 0.0 copy-start
  0.0 1.0 %copy-done = bf16[16,14336]{1,0:T(8,128)(2,1)S(1)} copy-done((bf16[16,14336]{1,0:T(8,128)(2,1)S(1)}, bf16[16,14336]{1,0:T(8,128)(2,1)}, u32[]{:S(2)}) %copy-start) | copy-done | bytes 458776
  1.0 0.0 copy-start.1
  1.0 1.0 %copy-done.1 = bf16[16,14336]{1,0:T(8,128)(2,1)S(1)} copy-done((bf16[16,14336]{1,0:T(8,128)(2,1)S(1)}, bf16[16,14336]{1,0:T(8,128)(2,1)}, u32[]{:S(2)}) %copy-start.1) | copy-done | bytes 458776
  2.0 0.7 cut_panels.1
  2.8 0.5 collective-permute-start.3
  3.3 2.6 %collective-permute-start.4 = (bf16[16,3584]{1,0:T(8,128)(2,1)S(1)}, bf16[16,3584]{1,0:T(8,128)(2,1)S(1)}, u32[]{:S(2)}, u32[]{:S(2)}) collective-permute-start(bf16[16,3584]{1,0:T(8,128)(2,1)S(1)} %get-tuple-element.22), channel_id=1, source_target_pairs={{0,2},{1,3},{2,0},{3,1},{4,6},{5,7},{6,4},{7,5},{8,10},{9,11},{10,... | collective-permute-start | bytes 344072 | tf_op jit(solution)/shard_map/ppermute | solution.py:207
  5.8 1.4 %collective-permute-start.5 = (bf16[16,3584]{1,0:T(8,128)(2,1)S(1)}, bf16[16,3584]{1,0:T(8,128)(2,1)S(1)}, u32[]{:S(2)}, u32[]{:S(2)}) collective-permute-start(bf16[16,3584]{1,0:T(8,128)(2,1)S(1)} %get-tuple-element.23), channel_id=1, source_target_pairs={{0,3},{1,0},{2,1},{3,2},{4,7},{5,4},{6,5},{7,6},{8,11},{9,8},{10,9... | collective-permute-start | bytes 344072 | tf_op jit(solution)/shard_map/ppermute | solution.py:207
  7.2 1.6 %collective-permute-start = (bf16[16,3584]{1,0:T(8,128)(2,1)S(1)}, bf16[16,3584]{1,0:T(8,128)(2,1)S(1)}, u32[]{:S(2)}, u32[]{:S(2)}) collective-permute-start(bf16[16,3584]{1,0:T(8,128)(2,1)S(1)} %get-tuple-element.17), channel_id=1, source_target_pairs={{0,4},{4,8},{8,12},{12,0},{1,5},{5,9},{9,13},{13,1},{2,6},{6,10},{... | collective-permute-start | bytes 344072 | tf_op jit(solution)/shard_map/ppermute | solution.py:207
  8.8 2.6 %collective-permute-start.1 = (bf16[16,3584]{1,0:T(8,128)(2,1)S(1)}, bf16[16,3584]{1,0:T(8,128)(2,1)S(1)}, u32[]{:S(2)}, u32[]{:S(2)}) collective-permute-start(bf16[16,3584]{1,0:T(8,128)(2,1)S(1)} %get-tuple-element.18), channel_id=1, source_target_pairs={{0,8},{4,12},{8,0},{12,4},{1,9},{5,13},{9,1},{13,5},{2,10},{6,14},... | collective-permute-start | bytes 344072 | tf_op jit(solution)/shard_map/ppermute | solution.py:207
  11.4 0.0 collective-permute-done.3.refs_1_
  11.4 1.3 %collective-permute-start.2 = (bf16[16,3584]{1,0:T(8,128)(2,1)S(1)}, bf16[16,3584]{1,0:T(8,128)(2,1)S(1)}, u32[]{:S(2)}, u32[]{:S(2)}) collective-permute-start(bf16[16,3584]{1,0:T(8,128)(2,1)S(1)} %get-tuple-element.19), channel_id=1, source_target_pairs={{0,12},{4,0},{8,4},{12,8},{1,13},{5,1},{9,5},{13,9},{2,14},{6,2},{... | collective-permute-start | bytes 344072 | tf_op jit(solution)/shard_map/ppermute | solution.py:207
  12.7 0.0 collective-permute-done.4.refs_2_
  12.7 0.0 collective-permute-done.5.refs_3_
  12.8 2.2 %collective-permute-done.refs_1_ = bf16[16,3584]{1,0:T(8,128)(2,1)S(1)} collective-permute-done((bf16[16,3584]{1,0:T(8,128)(2,1)S(1)}, bf16[16,3584]{1,0:T(8,128)(2,1)S(1)}, u32[]{:S(2)}, u32[]{:S(2)}) %collective-permute-start) | collective-permute-done | bytes 114720 | tf_op jit(solution)/shard_map/ppermute | solution.py:207
  15.0 3.3 %collective-permute-done.1.refs_2_ = bf16[16,3584]{1,0:T(8,128)(2,1)S(1)} collective-permute-done((bf16[16,3584]{1,0:T(8,128)(2,1)S(1)}, bf16[16,3584]{1,0:T(8,128)(2,1)S(1)}, u32[]{:S(2)}, u32[]{:S(2)}) %collective-permute-start.1) | collective-permute-done | bytes 114720 | tf_op jit(solution)/shard_map/ppermute | solution.py:207
  18.3 0.3 collective-permute-done.2.refs_3_
  18.6 1.0 %collective-permute-start.7 = (bf16[64,3584]{1,0:T(8,128)(2,1)S(1)}, bf16[64,3584]{1,0:T(8,128)(2,1)S(1)}, u32[]{:S(2)}, u32[]{:S(2)}) collective-permute-start(bf16[64,3584]{1,0:T(8,128)(2,1)S(1)} %join_rows.3.refs_0_), channel_id=1, source_target_pairs={{0,2},{1,3},{2,0},{3,1},{4,6},{5,7},{6,4},{7,5},{8,10},{9,11},{10,... | collective-permute-start | bytes 1376264 | tf_op jit(solution)/shard_map/ppermute | solution.py:207
  19.6 0.0 collective-permute-start.6
  19.7 11.0 %collective-permute-done.7.refs_2_ = bf16[64,3584]{1,0:T(8,128)(2,1)S(1)} collective-permute-done((bf16[64,3584]{1,0:T(8,128)(2,1)S(1)}, bf16[64,3584]{1,0:T(8,128)(2,1)S(1)}, u32[]{:S(2)}, u32[]{:S(2)}) %collective-permute-start.7) | collective-permute-done | bytes 458784 | tf_op jit(solution)/shard_map/ppermute | solution.py:207
  30.7 0.0 collective-permute-start.8
  30.7 3.0 %collective-permute-start.15 = (bf16[64,1536]{1,0:T(8,128)(2,1)S(1)}, bf16[64,1536]{1,0:T(8,128)(2,1)S(1)}, u32[]{:S(2)}, u32[]{:S(2)}) collective-permute-start(bf16[64,1536]{1,0:T(8,128)(2,1)S(1)} %get-tuple-element.26.refs_0_), channel_id=1, source_target_pairs={{0,4},{4,8},{8,12},{12,0},{1,5},{5,9},{9,13},{13,1},{2,6},{6,10},{... | collective-permute-start | bytes 589832 | tf_op jit(solution)/shard_map/ppermute | solution.py:207
  33.7 0.2 collective-permute-start.16
  33.9 2.2 %collective-permute-start.17 = (bf16[64,1536]{1,0:T(8,128)(2,1)S(1)}, bf16[64,1536]{1,0:T(8,128)(2,1)S(1)}, u32[]{:S(2)}, u32[]{:S(2)}) collective-permute-start(bf16[64,1536]{1,0:T(8,128)(2,1)S(1)} %get-tuple-element.26.refs_0_), channel_id=1, source_target_pairs={{0,12},{4,0},{8,4},{12,8},{1,13},{5,1},{9,5},{13,9},{2,14},{6,2},{... | collective-permute-start | bytes 589832 | tf_op jit(solution)/shard_map/ppermute | solution.py:207
  36.1 0.0 collective-permute-done.6.refs_1_
  36.1 0.0 collective-permute-start.12
  36.1 0.0 collective-permute-done.8.refs_3_
  36.1 2.6 %collective-permute-start.13 = (bf16[64,1280]{1,0:T(8,128)(2,1)S(1)}, bf16[64,1280]{1,0:T(8,128)(2,1)S(1)}, u32[]{:S(2)}, u32[]{:S(2)}) collective-permute-start(bf16[64,1280]{1,0:T(8,128)(2,1)S(1)} %get-tuple-element.25.refs_0_), channel_id=1, source_target_pairs={{0,8},{4,12},{8,0},{12,4},{1,9},{5,13},{9,1},{13,5},{2,10},{6,14},... | collective-permute-start | bytes 491528 | tf_op jit(solution)/shard_map/ppermute | solution.py:207
  38.7 2.3 %standardize_a.1.a_ref = bf16[3584,256]{1,0:T(8,128)(2,1)S(1)} custom-call(bf16[64,3584]{1,0:T(8,128)(2,1)S(1)} %join_rows.3.refs_0_, bf16[64,3584]{1,0:T(8,128)(2,1)S(1)} %collective-permute-done.6.refs_1_, bf16[64,3584]{1,0:T(8,128)(2,1)S(1)} %collective-permute-done.7.refs_2_, bf16[64,3584]{1,0:T(8,128)(2,1)S(1)} %collective-permute-done.8.refs_3_), custom_call_target="tpu_custom_call" | custom-call | flops 9175040 | bytes 3670016 | tf_op jit(solution)/shard_map/standardize_a/pallas_call | solution.py:124
  40.9 0.0 collective-permute-done.15.refs_1_
  41.0 1.3 %collective-permute-start.14 = (bf16[64,1280]{1,0:T(8,128)(2,1)S(1)}, bf16[64,1280]{1,0:T(8,128)(2,1)S(1)}, u32[]{:S(2)}, u32[]{:S(2)}) collective-permute-start(bf16[64,1280]{1,0:T(8,128)(2,1)S(1)} %get-tuple-element.25.refs_0_), channel_id=1, source_target_pairs={{0,12},{4,0},{8,4},{12,8},{1,13},{5,1},{9,5},{13,9},{2,14},{6,2},{... | collective-permute-start | bytes 491528 | tf_op jit(solution)/shard_map/ppermute | solution.py:207
  42.3 6.5 %collective-permute-done.16.refs_2_ = bf16[64,1536]{1,0:T(8,128)(2,1)S(1)} collective-permute-done((bf16[64,1536]{1,0:T(8,128)(2,1)S(1)}, bf16[64,1536]{1,0:T(8,128)(2,1)S(1)}, u32[]{:S(2)}, u32[]{:S(2)}) %collective-permute-start.16) | collective-permute-done | bytes 196640 | tf_op jit(solution)/shard_map/ppermute | solution.py:207
  48.8 0.0 collective-permute-start.10
  48.8 0.0 collective-permute-done.17.refs_3_
  48.8 5.7 %collective-permute-start.11 = (bf16[64,768]{1,0:T(8,128)(2,1)S(1)}, bf16[64,768]{1,0:T(8,128)(2,1)S(1)}, u32[]{:S(2)}, u32[]{:S(2)}) collective-permute-start(bf16[64,768]{1,0:T(8,128)(2,1)S(1)} %get-tuple-element.24.refs_4_.refs_0_), channel_id=1, source_target_pairs={{0,12},{4,0},{8,4},{12,8},{1,13},{5,1},{9,5},{13,9},{2,14},{6,2},{... | collective-permute-start | bytes 294920 | tf_op jit(solution)/shard_map/ppermute | solution.py:207
  54.5 9.4 %product_chunk.3.refs_4_ = f32[3584,3584]{1,0:T(8,128)} custom-call(bf16[3584,256]{1,0:T(8,128)(2,1)S(1)} %standardize_a.1.a_ref, bf16[64,1536]{1,0:T(8,128)(2,1)S(1)} %get-tuple-element.26.refs_0_, bf16[64,1536]{1,0:T(8,128)(2,1)S(1)} %collective-permute-done.15.refs_1_, bf16[64,1536]{1,0:T(8,128)(2,1)S(1)} %collective-permute-done.16.refs_2_, ...), custom_call_target="tpu_custom_call" | custom-call | flops 2818572288 | bytes 22020096 | tf_op jit(solution)/shard_map/product_chunk/pallas_call | solution.py:186
  63.9 0.0 collective-permute-done.12.refs_1_
  63.9 7.8 %collective-permute-start.9 = (bf16[64,768]{1,0:T(8,128)(2,1)S(1)}, bf16[64,768]{1,0:T(8,128)(2,1)S(1)}, u32[]{:S(2)}, u32[]{:S(2)}) collective-permute-start(bf16[64,768]{1,0:T(8,128)(2,1)S(1)} %get-tuple-element.24.refs_4_.refs_0_), channel_id=1, source_target_pairs={{0,4},{4,8},{8,12},{12,0},{1,5},{5,9},{9,13},{13,1},{2,6},{6,10},{... | collective-permute-start | bytes 294920 | tf_op jit(solution)/shard_map/ppermute | solution.py:207
  71.7 0.0 collective-permute-done.13.refs_2_
  71.7 0.0 collective-permute-done.14.refs_3_
  71.7 7.9 %product_chunk.4.refs_4_ = f32[3584,3584]{1,0:T(8,128)} custom-call(bf16[3584,256]{1,0:T(8,128)(2,1)S(1)} %standardize_a.1.a_ref, bf16[64,1280]{1,0:T(8,128)(2,1)S(1)} %get-tuple-element.25.refs_0_, bf16[64,1280]{1,0:T(8,128)(2,1)S(1)} %collective-permute-done.12.refs_1_, ...), custom_call_target="tpu_custom_call", output_to_operand_aliasing={{}: (5, {})} | custom-call | flops 2348810240 | bytes 18350080 | tf_op jit(solution)/shard_map/product_chunk/pallas_call | solution.py:186
  79.7 0.0 collective-permute-done.10.refs_2_
  79.7 0.0 collective-permute-done.11.refs_3_
  79.7 0.0 collective-permute-done.9.refs_1_
  79.7 5.1 %product_chunk.5 = f32[3584,3584]{1,0:T(8,128)} custom-call(bf16[3584,256]{1,0:T(8,128)(2,1)S(1)} %standardize_a.1.a_ref, bf16[64,768]{1,0:T(8,128)(2,1)S(1)} %get-tuple-element.24.refs_4_.refs_0_, bf16[64,768]{1,0:T(8,128)(2,1)S(1)} %collective-permute-done.9.refs_1_, ...), custom_call_target="tpu_custom_call", output_to_operand_aliasing={{}: (5, {})} | custom-call | flops 1409286144 | bytes 11010048 | tf_op jit(solution)/shard_map/product_chunk/pallas_call | solution.py:186
  (2 shorter events, 0.1 us)
Async XLA Ops:
  0.0 1.0 %copy-start = (bf16[16,14336]{1,0:T(8,128)(2,1)S(1)}, bf16[16,14336]{1,0:T(8,128)(2,1)}, u32[]{:S(2)}) copy-start(bf16[16,14336]{1,0:T(8,128)(2,1)} %a_ref.1) | copy-start | bytes 1376260
  1.0 1.0 %copy-start.1 = (bf16[16,14336]{1,0:T(8,128)(2,1)S(1)}, bf16[16,14336]{1,0:T(8,128)(2,1)}, u32[]{:S(2)}) copy-start(bf16[16,14336]{1,0:T(8,128)(2,1)} %b_ref.1) | copy-start | bytes 1376260
  2.8 8.6 %collective-permute-start.3 = (bf16[16,3584]{1,0:T(8,128)(2,1)S(1)}, bf16[16,3584]{1,0:T(8,128)(2,1)S(1)}, u32[]{:S(2)}, u32[]{:S(2)}) collective-permute-start(bf16[16,3584]{1,0:T(8,128)(2,1)S(1)} %get-tuple-element.21), channel_id=1, source_target_pairs={{0,1},{1,2},{2,3},{3,0},{4,5},{5,6},{6,7},{7,4},{8,9},{9,10},{10,1... | collective-permute-start | bytes 344072 | tf_op jit(solution)/shard_map/ppermute | solution.py:207
  3.3 9.5 %collective-permute-start.4 = (bf16[16,3584]{1,0:T(8,128)(2,1)S(1)}, bf16[16,3584]{1,0:T(8,128)(2,1)S(1)}, u32[]{:S(2)}, u32[]{:S(2)}) collective-permute-start(bf16[16,3584]{1,0:T(8,128)(2,1)S(1)} %get-tuple-element.22), channel_id=1, source_target_pairs={{0,2},{1,3},{2,0},{3,1},{4,6},{5,7},{6,4},{7,5},{8,10},{9,11},{10,... | collective-permute-start | bytes 344072 | tf_op jit(solution)/shard_map/ppermute | solution.py:207
  5.8 6.9 %collective-permute-start.5 = (bf16[16,3584]{1,0:T(8,128)(2,1)S(1)}, bf16[16,3584]{1,0:T(8,128)(2,1)S(1)}, u32[]{:S(2)}, u32[]{:S(2)}) collective-permute-start(bf16[16,3584]{1,0:T(8,128)(2,1)S(1)} %get-tuple-element.23), channel_id=1, source_target_pairs={{0,3},{1,0},{2,1},{3,2},{4,7},{5,4},{6,5},{7,6},{8,11},{9,8},{10,9... | collective-permute-start | bytes 344072 | tf_op jit(solution)/shard_map/ppermute | solution.py:207
  7.2 7.8 %collective-permute-start = (bf16[16,3584]{1,0:T(8,128)(2,1)S(1)}, bf16[16,3584]{1,0:T(8,128)(2,1)S(1)}, u32[]{:S(2)}, u32[]{:S(2)}) collective-permute-start(bf16[16,3584]{1,0:T(8,128)(2,1)S(1)} %get-tuple-element.17), channel_id=1, source_target_pairs={{0,4},{4,8},{8,12},{12,0},{1,5},{5,9},{9,13},{13,1},{2,6},{6,10},{... | collective-permute-start | bytes 344072 | tf_op jit(solution)/shard_map/ppermute | solution.py:207
  8.8 9.5 %collective-permute-start.1 = (bf16[16,3584]{1,0:T(8,128)(2,1)S(1)}, bf16[16,3584]{1,0:T(8,128)(2,1)S(1)}, u32[]{:S(2)}, u32[]{:S(2)}) collective-permute-start(bf16[16,3584]{1,0:T(8,128)(2,1)S(1)} %get-tuple-element.18), channel_id=1, source_target_pairs={{0,8},{4,12},{8,0},{12,4},{1,9},{5,13},{9,1},{13,5},{2,10},{6,14},... | collective-permute-start | bytes 344072 | tf_op jit(solution)/shard_map/ppermute | solution.py:207
  11.4 7.2 %collective-permute-start.2 = (bf16[16,3584]{1,0:T(8,128)(2,1)S(1)}, bf16[16,3584]{1,0:T(8,128)(2,1)S(1)}, u32[]{:S(2)}, u32[]{:S(2)}) collective-permute-start(bf16[16,3584]{1,0:T(8,128)(2,1)S(1)} %get-tuple-element.19), channel_id=1, source_target_pairs={{0,12},{4,0},{8,4},{12,8},{1,13},{5,1},{9,5},{13,9},{2,14},{6,2},{... | collective-permute-start | bytes 344072 | tf_op jit(solution)/shard_map/ppermute | solution.py:207
  18.6 12.1 %collective-permute-start.7 = (bf16[64,3584]{1,0:T(8,128)(2,1)S(1)}, bf16[64,3584]{1,0:T(8,128)(2,1)S(1)}, u32[]{:S(2)}, u32[]{:S(2)}) collective-permute-start(bf16[64,3584]{1,0:T(8,128)(2,1)S(1)} %join_rows.3.refs_0_), channel_id=1, source_target_pairs={{0,2},{1,3},{2,0},{3,1},{4,6},{5,7},{6,4},{7,5},{8,10},{9,11},{10,... | collective-permute-start | bytes 1376264 | tf_op jit(solution)/shard_map/ppermute | solution.py:207
  19.6 16.4 %collective-permute-start.6 = (bf16[64,3584]{1,0:T(8,128)(2,1)S(1)}, bf16[64,3584]{1,0:T(8,128)(2,1)S(1)}, u32[]{:S(2)}, u32[]{:S(2)}) collective-permute-start(bf16[64,3584]{1,0:T(8,128)(2,1)S(1)} %join_rows.3.refs_0_), channel_id=1, source_target_pairs={{0,1},{1,0},{2,3},{3,2},{4,5},{5,4},{6,7},{7,6},{8,9},{9,8},{10,11... | collective-permute-start | bytes 1376264 | tf_op jit(solution)/shard_map/ppermute | solution.py:211
  30.7 5.4 %collective-permute-start.8 = (bf16[64,3584]{1,0:T(8,128)(2,1)S(1)}, bf16[64,3584]{1,0:T(8,128)(2,1)S(1)}, u32[]{:S(2)}, u32[]{:S(2)}) collective-permute-start(bf16[64,3584]{1,0:T(8,128)(2,1)S(1)} %collective-permute-done.7.refs_2_), channel_id=1, source_target_pairs={{0,1},{1,0},{2,3},{3,2},{4,5},{5,4},{6,7},{7,6},{8,9},{9,8},{10,11... | collective-permute-start | bytes 1376264 | tf_op jit(solution)/shard_map/ppermute | solution.py:211
  30.7 10.3 %collective-permute-start.15 = (bf16[64,1536]{1,0:T(8,128)(2,1)S(1)}, bf16[64,1536]{1,0:T(8,128)(2,1)S(1)}, u32[]{:S(2)}, u32[]{:S(2)}) collective-permute-start(bf16[64,1536]{1,0:T(8,128)(2,1)S(1)} %get-tuple-element.26.refs_0_), channel_id=1, source_target_pairs={{0,4},{4,8},{8,12},{12,0},{1,5},{5,9},{9,13},{13,1},{2,6},{6,10},{... | collective-permute-start | bytes 589832 | tf_op jit(solution)/shard_map/ppermute | solution.py:207
  33.7 15.1 %collective-permute-start.16 = (bf16[64,1536]{1,0:T(8,128)(2,1)S(1)}, bf16[64,1536]{1,0:T(8,128)(2,1)S(1)}, u32[]{:S(2)}, u32[]{:S(2)}) collective-permute-start(bf16[64,1536]{1,0:T(8,128)(2,1)S(1)} %get-tuple-element.26.refs_0_), channel_id=1, source_target_pairs={{0,8},{4,12},{8,0},{12,4},{1,9},{5,13},{9,1},{13,5},{2,10},{6,14},... | collective-permute-start | bytes 589832 | tf_op jit(solution)/shard_map/ppermute | solution.py:207
  33.9 14.9 %collective-permute-start.17 = (bf16[64,1536]{1,0:T(8,128)(2,1)S(1)}, bf16[64,1536]{1,0:T(8,128)(2,1)S(1)}, u32[]{:S(2)}, u32[]{:S(2)}) collective-permute-start(bf16[64,1536]{1,0:T(8,128)(2,1)S(1)} %get-tuple-element.26.refs_0_), channel_id=1, source_target_pairs={{0,12},{4,0},{8,4},{12,8},{1,13},{5,1},{9,5},{13,9},{2,14},{6,2},{... | collective-permute-start | bytes 589832 | tf_op jit(solution)/shard_map/ppermute | solution.py:207
  36.1 27.8 %collective-permute-start.12 = (bf16[64,1280]{1,0:T(8,128)(2,1)S(1)}, bf16[64,1280]{1,0:T(8,128)(2,1)S(1)}, u32[]{:S(2)}, u32[]{:S(2)}) collective-permute-start(bf16[64,1280]{1,0:T(8,128)(2,1)S(1)} %get-tuple-element.25.refs_0_), channel_id=1, source_target_pairs={{0,4},{4,8},{8,12},{12,0},{1,5},{5,9},{9,13},{13,1},{2,6},{6,10},{... | collective-permute-start | bytes 491528 | tf_op jit(solution)/shard_map/ppermute | solution.py:207
  36.1 35.6 %collective-permute-start.13 = (bf16[64,1280]{1,0:T(8,128)(2,1)S(1)}, bf16[64,1280]{1,0:T(8,128)(2,1)S(1)}, u32[]{:S(2)}, u32[]{:S(2)}) collective-permute-start(bf16[64,1280]{1,0:T(8,128)(2,1)S(1)} %get-tuple-element.25.refs_0_), channel_id=1, source_target_pairs={{0,8},{4,12},{8,0},{12,4},{1,9},{5,13},{9,1},{13,5},{2,10},{6,14},... | collective-permute-start | bytes 491528 | tf_op jit(solution)/shard_map/ppermute | solution.py:207
  41.0 30.8 %collective-permute-start.14 = (bf16[64,1280]{1,0:T(8,128)(2,1)S(1)}, bf16[64,1280]{1,0:T(8,128)(2,1)S(1)}, u32[]{:S(2)}, u32[]{:S(2)}) collective-permute-start(bf16[64,1280]{1,0:T(8,128)(2,1)S(1)} %get-tuple-element.25.refs_0_), channel_id=1, source_target_pairs={{0,12},{4,0},{8,4},{12,8},{1,13},{5,1},{9,5},{13,9},{2,14},{6,2},{... | collective-permute-start | bytes 491528 | tf_op jit(solution)/shard_map/ppermute | solution.py:207
  48.8 30.9 %collective-permute-start.10 = (bf16[64,768]{1,0:T(8,128)(2,1)S(1)}, bf16[64,768]{1,0:T(8,128)(2,1)S(1)}, u32[]{:S(2)}, u32[]{:S(2)}) collective-permute-start(bf16[64,768]{1,0:T(8,128)(2,1)S(1)} %get-tuple-element.24.refs_4_.refs_0_), channel_id=1, source_target_pairs={{0,8},{4,12},{8,0},{12,4},{1,9},{5,13},{9,1},{13,5},{2,10},{6,14},... | collective-permute-start | bytes 294920 | tf_op jit(solution)/shard_map/ppermute | solution.py:207
  48.8 30.9 %collective-permute-start.11 = (bf16[64,768]{1,0:T(8,128)(2,1)S(1)}, bf16[64,768]{1,0:T(8,128)(2,1)S(1)}, u32[]{:S(2)}, u32[]{:S(2)}) collective-permute-start(bf16[64,768]{1,0:T(8,128)(2,1)S(1)} %get-tuple-element.24.refs_4_.refs_0_), channel_id=1, source_target_pairs={{0,12},{4,0},{8,4},{12,8},{1,13},{5,1},{9,5},{13,9},{2,14},{6,2},{... | collective-permute-start | bytes 294920 | tf_op jit(solution)/shard_map/ppermute | solution.py:207
  63.9 15.8 %collective-permute-start.9 = (bf16[64,768]{1,0:T(8,128)(2,1)S(1)}, bf16[64,768]{1,0:T(8,128)(2,1)S(1)}, u32[]{:S(2)}, u32[]{:S(2)}) collective-permute-start(bf16[64,768]{1,0:T(8,128)(2,1)S(1)} %get-tuple-element.24.refs_4_.refs_0_), channel_id=1, source_target_pairs={{0,4},{4,8},{8,12},{12,0},{1,5},{5,9},{9,13},{13,1},{2,6},{6,10},{... | collective-permute-start | bytes 294920 | tf_op jit(solution)/shard_map/ppermute | solution.py:207

commit v4 on v3

--- a/solution.py
+++ b/solution.py
@@ -80,39 +80,61 @@
     return outs[:n_fa], outs[n_fa:]
 
 
-def join_kernel(n_in, n_out, *refs):
-    tok = refs[0].shape[0]
-    column = 0
-    for out in refs[-n_out:]:
-        width = out.shape[1]
-        for i in range(n_in):
-            out[pl.ds(i * tok, tok), :] = refs[i][:, pl.ds(column, width)]
-        column += width
-
-
-def join_rows(pieces, widths, after=()):
-    rows = pieces[0].shape[0] * len(pieces)
+def join_kernel(shapes, *refs):
+    n_in = sum(len_in for len_in, _ in shapes)
+    n_out = sum(len_out for _, len_out in shapes)
+    ins, outs = refs[:n_in], refs[-n_out:]
+    for len_in, len_out in shapes:
+        tok = ins[0].shape[0]
+        column = 0
+        for out in outs[:len_out]:
+            width = out.shape[1]
+            for i in range(len_in):
+                out[pl.ds(i * tok, tok), :] = ins[i][:, pl.ds(column, width)]
+            column += width
+        ins, outs = ins[len_in:], outs[len_out:]
+
+
+def join_rows(groups, after=()):
+    pieces = [piece for group, _ in groups for piece in group]
+    shapes = [
+        jax.ShapeDtypeStruct((group[0].shape[0] * len(group), width), group[0].dtype)
+        for group, widths in groups
+        for width in widths
+    ]
     return pl.pallas_call(
-        functools.partial(join_kernel, len(pieces), len(widths)),
-        out_shape=[jax.ShapeDtypeStruct((rows, width), pieces[0].dtype) for width in widths],
+        functools.partial(join_kernel, [(len(group), len(widths)) for group, widths in groups]),
+        out_shape=shapes,
         in_specs=[pl.BlockSpec(memory_space=pltpu.VMEM)] * len(pieces)
         + [pl.BlockSpec(memory_space=pl.ANY)] * len(after),
-        out_specs=[pl.BlockSpec(memory_space=pltpu.VMEM)] * len(widths),
+        out_specs=[pl.BlockSpec(memory_space=pltpu.VMEM)] * len(shapes),
         compiler_params=pltpu.CompilerParams(vmem_limit_bytes=VMEM),
         name="join_rows",
     )(*pieces, *after)
+
+
+def stacked(pieces, after=()):
+    return join_rows([(pieces, [pieces[0].shape[1]])], after)[0]
+
+
+def order_of(source, fa, n_fa):
+    if n_fa != 4:
+        return lax.rem(fa + n_fa - source, n_fa)
+    neighbour = fa + 1 - 2 * lax.rem(fa, 2)
+    outer = jnp.where((source == 0) | (source == n_fa - 1), 3, 2)
+    return jnp.where(source == fa, 0, jnp.where(source == neighbour, 1, outer))
 
 
 def standardize_a_kernel(n_fa, n_fb, *refs):
     groups, out, rows = refs[:n_fb], refs[-2], refs[-1]
     tok = groups[0].shape[0] // n_fa
+    fa = lax.axis_index("fa")
     odd = lax.rem(lax.axis_index("fb"), 2)
+    places = [order_of(lax.rem(fa + n_fa - i, n_fa), fa, n_fa) for i in range(n_fa)]
     for place, ref in enumerate(groups):
         back = place if place % 2 == 0 else lax.rem(place - 2 + 2 * odd + n_fb, n_fb)
         for i in range(n_fa):
-            row = (i * n_fb + back) * tok
-            if place % 2:
-                row = pl.multiple_of(row, tok)
+            row = pl.multiple_of((places[i] * n_fb + back) * tok, tok)
             rows[pl.ds(row, tok), :] = ref[pl.ds(i * tok, tok), :].astype(jnp.float32)
     out[...] = standardize(rows[...]).T
 
@@ -136,46 +158,48 @@
     )(*groups)
 
 
-def product_kernel(n_fa, column, a_ref, *refs):
-    groups = refs[:n_fa]
+def product_kernel(n_groups, relayed, column, a_ref, *refs):
+    groups = refs[:n_groups]
     out, std, slots, sems = refs[-4:]
     total, width = std.shape
-    n_slots, block = slots.shape[0], slots.shape[1]
-    steps = a_ref.shape[0] // block
-
-    @pl.loop(0, width // 128)
-    def _(strip):
-        columns = pl.ds(pl.multiple_of(strip * 128, 128), 128)
-        values = jnp.concatenate([ref[:, columns].astype(jnp.float32) for ref in groups], axis=0)
-        std[:, columns] = standardize(values)
+    n_slots, height, strip = slots.shape
+    fa = lax.axis_index("fa")
+    at_end = (fa == 0) | (fa == 3)
 
     def copy_of(step):
         slot = lax.rem(step, n_slots)
-        place = pl.multiple_of(step * block, block)
-        return pltpu.make_async_copy(
-            slots.at[slot], out.at[pl.ds(place, block), pl.ds(column, width)], sems.at[slot]
-        )
-
-    @pl.loop(0, steps)
+        place = pl.multiple_of(column + step * strip, 128)
+        return pltpu.make_async_copy(slots.at[slot], out.at[:, pl.ds(place, strip)], sems.at[slot])
+
+    @pl.loop(0, width // 128)
+    def _(step):
+        columns = pl.ds(pl.multiple_of(step * 128, 128), 128)
+        pieces = [ref[:, columns].astype(jnp.float32) for ref in groups]
+        if relayed:
+            pieces = [pieces[0], jnp.where(at_end, pieces[2], pieces[1])]
+        std[:, columns] = standardize(jnp.concatenate(pieces, axis=0))
+
+    @pl.loop(0, width // strip)
     def _(step):
         @pl.when(step >= n_slots)
         def _():
             copy_of(step - n_slots).wait()
 
-        place = pl.multiple_of(step * block, block)
-        product = jnp.dot(a_ref[pl.ds(place, block), :], std[...], preferred_element_type=jnp.float32)
+        columns = pl.ds(pl.multiple_of(step * strip, 128), strip)
+        product = jnp.dot(a_ref[...], std[:, columns], preferred_element_type=jnp.float32)
         slots[lax.rem(step, n_slots)] = over_count(product, total)
         copy_of(step).start()
 
-    @pl.loop(max(steps - n_slots, 0), steps)
+    @pl.loop(max(width // strip - n_slots, 0), width // strip)
     def _(step):
         copy_of(step).wait()
 
 
-def product_chunk(std_a, groups, column, full_width, buffer):
+def product_chunk(std_a, groups, relayed, column, full_width, buffer):
     height, total = std_a.shape
     width = groups[0].shape[1]
-    block = block_of(height, 512)
+    strip = 256 if width % 256 == 0 else 128
+    n_slots = 4
     in_specs = [pl.BlockSpec(memory_space=pltpu.VMEM)] * (1 + len(groups))
     args = [std_a, *groups]
     aliases = {}
@@ -184,14 +208,14 @@
         in_specs.append(pl.BlockSpec(memory_space=pl.ANY))
         args.append(buffer)
     return pl.pallas_call(
-        functools.partial(product_kernel, len(groups), column),
+        functools.partial(product_kernel, len(groups), relayed, column),
         out_shape=jax.ShapeDtypeStruct((height, full_width), jnp.float32),
         in_specs=in_specs,
         out_specs=pl.BlockSpec(memory_space=pl.ANY),
         scratch_shapes=[
             pltpu.VMEM((total, width), jnp.bfloat16),
-            pltpu.VMEM((4, block, width), jnp.float32),
-            pltpu.SemaphoreType.DMA((4,)),
+            pltpu.VMEM((n_slots, height, strip), jnp.float32),
+            pltpu.SemaphoreType.DMA((n_slots,)),
         ],
         input_output_aliases=aliases,
         compiler_params=pltpu.CompilerParams(vmem_limit_bytes=VMEM),
@@ -214,24 +238,35 @@
 def per_device(a_acts, b_acts):
     n_fa = lax.axis_size("fa")
     n_fb = lax.axis_size("fb")
+    relayed = n_fa == 4
     panels_a, panels_b = cut_panels(a_acts, b_acts, n_fa, n_fb)
     own_a = [panels_a[0]] + [shifted(panels_a[s], "fa", s) for s in range(1, n_fa)]
     own_b = [panels_b[0]] + [shifted(panels_b[s], "fb", s) for s in range(1, n_fb)]
     full_width = panels_b[0].shape[1]
-    widths = chunk_widths(full_width, (6, 5, 3))
-    parts_b = join_rows(own_b, widths)
-    group_a = join_rows(own_a, [panels_a[0].shape[1]], parts_b[-1:])[0]
-    same_core = [group_a] + [shifted(group_a, "fb", 2 * s) for s in range(1, n_fb // 2)]
-    all_a = []
-    for block in same_core:
-        all_a += [block, swapped(block, "fb")]
+    widths = chunk_widths(full_width, (1, 1))
+    group_a, *parts_b = join_rows([(own_a, [panels_a[0].shape[1]]), (own_b, widths)])
+    if relayed:
+        pairs = []
+        for part in parts_b:
+            if pairs:
+                part = stacked([part], pairs[-1:])
+            pairs.append(stacked([part, swapped(part, "fa")]))
+        seconds = [lax.ppermute(pair, "fa", [(0, 0), (1, 2), (2, 1), (3, 3)]) for pair in pairs]
+        chunks = [[pair, second, swapped(second, "fa")] for pair, second in zip(pairs, seconds)]
+        ahead = pairs[:1]
+    else:
+        chunks = [[part] + [shifted(part, "fa", s) for s in range(1, n_fa)] for part in parts_b]
+        ahead = parts_b[:1]
+    all_a = [group_a, swapped(group_a, "fb")]
+    for s in range(1, n_fb // 2):
+        block = shifted(group_a, "fb", 2 * s)
+        all_a += [block, swapped(stacked([block], ahead), "fb")]
     std_a = standardize_a(all_a, n_fa, n_fb)
     buffer = None
     column = 0
-    for part in parts_b:
-        groups = [part] + [shifted(part, "fa", s) for s in range(1, n_fa)]
-        buffer = product_chunk(std_a, groups, column, full_width, buffer)
-        column += part.shape[1]
+    for groups in chunks:
+        buffer = product_chunk(std_a, groups, relayed, column, full_width, buffer)
+        column += groups[0].shape[1]
     return buffer
 
 

time: 85 us -> 77.1 us (0.907)
  waiting for transfers between devices: 23.4 us -> 15.5 us
    ppermute x16 -> x7, starting transfers between devices: 33.8 us -> 10.9 us  [shifted(): return lax.ppermute(x, axis, [(i, (i + step) % size) for i in range(size)])]
    ppermute x2 -> x6, starting transfers between devices: 0.01 us -> 22.1 us  [swapped(): lax.ppermute(x, axis, [(i, i ^ 1) for i in range(lax.axis_size(axis))])]
    ppermute x16 -> x7, waiting for transfers between devices: 23.4 us -> 4.58 us  [shifted(): return lax.ppermute(x, axis, [(i, (i + step) % size) for i in range(size)])]
    ppermute x2 -> x6, waiting for transfers between devices: 0.01 us -> 10.9 us  [swapped(): lax.ppermute(x, axis, [(i, i ^ 1) for i in range(lax.axis_size(axis))])]
    ppermute x0 -> x2, starting transfers between devices: none -> 1.38 us  [per_device(): lax.ppermute(pair, 'fa', [(0, 0), (1, 2), (2, 1), (3, 3)])]
    pallas_call x5 -> x7, Pallas kernels: 22.5 us -> 21.7 us  [the longest x2 21.6 us: product_chunk(): pl.pallas_call(functools.partial(product_kernel, len(groups), relayed, co...]
  transfers between devices with their start and end apart: 18 -> 15, of which waited for: 5 -> 5; matrix products, arithmetic and copies ran while one was open for 0% -> 0% of each run, Pallas kernels for 23% -> 17%
where the time goes in v4:
time: 77.1 us; the launch traced here: 76.9 us
  starting transfers between devices  34.3 us (44%)
  Pallas kernels  24.9 us (32%)
  waiting for transfers between devices  15.5 us (20%)
  local copies, waits for them, and re-layouts  2.04 us (3%)
    ppermute x6, starting transfers between devices, swapped(): lax.ppermute(x, axis, [(i, i ^ 1) for i in range(lax.axis_size(axis))])  22.1 us
    pallas_call x2, Pallas kernels, product_chunk(): pl.pallas_call(functools.partial(product_kernel, len(groups), relayed, co...  21.6 us
    ppermute x6, waiting for transfers between devices, swapped(): lax.ppermute(x, axis, [(i, i ^ 1) for i in range(lax.axis_size(axis))])  10.9 us
    ppermute x7, starting transfers between devices, shifted(): return lax.ppermute(x, axis, [(i, (i + step) % size) for i in range(size)])  10.9 us
    ppermute x7, waiting for transfers between devices, shifted(): return lax.ppermute(x, axis, [(i, (i + step) % size) for i in range(size)])  4.58 us
    pallas_call x1, Pallas kernels, standardize_a(): pl.pallas_call(functools.partial(standardize_a_kernel, n_fa, n_fb), out_s...  2.43 us
    unnamed x4, local copies, waits for them, and re-layouts  2.04 us
  transfers between devices with their start and end apart: 15, of which 5 were waited for; matrix products, arithmetic and copies ran while one was open for 0% of the time, Pallas kernels for 17%

profile of v4, /device:TPU:0, one launch (start us, length us, event | category | flops | bytes accessed | tf_op | source)
XLA Modules:
  0.0 76.9 jit_solution(11869065874687023204)
XLA Ops:
  0.0 0.0 copy-start
  0.0 1.0 %copy-done = bf16[16,14336]{1,0:T(8,128)(2,1)S(1)} copy-done((bf16[16,14336]{1,0:T(8,128)(2,1)S(1)}, bf16[16,14336]{1,0:T(8,128)(2,1)}, u32[]{:S(2)}) %copy-start) | copy-done | bytes 458776
  1.0 0.0 copy-start.1
  1.0 1.0 %copy-done.1 = bf16[16,14336]{1,0:T(8,128)(2,1)S(1)} copy-done((bf16[16,14336]{1,0:T(8,128)(2,1)S(1)}, bf16[16,14336]{1,0:T(8,128)(2,1)}, u32[]{:S(2)}) %copy-start.1) | copy-done | bytes 458776
  2.0 0.7 cut_panels.1
  2.8 3.1 %collective-permute-start = (bf16[16,3584]{1,0:T(8,128)(2,1)S(1)}, bf16[16,3584]{1,0:T(8,128)(2,1)S(1)}, u32[]{:S(2)}, u32[]{:S(2)}) collective-permute-start(bf16[16,3584]{1,0:T(8,128)(2,1)S(1)} %get-tuple-element.17), channel_id=1, source_target_pairs={{0,4},{4,8},{8,12},{12,0},{1,5},{5,9},{9,13},{13,1},{2,6},{6,10},{... | collective-permute-start | bytes 344072 | tf_op jit(solution)/shard_map/ppermute | solution.py:231
  5.8 2.6 %collective-permute-start.1 = (bf16[16,3584]{1,0:T(8,128)(2,1)S(1)}, bf16[16,3584]{1,0:T(8,128)(2,1)S(1)}, u32[]{:S(2)}, u32[]{:S(2)}) collective-permute-start(bf16[16,3584]{1,0:T(8,128)(2,1)S(1)} %get-tuple-element.18), channel_id=1, source_target_pairs={{0,8},{4,12},{8,0},{12,4},{1,9},{5,13},{9,1},{13,5},{2,10},{6,14},... | collective-permute-start | bytes 344072 | tf_op jit(solution)/shard_map/ppermute | solution.py:231
  8.4 1.3 %collective-permute-start.2 = (bf16[16,3584]{1,0:T(8,128)(2,1)S(1)}, bf16[16,3584]{1,0:T(8,128)(2,1)S(1)}, u32[]{:S(2)}, u32[]{:S(2)}) collective-permute-start(bf16[16,3584]{1,0:T(8,128)(2,1)S(1)} %get-tuple-element.19), channel_id=1, source_target_pairs={{0,12},{4,0},{8,4},{12,8},{1,13},{5,1},{9,5},{13,9},{2,14},{6,2},{... | collective-permute-start | bytes 344072 | tf_op jit(solution)/shard_map/ppermute | solution.py:231
  9.8 0.0 collective-permute-start.3
  9.8 1.5 %collective-permute-start.4 = (bf16[16,3584]{1,0:T(8,128)(2,1)S(1)}, bf16[16,3584]{1,0:T(8,128)(2,1)S(1)}, u32[]{:S(2)}, u32[]{:S(2)}) collective-permute-start(bf16[16,3584]{1,0:T(8,128)(2,1)S(1)} %get-tuple-element.22), channel_id=1, source_target_pairs={{0,2},{1,3},{2,0},{3,1},{4,6},{5,7},{6,4},{7,5},{8,10},{9,11},{10,... | collective-permute-start | bytes 344072 | tf_op jit(solution)/shard_map/ppermute | solution.py:231
  11.3 0.6 collective-permute-done.refs_1_
  11.9 0.8 %collective-permute-start.5 = (bf16[16,3584]{1,0:T(8,128)(2,1)S(1)}, bf16[16,3584]{1,0:T(8,128)(2,1)S(1)}, u32[]{:S(2)}, u32[]{:S(2)}) collective-permute-start(bf16[16,3584]{1,0:T(8,128)(2,1)S(1)} %get-tuple-element.23), channel_id=1, source_target_pairs={{0,3},{1,0},{2,1},{3,2},{4,7},{5,4},{6,5},{7,6},{8,11},{9,8},{10,9... | collective-permute-start | bytes 344072 | tf_op jit(solution)/shard_map/ppermute | solution.py:231
  12.7 3.3 %collective-permute-done.1.refs_2_ = bf16[16,3584]{1,0:T(8,128)(2,1)S(1)} collective-permute-done((bf16[16,3584]{1,0:T(8,128)(2,1)S(1)}, bf16[16,3584]{1,0:T(8,128)(2,1)S(1)}, u32[]{:S(2)}, u32[]{:S(2)}) %collective-permute-start.1) | collective-permute-done | bytes 114720 | tf_op jit(solution)/shard_map/ppermute | solution.py:231
  16.0 0.0 collective-permute-done.2.refs_3_
  16.0 0.0 collective-permute-done.3.refs_5_
  16.0 0.0 collective-permute-done.4.refs_6_
  16.0 0.7 collective-permute-done.5.refs_7_
  16.7 0.1 join_rows.5
  16.8 2.3 %collective-permute-start.8 = (bf16[64,1792]{1,0:T(8,128)(2,1)S(1)}, bf16[64,1792]{1,0:T(8,128)(2,1)S(1)}, u32[]{:S(2)}, u32[]{:S(2)}) collective-permute-start(bf16[64,1792]{1,0:T(8,128)(2,1)S(1)} %get-tuple-element.25.refs_0_), channel_id=1, source_target_pairs={{0,4},{4,0},{8,12},{12,8},{1,5},{5,1},{9,13},{13,9},{2,6},{6,2},{1... | collective-permute-start | bytes 688136 | tf_op jit(solution)/shard_map/ppermute | solution.py:235
  19.1 1.5 %collective-permute-start.7 = (bf16[64,3584]{1,0:T(8,128)(2,1)S(1)}, bf16[64,3584]{1,0:T(8,128)(2,1)S(1)}, u32[]{:S(2)}, u32[]{:S(2)}) collective-permute-start(bf16[64,3584]{1,0:T(8,128)(2,1)S(1)} %get-tuple-element.24.refs_0_), channel_id=1, source_target_pairs={{0,2},{1,3},{2,0},{3,1},{4,6},{5,7},{6,4},{7,5},{8,10},{9,11},{10,... | collective-permute-start | bytes 1376264 | tf_op jit(solution)/shard_map/ppermute | solution.py:231
  20.6 4.6 %collective-permute-done.8.refs_1_ = bf16[64,1792]{1,0:T(8,128)(2,1)S(1)} collective-permute-done((bf16[64,1792]{1,0:T(8,128)(2,1)S(1)}, bf16[64,1792]{1,0:T(8,128)(2,1)S(1)}, u32[]{:S(2)}, u32[]{:S(2)}) %collective-permute-start.8) | collective-permute-done | bytes 229408 | tf_op jit(solution)/shard_map/ppermute | solution.py:235
  25.3 0.7 collective-permute-start.13
  26.0 4.7 %collective-permute-start.10 = (bf16[64,1792]{1,0:T(8,128)(2,1)S(1)}, bf16[64,1792]{1,0:T(8,128)(2,1)S(1)}, u32[]{:S(2)}, u32[]{:S(2)}) collective-permute-start(bf16[64,1792]{1,0:T(8,128)(2,1)S(1)} %join_rows.8.refs_0_), channel_id=1, source_target_pairs={{0,4},{4,0},{8,12},{12,8},{1,5},{5,1},{9,13},{13,9},{2,6},{6,2},{1... | collective-permute-start | bytes 688136 | tf_op jit(solution)/shard_map/ppermute | solution.py:235
  30.7 6.3 %collective-permute-done.10.refs_1_ = bf16[64,1792]{1,0:T(8,128)(2,1)S(1)} collective-permute-done((bf16[64,1792]{1,0:T(8,128)(2,1)S(1)}, bf16[64,1792]{1,0:T(8,128)(2,1)S(1)}, u32[]{:S(2)}, u32[]{:S(2)}) %collective-permute-start.10) | collective-permute-done | bytes 229408 | tf_op jit(solution)/shard_map/ppermute | solution.py:235
  37.0 0.7 collective-permute-start.11
  37.7 0.1 collective-permute-start.6
  37.8 0.0 collective-permute-done.7.refs_0_.refs_2_
  37.9 0.5 collective-permute-start.9
  38.4 0.0 collective-permute-done.13.refs_1_
  38.4 3.7 %collective-permute-start.14 = (bf16[128,1792]{1,0:T(8,128)(2,1)S(1)}, bf16[128,1792]{1,0:T(8,128)(2,1)S(1)}, u32[]{:S(2)}, u32[]{:S(2)}) collective-permute-start(bf16[128,1792]{1,0:T(8,128)(2,1)S(1)} %collective-permute-done.13.refs_1_), channel_id=1, source_target_pairs={{0,4},{4,0},{8,12},{12,8},{1,5},{5,1},{9,13},{13,9},{2,6},{6,2},{1... | collective-permute-start | bytes 1376264 | tf_op jit(solution)/shard_map/ppermute | solution.py:235
  42.1 0.0 collective-permute-done.11.refs_1_
  42.1 10.8 %collective-permute-start.12 = (bf16[128,1792]{1,0:T(8,128)(2,1)S(1)}, bf16[128,1792]{1,0:T(8,128)(2,1)S(1)}, u32[]{:S(2)}, u32[]{:S(2)}) collective-permute-start(bf16[128,1792]{1,0:T(8,128)(2,1)S(1)} %collective-permute-done.11.refs_1_), channel_id=1, source_target_pairs={{0,4},{4,0},{8,12},{12,8},{1,5},{5,1},{9,13},{13,9},{2,6},{6,2},{1... | collective-permute-start | bytes 1376264 | tf_op jit(solution)/shard_map/ppermute | solution.py:235
  52.9 0.0 collective-permute-done.6.refs_1_
  52.9 0.0 collective-permute-done.9.refs_3_
  52.9 2.4 %standardize_a.1.a_ref = bf16[3584,256]{1,0:T(8,128)(2,1)S(1)} custom-call(bf16[64,3584]{1,0:T(8,128)(2,1)S(1)} %get-tuple-element.24.refs_0_, bf16[64,3584]{1,0:T(8,128)(2,1)S(1)} %collective-permute-done.6.refs_1_, bf16[64,3584]{1,0:T(8,128)(2,1)S(1)} %collective-permute-done.7.refs_0_.refs_2_, bf16[64,3584]{1,0:T(8,128)(2,1)S(1)} %collective-permute-done.9.refs_3_), custom_call_target="tpu_custom_call" | custom-call | flops 9175040 | bytes 3670016 | tf_op jit(solution)/shard_map/standardize_a/pallas_call | solution.py:146
  55.3 0.0 collective-permute-done.14.refs_2_
  55.3 10.8 %product_chunk.2.refs_3_ = f32[3584,3584]{1,0:T(8,128)} custom-call(bf16[3584,256]{1,0:T(8,128)(2,1)S(1)} %standardize_a.1.a_ref, bf16[128,1792]{1,0:T(8,128)(2,1)S(1)} %join_rows.6.refs_1_.refs_0_, bf16[128,1792]{1,0:T(8,128)(2,1)S(1)} %collective-permute-done.13.refs_1_, bf16[128,1792]{1,0:T(8,128)(2,1)S(1)} %collective-permute-done.14.refs_2_), custom_call_target="tpu_custom_call" | custom-call | flops 3288334336 | bytes 25690112 | tf_op jit(solution)/shard_map/product_chunk/pallas_call | solution.py:210
  66.1 0.0 collective-permute-done.12.refs_2_
  66.1 10.8 %product_chunk.3 = f32[3584,3584]{1,0:T(8,128)} custom-call(bf16[3584,256]{1,0:T(8,128)(2,1)S(1)} %standardize_a.1.a_ref, bf16[128,1792]{1,0:T(8,128)(2,1)S(1)} %join_rows.9.refs_0_, bf16[128,1792]{1,0:T(8,128)(2,1)S(1)} %collective-permute-done.11.refs_1_, bf16[128,1792]{1,0:T(8,128)(2,1)S(1)} %collective-permute-done.12.refs_2_, ...), custom_call_target="tpu_custom_call", output_to_operand_aliasing={{}: (4, {})} | custom-call | flops 3288334336 | bytes 25690112 | tf_op jit(solution)/shard_map/product_chunk/pallas_call | solution.py:210
  (4 shorter events, 0.1 us)
Async XLA Ops:
  0.0 1.0 %copy-start = (bf16[16,14336]{1,0:T(8,128)(2,1)S(1)}, bf16[16,14336]{1,0:T(8,128)(2,1)}, u32[]{:S(2)}) copy-start(bf16[16,14336]{1,0:T(8,128)(2,1)} %a_ref.1) | copy-start | bytes 1376260
  1.0 1.0 %copy-start.1 = (bf16[16,14336]{1,0:T(8,128)(2,1)S(1)}, bf16[16,14336]{1,0:T(8,128)(2,1)}, u32[]{:S(2)}) copy-start(bf16[16,14336]{1,0:T(8,128)(2,1)} %b_ref.1) | copy-start | bytes 1376260
  2.8 9.2 %collective-permute-start = (bf16[16,3584]{1,0:T(8,128)(2,1)S(1)}, bf16[16,3584]{1,0:T(8,128)(2,1)S(1)}, u32[]{:S(2)}, u32[]{:S(2)}) collective-permute-start(bf16[16,3584]{1,0:T(8,128)(2,1)S(1)} %get-tuple-element.17), channel_id=1, source_target_pairs={{0,4},{4,8},{8,12},{12,0},{1,5},{5,9},{9,13},{13,1},{2,6},{6,10},{... | collective-permute-start | bytes 344072 | tf_op jit(solution)/shard_map/ppermute | solution.py:231
  5.8 10.2 %collective-permute-start.1 = (bf16[16,3584]{1,0:T(8,128)(2,1)S(1)}, bf16[16,3584]{1,0:T(8,128)(2,1)S(1)}, u32[]{:S(2)}, u32[]{:S(2)}) collective-permute-start(bf16[16,3584]{1,0:T(8,128)(2,1)S(1)} %get-tuple-element.18), channel_id=1, source_target_pairs={{0,8},{4,12},{8,0},{12,4},{1,9},{5,13},{9,1},{13,5},{2,10},{6,14},... | collective-permute-start | bytes 344072 | tf_op jit(solution)/shard_map/ppermute | solution.py:231
  8.4 7.6 %collective-permute-start.2 = (bf16[16,3584]{1,0:T(8,128)(2,1)S(1)}, bf16[16,3584]{1,0:T(8,128)(2,1)S(1)}, u32[]{:S(2)}, u32[]{:S(2)}) collective-permute-start(bf16[16,3584]{1,0:T(8,128)(2,1)S(1)} %get-tuple-element.19), channel_id=1, source_target_pairs={{0,12},{4,0},{8,4},{12,8},{1,13},{5,1},{9,5},{13,9},{2,14},{6,2},{... | collective-permute-start | bytes 344072 | tf_op jit(solution)/shard_map/ppermute | solution.py:231
  9.8 6.2 %collective-permute-start.3 = (bf16[16,3584]{1,0:T(8,128)(2,1)S(1)}, bf16[16,3584]{1,0:T(8,128)(2,1)S(1)}, u32[]{:S(2)}, u32[]{:S(2)}) collective-permute-start(bf16[16,3584]{1,0:T(8,128)(2,1)S(1)} %get-tuple-element.21), channel_id=1, source_target_pairs={{0,1},{1,2},{2,3},{3,0},{4,5},{5,6},{6,7},{7,4},{8,9},{9,10},{10,1... | collective-permute-start | bytes 344072 | tf_op jit(solution)/shard_map/ppermute | solution.py:231
  9.8 6.2 %collective-permute-start.4 = (bf16[16,3584]{1,0:T(8,128)(2,1)S(1)}, bf16[16,3584]{1,0:T(8,128)(2,1)S(1)}, u32[]{:S(2)}, u32[]{:S(2)}) collective-permute-start(bf16[16,3584]{1,0:T(8,128)(2,1)S(1)} %get-tuple-element.22), channel_id=1, source_target_pairs={{0,2},{1,3},{2,0},{3,1},{4,6},{5,7},{6,4},{7,5},{8,10},{9,11},{10,... | collective-permute-start | bytes 344072 | tf_op jit(solution)/shard_map/ppermute | solution.py:231
  11.9 4.8 %collective-permute-start.5 = (bf16[16,3584]{1,0:T(8,128)(2,1)S(1)}, bf16[16,3584]{1,0:T(8,128)(2,1)S(1)}, u32[]{:S(2)}, u32[]{:S(2)}) collective-permute-start(bf16[16,3584]{1,0:T(8,128)(2,1)S(1)} %get-tuple-element.23), channel_id=1, source_target_pairs={{0,3},{1,0},{2,1},{3,2},{4,7},{5,4},{6,5},{7,6},{8,11},{9,8},{10,9... | collective-permute-start | bytes 344072 | tf_op jit(solution)/shard_map/ppermute | solution.py:231
  16.8 8.5 %collective-permute-start.8 = (bf16[64,1792]{1,0:T(8,128)(2,1)S(1)}, bf16[64,1792]{1,0:T(8,128)(2,1)S(1)}, u32[]{:S(2)}, u32[]{:S(2)}) collective-permute-start(bf16[64,1792]{1,0:T(8,128)(2,1)S(1)} %get-tuple-element.25.refs_0_), channel_id=1, source_target_pairs={{0,4},{4,0},{8,12},{12,8},{1,5},{5,1},{9,13},{13,9},{2,6},{6,2},{1... | collective-permute-start | bytes 688136 | tf_op jit(solution)/shard_map/ppermute | solution.py:235
  19.1 18.7 %collective-permute-start.7 = (bf16[64,3584]{1,0:T(8,128)(2,1)S(1)}, bf16[64,3584]{1,0:T(8,128)(2,1)S(1)}, u32[]{:S(2)}, u32[]{:S(2)}) collective-permute-start(bf16[64,3584]{1,0:T(8,128)(2,1)S(1)} %get-tuple-element.24.refs_0_), channel_id=1, source_target_pairs={{0,2},{1,3},{2,0},{3,1},{4,6},{5,7},{6,4},{7,5},{8,10},{9,11},{10,... | collective-permute-start | bytes 1376264 | tf_op jit(solution)/shard_map/ppermute | solution.py:231
  25.3 13.1 %collective-permute-start.13 = (bf16[128,1792]{1,0:T(8,128)(2,1)S(1)}, bf16[128,1792]{1,0:T(8,128)(2,1)S(1)}, u32[]{:S(2)}, u32[]{:S(2)}) collective-permute-start(bf16[128,1792]{1,0:T(8,128)(2,1)S(1)} %join_rows.6.refs_1_.refs_0_), channel_id=1, source_target_pairs={{0,0},{4,8},{8,4},{12,12},{1,1},{5,9},{9,5},{13,13},{2,2},{6,10},{... | collective-permute-start | bytes 1376264 | tf_op jit(solution)/shard_map/ppermute | solution.py:254
  26.0 11.0 %collective-permute-start.10 = (bf16[64,1792]{1,0:T(8,128)(2,1)S(1)}, bf16[64,1792]{1,0:T(8,128)(2,1)S(1)}, u32[]{:S(2)}, u32[]{:S(2)}) collective-permute-start(bf16[64,1792]{1,0:T(8,128)(2,1)S(1)} %join_rows.8.refs_0_), channel_id=1, source_target_pairs={{0,4},{4,0},{8,12},{12,8},{1,5},{5,1},{9,13},{13,9},{2,6},{6,2},{1... | collective-permute-start | bytes 688136 | tf_op jit(solution)/shard_map/ppermute | solution.py:235
  37.0 5.1 %collective-permute-start.11 = (bf16[128,1792]{1,0:T(8,128)(2,1)S(1)}, bf16[128,1792]{1,0:T(8,128)(2,1)S(1)}, u32[]{:S(2)}, u32[]{:S(2)}) collective-permute-start(bf16[128,1792]{1,0:T(8,128)(2,1)S(1)} %join_rows.9.refs_0_), channel_id=1, source_target_pairs={{0,0},{4,8},{8,4},{12,12},{1,1},{5,9},{9,5},{13,13},{2,2},{6,10},{... | collective-permute-start | bytes 1376264 | tf_op jit(solution)/shard_map/ppermute | solution.py:254
  37.7 15.1 %collective-permute-start.6 = (bf16[64,3584]{1,0:T(8,128)(2,1)S(1)}, bf16[64,3584]{1,0:T(8,128)(2,1)S(1)}, u32[]{:S(2)}, u32[]{:S(2)}) collective-permute-start(bf16[64,3584]{1,0:T(8,128)(2,1)S(1)} %get-tuple-element.24.refs_0_), channel_id=1, source_target_pairs={{0,1},{1,0},{2,3},{3,2},{4,5},{5,4},{6,7},{7,6},{8,9},{9,8},{10,11... | collective-permute-start | bytes 1376264 | tf_op jit(solution)/shard_map/ppermute | solution.py:235
  37.9 15.0 %collective-permute-start.9 = (bf16[64,3584]{1,0:T(8,128)(2,1)S(1)}, bf16[64,3584]{1,0:T(8,128)(2,1)S(1)}, u32[]{:S(2)}, u32[]{:S(2)}) collective-permute-start(bf16[64,3584]{1,0:T(8,128)(2,1)S(1)} %join_rows.7), channel_id=1, source_target_pairs={{0,1},{1,0},{2,3},{3,2},{4,5},{5,4},{6,7},{7,6},{8,9},{9,8},{10,11... | collective-permute-start | bytes 1376264 | tf_op jit(solution)/shard_map/ppermute | solution.py:235
  38.4 16.9 %collective-permute-start.14 = (bf16[128,1792]{1,0:T(8,128)(2,1)S(1)}, bf16[128,1792]{1,0:T(8,128)(2,1)S(1)}, u32[]{:S(2)}, u32[]{:S(2)}) collective-permute-start(bf16[128,1792]{1,0:T(8,128)(2,1)S(1)} %collective-permute-done.13.refs_1_), channel_id=1, source_target_pairs={{0,4},{4,0},{8,12},{12,8},{1,5},{5,1},{9,13},{13,9},{2,6},{6,2},{1... | collective-permute-start | bytes 1376264 | tf_op jit(solution)/shard_map/ppermute | solution.py:235
  42.1 24.0 %collective-permute-start.12 = (bf16[128,1792]{1,0:T(8,128)(2,1)S(1)}, bf16[128,1792]{1,0:T(8,128)(2,1)S(1)}, u32[]{:S(2)}, u32[]{:S(2)}) collective-permute-start(bf16[128,1792]{1,0:T(8,128)(2,1)S(1)} %collective-permute-done.11.refs_1_), channel_id=1, source_target_pairs={{0,4},{4,0},{8,12},{12,8},{1,5},{5,1},{9,13},{13,9},{2,6},{6,2},{1... | collective-permute-start | bytes 1376264 | tf_op jit(solution)/shard_map/ppermute | solution.py:235

commit v5 on v4

--- a/solution.py
+++ b/solution.py
@@ -29,7 +29,7 @@
 
 
 def over_count(values, count):
-    if count & (count - 1) == 0:
+    if power_of_two(count):
         return values * (1.0 / count)
     return values / count
 
@@ -40,6 +40,16 @@
     centred = values - mean
     var = over_count(jnp.sum(centred * centred, axis=0, keepdims=True), count)
     return (centred * lax.rsqrt(var + EPS)).astype(jnp.bfloat16)
+
+
+def power_of_two(count):
+    return count & (count - 1) == 0
+
+
+def partner(place, step, size):
+    if power_of_two(size):
+        return place ^ step
+    return (place + step) % size
 
 
 def cut_kernel(n_fa, n_fb, a_ref, b_ref, *refs):
@@ -50,10 +60,10 @@
     fb = lax.axis_index("fb")
     copies = []
     for step in range(n_fa):
-        start = pl.multiple_of(lax.rem(fa + step, n_fa) * width_a, 128)
+        start = pl.multiple_of(partner(fa, step, n_fa) * width_a, 128)
         copies.append((a_ref.at[:, pl.ds(start, width_a)], outs[step]))
     for step in range(n_fb):
-        start = pl.multiple_of(lax.rem(fb + step, n_fb) * width_b, 128)
+        start = pl.multiple_of(partner(fb, step, n_fb) * width_b, 128)
         copies.append((b_ref.at[:, pl.ds(start, width_b)], outs[n_fa + step]))
     started = []
     for place, (src, dst) in enumerate(copies):
@@ -117,26 +127,13 @@
     return join_rows([(pieces, [pieces[0].shape[1]])], after)[0]
 
 
-def order_of(source, fa, n_fa):
-    if n_fa != 4:
-        return lax.rem(fa + n_fa - source, n_fa)
-    neighbour = fa + 1 - 2 * lax.rem(fa, 2)
-    outer = jnp.where((source == 0) | (source == n_fa - 1), 3, 2)
-    return jnp.where(source == fa, 0, jnp.where(source == neighbour, 1, outer))
-
-
 def standardize_a_kernel(n_fa, n_fb, *refs):
-    groups, out, rows = refs[:n_fb], refs[-2], refs[-1]
+    groups, out = refs[:n_fb], refs[-1]
     tok = groups[0].shape[0] // n_fa
-    fa = lax.axis_index("fa")
-    odd = lax.rem(lax.axis_index("fb"), 2)
-    places = [order_of(lax.rem(fa + n_fa - i, n_fa), fa, n_fa) for i in range(n_fa)]
-    for place, ref in enumerate(groups):
-        back = place if place % 2 == 0 else lax.rem(place - 2 + 2 * odd + n_fb, n_fb)
-        for i in range(n_fa):
-            row = pl.multiple_of((places[i] * n_fb + back) * tok, tok)
-            rows[pl.ds(row, tok), :] = ref[pl.ds(i * tok, tok), :].astype(jnp.float32)
-    out[...] = standardize(rows[...]).T
+    pieces = [
+        group[pl.ds(i * tok, tok), :].astype(jnp.float32) for i in range(n_fa) for group in groups
+    ]
+    out[...] = standardize(jnp.concatenate(pieces, axis=0)).T
 
 
 def standardize_a(groups, n_fa, n_fb):
@@ -149,7 +146,6 @@
         grid=(width // block,),
         in_specs=[pl.BlockSpec((rows, block), lambda i: (0, i))] * n_fb,
         out_specs=pl.BlockSpec((block, total), lambda i: (i, 0)),
-        scratch_shapes=[pltpu.VMEM((total, block), jnp.float32)],
         compiler_params=pltpu.CompilerParams(vmem_limit_bytes=VMEM),
         cost_estimate=pl.CostEstimate(
             flops=10 * width * total, bytes_accessed=4 * width * total, transcendentals=0
@@ -158,26 +154,16 @@
     )(*groups)
 
 
-def product_kernel(n_groups, relayed, column, a_ref, *refs):
+def product_kernel(n_groups, column, a_ref, *refs):
     groups = refs[:n_groups]
-    out, std, slots, sems = refs[-4:]
-    total, width = std.shape
+    out, slots, sems = refs[-3:]
+    total, width = a_ref.shape[1], groups[0].shape[1]
     n_slots, height, strip = slots.shape
-    fa = lax.axis_index("fa")
-    at_end = (fa == 0) | (fa == 3)
 
     def copy_of(step):
         slot = lax.rem(step, n_slots)
         place = pl.multiple_of(column + step * strip, 128)
         return pltpu.make_async_copy(slots.at[slot], out.at[:, pl.ds(place, strip)], sems.at[slot])
-
-    @pl.loop(0, width // 128)
-    def _(step):
-        columns = pl.ds(pl.multiple_of(step * 128, 128), 128)
-        pieces = [ref[:, columns].astype(jnp.float32) for ref in groups]
-        if relayed:
-            pieces = [pieces[0], jnp.where(at_end, pieces[2], pieces[1])]
-        std[:, columns] = standardize(jnp.concatenate(pieces, axis=0))
 
     @pl.loop(0, width // strip)
     def _(step):
@@ -185,8 +171,13 @@
         def _():
             copy_of(step - n_slots).wait()
 
-        columns = pl.ds(pl.multiple_of(step * strip, 128), strip)
-        product = jnp.dot(a_ref[...], std[:, columns], preferred_element_type=jnp.float32)
+        parts = []
+        for part in range(strip // 128):
+            columns = pl.ds(pl.multiple_of(step * strip + part * 128, 128), 128)
+            pieces = [ref[:, columns].astype(jnp.float32) for ref in groups]
+            parts.append(standardize(jnp.concatenate(pieces, axis=0)))
+        std = jnp.concatenate(parts, axis=1)
+        product = jnp.dot(a_ref[...], std, preferred_element_type=jnp.float32)
         slots[lax.rem(step, n_slots)] = over_count(product, total)
         copy_of(step).start()
 
@@ -195,25 +186,25 @@
         copy_of(step).wait()
 
 
-def product_chunk(std_a, groups, relayed, column, full_width, buffer):
+def product_chunk(std_a, groups, column, full_width, buffer, after=()):
     height, total = std_a.shape
     width = groups[0].shape[1]
     strip = 256 if width % 256 == 0 else 128
     n_slots = 4
     in_specs = [pl.BlockSpec(memory_space=pltpu.VMEM)] * (1 + len(groups))
-    args = [std_a, *groups]
+    in_specs += [pl.BlockSpec(memory_space=pl.ANY)] * len(after)
+    args = [std_a, *groups, *after]
     aliases = {}
     if buffer is not None:
         aliases = {len(args): 0}
         in_specs.append(pl.BlockSpec(memory_space=pl.ANY))
         args.append(buffer)
     return pl.pallas_call(
-        functools.partial(product_kernel, len(groups), relayed, column),
+        functools.partial(product_kernel, len(groups), column),
         out_shape=jax.ShapeDtypeStruct((height, full_width), jnp.float32),
         in_specs=in_specs,
         out_specs=pl.BlockSpec(memory_space=pl.ANY),
         scratch_shapes=[
-            pltpu.VMEM((total, width), jnp.bfloat16),
             pltpu.VMEM((n_slots, height, strip), jnp.float32),
             pltpu.SemaphoreType.DMA((n_slots,)),
         ],
@@ -226,46 +217,42 @@
     )(*args)
 
 
-def shifted(x, axis, step):
+def sent(x, axis, step):
     size = lax.axis_size(axis)
-    return lax.ppermute(x, axis, [(i, (i + step) % size) for i in range(size)])
-
-
-def swapped(x, axis):
-    return lax.ppermute(x, axis, [(i, i ^ 1) for i in range(lax.axis_size(axis))])
+    return lax.ppermute(x, axis, [(i, partner(i, step, size)) for i in range(size)])
+
+
+def gathered(x, axis, through=None):
+    size = lax.axis_size(axis)
+    blocks = [x]
+    for step in range(1, size):
+        low = step & -step
+        if through is None or low == step or not power_of_two(size):
+            blocks.append(sent(x, axis, step))
+        else:
+            blocks.append(sent(through(blocks[step - low]), axis, low))
+    return blocks
 
 
 def per_device(a_acts, b_acts):
     n_fa = lax.axis_size("fa")
     n_fb = lax.axis_size("fb")
-    relayed = n_fa == 4
     panels_a, panels_b = cut_panels(a_acts, b_acts, n_fa, n_fb)
-    own_a = [panels_a[0]] + [shifted(panels_a[s], "fa", s) for s in range(1, n_fa)]
-    own_b = [panels_b[0]] + [shifted(panels_b[s], "fb", s) for s in range(1, n_fb)]
+    own_a = [panels_a[0]] + [sent(panels_a[s], "fa", s) for s in range(1, n_fa)]
+    own_b = [panels_b[0]] + [sent(panels_b[s], "fb", s) for s in range(1, n_fb)]
     full_width = panels_b[0].shape[1]
-    widths = chunk_widths(full_width, (1, 1))
+    widths = chunk_widths(full_width, (4, 5, 5))
     group_a, *parts_b = join_rows([(own_a, [panels_a[0].shape[1]]), (own_b, widths)])
-    if relayed:
-        pairs = []
-        for part in parts_b:
-            if pairs:
-                part = stacked([part], pairs[-1:])
-            pairs.append(stacked([part, swapped(part, "fa")]))
-        seconds = [lax.ppermute(pair, "fa", [(0, 0), (1, 2), (2, 1), (3, 3)]) for pair in pairs]
-        chunks = [[pair, second, swapped(second, "fa")] for pair, second in zip(pairs, seconds)]
-        ahead = pairs[:1]
-    else:
-        chunks = [[part] + [shifted(part, "fa", s) for s in range(1, n_fa)] for part in parts_b]
-        ahead = parts_b[:1]
-    all_a = [group_a, swapped(group_a, "fb")]
-    for s in range(1, n_fb // 2):
-        block = shifted(group_a, "fb", 2 * s)
-        all_a += [block, swapped(stacked([block], ahead), "fb")]
+    chunks = [gathered(part, "fa", lambda block: block) for part in parts_b[:-1]]
+    chunks.append(gathered(parts_b[-1], "fa"))
+    far = n_fa // 2
+    all_a = gathered(group_a, "fb", lambda block: stacked([block], [chunks[0][1]] + [chunk[far] for chunk in chunks[:-1]]))
     std_a = standardize_a(all_a, n_fa, n_fb)
     buffer = None
     column = 0
-    for groups in chunks:
-        buffer = product_chunk(std_a, groups, relayed, column, full_width, buffer)
+    for place, groups in enumerate(chunks):
+        after = [later[far] for later in chunks[place + 1 : -1]]
+        buffer = product_chunk(std_a, groups, column, full_width, buffer, after)
         column += groups[0].shape[1]
     return buffer
 

time: 77.1 us -> 72.6 us (0.942)
  starting transfers between devices: 34.3 us -> 20.4 us
  waiting for transfers between devices: 15.5 us -> 26.3 us
  Pallas kernels: 24.9 us -> 23.5 us
    ppermute x15 -> x18, starting transfers between devices: 34.3 us -> 20.4 us  [sent(): lax.ppermute(x, axis, [(i, partner(i, step, size)) for i in range(size)])]
    ppermute x15 -> x18, waiting for transfers between devices: 15.5 us -> 26.3 us  [sent(): lax.ppermute(x, axis, [(i, partner(i, step, size)) for i in range(size)])]
    pallas_call x2 -> x3, Pallas kernels: 21.6 us -> 20.6 us  [product_chunk(): pl.pallas_call(functools.partial(product_kernel, len(groups), column), ou...]
  transfers between devices with their start and end apart: 15 -> 18, of which waited for: 5 -> 5; matrix products, arithmetic and copies ran while one was open for 0% -> 0% of each run, Pallas kernels for 17% -> 21%
where the time goes in v5:
time: 72.6 us; the launch traced here: 72.4 us
  waiting for transfers between devices  26.3 us (36%)
  Pallas kernels  23.5 us (32%)
  starting transfers between devices  20.4 us (28%)
  local copies, waits for them, and re-layouts  2.04 us (3%)
    ppermute x18, waiting for transfers between devices, sent(): lax.ppermute(x, axis, [(i, partner(i, step, size)) for i in range(size)])  26.3 us
    pallas_call x3, Pallas kernels, product_chunk(): pl.pallas_call(functools.partial(product_kernel, len(groups), column), ou...  20.6 us
    ppermute x18, starting transfers between devices, sent(): lax.ppermute(x, axis, [(i, partner(i, step, size)) for i in range(size)])  20.4 us
    pallas_call x1, Pallas kernels, standardize_a(): pl.pallas_call(functools.partial(standardize_a_kernel, n_fa, n_fb), out_s...  2.1 us
    unnamed x4, local copies, waits for them, and re-layouts  2.04 us
  transfers between devices with their start and end apart: 18, of which 5 were waited for; matrix products, arithmetic and copies ran while one was open for 0% of the time, Pallas kernels for 21%

profile of v5, /device:TPU:0, one launch (start us, length us, event | category | flops | bytes accessed | tf_op | source)
XLA Modules:
  0.0 72.4 jit_solution(11204841054124467934)
XLA Ops:
  0.0 0.0 copy-start
  0.0 1.0 %copy-done = bf16[16,14336]{1,0:T(8,128)(2,1)S(1)} copy-done((bf16[16,14336]{1,0:T(8,128)(2,1)S(1)}, bf16[16,14336]{1,0:T(8,128)(2,1)}, u32[]{:S(2)}) %copy-start) | copy-done | bytes 458776
  1.0 0.0 copy-start.1
  1.0 1.0 %copy-done.1 = bf16[16,14336]{1,0:T(8,128)(2,1)S(1)} copy-done((bf16[16,14336]{1,0:T(8,128)(2,1)S(1)}, bf16[16,14336]{1,0:T(8,128)(2,1)}, u32[]{:S(2)}) %copy-start.1) | copy-done | bytes 458776
  2.0 0.7 cut_panels.1
  2.7 3.1 %collective-permute-start = (bf16[16,3584]{1,0:T(8,128)(2,1)S(1)}, bf16[16,3584]{1,0:T(8,128)(2,1)S(1)}, u32[]{:S(2)}, u32[]{:S(2)}) collective-permute-start(bf16[16,3584]{1,0:T(8,128)(2,1)S(1)} %get-tuple-element.18), channel_id=1, source_target_pairs={{0,4},{4,0},{8,12},{12,8},{1,5},{5,1},{9,13},{13,9},{2,6},{6,2},{1... | collective-permute-start | bytes 344072 | tf_op jit(solution)/shard_map/ppermute | solution.py:222
  5.8 2.6 %collective-permute-start.1 = (bf16[16,3584]{1,0:T(8,128)(2,1)S(1)}, bf16[16,3584]{1,0:T(8,128)(2,1)S(1)}, u32[]{:S(2)}, u32[]{:S(2)}) collective-permute-start(bf16[16,3584]{1,0:T(8,128)(2,1)S(1)} %get-tuple-element.19), channel_id=1, source_target_pairs={{0,8},{4,12},{8,0},{12,4},{1,9},{5,13},{9,1},{13,5},{2,10},{6,14},... | collective-permute-start | bytes 344072 | tf_op jit(solution)/shard_map/ppermute | solution.py:222
  8.4 0.0 collective-permute-start.2
  8.4 0.0 collective-permute-start.3
  8.4 1.7 %collective-permute-start.4 = (bf16[16,3584]{1,0:T(8,128)(2,1)S(1)}, bf16[16,3584]{1,0:T(8,128)(2,1)S(1)}, u32[]{:S(2)}, u32[]{:S(2)}) collective-permute-start(bf16[16,3584]{1,0:T(8,128)(2,1)S(1)} %get-tuple-element.23), channel_id=1, source_target_pairs={{0,2},{1,3},{2,0},{3,1},{4,6},{5,7},{6,4},{7,5},{8,10},{9,11},{10,... | collective-permute-start | bytes 344072 | tf_op jit(solution)/shard_map/ppermute | solution.py:222
  10.1 0.0 collective-permute-done.refs_1_
  10.1 0.1 collective-permute-start.5
  10.3 7.2 %collective-permute-done.1.refs_2_ = bf16[16,3584]{1,0:T(8,128)(2,1)S(1)} collective-permute-done((bf16[16,3584]{1,0:T(8,128)(2,1)S(1)}, bf16[16,3584]{1,0:T(8,128)(2,1)S(1)}, u32[]{:S(2)}, u32[]{:S(2)}) %collective-permute-start.1) | collective-permute-done | bytes 114720 | tf_op jit(solution)/shard_map/ppermute | solution.py:222
  17.5 0.0 collective-permute-done.2.refs_3_
  17.5 0.0 collective-permute-done.3.refs_5_
  17.5 0.0 collective-permute-done.4.refs_6_
  17.5 0.0 collective-permute-done.5.refs_7_
  17.5 0.1 join_rows.2
  17.6 1.6 %collective-permute-start.7 = (bf16[64,3584]{1,0:T(8,128)(2,1)S(1)}, bf16[64,3584]{1,0:T(8,128)(2,1)S(1)}, u32[]{:S(2)}, u32[]{:S(2)}) collective-permute-start(bf16[64,3584]{1,0:T(8,128)(2,1)S(1)} %get-tuple-element.25.refs_0_), channel_id=1, source_target_pairs={{0,2},{1,3},{2,0},{3,1},{4,6},{5,7},{6,4},{7,5},{8,10},{9,11},{10,... | collective-permute-start | bytes 1376264 | tf_op jit(solution)/shard_map/ppermute | solution.py:222
  19.2 2.8 %collective-permute-start.10 = (bf16[64,1280]{1,0:T(8,128)(2,1)S(1)}, bf16[64,1280]{1,0:T(8,128)(2,1)S(1)}, u32[]{:S(2)}, u32[]{:S(2)}) collective-permute-start(bf16[64,1280]{1,0:T(8,128)(2,1)S(1)} %get-tuple-element.27.refs_0_), channel_id=1, source_target_pairs={{0,8},{4,12},{8,0},{12,4},{1,9},{5,13},{9,1},{13,5},{2,10},{6,14},... | collective-permute-start | bytes 491528 | tf_op jit(solution)/shard_map/ppermute | solution.py:222
  22.0 0.2 collective-permute-start.8
  22.2 1.7 %collective-permute-start.9 = (bf16[64,1024]{1,0:T(8,128)(2,1)S(1)}, bf16[64,1024]{1,0:T(8,128)(2,1)S(1)}, u32[]{:S(2)}, u32[]{:S(2)}) collective-permute-start(bf16[64,1024]{1,0:T(8,128)(2,1)S(1)} %get-tuple-element.26.refs_0_), channel_id=1, source_target_pairs={{0,8},{4,12},{8,0},{12,4},{1,9},{5,13},{9,1},{13,5},{2,10},{6,14},... | collective-permute-start | bytes 393224 | tf_op jit(solution)/shard_map/ppermute | solution.py:222
  23.9 0.0 collective-permute-start.6
  23.9 4.2 %collective-permute-done.8.refs_1_ = bf16[64,1024]{1,0:T(8,128)(2,1)S(1)} collective-permute-done((bf16[64,1024]{1,0:T(8,128)(2,1)S(1)}, bf16[64,1024]{1,0:T(8,128)(2,1)S(1)}, u32[]{:S(2)}, u32[]{:S(2)}) %collective-permute-start.8) | collective-permute-done | bytes 131104 | tf_op jit(solution)/shard_map/ppermute | solution.py:222
  28.1 6.1 %collective-permute-done.9.refs_2_ = bf16[64,1024]{1,0:T(8,128)(2,1)S(1)} collective-permute-done((bf16[64,1024]{1,0:T(8,128)(2,1)S(1)}, bf16[64,1024]{1,0:T(8,128)(2,1)S(1)}, u32[]{:S(2)}, u32[]{:S(2)}) %collective-permute-start.9) | collective-permute-done | bytes 131104 | tf_op jit(solution)/shard_map/ppermute | solution.py:222
  34.2 0.0 collective-permute-done.10.refs_3_.refs_4_.refs_2_
  34.2 0.0 collective-permute-done.7.refs_0_.refs_2_
  34.3 0.1 collective-permute-start.11
  34.4 0.3 collective-permute-start.17
  34.6 1.8 %collective-permute-start.15 = (bf16[64,1280]{1,0:T(8,128)(2,1)S(1)}, bf16[64,1280]{1,0:T(8,128)(2,1)S(1)}, u32[]{:S(2)}, u32[]{:S(2)}) collective-permute-start(bf16[64,1280]{1,0:T(8,128)(2,1)S(1)} %get-tuple-element.27.refs_0_), channel_id=1, source_target_pairs={{0,4},{4,0},{8,12},{12,8},{1,5},{5,1},{9,13},{13,9},{2,6},{6,2},{1... | collective-permute-start | bytes 491528 | tf_op jit(solution)/shard_map/ppermute | solution.py:222
  36.5 0.2 collective-permute-start.12
  36.7 0.0 collective-permute-done.6.refs_1_
  36.7 3.4 %collective-permute-start.13 = (bf16[64,1280]{1,0:T(8,128)(2,1)S(1)}, bf16[64,1280]{1,0:T(8,128)(2,1)S(1)}, u32[]{:S(2)}, u32[]{:S(2)}) collective-permute-start(bf16[64,1280]{1,0:T(8,128)(2,1)S(1)} %get-tuple-element.28.refs_0_), channel_id=1, source_target_pairs={{0,8},{4,12},{8,0},{12,4},{1,9},{5,13},{9,1},{13,5},{2,10},{6,14},... | collective-permute-start | bytes 491528 | tf_op jit(solution)/shard_map/ppermute | solution.py:222
  40.0 0.0 collective-permute-done.11.refs_3_
  40.0 0.8 %collective-permute-start.14 = (bf16[64,1280]{1,0:T(8,128)(2,1)S(1)}, bf16[64,1280]{1,0:T(8,128)(2,1)S(1)}, u32[]{:S(2)}, u32[]{:S(2)}) collective-permute-start(bf16[64,1280]{1,0:T(8,128)(2,1)S(1)} %get-tuple-element.28.refs_0_), channel_id=1, source_target_pairs={{0,12},{4,8},{8,4},{12,0},{1,13},{5,9},{9,5},{13,1},{2,14},{6,10},... | collective-permute-start | bytes 491528 | tf_op jit(solution)/shard_map/ppermute | solution.py:222
  40.9 2.1 %standardize_a.1.a_ref = bf16[3584,256]{1,0:T(8,128)(2,1)S(1)} custom-call(bf16[64,3584]{1,0:T(8,128)(2,1)S(1)} %get-tuple-element.25.refs_0_, bf16[64,3584]{1,0:T(8,128)(2,1)S(1)} %collective-permute-done.6.refs_1_, bf16[64,3584]{1,0:T(8,128)(2,1)S(1)} %collective-permute-done.7.refs_0_.refs_2_, bf16[64,3584]{1,0:T(8,128)(2,1)S(1)} %collective-permute-done.11.refs_3_), custom_call_target="tpu_custom_call" | custom-call | flops 9175040 | bytes 3670016 | tf_op jit(solution)/shard_map/standardize_a/pallas_call | solution.py:143
  43.0 0.4 collective-permute-done.17.refs_3_
  43.4 0.0 collective-permute-start.16
  43.4 6.1 %product_chunk.3.refs_4_ = f32[3584,3584]{1,0:T(8,128)} custom-call(bf16[3584,256]{1,0:T(8,128)(2,1)S(1)} %standardize_a.1.a_ref, bf16[64,1024]{1,0:T(8,128)(2,1)S(1)} %get-tuple-element.26.refs_0_, bf16[64,1024]{1,0:T(8,128)(2,1)S(1)} %collective-permute-done.8.refs_1_, bf16[64,1024]{1,0:T(8,128)(2,1)S(1)} %collective-permute-done.9.refs_2_, ...), custom_call_target="tpu_custom_call" | custom-call | flops 1879048192 | bytes 14680064 | tf_op jit(solution)/shard_map/product_chunk/pallas_call | solution.py:202
  49.5 0.0 collective-permute-done.15.refs_1_
  49.5 8.3 %collective-permute-done.16.refs_3_ = bf16[64,1280]{1,0:T(8,128)(2,1)S(1)} collective-permute-done((bf16[64,1280]{1,0:T(8,128)(2,1)S(1)}, bf16[64,1280]{1,0:T(8,128)(2,1)S(1)}, u32[]{:S(2)}, u32[]{:S(2)}) %collective-permute-start.16) | collective-permute-done | bytes 163872 | tf_op jit(solution)/shard_map/ppermute | solution.py:222
  57.8 7.2 %product_chunk.4.refs_4_ = f32[3584,3584]{1,0:T(8,128)} custom-call(bf16[3584,256]{1,0:T(8,128)(2,1)S(1)} %standardize_a.1.a_ref, bf16[64,1280]{1,0:T(8,128)(2,1)S(1)} %get-tuple-element.27.refs_0_, bf16[64,1280]{1,0:T(8,128)(2,1)S(1)} %collective-permute-done.15.refs_1_, ...), custom_call_target="tpu_custom_call", output_to_operand_aliasing={{}: (5, {})} | custom-call | flops 2348810240 | bytes 18350080 | tf_op jit(solution)/shard_map/product_chunk/pallas_call | solution.py:202
  65.1 0.0 collective-permute-done.12.refs_1_
  65.1 0.0 collective-permute-done.13.refs_2_
  65.1 0.0 collective-permute-done.14.refs_3_
  65.1 7.2 %product_chunk.5 = f32[3584,3584]{1,0:T(8,128)} custom-call(bf16[3584,256]{1,0:T(8,128)(2,1)S(1)} %standardize_a.1.a_ref, bf16[64,1280]{1,0:T(8,128)(2,1)S(1)} %get-tuple-element.28.refs_0_, bf16[64,1280]{1,0:T(8,128)(2,1)S(1)} %collective-permute-done.12.refs_1_, ...), custom_call_target="tpu_custom_call", output_to_operand_aliasing={{}: (5, {})} | custom-call | flops 2348810240 | bytes 18350080 | tf_op jit(solution)/shard_map/product_chunk/pallas_call | solution.py:202
  (1 shorter events, 0.0 us)
Async XLA Ops:
  0.0 1.0 %copy-start = (bf16[16,14336]{1,0:T(8,128)(2,1)S(1)}, bf16[16,14336]{1,0:T(8,128)(2,1)}, u32[]{:S(2)}) copy-start(bf16[16,14336]{1,0:T(8,128)(2,1)} %a_ref.1) | copy-start | bytes 1376260
  1.0 1.0 %copy-start.1 = (bf16[16,14336]{1,0:T(8,128)(2,1)S(1)}, bf16[16,14336]{1,0:T(8,128)(2,1)}, u32[]{:S(2)}) copy-start(bf16[16,14336]{1,0:T(8,128)(2,1)} %b_ref.1) | copy-start | bytes 1376260
  2.7 7.4 %collective-permute-start = (bf16[16,3584]{1,0:T(8,128)(2,1)S(1)}, bf16[16,3584]{1,0:T(8,128)(2,1)S(1)}, u32[]{:S(2)}, u32[]{:S(2)}) collective-permute-start(bf16[16,3584]{1,0:T(8,128)(2,1)S(1)} %get-tuple-element.18), channel_id=1, source_target_pairs={{0,4},{4,0},{8,12},{12,8},{1,5},{5,1},{9,13},{13,9},{2,6},{6,2},{1... | collective-permute-start | bytes 344072 | tf_op jit(solution)/shard_map/ppermute | solution.py:222
  5.8 11.7 %collective-permute-start.1 = (bf16[16,3584]{1,0:T(8,128)(2,1)S(1)}, bf16[16,3584]{1,0:T(8,128)(2,1)S(1)}, u32[]{:S(2)}, u32[]{:S(2)}) collective-permute-start(bf16[16,3584]{1,0:T(8,128)(2,1)S(1)} %get-tuple-element.19), channel_id=1, source_target_pairs={{0,8},{4,12},{8,0},{12,4},{1,9},{5,13},{9,1},{13,5},{2,10},{6,14},... | collective-permute-start | bytes 344072 | tf_op jit(solution)/shard_map/ppermute | solution.py:222
  8.4 9.1 %collective-permute-start.2 = (bf16[16,3584]{1,0:T(8,128)(2,1)S(1)}, bf16[16,3584]{1,0:T(8,128)(2,1)S(1)}, u32[]{:S(2)}, u32[]{:S(2)}) collective-permute-start(bf16[16,3584]{1,0:T(8,128)(2,1)S(1)} %get-tuple-element.20), channel_id=1, source_target_pairs={{0,12},{4,8},{8,4},{12,0},{1,13},{5,9},{9,5},{13,1},{2,14},{6,10},... | collective-permute-start | bytes 344072 | tf_op jit(solution)/shard_map/ppermute | solution.py:222
  8.4 9.1 %collective-permute-start.3 = (bf16[16,3584]{1,0:T(8,128)(2,1)S(1)}, bf16[16,3584]{1,0:T(8,128)(2,1)S(1)}, u32[]{:S(2)}, u32[]{:S(2)}) collective-permute-start(bf16[16,3584]{1,0:T(8,128)(2,1)S(1)} %get-tuple-element.22), channel_id=1, source_target_pairs={{0,1},{1,0},{2,3},{3,2},{4,5},{5,4},{6,7},{7,6},{8,9},{9,8},{10,11... | collective-permute-start | bytes 344072 | tf_op jit(solution)/shard_map/ppermute | solution.py:222
  8.4 9.1 %collective-permute-start.4 = (bf16[16,3584]{1,0:T(8,128)(2,1)S(1)}, bf16[16,3584]{1,0:T(8,128)(2,1)S(1)}, u32[]{:S(2)}, u32[]{:S(2)}) collective-permute-start(bf16[16,3584]{1,0:T(8,128)(2,1)S(1)} %get-tuple-element.23), channel_id=1, source_target_pairs={{0,2},{1,3},{2,0},{3,1},{4,6},{5,7},{6,4},{7,5},{8,10},{9,11},{10,... | collective-permute-start | bytes 344072 | tf_op jit(solution)/shard_map/ppermute | solution.py:222
  10.1 7.4 %collective-permute-start.5 = (bf16[16,3584]{1,0:T(8,128)(2,1)S(1)}, bf16[16,3584]{1,0:T(8,128)(2,1)S(1)}, u32[]{:S(2)}, u32[]{:S(2)}) collective-permute-start(bf16[16,3584]{1,0:T(8,128)(2,1)S(1)} %get-tuple-element.24), channel_id=1, source_target_pairs={{0,3},{1,2},{2,1},{3,0},{4,7},{5,6},{6,5},{7,4},{8,11},{9,10},{10,... | collective-permute-start | bytes 344072 | tf_op jit(solution)/shard_map/ppermute | solution.py:222
  17.6 16.6 %collective-permute-start.7 = (bf16[64,3584]{1,0:T(8,128)(2,1)S(1)}, bf16[64,3584]{1,0:T(8,128)(2,1)S(1)}, u32[]{:S(2)}, u32[]{:S(2)}) collective-permute-start(bf16[64,3584]{1,0:T(8,128)(2,1)S(1)} %get-tuple-element.25.refs_0_), channel_id=1, source_target_pairs={{0,2},{1,3},{2,0},{3,1},{4,6},{5,7},{6,4},{7,5},{8,10},{9,11},{10,... | collective-permute-start | bytes 1376264 | tf_op jit(solution)/shard_map/ppermute | solution.py:222
  19.2 15.1 %collective-permute-start.10 = (bf16[64,1280]{1,0:T(8,128)(2,1)S(1)}, bf16[64,1280]{1,0:T(8,128)(2,1)S(1)}, u32[]{:S(2)}, u32[]{:S(2)}) collective-permute-start(bf16[64,1280]{1,0:T(8,128)(2,1)S(1)} %get-tuple-element.27.refs_0_), channel_id=1, source_target_pairs={{0,8},{4,12},{8,0},{12,4},{1,9},{5,13},{9,1},{13,5},{2,10},{6,14},... | collective-permute-start | bytes 491528 | tf_op jit(solution)/shard_map/ppermute | solution.py:222
  22.0 6.1 %collective-permute-start.8 = (bf16[64,1024]{1,0:T(8,128)(2,1)S(1)}, bf16[64,1024]{1,0:T(8,128)(2,1)S(1)}, u32[]{:S(2)}, u32[]{:S(2)}) collective-permute-start(bf16[64,1024]{1,0:T(8,128)(2,1)S(1)} %get-tuple-element.26.refs_0_), channel_id=1, source_target_pairs={{0,4},{4,0},{8,12},{12,8},{1,5},{5,1},{9,13},{13,9},{2,6},{6,2},{1... | collective-permute-start | bytes 393224 | tf_op jit(solution)/shard_map/ppermute | solution.py:222
  22.2 12.0 %collective-permute-start.9 = (bf16[64,1024]{1,0:T(8,128)(2,1)S(1)}, bf16[64,1024]{1,0:T(8,128)(2,1)S(1)}, u32[]{:S(2)}, u32[]{:S(2)}) collective-permute-start(bf16[64,1024]{1,0:T(8,128)(2,1)S(1)} %get-tuple-element.26.refs_0_), channel_id=1, source_target_pairs={{0,8},{4,12},{8,0},{12,4},{1,9},{5,13},{9,1},{13,5},{2,10},{6,14},... | collective-permute-start | bytes 393224 | tf_op jit(solution)/shard_map/ppermute | solution.py:222
  23.9 12.8 %collective-permute-start.6 = (bf16[64,3584]{1,0:T(8,128)(2,1)S(1)}, bf16[64,3584]{1,0:T(8,128)(2,1)S(1)}, u32[]{:S(2)}, u32[]{:S(2)}) collective-permute-start(bf16[64,3584]{1,0:T(8,128)(2,1)S(1)} %get-tuple-element.25.refs_0_), channel_id=1, source_target_pairs={{0,1},{1,0},{2,3},{3,2},{4,5},{5,4},{6,7},{7,6},{8,9},{9,8},{10,11... | collective-permute-start | bytes 1376264 | tf_op jit(solution)/shard_map/ppermute | solution.py:222
  34.3 5.8 %collective-permute-start.11 = (bf16[64,3584]{1,0:T(8,128)(2,1)S(1)}, bf16[64,3584]{1,0:T(8,128)(2,1)S(1)}, u32[]{:S(2)}, u32[]{:S(2)}) collective-permute-start(bf16[64,3584]{1,0:T(8,128)(2,1)S(1)} %join_rows.3), channel_id=1, source_target_pairs={{0,1},{1,0},{2,3},{3,2},{4,5},{5,4},{6,7},{7,6},{8,9},{9,8},{10,11... | collective-permute-start | bytes 1376264 | tf_op jit(solution)/shard_map/ppermute | solution.py:222
  34.4 9.0 %collective-permute-start.17 = (bf16[64,1024]{1,0:T(8,128)(2,1)S(1)}, bf16[64,1024]{1,0:T(8,128)(2,1)S(1)}, u32[]{:S(2)}, u32[]{:S(2)}) collective-permute-start(bf16[64,1024]{1,0:T(8,128)(2,1)S(1)} %collective-permute-done.9.refs_2_), channel_id=1, source_target_pairs={{0,4},{4,0},{8,12},{12,8},{1,5},{5,1},{9,13},{13,9},{2,6},{6,2},{1... | collective-permute-start | bytes 393224 | tf_op jit(solution)/shard_map/ppermute | solution.py:222
  34.6 14.9 %collective-permute-start.15 = (bf16[64,1280]{1,0:T(8,128)(2,1)S(1)}, bf16[64,1280]{1,0:T(8,128)(2,1)S(1)}, u32[]{:S(2)}, u32[]{:S(2)}) collective-permute-start(bf16[64,1280]{1,0:T(8,128)(2,1)S(1)} %get-tuple-element.27.refs_0_), channel_id=1, source_target_pairs={{0,4},{4,0},{8,12},{12,8},{1,5},{5,1},{9,13},{13,9},{2,6},{6,2},{1... | collective-permute-start | bytes 491528 | tf_op jit(solution)/shard_map/ppermute | solution.py:222
  36.5 28.6 %collective-permute-start.12 = (bf16[64,1280]{1,0:T(8,128)(2,1)S(1)}, bf16[64,1280]{1,0:T(8,128)(2,1)S(1)}, u32[]{:S(2)}, u32[]{:S(2)}) collective-permute-start(bf16[64,1280]{1,0:T(8,128)(2,1)S(1)} %get-tuple-element.28.refs_0_), channel_id=1, source_target_pairs={{0,4},{4,0},{8,12},{12,8},{1,5},{5,1},{9,13},{13,9},{2,6},{6,2},{1... | collective-permute-start | bytes 491528 | tf_op jit(solution)/shard_map/ppermute | solution.py:222
  36.7 28.4 %collective-permute-start.13 = (bf16[64,1280]{1,0:T(8,128)(2,1)S(1)}, bf16[64,1280]{1,0:T(8,128)(2,1)S(1)}, u32[]{:S(2)}, u32[]{:S(2)}) collective-permute-start(bf16[64,1280]{1,0:T(8,128)(2,1)S(1)} %get-tuple-element.28.refs_0_), channel_id=1, source_target_pairs={{0,8},{4,12},{8,0},{12,4},{1,9},{5,13},{9,1},{13,5},{2,10},{6,14},... | collective-permute-start | bytes 491528 | tf_op jit(solution)/shard_map/ppermute | solution.py:222
  40.0 25.1 %collective-permute-start.14 = (bf16[64,1280]{1,0:T(8,128)(2,1)S(1)}, bf16[64,1280]{1,0:T(8,128)(2,1)S(1)}, u32[]{:S(2)}, u32[]{:S(2)}) collective-permute-start(bf16[64,1280]{1,0:T(8,128)(2,1)S(1)} %get-tuple-element.28.refs_0_), channel_id=1, source_target_pairs={{0,12},{4,8},{8,4},{12,0},{1,13},{5,9},{9,5},{13,1},{2,14},{6,10},... | collective-permute-start | bytes 491528 | tf_op jit(solution)/shard_map/ppermute | solution.py:222
  43.4 14.5 %collective-permute-start.16 = (bf16[64,1280]{1,0:T(8,128)(2,1)S(1)}, bf16[64,1280]{1,0:T(8,128)(2,1)S(1)}, u32[]{:S(2)}, u32[]{:S(2)}) collective-permute-start(bf16[64,1280]{1,0:T(8,128)(2,1)S(1)} %collective-permute-done.10.refs_3_.refs_4_.refs_2_), channel_id=1, source_target_pairs={{0,4},{4,0},{8,12},{12,8},{1,5},{5,1},{9,13},{13,9},{2,6},{6,2},{1... | collective-permute-start | bytes 491528 | tf_op jit(solution)/shard_map/ppermute | solution.py:222

commit v6 on v5

--- a/solution.py
+++ b/solution.py
@@ -81,7 +81,7 @@
     outs = pl.pallas_call(
         functools.partial(cut_kernel, n_fa, n_fb),
         out_shape=shapes,
-        in_specs=[pl.BlockSpec(memory_space=pl.ANY)] * 2,
+        in_specs=[pl.BlockSpec(memory_space=pltpu.HBM)] * 2,
         out_specs=[pl.BlockSpec(memory_space=pltpu.VMEM)] * len(shapes),
         scratch_shapes=[pltpu.SemaphoreType.DMA((len(shapes),))],
         compiler_params=pltpu.CompilerParams(vmem_limit_bytes=VMEM),
@@ -222,36 +222,44 @@
     return lax.ppermute(x, axis, [(i, partner(i, step, size)) for i in range(size)])
 
 
-def gathered(x, axis, through=None):
-    size = lax.axis_size(axis)
-    blocks = [x]
-    for step in range(1, size):
-        low = step & -step
-        if through is None or low == step or not power_of_two(size):
-            blocks.append(sent(x, axis, step))
-        else:
-            blocks.append(sent(through(blocks[step - low]), axis, low))
-    return blocks
-
-
 def per_device(a_acts, b_acts):
     n_fa = lax.axis_size("fa")
     n_fb = lax.axis_size("fb")
     panels_a, panels_b = cut_panels(a_acts, b_acts, n_fa, n_fb)
     own_a = [panels_a[0]] + [sent(panels_a[s], "fa", s) for s in range(1, n_fa)]
     own_b = [panels_b[0]] + [sent(panels_b[s], "fb", s) for s in range(1, n_fb)]
-    full_width = panels_b[0].shape[1]
-    widths = chunk_widths(full_width, (4, 5, 5))
-    group_a, *parts_b = join_rows([(own_a, [panels_a[0].shape[1]]), (own_b, widths)])
-    chunks = [gathered(part, "fa", lambda block: block) for part in parts_b[:-1]]
-    chunks.append(gathered(parts_b[-1], "fa"))
-    far = n_fa // 2
-    all_a = gathered(group_a, "fb", lambda block: stacked([block], [chunks[0][1]] + [chunk[far] for chunk in chunks[:-1]]))
+    width_a, full_width = panels_a[0].shape[1], panels_b[0].shape[1]
+    widths = chunk_widths(full_width, (1, 1))
+    group_a, *parts_b = join_rows([(own_a, [width_a]), (own_b, widths), (own_b, [full_width])])
+    group_b = parts_b.pop()
+
+    whole = sent(group_b, "fa", 1)
+    chunks = []
+    for part in parts_b:
+        blocks = [part, None]
+        for step in range(2, n_fa):
+            low = step & -step
+            forward = power_of_two(n_fa) and low != step
+            if forward and blocks[step - low] is not None:
+                blocks.append(sent(blocks[step - low], "fa", low))
+            else:
+                blocks.append(sent(part, "fa", step))
+        chunks.append(blocks)
+    for blocks, block in zip(chunks, join_rows([([whole], widths)])):
+        blocks[1] = block
+
+    all_a = [group_a]
+    for step in range(1, n_fb):
+        low = step & -step
+        if power_of_two(n_fb) and low != step:
+            all_a.append(sent(stacked([all_a[step-low]],[chunks[0][2]]), "fb", low))
+        else:
+            all_a.append(sent(group_a, "fb", step))
     std_a = standardize_a(all_a, n_fa, n_fb)
     buffer = None
     column = 0
     for place, groups in enumerate(chunks):
-        after = [later[far] for later in chunks[place + 1 : -1]]
+        after = [later[2] for later in chunks[place + 1 : place + 2]]
         buffer = product_chunk(std_a, groups, column, full_width, buffer, after)
         column += groups[0].shape[1]
     return buffer

time: 72.6 us -> 68.1 us (0.938)
  starting transfers between devices: 20.4 us -> 15.8 us
  waiting for transfers between devices: 26.3 us -> 28.1 us
  Pallas kernels: 23.5 us -> 21.9 us
    ppermute x18 -> x14, starting transfers between devices: 20.4 us -> 15.8 us  [sent(): lax.ppermute(x, axis, [(i, partner(i, step, size)) for i in range(size)])]
    ppermute x18 -> x14, waiting for transfers between devices: 26.3 us -> 28.1 us  [sent(): lax.ppermute(x, axis, [(i, partner(i, step, size)) for i in range(size)])]
    pallas_call x3 -> x2, Pallas kernels: 20.6 us -> 18.9 us  [product_chunk(): pl.pallas_call(functools.partial(product_kernel, len(groups), column), ou...]
  transfers between devices with their start and end apart: 18 -> 14, of which waited for: 5 -> 4; matrix products, arithmetic and copies ran while one was open for 0% -> 0% of each run, Pallas kernels for 21% -> 17%
where the time goes in v6:
time: 68.1 us; the launch traced here: 67.9 us
  waiting for transfers between devices  28.1 us (41%)
  Pallas kernels  21.9 us (32%)
  starting transfers between devices  15.8 us (23%)
  local copies, waits for them, and re-layouts  2.04 us (3%)
    ppermute x14, waiting for transfers between devices, sent(): lax.ppermute(x, axis, [(i, partner(i, step, size)) for i in range(size)])  28.1 us
    pallas_call x2, Pallas kernels, product_chunk(): pl.pallas_call(functools.partial(product_kernel, len(groups), column), ou...  18.9 us
    ppermute x14, starting transfers between devices, sent(): lax.ppermute(x, axis, [(i, partner(i, step, size)) for i in range(size)])  15.8 us
    pallas_call x1, Pallas kernels, standardize_a(): pl.pallas_call(functools.partial(standardize_a_kernel, n_fa, n_fb), out_s...  2.12 us
    unnamed x4, local copies, waits for them, and re-layouts  2.04 us
  transfers between devices with their start and end apart: 14, of which 4 were waited for; matrix products, arithmetic and copies ran while one was open for 0% of the time, Pallas kernels for 17%

profile of v6, /device:TPU:0, one launch (start us, length us, event | category | flops | bytes accessed | tf_op | source)
XLA Modules:
  0.0 67.9 jit_solution(1908715737008139313)
XLA Ops:
  0.0 0.0 copy-start
  0.0 1.0 %copy-done = bf16[16,14336]{1,0:T(8,128)(2,1)S(1)} copy-done((bf16[16,14336]{1,0:T(8,128)(2,1)S(1)}, bf16[16,14336]{1,0:T(8,128)(2,1)}, u32[]{:S(2)}) %copy-start) | copy-done | bytes 458776
  1.0 0.0 copy-start.1
  1.0 1.0 %copy-done.1 = bf16[16,14336]{1,0:T(8,128)(2,1)S(1)} copy-done((bf16[16,14336]{1,0:T(8,128)(2,1)S(1)}, bf16[16,14336]{1,0:T(8,128)(2,1)}, u32[]{:S(2)}) %copy-start.1) | copy-done | bytes 458776
  2.0 0.7 %cut_panels.1 = (bf16[16,3584]{1,0:T(8,128)(2,1)S(1)}, bf16[16,3584]{1,0:T(8,128)(2,1)S(1)}, bf16[16,3584]{1,0:T(8,128)(2,1)S(1)}, bf16[16,3584]{1,0:T(8,128)(2,...) custom-call(bf16[16,14336]{1,0:T(8,128)(2,1)S(1)} %copy-done, ...), custom_call_target="tpu_custom_call" | custom-call | tf_op jit(solution)/shard_map/cut_panels/pallas_call | solution.py:81
  2.7 3.1 %collective-permute-start = (bf16[16,3584]{1,0:T(8,128)(2,1)S(1)}, bf16[16,3584]{1,0:T(8,128)(2,1)S(1)}, u32[]{:S(2)}, u32[]{:S(2)}) collective-permute-start(bf16[16,3584]{1,0:T(8,128)(2,1)S(1)} %get-tuple-element.20), channel_id=1, source_target_pairs={{0,4},{4,0},{8,12},{12,8},{1,5},{5,1},{9,13},{13,9},{2,6},{6,2},{1... | collective-permute-start | bytes 344072 | tf_op jit(solution)/shard_map/ppermute | solution.py:222
  5.8 2.6 %collective-permute-start.1 = (bf16[16,3584]{1,0:T(8,128)(2,1)S(1)}, bf16[16,3584]{1,0:T(8,128)(2,1)S(1)}, u32[]{:S(2)}, u32[]{:S(2)}) collective-permute-start(bf16[16,3584]{1,0:T(8,128)(2,1)S(1)} %get-tuple-element.21), channel_id=1, source_target_pairs={{0,8},{4,12},{8,0},{12,4},{1,9},{5,13},{9,1},{13,5},{2,10},{6,14},... | collective-permute-start | bytes 344072 | tf_op jit(solution)/shard_map/ppermute | solution.py:222
  8.4 0.0 collective-permute-start.2
  8.4 0.0 collective-permute-start.3
  8.4 1.7 %collective-permute-start.4 = (bf16[16,3584]{1,0:T(8,128)(2,1)S(1)}, bf16[16,3584]{1,0:T(8,128)(2,1)S(1)}, u32[]{:S(2)}, u32[]{:S(2)}) collective-permute-start(bf16[16,3584]{1,0:T(8,128)(2,1)S(1)} %get-tuple-element.25), channel_id=1, source_target_pairs={{0,2},{1,3},{2,0},{3,1},{4,6},{5,7},{6,4},{7,5},{8,10},{9,11},{10,... | collective-permute-start | bytes 344072 | tf_op jit(solution)/shard_map/ppermute | solution.py:222
  10.1 0.0 collective-permute-done.refs_1_
  10.1 0.1 collective-permute-start.5
  10.3 7.2 %collective-permute-done.1.refs_2_ = bf16[16,3584]{1,0:T(8,128)(2,1)S(1)} collective-permute-done((bf16[16,3584]{1,0:T(8,128)(2,1)S(1)}, bf16[16,3584]{1,0:T(8,128)(2,1)S(1)}, u32[]{:S(2)}, u32[]{:S(2)}) %collective-permute-start.1) | collective-permute-done | bytes 114720 | tf_op jit(solution)/shard_map/ppermute | solution.py:222
  17.5 0.0 collective-permute-done.2.refs_3_
  17.5 0.0 collective-permute-done.3.refs_5_.refs_9_
  17.5 0.0 collective-permute-done.4.refs_6_.refs_10_
  17.5 0.0 collective-permute-done.5.refs_7_.refs_11_
  17.5 0.1 join_rows.3
  17.6 1.6 %collective-permute-start.7 = (bf16[64,3584]{1,0:T(8,128)(2,1)S(1)}, bf16[64,3584]{1,0:T(8,128)(2,1)S(1)}, u32[]{:S(2)}, u32[]{:S(2)}) collective-permute-start(bf16[64,3584]{1,0:T(8,128)(2,1)S(1)} %get-tuple-element.27.refs_0_), channel_id=1, source_target_pairs={{0,2},{1,3},{2,0},{3,1},{4,6},{5,7},{6,4},{7,5},{8,10},{9,11},{10,... | collective-permute-start | bytes 1376264 | tf_op jit(solution)/shard_map/ppermute | solution.py:222
  19.2 2.8 %collective-permute-start.8 = (bf16[64,1792]{1,0:T(8,128)(2,1)S(1)}, bf16[64,1792]{1,0:T(8,128)(2,1)S(1)}, u32[]{:S(2)}, u32[]{:S(2)}) collective-permute-start(bf16[64,1792]{1,0:T(8,128)(2,1)S(1)} %get-tuple-element.28.refs_0_), channel_id=1, source_target_pairs={{0,8},{4,12},{8,0},{12,4},{1,9},{5,13},{9,1},{13,5},{2,10},{6,14},... | collective-permute-start | bytes 688136 | tf_op jit(solution)/shard_map/ppermute | solution.py:222
  22.0 0.0 collective-permute-start.6
  22.0 0.2 collective-permute-start.10
  22.2 9.3 %collective-permute-done.8.refs_1_.refs_2_ = bf16[64,1792]{1,0:T(8,128)(2,1)S(1)} collective-permute-done((bf16[64,1792]{1,0:T(8,128)(2,1)S(1)}, bf16[64,1792]{1,0:T(8,128)(2,1)S(1)}, u32[]{:S(2)}, u32[]{:S(2)}) %collective-permute-start.8) | collective-permute-done | bytes 229408 | tf_op jit(solution)/shard_map/ppermute | solution.py:222
  31.6 0.0 collective-permute-done.7.refs_0_.refs_2_
  31.6 0.1 collective-permute-start.9
  31.7 0.1 collective-permute-start.11
  31.8 3.5 %collective-permute-start.13 = (bf16[64,1792]{1,0:T(8,128)(2,1)S(1)}, bf16[64,1792]{1,0:T(8,128)(2,1)S(1)}, u32[]{:S(2)}, u32[]{:S(2)}) collective-permute-start(bf16[64,1792]{1,0:T(8,128)(2,1)S(1)} %collective-permute-done.8.refs_1_.refs_2_), channel_id=1, source_target_pairs={{0,4},{4,0},{8,12},{12,8},{1,5},{5,1},{9,13},{13,9},{2,6},{6,2},{1... | collective-permute-start | bytes 688136 | tf_op jit(solution)/shard_map/ppermute | solution.py:222
  35.3 10.3 %collective-permute-done.11.refs_4_.refs_2_ = bf16[64,1792]{1,0:T(8,128)(2,1)S(1)} collective-permute-done((bf16[64,1792]{1,0:T(8,128)(2,1)S(1)}, bf16[64,1792]{1,0:T(8,128)(2,1)S(1)}, u32[]{:S(2)}, u32[]{:S(2)}) %collective-permute-start.11) | collective-permute-done | bytes 229408 | tf_op jit(solution)/shard_map/ppermute | solution.py:222
  45.6 0.0 collective-permute-start.12
  45.6 0.0 collective-permute-done.10.refs_0_
  45.7 0.0 collective-permute-done.6.refs_1_
  45.7 0.0 collective-permute-done.9.refs_3_
  45.7 2.1 %standardize_a.1.a_ref = bf16[3584,256]{1,0:T(8,128)(2,1)S(1)} custom-call(bf16[64,3584]{1,0:T(8,128)(2,1)S(1)} %get-tuple-element.27.refs_0_, bf16[64,3584]{1,0:T(8,128)(2,1)S(1)} %collective-permute-done.6.refs_1_, bf16[64,3584]{1,0:T(8,128)(2,1)S(1)} %collective-permute-done.7.refs_0_.refs_2_, bf16[64,3584]{1,0:T(8,128)(2,1)S(1)} %collective-permute-done.9.refs_3_), custom_call_target="tpu_custom_call" | custom-call | flops 9175040 | bytes 3670016 | tf_op jit(solution)/shard_map/standardize_a/pallas_call | solution.py:143
  47.8 1.2 %collective-permute-done.13.refs_3_ = bf16[64,1792]{1,0:T(8,128)(2,1)S(1)} collective-permute-done((bf16[64,1792]{1,0:T(8,128)(2,1)S(1)}, bf16[64,1792]{1,0:T(8,128)(2,1)S(1)}, u32[]{:S(2)}, u32[]{:S(2)}) %collective-permute-start.13) | collective-permute-done | bytes 229408 | tf_op jit(solution)/shard_map/ppermute | solution.py:222
  49.0 9.4 %product_chunk.2.refs_4_ = f32[3584,3584]{1,0:T(8,128)} custom-call(bf16[3584,256]{1,0:T(8,128)(2,1)S(1)} %standardize_a.1.a_ref, bf16[64,1792]{1,0:T(8,128)(2,1)S(1)} %get-tuple-element.28.refs_0_, bf16[64,1792]{1,0:T(8,128)(2,1)S(1)} %get-tuple-element.32.refs_1_, bf16[64,1792]{1,0:T(8,128)(2,1)S(1)} %collective-permute-done.8.refs_1_.refs_2_, ...), custom_call_target="tpu_custom_call" | custom-call | flops 3288334336 | bytes 25690112 | tf_op jit(solution)/shard_map/product_chunk/pallas_call | solution.py:202
  58.4 0.0 collective-permute-done.12.refs_3_
  58.4 9.4 %product_chunk.3 = f32[3584,3584]{1,0:T(8,128)} custom-call(bf16[3584,256]{1,0:T(8,128)(2,1)S(1)} %standardize_a.1.a_ref, bf16[64,1792]{1,0:T(8,128)(2,1)S(1)} %get-tuple-element.29.refs_0_, bf16[64,1792]{1,0:T(8,128)(2,1)S(1)} %get-tuple-element.31.refs_1_, ...), custom_call_target="tpu_custom_call", output_to_operand_aliasing={{}: (5, {})} | custom-call | flops 3288334336 | bytes 25690112 | tf_op jit(solution)/shard_map/product_chunk/pallas_call | solution.py:202
  (2 shorter events, 0.1 us)
Async XLA Ops:
  0.0 1.0 %copy-start = (bf16[16,14336]{1,0:T(8,128)(2,1)S(1)}, bf16[16,14336]{1,0:T(8,128)(2,1)}, u32[]{:S(2)}) copy-start(bf16[16,14336]{1,0:T(8,128)(2,1)} %a_ref.1) | copy-start | bytes 1376260
  1.0 1.0 %copy-start.1 = (bf16[16,14336]{1,0:T(8,128)(2,1)S(1)}, bf16[16,14336]{1,0:T(8,128)(2,1)}, u32[]{:S(2)}) copy-start(bf16[16,14336]{1,0:T(8,128)(2,1)} %b_ref.1) | copy-start | bytes 1376260
  2.7 7.4 %collective-permute-start = (bf16[16,3584]{1,0:T(8,128)(2,1)S(1)}, bf16[16,3584]{1,0:T(8,128)(2,1)S(1)}, u32[]{:S(2)}, u32[]{:S(2)}) collective-permute-start(bf16[16,3584]{1,0:T(8,128)(2,1)S(1)} %get-tuple-element.20), channel_id=1, source_target_pairs={{0,4},{4,0},{8,12},{12,8},{1,5},{5,1},{9,13},{13,9},{2,6},{6,2},{1... | collective-permute-start | bytes 344072 | tf_op jit(solution)/shard_map/ppermute | solution.py:222
  5.8 11.7 %collective-permute-start.1 = (bf16[16,3584]{1,0:T(8,128)(2,1)S(1)}, bf16[16,3584]{1,0:T(8,128)(2,1)S(1)}, u32[]{:S(2)}, u32[]{:S(2)}) collective-permute-start(bf16[16,3584]{1,0:T(8,128)(2,1)S(1)} %get-tuple-element.21), channel_id=1, source_target_pairs={{0,8},{4,12},{8,0},{12,4},{1,9},{5,13},{9,1},{13,5},{2,10},{6,14},... | collective-permute-start | bytes 344072 | tf_op jit(solution)/shard_map/ppermute | solution.py:222
  8.4 9.1 %collective-permute-start.2 = (bf16[16,3584]{1,0:T(8,128)(2,1)S(1)}, bf16[16,3584]{1,0:T(8,128)(2,1)S(1)}, u32[]{:S(2)}, u32[]{:S(2)}) collective-permute-start(bf16[16,3584]{1,0:T(8,128)(2,1)S(1)} %get-tuple-element.22), channel_id=1, source_target_pairs={{0,12},{4,8},{8,4},{12,0},{1,13},{5,9},{9,5},{13,1},{2,14},{6,10},... | collective-permute-start | bytes 344072 | tf_op jit(solution)/shard_map/ppermute | solution.py:222
  8.4 9.1 %collective-permute-start.3 = (bf16[16,3584]{1,0:T(8,128)(2,1)S(1)}, bf16[16,3584]{1,0:T(8,128)(2,1)S(1)}, u32[]{:S(2)}, u32[]{:S(2)}) collective-permute-start(bf16[16,3584]{1,0:T(8,128)(2,1)S(1)} %get-tuple-element.24), channel_id=1, source_target_pairs={{0,1},{1,0},{2,3},{3,2},{4,5},{5,4},{6,7},{7,6},{8,9},{9,8},{10,11... | collective-permute-start | bytes 344072 | tf_op jit(solution)/shard_map/ppermute | solution.py:222
  8.4 9.1 %collective-permute-start.4 = (bf16[16,3584]{1,0:T(8,128)(2,1)S(1)}, bf16[16,3584]{1,0:T(8,128)(2,1)S(1)}, u32[]{:S(2)}, u32[]{:S(2)}) collective-permute-start(bf16[16,3584]{1,0:T(8,128)(2,1)S(1)} %get-tuple-element.25), channel_id=1, source_target_pairs={{0,2},{1,3},{2,0},{3,1},{4,6},{5,7},{6,4},{7,5},{8,10},{9,11},{10,... | collective-permute-start | bytes 344072 | tf_op jit(solution)/shard_map/ppermute | solution.py:222
  10.1 7.4 %collective-permute-start.5 = (bf16[16,3584]{1,0:T(8,128)(2,1)S(1)}, bf16[16,3584]{1,0:T(8,128)(2,1)S(1)}, u32[]{:S(2)}, u32[]{:S(2)}) collective-permute-start(bf16[16,3584]{1,0:T(8,128)(2,1)S(1)} %get-tuple-element.26), channel_id=1, source_target_pairs={{0,3},{1,2},{2,1},{3,0},{4,7},{5,6},{6,5},{7,4},{8,11},{9,10},{10,... | collective-permute-start | bytes 344072 | tf_op jit(solution)/shard_map/ppermute | solution.py:222
  17.6 13.9 %collective-permute-start.7 = (bf16[64,3584]{1,0:T(8,128)(2,1)S(1)}, bf16[64,3584]{1,0:T(8,128)(2,1)S(1)}, u32[]{:S(2)}, u32[]{:S(2)}) collective-permute-start(bf16[64,3584]{1,0:T(8,128)(2,1)S(1)} %get-tuple-element.27.refs_0_), channel_id=1, source_target_pairs={{0,2},{1,3},{2,0},{3,1},{4,6},{5,7},{6,4},{7,5},{8,10},{9,11},{10,... | collective-permute-start | bytes 1376264 | tf_op jit(solution)/shard_map/ppermute | solution.py:222
  19.2 12.4 %collective-permute-start.8 = (bf16[64,1792]{1,0:T(8,128)(2,1)S(1)}, bf16[64,1792]{1,0:T(8,128)(2,1)S(1)}, u32[]{:S(2)}, u32[]{:S(2)}) collective-permute-start(bf16[64,1792]{1,0:T(8,128)(2,1)S(1)} %get-tuple-element.28.refs_0_), channel_id=1, source_target_pairs={{0,8},{4,12},{8,0},{12,4},{1,9},{5,13},{9,1},{13,5},{2,10},{6,14},... | collective-permute-start | bytes 688136 | tf_op jit(solution)/shard_map/ppermute | solution.py:222
  22.0 23.7 %collective-permute-start.6 = (bf16[64,3584]{1,0:T(8,128)(2,1)S(1)}, bf16[64,3584]{1,0:T(8,128)(2,1)S(1)}, u32[]{:S(2)}, u32[]{:S(2)}) collective-permute-start(bf16[64,3584]{1,0:T(8,128)(2,1)S(1)} %get-tuple-element.27.refs_0_), channel_id=1, source_target_pairs={{0,1},{1,0},{2,3},{3,2},{4,5},{5,4},{6,7},{7,6},{8,9},{9,8},{10,11... | collective-permute-start | bytes 1376264 | tf_op jit(solution)/shard_map/ppermute | solution.py:222
  22.0 23.6 %collective-permute-start.10 = (bf16[64,3584]{1,0:T(8,128)(2,1)S(1)}, bf16[64,3584]{1,0:T(8,128)(2,1)S(1)}, u32[]{:S(2)}, u32[]{:S(2)}) collective-permute-start(bf16[64,3584]{1,0:T(8,128)(2,1)S(1)} %get-tuple-element.30), channel_id=1, source_target_pairs={{0,4},{4,0},{8,12},{12,8},{1,5},{5,1},{9,13},{13,9},{2,6},{6,2},{1... | collective-permute-start | bytes 1376264 | tf_op jit(solution)/shard_map/ppermute | solution.py:222
  31.6 14.1 %collective-permute-start.9 = (bf16[64,3584]{1,0:T(8,128)(2,1)S(1)}, bf16[64,3584]{1,0:T(8,128)(2,1)S(1)}, u32[]{:S(2)}, u32[]{:S(2)}) collective-permute-start(bf16[64,3584]{1,0:T(8,128)(2,1)S(1)} %join_rows.4), channel_id=1, source_target_pairs={{0,1},{1,0},{2,3},{3,2},{4,5},{5,4},{6,7},{7,6},{8,9},{9,8},{10,11... | collective-permute-start | bytes 1376264 | tf_op jit(solution)/shard_map/ppermute | solution.py:222
  31.7 13.9 %collective-permute-start.11 = (bf16[64,1792]{1,0:T(8,128)(2,1)S(1)}, bf16[64,1792]{1,0:T(8,128)(2,1)S(1)}, u32[]{:S(2)}, u32[]{:S(2)}) collective-permute-start(bf16[64,1792]{1,0:T(8,128)(2,1)S(1)} %get-tuple-element.29.refs_0_), channel_id=1, source_target_pairs={{0,8},{4,12},{8,0},{12,4},{1,9},{5,13},{9,1},{13,5},{2,10},{6,14},... | collective-permute-start | bytes 688136 | tf_op jit(solution)/shard_map/ppermute | solution.py:222
  31.8 17.2 %collective-permute-start.13 = (bf16[64,1792]{1,0:T(8,128)(2,1)S(1)}, bf16[64,1792]{1,0:T(8,128)(2,1)S(1)}, u32[]{:S(2)}, u32[]{:S(2)}) collective-permute-start(bf16[64,1792]{1,0:T(8,128)(2,1)S(1)} %collective-permute-done.8.refs_1_.refs_2_), channel_id=1, source_target_pairs={{0,4},{4,0},{8,12},{12,8},{1,5},{5,1},{9,13},{13,9},{2,6},{6,2},{1... | collective-permute-start | bytes 688136 | tf_op jit(solution)/shard_map/ppermute | solution.py:222
  45.6 12.8 %collective-permute-start.12 = (bf16[64,1792]{1,0:T(8,128)(2,1)S(1)}, bf16[64,1792]{1,0:T(8,128)(2,1)S(1)}, u32[]{:S(2)}, u32[]{:S(2)}) collective-permute-start(bf16[64,1792]{1,0:T(8,128)(2,1)S(1)} %collective-permute-done.11.refs_4_.refs_2_), channel_id=1, source_target_pairs={{0,4},{4,0},{8,12},{12,8},{1,5},{5,1},{9,13},{13,9},{2,6},{6,2},{1... | collective-permute-start | bytes 688136 | tf_op jit(solution)/shard_map/ppermute | solution.py:222

commit v7 on v6

--- a/solution.py
+++ b/solution.py
@@ -91,12 +91,11 @@
 
 
 def join_kernel(shapes, *refs):
-    n_in = sum(len_in for len_in, _ in shapes)
-    n_out = sum(len_out for _, len_out in shapes)
+    n_in = sum(len_in for len_in, _, _ in shapes)
+    n_out = sum(len_out for _, len_out, _ in shapes)
     ins, outs = refs[:n_in], refs[-n_out:]
-    for len_in, len_out in shapes:
+    for len_in, len_out, column in shapes:
         tok = ins[0].shape[0]
-        column = 0
         for out in outs[:len_out]:
             width = out.shape[1]
             for i in range(len_in):
@@ -106,14 +105,14 @@
 
 
 def join_rows(groups, after=()):
-    pieces = [piece for group, _ in groups for piece in group]
+    pieces = [piece for group, _, _ in groups for piece in group]
     shapes = [
         jax.ShapeDtypeStruct((group[0].shape[0] * len(group), width), group[0].dtype)
-        for group, widths in groups
+        for group, widths, _ in groups
         for width in widths
     ]
     return pl.pallas_call(
-        functools.partial(join_kernel, [(len(group), len(widths)) for group, widths in groups]),
+        functools.partial(join_kernel, [(len(group), len(widths), column) for group, widths, column in groups]),
         out_shape=shapes,
         in_specs=[pl.BlockSpec(memory_space=pltpu.VMEM)] * len(pieces)
         + [pl.BlockSpec(memory_space=pl.ANY)] * len(after),
@@ -124,7 +123,7 @@
 
 
 def stacked(pieces, after=()):
-    return join_rows([(pieces, [pieces[0].shape[1]])], after)[0]
+    return join_rows([(pieces, [pieces[0].shape[1]], 0)], after)[0]
 
 
 def standardize_a_kernel(n_fa, n_fb, *refs):
@@ -156,7 +155,8 @@
 
 def product_kernel(n_groups, column, a_ref, *refs):
     groups = refs[:n_groups]
-    out, slots, sems = refs[-3:]
+    out, token, slots, sems = refs[-4:]
+    token[...] = jnp.zeros_like(token)
     total, width = a_ref.shape[1], groups[0].shape[1]
     n_slots, height, strip = slots.shape
 
@@ -201,9 +201,12 @@
         args.append(buffer)
     return pl.pallas_call(
         functools.partial(product_kernel, len(groups), column),
-        out_shape=jax.ShapeDtypeStruct((height, full_width), jnp.float32),
+        out_shape=[
+            jax.ShapeDtypeStruct((height, full_width), jnp.float32),
+            jax.ShapeDtypeStruct((8, 128), jnp.float32),
+        ],
         in_specs=in_specs,
-        out_specs=pl.BlockSpec(memory_space=pl.ANY),
+        out_specs=[pl.BlockSpec(memory_space=pl.ANY), pl.BlockSpec(memory_space=pltpu.VMEM)],
         scratch_shapes=[
             pltpu.VMEM((n_slots, height, strip), jnp.float32),
             pltpu.SemaphoreType.DMA((n_slots,)),
@@ -220,6 +223,14 @@
 def sent(x, axis, step):
     size = lax.axis_size(axis)
     return lax.ppermute(x, axis, [(i, partner(i, step, size)) for i in range(size)])
+
+
+def forwarded(block, axis, step, blocks, after=()):
+    low = step & -step
+    if power_of_two(lax.axis_size(axis)):
+        held = blocks[step - low]
+        return sent(stacked([held], after) if after else held, axis, low)
+    return sent(block, axis, step)
 
 
 def per_device(a_acts, b_acts):
@@ -229,38 +240,43 @@
     own_a = [panels_a[0]] + [sent(panels_a[s], "fa", s) for s in range(1, n_fa)]
     own_b = [panels_b[0]] + [sent(panels_b[s], "fb", s) for s in range(1, n_fb)]
     width_a, full_width = panels_a[0].shape[1], panels_b[0].shape[1]
-    widths = chunk_widths(full_width, (1, 1))
-    group_a, *parts_b = join_rows([(own_a, [width_a]), (own_b, widths), (own_b, [full_width])])
-    group_b = parts_b.pop()
-
-    whole = sent(group_b, "fa", 1)
+    widths = chunk_widths(full_width, (4, 5, 5))
+    group_a, *parts_b, rest = join_rows(
+        [(own_a, [width_a], 0), (own_b, widths, 0), (own_b, [sum(widths[1:])], widths[0])]
+    )
+    near = sent(parts_b[0], "fa", 1)
+
     chunks = []
-    for part in parts_b:
-        blocks = [part, None]
-        for step in range(2, n_fa):
-            low = step & -step
-            forward = power_of_two(n_fa) and low != step
-            if forward and blocks[step - low] is not None:
-                blocks.append(sent(blocks[step - low], "fa", low))
-            else:
-                blocks.append(sent(part, "fa", step))
-        chunks.append(blocks)
-    for blocks, block in zip(chunks, join_rows([([whole], widths)])):
-        blocks[1] = block
+    for place, part in enumerate(parts_b):
+        if place:
+            part = stacked([part], [chunks[-1][2]])
+        chunks.append([part, near, sent(part, "fa", 2)])
+    near_rest = sent(stacked([rest], [chunks[0][2]]), "fa", 1)
 
     all_a = [group_a]
     for step in range(1, n_fb):
-        low = step & -step
-        if power_of_two(n_fb) and low != step:
-            all_a.append(sent(stacked([all_a[step-low]],[chunks[0][2]]), "fb", low))
+        if power_of_two(step):
+            all_a.append(sent(group_a, "fb", step))
         else:
-            all_a.append(sent(group_a, "fb", step))
+            all_a.append(forwarded(group_a, "fb", step, all_a, chunks[0][1:3]))
     std_a = standardize_a(all_a, n_fa, n_fb)
+
     buffer = None
     column = 0
+    done = []
     for place, groups in enumerate(chunks):
+        hold = [[], [std_a], done[:1]][min(place, 2)]
+        if place == 1:
+            for later, block in zip(chunks[1:], join_rows([([near_rest], widths[1:], 0)], done)):
+                later[1] = block
+        for step in range(3, n_fa):
+            if power_of_two(step):
+                groups.append(sent(groups[0], "fa", step))
+            else:
+                groups.append(forwarded(groups[0], "fa", step, groups, hold if step == 3 else ()))
         after = [later[2] for later in chunks[place + 1 : place + 2]]
-        buffer = product_chunk(std_a, groups, column, full_width, buffer, after)
+        buffer, token = product_chunk(std_a, groups, column, full_width, buffer, after)
+        done.append(token)
         column += groups[0].shape[1]
     return buffer
 

time: 68.1 us -> 73.3 us (1.076)
  starting transfers between devices: 15.8 us -> 20.7 us
  Pallas kernels: 21.9 us -> 24.8 us
  waiting for transfers between devices: 28.1 us -> 25.4 us
    ppermute x14 -> x17, starting transfers between devices: 15.8 us -> 20.7 us  [sent(): lax.ppermute(x, axis, [(i, partner(i, step, size)) for i in range(size)])]
    pallas_call x2 -> x3, Pallas kernels: 18.9 us -> 21.8 us  [product_chunk(): pl.pallas_call(functools.partial(product_kernel, len(groups), column), ou...]
    ppermute x14 -> x17, waiting for transfers between devices: 28.1 us -> 25.4 us  [sent(): lax.ppermute(x, axis, [(i, partner(i, step, size)) for i in range(size)])]
  transfers between devices with their start and end apart: 14 -> 17, of which waited for: 4 -> 6; matrix products, arithmetic and copies ran while one was open for 0% -> 0% of each run, Pallas kernels for 17% -> 22%
where the time goes in v7:
time: 73.3 us; the launch traced here: 73.1 us
  waiting for transfers between devices  25.4 us (35%)
  Pallas kernels  24.8 us (34%)
  starting transfers between devices  20.7 us (28%)
  local copies, waits for them, and re-layouts  2.04 us (3%)
    ppermute x17, waiting for transfers between devices, sent(): lax.ppermute(x, axis, [(i, partner(i, step, size)) for i in range(size)])  25.4 us
    pallas_call x3, Pallas kernels, product_chunk(): pl.pallas_call(functools.partial(product_kernel, len(groups), column), ou...  21.8 us
    ppermute x17, starting transfers between devices, sent(): lax.ppermute(x, axis, [(i, partner(i, step, size)) for i in range(size)])  20.7 us
    pallas_call x1, Pallas kernels, standardize_a(): pl.pallas_call(functools.partial(standardize_a_kernel, n_fa, n_fb), out_s...  2.12 us
    unnamed x4, local copies, waits for them, and re-layouts  2.04 us
  transfers between devices with their start and end apart: 17, of which 6 were waited for; matrix products, arithmetic and copies ran while one was open for 0% of the time, Pallas kernels for 22%

profile of v7, /device:TPU:0, one launch (start us, length us, event | category | flops | bytes accessed | tf_op | source)
XLA Modules:
  0.0 73.1 jit_solution(17853708595913209100)
XLA Ops:
  0.0 0.0 copy-start
  0.0 1.0 %copy-done = bf16[16,14336]{1,0:T(8,128)(2,1)S(1)} copy-done((bf16[16,14336]{1,0:T(8,128)(2,1)S(1)}, bf16[16,14336]{1,0:T(8,128)(2,1)}, u32[]{:S(2)}) %copy-start) | copy-done | bytes 458776
  1.0 0.0 copy-start.1
  1.0 1.0 %copy-done.1 = bf16[16,14336]{1,0:T(8,128)(2,1)S(1)} copy-done((bf16[16,14336]{1,0:T(8,128)(2,1)S(1)}, bf16[16,14336]{1,0:T(8,128)(2,1)}, u32[]{:S(2)}) %copy-start.1) | copy-done | bytes 458776
  2.0 0.7 cut_panels.1
  2.7 3.1 %collective-permute-start = (bf16[16,3584]{1,0:T(8,128)(2,1)S(1)}, bf16[16,3584]{1,0:T(8,128)(2,1)S(1)}, u32[]{:S(2)}, u32[]{:S(2)}) collective-permute-start(bf16[16,3584]{1,0:T(8,128)(2,1)S(1)} %get-tuple-element.25), channel_id=1, source_target_pairs={{0,4},{4,0},{8,12},{12,8},{1,5},{5,1},{9,13},{13,9},{2,6},{6,2},{1... | collective-permute-start | bytes 344072 | tf_op jit(solution)/shard_map/ppermute | solution.py:225
  5.8 2.6 %collective-permute-start.1 = (bf16[16,3584]{1,0:T(8,128)(2,1)S(1)}, bf16[16,3584]{1,0:T(8,128)(2,1)S(1)}, u32[]{:S(2)}, u32[]{:S(2)}) collective-permute-start(bf16[16,3584]{1,0:T(8,128)(2,1)S(1)} %get-tuple-element.26), channel_id=1, source_target_pairs={{0,8},{4,12},{8,0},{12,4},{1,9},{5,13},{9,1},{13,5},{2,10},{6,14},... | collective-permute-start | bytes 344072 | tf_op jit(solution)/shard_map/ppermute | solution.py:225
  8.4 0.0 collective-permute-start.2
  8.4 0.0 collective-permute-start.3
  8.4 1.7 %collective-permute-start.4 = (bf16[16,3584]{1,0:T(8,128)(2,1)S(1)}, bf16[16,3584]{1,0:T(8,128)(2,1)S(1)}, u32[]{:S(2)}, u32[]{:S(2)}) collective-permute-start(bf16[16,3584]{1,0:T(8,128)(2,1)S(1)} %get-tuple-element.30), channel_id=1, source_target_pairs={{0,2},{1,3},{2,0},{3,1},{4,6},{5,7},{6,4},{7,5},{8,10},{9,11},{10,... | collective-permute-start | bytes 344072 | tf_op jit(solution)/shard_map/ppermute | solution.py:225
  10.1 0.0 collective-permute-done.refs_1_
  10.1 0.1 collective-permute-start.5
  10.3 7.2 %collective-permute-done.1.refs_2_ = bf16[16,3584]{1,0:T(8,128)(2,1)S(1)} collective-permute-done((bf16[16,3584]{1,0:T(8,128)(2,1)S(1)}, bf16[16,3584]{1,0:T(8,128)(2,1)S(1)}, u32[]{:S(2)}, u32[]{:S(2)}) %collective-permute-start.1) | collective-permute-done | bytes 114720 | tf_op jit(solution)/shard_map/ppermute | solution.py:225
  17.5 0.0 collective-permute-done.2.refs_3_
  17.5 0.0 collective-permute-done.3.refs_5_.refs_9_
  17.5 0.0 collective-permute-done.4.refs_6_.refs_10_
  17.5 0.0 collective-permute-done.5.refs_7_.refs_11_
  17.5 0.1 join_rows.8
  17.6 1.6 %collective-permute-start.7 = (bf16[64,3584]{1,0:T(8,128)(2,1)S(1)}, bf16[64,3584]{1,0:T(8,128)(2,1)S(1)}, u32[]{:S(2)}, u32[]{:S(2)}) collective-permute-start(bf16[64,3584]{1,0:T(8,128)(2,1)S(1)} %get-tuple-element.32.refs_0_), channel_id=1, source_target_pairs={{0,2},{1,3},{2,0},{3,1},{4,6},{5,7},{6,4},{7,5},{8,10},{9,11},{10,... | collective-permute-start | bytes 1376264 | tf_op jit(solution)/shard_map/ppermute | solution.py:225
  19.2 2.8 %collective-permute-start.9 = (bf16[64,1024]{1,0:T(8,128)(2,1)S(1)}, bf16[64,1024]{1,0:T(8,128)(2,1)S(1)}, u32[]{:S(2)}, u32[]{:S(2)}) collective-permute-start(bf16[64,1024]{1,0:T(8,128)(2,1)S(1)} %get-tuple-element.33.refs_0_), channel_id=1, source_target_pairs={{0,8},{4,12},{8,0},{12,4},{1,9},{5,13},{9,1},{13,5},{2,10},{6,14},... | collective-permute-start | bytes 393224 | tf_op jit(solution)/shard_map/ppermute | solution.py:225
  22.0 0.2 collective-permute-start.8
  22.2 0.0 collective-permute-start.6
  22.2 5.2 %collective-permute-done.9.refs_2_.refs_1_ = bf16[64,1024]{1,0:T(8,128)(2,1)S(1)} collective-permute-done((bf16[64,1024]{1,0:T(8,128)(2,1)S(1)}, bf16[64,1024]{1,0:T(8,128)(2,1)S(1)}, u32[]{:S(2)}, u32[]{:S(2)}) %collective-permute-start.9) | collective-permute-done | bytes 131104 | tf_op jit(solution)/shard_map/ppermute | solution.py:225
  27.4 0.2 collective-permute-done.8.refs_1_
  27.6 1.6 %collective-permute-done.7.refs_0_.refs_2_ = bf16[64,3584]{1,0:T(8,128)(2,1)S(1)} collective-permute-done((bf16[64,3584]{1,0:T(8,128)(2,1)S(1)}, bf16[64,3584]{1,0:T(8,128)(2,1)S(1)}, u32[]{:S(2)}, u32[]{:S(2)}) %collective-permute-start.7) | collective-permute-done | bytes 458784 | tf_op jit(solution)/shard_map/ppermute | solution.py:225
  29.2 0.1 collective-permute-start.10
  29.3 2.4 %collective-permute-start.11 = (bf16[64,1280]{1,0:T(8,128)(2,1)S(1)}, bf16[64,1280]{1,0:T(8,128)(2,1)S(1)}, u32[]{:S(2)}, u32[]{:S(2)}) collective-permute-start(bf16[64,1280]{1,0:T(8,128)(2,1)S(1)} %join_rows.10.refs_0_), channel_id=1, source_target_pairs={{0,8},{4,12},{8,0},{12,4},{1,9},{5,13},{9,1},{13,5},{2,10},{6,14},... | collective-permute-start | bytes 491528 | tf_op jit(solution)/shard_map/ppermute | solution.py:225
  31.7 1.8 %collective-permute-start.12 = (bf16[64,2560]{1,0:T(8,128)(2,1)S(1)}, bf16[64,2560]{1,0:T(8,128)(2,1)S(1)}, u32[]{:S(2)}, u32[]{:S(2)}) collective-permute-start(bf16[64,2560]{1,0:T(8,128)(2,1)S(1)} %join_rows.12), channel_id=1, source_target_pairs={{0,4},{4,0},{8,12},{12,8},{1,5},{5,1},{9,13},{13,9},{2,6},{6,2},{1... | collective-permute-start | bytes 983048 | tf_op jit(solution)/shard_map/ppermute | solution.py:225
  33.5 0.2 collective-permute-start.13
  33.8 6.7 %collective-permute-done.11.refs_1_.refs_4_.refs_0_.refs_2_ = bf16[64,1280]{1,0:T(8,128)(2,1)S(1)} collective-permute-done((bf16[64,1280]{1,0:T(8,128)(2,1)S(1)}, bf16[64,1280]{1,0:T(8,128)(2,1)S(1)}, u32[]{:S(2)}, u32[]{:S(2)}) %collective-permute-start.11) | collective-permute-done | bytes 163872 | tf_op jit(solution)/shard_map/ppermute | solution.py:225
  40.5 0.1 collective-permute-start.14
  40.5 0.0 collective-permute-done.6.refs_1_
  40.5 0.0 collective-permute-done.10.refs_3_
  40.6 2.1 %standardize_a.1.a_ref.refs_1_ = bf16[3584,256]{1,0:T(8,128)(2,1)S(1)} custom-call(bf16[64,3584]{1,0:T(8,128)(2,1)S(1)} %get-tuple-element.32.refs_0_, bf16[64,3584]{1,0:T(8,128)(2,1)S(1)} %collective-permute-done.6.refs_1_, bf16[64,3584]{1,0:T(8,128)(2,1)S(1)} %collective-permute-done.7.refs_0_.refs_2_, bf16[64,3584]{1,0:T(8,128)(2,1)S(1)} %collective-permute-done.10.refs_3_), custom_call_target="tpu_custom_call" | custom-call | flops 9175040 | bytes 3670016 | tf_op jit(solution)/shard_map/standardize_a/pallas_call | solution.py:142
  42.7 3.8 %collective-permute-start.16 = (bf16[64,1280]{1,0:T(8,128)(2,1)S(1)}, bf16[64,1280]{1,0:T(8,128)(2,1)S(1)}, u32[]{:S(2)}, u32[]{:S(2)}) collective-permute-start(bf16[64,1280]{1,0:T(8,128)(2,1)S(1)} %join_rows.15), channel_id=1, source_target_pairs={{0,4},{4,0},{8,12},{12,8},{1,5},{5,1},{9,13},{13,9},{2,6},{6,2},{1... | collective-permute-start | bytes 491528 | tf_op jit(solution)/shard_map/ppermute | solution.py:225
  46.5 4.6 %collective-permute-done.13.refs_3_ = bf16[64,1024]{1,0:T(8,128)(2,1)S(1)} collective-permute-done((bf16[64,1024]{1,0:T(8,128)(2,1)S(1)}, bf16[64,1024]{1,0:T(8,128)(2,1)S(1)}, u32[]{:S(2)}, u32[]{:S(2)}) %collective-permute-start.13) | collective-permute-done | bytes 131104 | tf_op jit(solution)/shard_map/ppermute | solution.py:225
  51.1 6.1 %product_chunk.3 = (f32[3584,3584]{1,0:T(8,128)}, f32[8,128]{1,0:T(8,128)S(1)}) custom-call(bf16[3584,256]{1,0:T(8,128)(2,1)S(1)} %standardize_a.1.a_ref.refs_1_, bf16[64,1024]{1,0:T(8,128)(2,1)S(1)} %get-tuple-element.33.refs_0_, bf16[64,1024]{1,0:T(8,128)(2,1)S(1)} %collective-permute-done.8.refs_1_, ...), custom_call_target="tpu_custom_call" | custom-call | flops 1879048192 | bytes 14680064 | tf_op jit(solution)/shard_map/product_chunk/pallas_call | solution.py:202
  57.3 0.0 collective-permute-done.14.refs_0_.refs_4_.refs_2_
  57.3 0.1 collective-permute-start.15
  57.4 0.0 collective-permute-done.12.refs_0_
  57.4 0.0 collective-permute-done.16.refs_3_
  57.4 7.8 %product_chunk.4 = (f32[3584,3584]{1,0:T(8,128)}, f32[8,128]{1,0:T(8,128)}) custom-call(bf16[3584,256]{1,0:T(8,128)(2,1)S(1)} %standardize_a.1.a_ref.refs_1_, bf16[64,1280]{1,0:T(8,128)(2,1)S(1)} %join_rows.10.refs_0_, bf16[64,1280]{1,0:T(8,128)(2,1)S(1)} %get-tuple-element.39.refs_1_, ...), custom_call_target="tpu_custom_call", output_to_operand_aliasing={{0}: (6, {})} | custom-call | flops 2348810240 | bytes 18350080 | tf_op jit(solution)/shard_map/product_chunk/pallas_call | solution.py:202
  65.3 0.0 collective-permute-done.15.refs_3_
  65.3 7.8 %product_chunk.5 = (f32[3584,3584]{1,0:T(8,128)}, f32[8,128]{1,0:T(8,128)}) custom-call(bf16[3584,256]{1,0:T(8,128)(2,1)S(1)} %standardize_a.1.a_ref.refs_1_, bf16[64,1280]{1,0:T(8,128)(2,1)S(1)} %join_rows.11.refs_0_, bf16[64,1280]{1,0:T(8,128)(2,1)S(1)} %get-tuple-element.38.refs_1_, ...), custom_call_target="tpu_custom_call", output_to_operand_aliasing={{0}: (5, {})} | custom-call | flops 2348810240 | bytes 18350080 | tf_op jit(solution)/shard_map/product_chunk/pallas_call | solution.py:202
  (7 shorter events, 0.1 us)
Async XLA Ops:
  0.0 1.0 %copy-start = (bf16[16,14336]{1,0:T(8,128)(2,1)S(1)}, bf16[16,14336]{1,0:T(8,128)(2,1)}, u32[]{:S(2)}) copy-start(bf16[16,14336]{1,0:T(8,128)(2,1)} %a_ref.1) | copy-start | bytes 1376260
  1.0 1.0 %copy-start.1 = (bf16[16,14336]{1,0:T(8,128)(2,1)S(1)}, bf16[16,14336]{1,0:T(8,128)(2,1)}, u32[]{:S(2)}) copy-start(bf16[16,14336]{1,0:T(8,128)(2,1)} %b_ref.1) | copy-start | bytes 1376260
  2.7 7.4 %collective-permute-start = (bf16[16,3584]{1,0:T(8,128)(2,1)S(1)}, bf16[16,3584]{1,0:T(8,128)(2,1)S(1)}, u32[]{:S(2)}, u32[]{:S(2)}) collective-permute-start(bf16[16,3584]{1,0:T(8,128)(2,1)S(1)} %get-tuple-element.25), channel_id=1, source_target_pairs={{0,4},{4,0},{8,12},{12,8},{1,5},{5,1},{9,13},{13,9},{2,6},{6,2},{1... | collective-permute-start | bytes 344072 | tf_op jit(solution)/shard_map/ppermute | solution.py:225
  5.8 11.7 %collective-permute-start.1 = (bf16[16,3584]{1,0:T(8,128)(2,1)S(1)}, bf16[16,3584]{1,0:T(8,128)(2,1)S(1)}, u32[]{:S(2)}, u32[]{:S(2)}) collective-permute-start(bf16[16,3584]{1,0:T(8,128)(2,1)S(1)} %get-tuple-element.26), channel_id=1, source_target_pairs={{0,8},{4,12},{8,0},{12,4},{1,9},{5,13},{9,1},{13,5},{2,10},{6,14},... | collective-permute-start | bytes 344072 | tf_op jit(solution)/shard_map/ppermute | solution.py:225
  8.4 9.1 %collective-permute-start.2 = (bf16[16,3584]{1,0:T(8,128)(2,1)S(1)}, bf16[16,3584]{1,0:T(8,128)(2,1)S(1)}, u32[]{:S(2)}, u32[]{:S(2)}) collective-permute-start(bf16[16,3584]{1,0:T(8,128)(2,1)S(1)} %get-tuple-element.27), channel_id=1, source_target_pairs={{0,12},{4,8},{8,4},{12,0},{1,13},{5,9},{9,5},{13,1},{2,14},{6,10},... | collective-permute-start | bytes 344072 | tf_op jit(solution)/shard_map/ppermute | solution.py:225
  8.4 9.1 %collective-permute-start.3 = (bf16[16,3584]{1,0:T(8,128)(2,1)S(1)}, bf16[16,3584]{1,0:T(8,128)(2,1)S(1)}, u32[]{:S(2)}, u32[]{:S(2)}) collective-permute-start(bf16[16,3584]{1,0:T(8,128)(2,1)S(1)} %get-tuple-element.29), channel_id=1, source_target_pairs={{0,1},{1,0},{2,3},{3,2},{4,5},{5,4},{6,7},{7,6},{8,9},{9,8},{10,11... | collective-permute-start | bytes 344072 | tf_op jit(solution)/shard_map/ppermute | solution.py:225
  8.4 9.1 %collective-permute-start.4 = (bf16[16,3584]{1,0:T(8,128)(2,1)S(1)}, bf16[16,3584]{1,0:T(8,128)(2,1)S(1)}, u32[]{:S(2)}, u32[]{:S(2)}) collective-permute-start(bf16[16,3584]{1,0:T(8,128)(2,1)S(1)} %get-tuple-element.30), channel_id=1, source_target_pairs={{0,2},{1,3},{2,0},{3,1},{4,6},{5,7},{6,4},{7,5},{8,10},{9,11},{10,... | collective-permute-start | bytes 344072 | tf_op jit(solution)/shard_map/ppermute | solution.py:225
  10.1 7.4 %collective-permute-start.5 = (bf16[16,3584]{1,0:T(8,128)(2,1)S(1)}, bf16[16,3584]{1,0:T(8,128)(2,1)S(1)}, u32[]{:S(2)}, u32[]{:S(2)}) collective-permute-start(bf16[16,3584]{1,0:T(8,128)(2,1)S(1)} %get-tuple-element.31), channel_id=1, source_target_pairs={{0,3},{1,2},{2,1},{3,0},{4,7},{5,6},{6,5},{7,4},{8,11},{9,10},{10,... | collective-permute-start | bytes 344072 | tf_op jit(solution)/shard_map/ppermute | solution.py:225
  17.6 11.5 %collective-permute-start.7 = (bf16[64,3584]{1,0:T(8,128)(2,1)S(1)}, bf16[64,3584]{1,0:T(8,128)(2,1)S(1)}, u32[]{:S(2)}, u32[]{:S(2)}) collective-permute-start(bf16[64,3584]{1,0:T(8,128)(2,1)S(1)} %get-tuple-element.32.refs_0_), channel_id=1, source_target_pairs={{0,2},{1,3},{2,0},{3,1},{4,6},{5,7},{6,4},{7,5},{8,10},{9,11},{10,... | collective-permute-start | bytes 1376264 | tf_op jit(solution)/shard_map/ppermute | solution.py:225
  19.2 8.2 %collective-permute-start.9 = (bf16[64,1024]{1,0:T(8,128)(2,1)S(1)}, bf16[64,1024]{1,0:T(8,128)(2,1)S(1)}, u32[]{:S(2)}, u32[]{:S(2)}) collective-permute-start(bf16[64,1024]{1,0:T(8,128)(2,1)S(1)} %get-tuple-element.33.refs_0_), channel_id=1, source_target_pairs={{0,8},{4,12},{8,0},{12,4},{1,9},{5,13},{9,1},{13,5},{2,10},{6,14},... | collective-permute-start | bytes 393224 | tf_op jit(solution)/shard_map/ppermute | solution.py:225
  22.0 5.6 %collective-permute-start.8 = (bf16[64,1024]{1,0:T(8,128)(2,1)S(1)}, bf16[64,1024]{1,0:T(8,128)(2,1)S(1)}, u32[]{:S(2)}, u32[]{:S(2)}) collective-permute-start(bf16[64,1024]{1,0:T(8,128)(2,1)S(1)} %get-tuple-element.33.refs_0_), channel_id=1, source_target_pairs={{0,4},{4,0},{8,12},{12,8},{1,5},{5,1},{9,13},{13,9},{2,6},{6,2},{1... | collective-permute-start | bytes 393224 | tf_op jit(solution)/shard_map/ppermute | solution.py:225
  22.2 18.3 %collective-permute-start.6 = (bf16[64,3584]{1,0:T(8,128)(2,1)S(1)}, bf16[64,3584]{1,0:T(8,128)(2,1)S(1)}, u32[]{:S(2)}, u32[]{:S(2)}) collective-permute-start(bf16[64,3584]{1,0:T(8,128)(2,1)S(1)} %get-tuple-element.32.refs_0_), channel_id=1, source_target_pairs={{0,1},{1,0},{2,3},{3,2},{4,5},{5,4},{6,7},{7,6},{8,9},{9,8},{10,11... | collective-permute-start | bytes 1376264 | tf_op jit(solution)/shard_map/ppermute | solution.py:225
  29.2 11.4 %collective-permute-start.10 = (bf16[64,3584]{1,0:T(8,128)(2,1)S(1)}, bf16[64,3584]{1,0:T(8,128)(2,1)S(1)}, u32[]{:S(2)}, u32[]{:S(2)}) collective-permute-start(bf16[64,3584]{1,0:T(8,128)(2,1)S(1)} %join_rows.9), channel_id=1, source_target_pairs={{0,1},{1,0},{2,3},{3,2},{4,5},{5,4},{6,7},{7,6},{8,9},{9,8},{10,11... | collective-permute-start | bytes 1376264 | tf_op jit(solution)/shard_map/ppermute | solution.py:225
  29.3 11.2 %collective-permute-start.11 = (bf16[64,1280]{1,0:T(8,128)(2,1)S(1)}, bf16[64,1280]{1,0:T(8,128)(2,1)S(1)}, u32[]{:S(2)}, u32[]{:S(2)}) collective-permute-start(bf16[64,1280]{1,0:T(8,128)(2,1)S(1)} %join_rows.10.refs_0_), channel_id=1, source_target_pairs={{0,8},{4,12},{8,0},{12,4},{1,9},{5,13},{9,1},{13,5},{2,10},{6,14},... | collective-permute-start | bytes 491528 | tf_op jit(solution)/shard_map/ppermute | solution.py:225
  31.7 25.7 %collective-permute-start.12 = (bf16[64,2560]{1,0:T(8,128)(2,1)S(1)}, bf16[64,2560]{1,0:T(8,128)(2,1)S(1)}, u32[]{:S(2)}, u32[]{:S(2)}) collective-permute-start(bf16[64,2560]{1,0:T(8,128)(2,1)S(1)} %join_rows.12), channel_id=1, source_target_pairs={{0,4},{4,0},{8,12},{12,8},{1,5},{5,1},{9,13},{13,9},{2,6},{6,2},{1... | collective-permute-start | bytes 983048 | tf_op jit(solution)/shard_map/ppermute | solution.py:225
  33.5 17.6 %collective-permute-start.13 = (bf16[64,1024]{1,0:T(8,128)(2,1)S(1)}, bf16[64,1024]{1,0:T(8,128)(2,1)S(1)}, u32[]{:S(2)}, u32[]{:S(2)}) collective-permute-start(bf16[64,1024]{1,0:T(8,128)(2,1)S(1)} %collective-permute-done.9.refs_2_.refs_1_), channel_id=1, source_target_pairs={{0,4},{4,0},{8,12},{12,8},{1,5},{5,1},{9,13},{13,9},{2,6},{6,2},{1... | collective-permute-start | bytes 393224 | tf_op jit(solution)/shard_map/ppermute | solution.py:225
  40.5 16.8 %collective-permute-start.14 = (bf16[64,1280]{1,0:T(8,128)(2,1)S(1)}, bf16[64,1280]{1,0:T(8,128)(2,1)S(1)}, u32[]{:S(2)}, u32[]{:S(2)}) collective-permute-start(bf16[64,1280]{1,0:T(8,128)(2,1)S(1)} %join_rows.11.refs_0_), channel_id=1, source_target_pairs={{0,8},{4,12},{8,0},{12,4},{1,9},{5,13},{9,1},{13,5},{2,10},{6,14},... | collective-permute-start | bytes 491528 | tf_op jit(solution)/shard_map/ppermute | solution.py:225
  42.7 14.7 %collective-permute-start.16 = (bf16[64,1280]{1,0:T(8,128)(2,1)S(1)}, bf16[64,1280]{1,0:T(8,128)(2,1)S(1)}, u32[]{:S(2)}, u32[]{:S(2)}) collective-permute-start(bf16[64,1280]{1,0:T(8,128)(2,1)S(1)} %join_rows.15), channel_id=1, source_target_pairs={{0,4},{4,0},{8,12},{12,8},{1,5},{5,1},{9,13},{13,9},{2,6},{6,2},{1... | collective-permute-start | bytes 491528 | tf_op jit(solution)/shard_map/ppermute | solution.py:225
  57.3 8.0 %collective-permute-start.15 = (bf16[64,1280]{1,0:T(8,128)(2,1)S(1)}, bf16[64,1280]{1,0:T(8,128)(2,1)S(1)}, u32[]{:S(2)}, u32[]{:S(2)}) collective-permute-start(bf16[64,1280]{1,0:T(8,128)(2,1)S(1)} %join_rows.14), channel_id=1, source_target_pairs={{0,4},{4,0},{8,12},{12,8},{1,5},{5,1},{9,13},{13,9},{2,6},{6,2},{1... | collective-permute-start | bytes 491528 | tf_op jit(solution)/shard_map/ppermute | solution.py:225

commit v8 on v7

--- a/solution.py
+++ b/solution.py
@@ -84,7 +84,7 @@
         in_specs=[pl.BlockSpec(memory_space=pltpu.HBM)] * 2,
         out_specs=[pl.BlockSpec(memory_space=pltpu.VMEM)] * len(shapes),
         scratch_shapes=[pltpu.SemaphoreType.DMA((len(shapes),))],
-        compiler_params=pltpu.CompilerParams(vmem_limit_bytes=VMEM),
+        compiler_params=pltpu.CompilerParams(vmem_limit_bytes=60*1024*1024),
         name="cut_panels",
     )(a_acts, b_acts)
     return outs[:n_fa], outs[n_fa:]
@@ -155,8 +155,7 @@
 
 def product_kernel(n_groups, column, a_ref, *refs):
     groups = refs[:n_groups]
-    out, token, slots, sems = refs[-4:]
-    token[...] = jnp.zeros_like(token)
+    out, slots, sems = refs[-3:]
     total, width = a_ref.shape[1], groups[0].shape[1]
     n_slots, height, strip = slots.shape
 
@@ -201,12 +200,9 @@
         args.append(buffer)
     return pl.pallas_call(
         functools.partial(product_kernel, len(groups), column),
-        out_shape=[
-            jax.ShapeDtypeStruct((height, full_width), jnp.float32),
-            jax.ShapeDtypeStruct((8, 128), jnp.float32),
-        ],
+        out_shape=jax.ShapeDtypeStruct((height, full_width), jnp.float32),
         in_specs=in_specs,
-        out_specs=[pl.BlockSpec(memory_space=pl.ANY), pl.BlockSpec(memory_space=pltpu.VMEM)],
+        out_specs=pl.BlockSpec(memory_space=pl.ANY),
         scratch_shapes=[
             pltpu.VMEM((n_slots, height, strip), jnp.float32),
             pltpu.SemaphoreType.DMA((n_slots,)),
@@ -240,19 +236,11 @@
     own_a = [panels_a[0]] + [sent(panels_a[s], "fa", s) for s in range(1, n_fa)]
     own_b = [panels_b[0]] + [sent(panels_b[s], "fb", s) for s in range(1, n_fb)]
     width_a, full_width = panels_a[0].shape[1], panels_b[0].shape[1]
-    widths = chunk_widths(full_width, (4, 5, 5))
-    group_a, *parts_b, rest = join_rows(
-        [(own_a, [width_a], 0), (own_b, widths, 0), (own_b, [sum(widths[1:])], widths[0])]
-    )
-    near = sent(parts_b[0], "fa", 1)
-
-    chunks = []
-    for place, part in enumerate(parts_b):
-        if place:
-            part = stacked([part], [chunks[-1][2]])
-        chunks.append([part, near, sent(part, "fa", 2)])
-    near_rest = sent(stacked([rest], [chunks[0][2]]), "fa", 1)
-
+    widths = chunk_widths(full_width, (8, 6))
+    group_a, *parts_b = join_rows([(own_a, [width_a], 0), (own_b, widths, 0)])
+
+    first = parts_b[0]
+    chunks = [[first, sent(first, "fa", 1), sent(first, "fa", 2)]]
     all_a = [group_a]
     for step in range(1, n_fb):
         if power_of_two(step):
@@ -260,23 +248,23 @@
         else:
             all_a.append(forwarded(group_a, "fb", step, all_a, chunks[0][1:3]))
     std_a = standardize_a(all_a, n_fa, n_fb)
+    for part in parts_b[1:]:
+        part = stacked([part], chunks[-1][2:3])
+        across = sent(part, "fa", 2)
+        near = sent(stacked([part], [across, std_a]), "fa", 1)
+        chunks.append([part, near, across])
 
     buffer = None
     column = 0
-    done = []
     for place, groups in enumerate(chunks):
-        hold = [[], [std_a], done[:1]][min(place, 2)]
-        if place == 1:
-            for later, block in zip(chunks[1:], join_rows([([near_rest], widths[1:], 0)], done)):
-                later[1] = block
+        hold = [std_a] if place else []
         for step in range(3, n_fa):
             if power_of_two(step):
                 groups.append(sent(groups[0], "fa", step))
             else:
                 groups.append(forwarded(groups[0], "fa", step, groups, hold if step == 3 else ()))
         after = [later[2] for later in chunks[place + 1 : place + 2]]
-        buffer, token = product_chunk(std_a, groups, column, full_width, buffer, after)
-        done.append(token)
+        buffer = product_chunk(std_a, groups, column, full_width, buffer, after)
         column += groups[0].shape[1]
     return buffer
 

time: 73.3 us -> 68.5 us (0.935)
  starting transfers between devices: 20.7 us -> 18.8 us
  Pallas kernels: 24.8 us -> 23.4 us
  waiting for transfers between devices: 25.4 us -> 24.3 us
    pallas_call x3 -> x2, Pallas kernels: 21.8 us -> 18.9 us  [product_chunk(): pl.pallas_call(functools.partial(product_kernel, len(groups), column), ou...]
    ppermute x17 -> x15, starting transfers between devices: 20.7 us -> 18.8 us  [sent(): lax.ppermute(x, axis, [(i, partner(i, step, size)) for i in range(size)])]
    pallas_call x1, Pallas kernels: 0.69 us -> 2.21 us  [cut_panels(): pl.pallas_call(functools.partial(cut_kernel, n_fa, n_fb), out_shape=shape...]
    ppermute x17 -> x15, waiting for transfers between devices: 25.4 us -> 24.3 us  [sent(): lax.ppermute(x, axis, [(i, partner(i, step, size)) for i in range(size)])]
  transfers between devices with their start and end apart: 17 -> 15, of which waited for: 6 -> 4; matrix products, arithmetic and copies ran while one was open for 0% -> 0% of each run, Pallas kernels for 22% -> 19%
where the time goes in v8:
time: 68.5 us; the launch traced here: 68.4 us
  waiting for transfers between devices  24.3 us (35%)
  Pallas kernels  23.4 us (34%)
  starting transfers between devices  18.8 us (27%)
  local copies, waits for them, and re-layouts  1.79 us (3%)
    ppermute x15, waiting for transfers between devices, sent(): lax.ppermute(x, axis, [(i, partner(i, step, size)) for i in range(size)])  24.3 us
    pallas_call x2, Pallas kernels, product_chunk(): pl.pallas_call(functools.partial(product_kernel, len(groups), column), ou...  18.9 us
    ppermute x15, starting transfers between devices, sent(): lax.ppermute(x, axis, [(i, partner(i, step, size)) for i in range(size)])  18.8 us
    pallas_call x1, Pallas kernels, cut_panels(): pl.pallas_call(functools.partial(cut_kernel, n_fa, n_fb), out_shape=shape...  2.21 us
    pallas_call x1, Pallas kernels, standardize_a(): pl.pallas_call(functools.partial(standardize_a_kernel, n_fa, n_fb), out_s...  2.11 us
    unnamed x4, local copies, waits for them, and re-layouts  1.79 us
  transfers between devices with their start and end apart: 15, of which 4 were waited for; matrix products, arithmetic and copies ran while one was open for 0% of the time, Pallas kernels for 19%

profile of v8, /device:TPU:0, one launch (start us, length us, event | category | flops | bytes accessed | tf_op | source)
XLA Modules:
  0.0 68.4 jit_solution(2214018628597074133)
XLA Ops:
  0.0 2.2 %cut_panels.1 = (bf16[16,3584]{1,0:T(8,128)(2,1)}, bf16[16,3584]{1,0:T(8,128)(2,1)}, bf16[16,3584]{1,0:T(8,128)(2,1)}, bf16[16,3584]{1,0:T(8,128)(2,1)}, bf16[16...) custom-call(bf16[16,14336]{1,0:T(8,128)(2,1)} %a_ref.1, ...), custom_call_target="tpu_custom_call" | custom-call | tf_op jit(solution)/shard_map/cut_panels/pallas_call | solution.py:81
  2.2 3.1 %collective-permute-start = (bf16[16,3584]{1,0:T(8,128)(2,1)}, bf16[16,3584]{1,0:T(8,128)(2,1)S(1)}, u32[]{:S(2)}, u32[]{:S(2)}) collective-permute-start(bf16[16,3584]{1,0:T(8,128)(2,1)} %get-tuple-element.17), channel_id=1, source_target_pairs={{0,4},{4,0},{8,12},{12,8},{1,5},{5,1},{9,13},{13,9},{2,6},{6,2},{1... | collective-permute-start | bytes 344072 | tf_op jit(solution)/shard_map/ppermute | solution.py:221
  5.3 2.6 %collective-permute-start.1 = (bf16[16,3584]{1,0:T(8,128)(2,1)}, bf16[16,3584]{1,0:T(8,128)(2,1)S(1)}, u32[]{:S(2)}, u32[]{:S(2)}) collective-permute-start(bf16[16,3584]{1,0:T(8,128)(2,1)} %get-tuple-element.18), channel_id=1, source_target_pairs={{0,8},{4,12},{8,0},{12,4},{1,9},{5,13},{9,1},{13,5},{2,10},{6,14},... | collective-permute-start | bytes 344072 | tf_op jit(solution)/shard_map/ppermute | solution.py:221
  7.9 0.0 collective-permute-start.2
  7.9 0.0 collective-permute-start.3
  7.9 1.7 %collective-permute-start.4 = (bf16[16,3584]{1,0:T(8,128)(2,1)}, bf16[16,3584]{1,0:T(8,128)(2,1)S(1)}, u32[]{:S(2)}, u32[]{:S(2)}) collective-permute-start(bf16[16,3584]{1,0:T(8,128)(2,1)} %get-tuple-element.22), channel_id=1, source_target_pairs={{0,2},{1,3},{2,0},{3,1},{4,6},{5,7},{6,4},{7,5},{8,10},{9,11},{10,... | collective-permute-start | bytes 344072 | tf_op jit(solution)/shard_map/ppermute | solution.py:221
  9.6 0.0 collective-permute-done.refs_1_
  9.6 0.1 collective-permute-start.5
  9.8 7.4 %collective-permute-done.1.refs_2_ = bf16[16,3584]{1,0:T(8,128)(2,1)S(1)} collective-permute-done((bf16[16,3584]{1,0:T(8,128)(2,1)}, bf16[16,3584]{1,0:T(8,128)(2,1)S(1)}, u32[]{:S(2)}, u32[]{:S(2)}) %collective-permute-start.1) | collective-permute-done | bytes 114720 | tf_op jit(solution)/shard_map/ppermute | solution.py:221
  17.2 0.0 collective-permute-done.2.refs_3_
  17.2 0.0 collective-permute-done.3.refs_5_
  17.2 0.0 collective-permute-done.4.refs_6_
  17.2 0.0 collective-permute-done.5.refs_7_
  17.2 0.0 copy-start
  17.3 0.9 %copy-done = bf16[16,3584]{1,0:T(8,128)(2,1)S(1)} copy-done((bf16[16,3584]{1,0:T(8,128)(2,1)S(1)}, bf16[16,3584]{1,0:T(8,128)(2,1)}, u32[]{:S(2)}) %copy-start) | copy-done | bytes 114712
  18.1 0.0 copy-start.1
  18.1 0.9 %copy-done.1 = bf16[16,3584]{1,0:T(8,128)(2,1)S(1)} copy-done((bf16[16,3584]{1,0:T(8,128)(2,1)S(1)}, bf16[16,3584]{1,0:T(8,128)(2,1)}, u32[]{:S(2)}) %copy-start.1) | copy-done | bytes 114712
  19.0 0.1 join_rows.5
  19.1 1.6 %collective-permute-start.7 = (bf16[64,3584]{1,0:T(8,128)(2,1)S(1)}, bf16[64,3584]{1,0:T(8,128)(2,1)S(1)}, u32[]{:S(2)}, u32[]{:S(2)}) collective-permute-start(bf16[64,3584]{1,0:T(8,128)(2,1)S(1)} %get-tuple-element.24.refs_0_), channel_id=1, source_target_pairs={{0,2},{1,3},{2,0},{3,1},{4,6},{5,7},{6,4},{7,5},{8,10},{9,11},{10,... | collective-permute-start | bytes 1376264 | tf_op jit(solution)/shard_map/ppermute | solution.py:221
  20.7 2.8 %collective-permute-start.9 = (bf16[64,2048]{1,0:T(8,128)(2,1)S(1)}, bf16[64,2048]{1,0:T(8,128)(2,1)S(1)}, u32[]{:S(2)}, u32[]{:S(2)}) collective-permute-start(bf16[64,2048]{1,0:T(8,128)(2,1)S(1)} %get-tuple-element.25.refs_0_), channel_id=1, source_target_pairs={{0,8},{4,12},{8,0},{12,4},{1,9},{5,13},{9,1},{13,5},{2,10},{6,14},... | collective-permute-start | bytes 786440 | tf_op jit(solution)/shard_map/ppermute | solution.py:221
  23.5 0.2 collective-permute-start.8
  23.7 0.0 collective-permute-start.6
  23.7 10.7 %collective-permute-done.9.refs_2_.refs_1_ = bf16[64,2048]{1,0:T(8,128)(2,1)S(1)} collective-permute-done((bf16[64,2048]{1,0:T(8,128)(2,1)S(1)}, bf16[64,2048]{1,0:T(8,128)(2,1)S(1)}, u32[]{:S(2)}, u32[]{:S(2)}) %collective-permute-start.9) | collective-permute-done | bytes 262176 | tf_op jit(solution)/shard_map/ppermute | solution.py:221
  34.4 0.2 collective-permute-done.8.refs_1_
  34.6 0.0 collective-permute-done.7.refs_0_.refs_2_
  34.7 0.1 collective-permute-start.10
  34.8 1.0 %collective-permute-start.14 = (bf16[64,2048]{1,0:T(8,128)(2,1)S(1)}, bf16[64,2048]{1,0:T(8,128)(2,1)S(1)}, u32[]{:S(2)}, u32[]{:S(2)}) collective-permute-start(bf16[64,2048]{1,0:T(8,128)(2,1)S(1)} %collective-permute-done.9.refs_2_.refs_1_), channel_id=1, source_target_pairs={{0,4},{4,0},{8,12},{12,8},{1,5},{5,1},{9,13},{13,9},{2,6},{6,2},{1... | collective-permute-start | bytes 786440 | tf_op jit(solution)/shard_map/ppermute | solution.py:221
  35.8 2.4 %collective-permute-start.11 = (bf16[64,1536]{1,0:T(8,128)(2,1)S(1)}, bf16[64,1536]{1,0:T(8,128)(2,1)S(1)}, u32[]{:S(2)}, u32[]{:S(2)}) collective-permute-start(bf16[64,1536]{1,0:T(8,128)(2,1)S(1)} %join_rows.7.refs_0_), channel_id=1, source_target_pairs={{0,8},{4,12},{8,0},{12,4},{1,9},{5,13},{9,1},{13,5},{2,10},{6,14},... | collective-permute-start | bytes 589832 | tf_op jit(solution)/shard_map/ppermute | solution.py:221
  38.2 0.0 collective-permute-done.6.refs_1_
  38.2 0.0 collective-permute-done.10.refs_3_
  38.2 2.1 %standardize_a.1.refs_2_.refs_1_.a_ref = bf16[3584,256]{1,0:T(8,128)(2,1)S(1)} custom-call(bf16[64,3584]{1,0:T(8,128)(2,1)S(1)} %get-tuple-element.24.refs_0_, bf16[64,3584]{1,0:T(8,128)(2,1)S(1)} %collective-permute-done.6.refs_1_, bf16[64,3584]{1,0:T(8,128)(2,1)S(1)} %collective-permute-done.7.refs_0_.refs_2_, ...), custom_call_target="tpu_custom_call" | custom-call | flops 9175040 | bytes 3670016 | tf_op jit(solution)/shard_map/standardize_a/pallas_call | solution.py:142
  40.3 5.9 %collective-permute-done.11.refs_1_.refs_0_.refs_4_.refs_2_ = bf16[64,1536]{1,0:T(8,128)(2,1)S(1)} collective-permute-done((bf16[64,1536]{1,0:T(8,128)(2,1)S(1)}, bf16[64,1536]{1,0:T(8,128)(2,1)S(1)}, u32[]{:S(2)}, u32[]{:S(2)}) %collective-permute-start.11) | collective-permute-done | bytes 196640 | tf_op jit(solution)/shard_map/ppermute | solution.py:221
  46.2 3.1 %collective-permute-start.12 = (bf16[64,1536]{1,0:T(8,128)(2,1)S(1)}, bf16[64,1536]{1,0:T(8,128)(2,1)S(1)}, u32[]{:S(2)}, u32[]{:S(2)}) collective-permute-start(bf16[64,1536]{1,0:T(8,128)(2,1)S(1)} %join_rows.8), channel_id=1, source_target_pairs={{0,4},{4,0},{8,12},{12,8},{1,5},{5,1},{9,13},{13,9},{2,6},{6,2},{1... | collective-permute-start | bytes 589832 | tf_op jit(solution)/shard_map/ppermute | solution.py:221
  49.3 0.1 collective-permute-start.13
  49.4 0.0 collective-permute-done.14.refs_3_
  49.4 10.6 %product_chunk.2.refs_4_ = f32[3584,3584]{1,0:T(8,128)} custom-call(bf16[3584,256]{1,0:T(8,128)(2,1)S(1)} %standardize_a.1.refs_2_.refs_1_.a_ref, bf16[64,2048]{1,0:T(8,128)(2,1)S(1)} %get-tuple-element.25.refs_0_, bf16[64,2048]{1,0:T(8,128)(2,1)S(1)} %collective-permute-done.8.refs_1_, bf16[64,2048]{1,0:T(8,128)(2,1)S(1)} %collective-permute-done.9.refs_2_.refs_1_, ...), custom_call_target="tpu_custom_call" | custom-call | flops 3758096384 | bytes 29360128 | tf_op jit(solution)/shard_map/product_chunk/pallas_call | solution.py:201
  60.0 0.0 collective-permute-done.12.refs_1_
  60.0 0.0 collective-permute-done.13.refs_3_
  60.0 8.4 %product_chunk.3 = f32[3584,3584]{1,0:T(8,128)} custom-call(bf16[3584,256]{1,0:T(8,128)(2,1)S(1)} %standardize_a.1.refs_2_.refs_1_.a_ref, bf16[64,1536]{1,0:T(8,128)(2,1)S(1)} %join_rows.7.refs_0_, bf16[64,1536]{1,0:T(8,128)(2,1)S(1)} %collective-permute-done.12.refs_1_, ...), custom_call_target="tpu_custom_call", output_to_operand_aliasing={{}: (5, {})} | custom-call | flops 2818572288 | bytes 22020096 | tf_op jit(solution)/shard_map/product_chunk/pallas_call | solution.py:201
  (4 shorter events, 0.1 us)
Async XLA Ops:
  2.2 7.4 %collective-permute-start = (bf16[16,3584]{1,0:T(8,128)(2,1)}, bf16[16,3584]{1,0:T(8,128)(2,1)S(1)}, u32[]{:S(2)}, u32[]{:S(2)}) collective-permute-start(bf16[16,3584]{1,0:T(8,128)(2,1)} %get-tuple-element.17), channel_id=1, source_target_pairs={{0,4},{4,0},{8,12},{12,8},{1,5},{5,1},{9,13},{13,9},{2,6},{6,2},{1... | collective-permute-start | bytes 344072 | tf_op jit(solution)/shard_map/ppermute | solution.py:221
  5.3 11.9 %collective-permute-start.1 = (bf16[16,3584]{1,0:T(8,128)(2,1)}, bf16[16,3584]{1,0:T(8,128)(2,1)S(1)}, u32[]{:S(2)}, u32[]{:S(2)}) collective-permute-start(bf16[16,3584]{1,0:T(8,128)(2,1)} %get-tuple-element.18), channel_id=1, source_target_pairs={{0,8},{4,12},{8,0},{12,4},{1,9},{5,13},{9,1},{13,5},{2,10},{6,14},... | collective-permute-start | bytes 344072 | tf_op jit(solution)/shard_map/ppermute | solution.py:221
  7.9 9.3 %collective-permute-start.2 = (bf16[16,3584]{1,0:T(8,128)(2,1)}, bf16[16,3584]{1,0:T(8,128)(2,1)S(1)}, u32[]{:S(2)}, u32[]{:S(2)}) collective-permute-start(bf16[16,3584]{1,0:T(8,128)(2,1)} %get-tuple-element.19), channel_id=1, source_target_pairs={{0,12},{4,8},{8,4},{12,0},{1,13},{5,9},{9,5},{13,1},{2,14},{6,10},... | collective-permute-start | bytes 344072 | tf_op jit(solution)/shard_map/ppermute | solution.py:221
  7.9 9.3 %collective-permute-start.3 = (bf16[16,3584]{1,0:T(8,128)(2,1)}, bf16[16,3584]{1,0:T(8,128)(2,1)S(1)}, u32[]{:S(2)}, u32[]{:S(2)}) collective-permute-start(bf16[16,3584]{1,0:T(8,128)(2,1)} %get-tuple-element.21), channel_id=1, source_target_pairs={{0,1},{1,0},{2,3},{3,2},{4,5},{5,4},{6,7},{7,6},{8,9},{9,8},{10,11... | collective-permute-start | bytes 344072 | tf_op jit(solution)/shard_map/ppermute | solution.py:221
  7.9 9.3 %collective-permute-start.4 = (bf16[16,3584]{1,0:T(8,128)(2,1)}, bf16[16,3584]{1,0:T(8,128)(2,1)S(1)}, u32[]{:S(2)}, u32[]{:S(2)}) collective-permute-start(bf16[16,3584]{1,0:T(8,128)(2,1)} %get-tuple-element.22), channel_id=1, source_target_pairs={{0,2},{1,3},{2,0},{3,1},{4,6},{5,7},{6,4},{7,5},{8,10},{9,11},{10,... | collective-permute-start | bytes 344072 | tf_op jit(solution)/shard_map/ppermute | solution.py:221
  9.6 7.6 %collective-permute-start.5 = (bf16[16,3584]{1,0:T(8,128)(2,1)}, bf16[16,3584]{1,0:T(8,128)(2,1)S(1)}, u32[]{:S(2)}, u32[]{:S(2)}) collective-permute-start(bf16[16,3584]{1,0:T(8,128)(2,1)} %get-tuple-element.23), channel_id=1, source_target_pairs={{0,3},{1,2},{2,1},{3,0},{4,7},{5,6},{6,5},{7,4},{8,11},{9,10},{10,... | collective-permute-start | bytes 344072 | tf_op jit(solution)/shard_map/ppermute | solution.py:221
  17.2 0.9 %copy-start = (bf16[16,3584]{1,0:T(8,128)(2,1)S(1)}, bf16[16,3584]{1,0:T(8,128)(2,1)}, u32[]{:S(2)}) copy-start(bf16[16,3584]{1,0:T(8,128)(2,1)} %get-tuple-element.16.refs_0_) | copy-start | bytes 344068
  18.1 0.9 %copy-start.1 = (bf16[16,3584]{1,0:T(8,128)(2,1)S(1)}, bf16[16,3584]{1,0:T(8,128)(2,1)}, u32[]{:S(2)}) copy-start(bf16[16,3584]{1,0:T(8,128)(2,1)} %get-tuple-element.20.refs_4_) | copy-start | bytes 344068
  19.1 15.5 %collective-permute-start.7 = (bf16[64,3584]{1,0:T(8,128)(2,1)S(1)}, bf16[64,3584]{1,0:T(8,128)(2,1)S(1)}, u32[]{:S(2)}, u32[]{:S(2)}) collective-permute-start(bf16[64,3584]{1,0:T(8,128)(2,1)S(1)} %get-tuple-element.24.refs_0_), channel_id=1, source_target_pairs={{0,2},{1,3},{2,0},{3,1},{4,6},{5,7},{6,4},{7,5},{8,10},{9,11},{10,... | collective-permute-start | bytes 1376264 | tf_op jit(solution)/shard_map/ppermute | solution.py:221
  20.7 13.8 %collective-permute-start.9 = (bf16[64,2048]{1,0:T(8,128)(2,1)S(1)}, bf16[64,2048]{1,0:T(8,128)(2,1)S(1)}, u32[]{:S(2)}, u32[]{:S(2)}) collective-permute-start(bf16[64,2048]{1,0:T(8,128)(2,1)S(1)} %get-tuple-element.25.refs_0_), channel_id=1, source_target_pairs={{0,8},{4,12},{8,0},{12,4},{1,9},{5,13},{9,1},{13,5},{2,10},{6,14},... | collective-permute-start | bytes 786440 | tf_op jit(solution)/shard_map/ppermute | solution.py:221
  23.5 11.2 %collective-permute-start.8 = (bf16[64,2048]{1,0:T(8,128)(2,1)S(1)}, bf16[64,2048]{1,0:T(8,128)(2,1)S(1)}, u32[]{:S(2)}, u32[]{:S(2)}) collective-permute-start(bf16[64,2048]{1,0:T(8,128)(2,1)S(1)} %get-tuple-element.25.refs_0_), channel_id=1, source_target_pairs={{0,4},{4,0},{8,12},{12,8},{1,5},{5,1},{9,13},{13,9},{2,6},{6,2},{1... | collective-permute-start | bytes 786440 | tf_op jit(solution)/shard_map/ppermute | solution.py:221
  23.7 14.5 %collective-permute-start.6 = (bf16[64,3584]{1,0:T(8,128)(2,1)S(1)}, bf16[64,3584]{1,0:T(8,128)(2,1)S(1)}, u32[]{:S(2)}, u32[]{:S(2)}) collective-permute-start(bf16[64,3584]{1,0:T(8,128)(2,1)S(1)} %get-tuple-element.24.refs_0_), channel_id=1, source_target_pairs={{0,1},{1,0},{2,3},{3,2},{4,5},{5,4},{6,7},{7,6},{8,9},{9,8},{10,11... | collective-permute-start | bytes 1376264 | tf_op jit(solution)/shard_map/ppermute | solution.py:221
  34.7 3.5 %collective-permute-start.10 = (bf16[64,3584]{1,0:T(8,128)(2,1)S(1)}, bf16[64,3584]{1,0:T(8,128)(2,1)S(1)}, u32[]{:S(2)}, u32[]{:S(2)}) collective-permute-start(bf16[64,3584]{1,0:T(8,128)(2,1)S(1)} %join_rows.6), channel_id=1, source_target_pairs={{0,1},{1,0},{2,3},{3,2},{4,5},{5,4},{6,7},{7,6},{8,9},{9,8},{10,11... | collective-permute-start | bytes 1376264 | tf_op jit(solution)/shard_map/ppermute | solution.py:221
  34.8 14.6 %collective-permute-start.14 = (bf16[64,2048]{1,0:T(8,128)(2,1)S(1)}, bf16[64,2048]{1,0:T(8,128)(2,1)S(1)}, u32[]{:S(2)}, u32[]{:S(2)}) collective-permute-start(bf16[64,2048]{1,0:T(8,128)(2,1)S(1)} %collective-permute-done.9.refs_2_.refs_1_), channel_id=1, source_target_pairs={{0,4},{4,0},{8,12},{12,8},{1,5},{5,1},{9,13},{13,9},{2,6},{6,2},{1... | collective-permute-start | bytes 786440 | tf_op jit(solution)/shard_map/ppermute | solution.py:221
  35.8 10.4 %collective-permute-start.11 = (bf16[64,1536]{1,0:T(8,128)(2,1)S(1)}, bf16[64,1536]{1,0:T(8,128)(2,1)S(1)}, u32[]{:S(2)}, u32[]{:S(2)}) collective-permute-start(bf16[64,1536]{1,0:T(8,128)(2,1)S(1)} %join_rows.7.refs_0_), channel_id=1, source_target_pairs={{0,8},{4,12},{8,0},{12,4},{1,9},{5,13},{9,1},{13,5},{2,10},{6,14},... | collective-permute-start | bytes 589832 | tf_op jit(solution)/shard_map/ppermute | solution.py:221
  46.2 13.8 %collective-permute-start.12 = (bf16[64,1536]{1,0:T(8,128)(2,1)S(1)}, bf16[64,1536]{1,0:T(8,128)(2,1)S(1)}, u32[]{:S(2)}, u32[]{:S(2)}) collective-permute-start(bf16[64,1536]{1,0:T(8,128)(2,1)S(1)} %join_rows.8), channel_id=1, source_target_pairs={{0,4},{4,0},{8,12},{12,8},{1,5},{5,1},{9,13},{13,9},{2,6},{6,2},{1... | collective-permute-start | bytes 589832 | tf_op jit(solution)/shard_map/ppermute | solution.py:221
  49.3 10.7 %collective-permute-start.13 = (bf16[64,1536]{1,0:T(8,128)(2,1)S(1)}, bf16[64,1536]{1,0:T(8,128)(2,1)S(1)}, u32[]{:S(2)}, u32[]{:S(2)}) collective-permute-start(bf16[64,1536]{1,0:T(8,128)(2,1)S(1)} %join_rows.9), channel_id=1, source_target_pairs={{0,4},{4,0},{8,12},{12,8},{1,5},{5,1},{9,13},{13,9},{2,6},{6,2},{1... | collective-permute-start | bytes 589832 | tf_op jit(solution)/shard_map/ppermute | solution.py:221

commit v9 on v8

--- a/solution.py
+++ b/solution.py
@@ -84,7 +84,7 @@
         in_specs=[pl.BlockSpec(memory_space=pltpu.HBM)] * 2,
         out_specs=[pl.BlockSpec(memory_space=pltpu.VMEM)] * len(shapes),
         scratch_shapes=[pltpu.SemaphoreType.DMA((len(shapes),))],
-        compiler_params=pltpu.CompilerParams(vmem_limit_bytes=60*1024*1024),
+        compiler_params=pltpu.CompilerParams(vmem_limit_bytes=VMEM),
         name="cut_panels",
     )(a_acts, b_acts)
     return outs[:n_fa], outs[n_fa:]
@@ -233,14 +233,22 @@
     n_fa = lax.axis_size("fa")
     n_fb = lax.axis_size("fb")
     panels_a, panels_b = cut_panels(a_acts, b_acts, n_fa, n_fb)
-    own_a = [panels_a[0]] + [sent(panels_a[s], "fa", s) for s in range(1, n_fa)]
+    own_a = [panels_a[0]] + [sent(panels_a[s], "fa", s) for s in reversed(range(1, n_fa))]
     own_b = [panels_b[0]] + [sent(panels_b[s], "fb", s) for s in range(1, n_fb)]
     width_a, full_width = panels_a[0].shape[1], panels_b[0].shape[1]
     widths = chunk_widths(full_width, (8, 6))
     group_a, *parts_b = join_rows([(own_a, [width_a], 0), (own_b, widths, 0)])
 
+    def forward(groups, hold):
+        for step in range(3, n_fa):
+            if power_of_two(step):
+                groups.append(sent(groups[0], "fa", step))
+            else:
+                groups.append(forwarded(groups[0], "fa", step, groups, hold if step == 3 else ()))
+
     first = parts_b[0]
     chunks = [[first, sent(first, "fa", 1), sent(first, "fa", 2)]]
+    forward(chunks[0], ())
     all_a = [group_a]
     for step in range(1, n_fb):
         if power_of_two(step):
@@ -249,22 +257,18 @@
             all_a.append(forwarded(group_a, "fb", step, all_a, chunks[0][1:3]))
     std_a = standardize_a(all_a, n_fa, n_fb)
     for part in parts_b[1:]:
-        part = stacked([part], chunks[-1][2:3])
-        across = sent(part, "fa", 2)
-        near = sent(stacked([part], [across, std_a]), "fa", 1)
-        chunks.append([part, near, across])
+        across = sent(stacked([part], chunks[-1][2:3]), "fa", 2)
+        near = sent(stacked([part], [chunks[-1][3], std_a]), "fa", 1)
+        groups = [part, near, across]
+        forward(groups, [std_a])
+        chunks.append(groups)
 
     buffer = None
     column = 0
     for place, groups in enumerate(chunks):
-        hold = [std_a] if place else []
-        for step in range(3, n_fa):
-            if power_of_two(step):
-                groups.append(sent(groups[0], "fa", step))
-            else:
-                groups.append(forwarded(groups[0], "fa", step, groups, hold if step == 3 else ()))
         after = [later[2] for later in chunks[place + 1 : place + 2]]
-        buffer = product_chunk(std_a, groups, column, full_width, buffer, after)
+        ordered = groups[:1] + groups[:0:-1]
+        buffer = product_chunk(std_a, ordered, column, full_width, buffer, after)
         column += groups[0].shape[1]
     return buffer
 

time: 68.5 us -> 71.1 us (1.038)
  waiting for transfers between devices: 24.3 us -> 29.5 us
  Pallas kernels: 23.4 us -> 21.8 us
  starting transfers between devices: 18.8 us -> 17.4 us
    ppermute x15, waiting for transfers between devices: 24.3 us -> 29.5 us  [sent(): lax.ppermute(x, axis, [(i, partner(i, step, size)) for i in range(size)])]
    pallas_call x1, Pallas kernels: 2.21 us -> 0.69 us  [cut_panels(): pl.pallas_call(functools.partial(cut_kernel, n_fa, n_fb), out_shape=shape...]
    ppermute x15, starting transfers between devices: 18.8 us -> 17.4 us  [sent(): lax.ppermute(x, axis, [(i, partner(i, step, size)) for i in range(size)])]
  transfers between devices with their start and end apart: 15 -> 15, of which waited for: 4 -> 6; matrix products, arithmetic and copies ran while one was open for 0% -> 0% of each run, Pallas kernels for 19% -> 18%
where the time goes in v9:
time: 71.1 us; the launch traced here: 70.9 us
  waiting for transfers between devices  29.5 us (41%)
  Pallas kernels  21.8 us (31%)
  starting transfers between devices  17.4 us (24%)
  local copies, waits for them, and re-layouts  2.04 us (3%)
    ppermute x15, waiting for transfers between devices, sent(): lax.ppermute(x, axis, [(i, partner(i, step, size)) for i in range(size)])  29.5 us
    pallas_call x2, Pallas kernels, product_chunk(): pl.pallas_call(functools.partial(product_kernel, len(groups), column), ou...  18.9 us
    ppermute x15, starting transfers between devices, sent(): lax.ppermute(x, axis, [(i, partner(i, step, size)) for i in range(size)])  17.4 us
    pallas_call x1, Pallas kernels, standardize_a(): pl.pallas_call(functools.partial(standardize_a_kernel, n_fa, n_fb), out_s...  2.1 us
    unnamed x4, local copies, waits for them, and re-layouts  2.04 us
  transfers between devices with their start and end apart: 15, of which 6 were waited for; matrix products, arithmetic and copies ran while one was open for 0% of the time, Pallas kernels for 18%

profile of v9, /device:TPU:0, one launch (start us, length us, event | category | flops | bytes accessed | tf_op | source)
XLA Modules:
  0.0 70.9 jit_solution(11869135917437107812)
XLA Ops:
  0.0 0.0 copy-start
  0.0 1.0 %copy-done = bf16[16,14336]{1,0:T(8,128)(2,1)S(1)} copy-done((bf16[16,14336]{1,0:T(8,128)(2,1)S(1)}, bf16[16,14336]{1,0:T(8,128)(2,1)}, u32[]{:S(2)}) %copy-start) | copy-done | bytes 458776
  1.0 0.0 copy-start.1
  1.0 1.0 %copy-done.1 = bf16[16,14336]{1,0:T(8,128)(2,1)S(1)} copy-done((bf16[16,14336]{1,0:T(8,128)(2,1)S(1)}, bf16[16,14336]{1,0:T(8,128)(2,1)}, u32[]{:S(2)}) %copy-start.1) | copy-done | bytes 458776
  2.0 0.7 cut_panels.1
  2.7 5.1 %collective-permute-start = (bf16[16,3584]{1,0:T(8,128)(2,1)S(1)}, bf16[16,3584]{1,0:T(8,128)(2,1)S(1)}, u32[]{:S(2)}, u32[]{:S(2)}) collective-permute-start(bf16[16,3584]{1,0:T(8,128)(2,1)S(1)} %get-tuple-element.17), channel_id=1, source_target_pairs={{0,12},{4,8},{8,4},{12,0},{1,13},{5,9},{9,5},{13,1},{2,14},{6,10},... | collective-permute-start | bytes 344072 | tf_op jit(solution)/shard_map/ppermute | solution.py:221
  7.9 0.0 collective-permute-start.1
  7.9 0.6 collective-permute-start.2
  8.5 0.0 collective-permute-start.3
  8.5 1.6 %collective-permute-start.4 = (bf16[16,3584]{1,0:T(8,128)(2,1)S(1)}, bf16[16,3584]{1,0:T(8,128)(2,1)S(1)}, u32[]{:S(2)}, u32[]{:S(2)}) collective-permute-start(bf16[16,3584]{1,0:T(8,128)(2,1)S(1)} %get-tuple-element.22), channel_id=1, source_target_pairs={{0,2},{1,3},{2,0},{3,1},{4,6},{5,7},{6,4},{7,5},{8,10},{9,11},{10,... | collective-permute-start | bytes 344072 | tf_op jit(solution)/shard_map/ppermute | solution.py:221
  10.1 1.8 %collective-permute-done.refs_1_ = bf16[16,3584]{1,0:T(8,128)(2,1)S(1)} collective-permute-done((bf16[16,3584]{1,0:T(8,128)(2,1)S(1)}, bf16[16,3584]{1,0:T(8,128)(2,1)S(1)}, u32[]{:S(2)}, u32[]{:S(2)}) %collective-permute-start) | collective-permute-done | bytes 114720 | tf_op jit(solution)/shard_map/ppermute | solution.py:221
  11.9 0.0 collective-permute-start.5
  11.9 5.6 %collective-permute-done.1.refs_2_ = bf16[16,3584]{1,0:T(8,128)(2,1)S(1)} collective-permute-done((bf16[16,3584]{1,0:T(8,128)(2,1)S(1)}, bf16[16,3584]{1,0:T(8,128)(2,1)S(1)}, u32[]{:S(2)}, u32[]{:S(2)}) %collective-permute-start.1) | collective-permute-done | bytes 114720 | tf_op jit(solution)/shard_map/ppermute | solution.py:221
  17.5 0.0 collective-permute-done.2.refs_3_
  17.5 0.0 collective-permute-done.3.refs_5_
  17.5 0.0 collective-permute-done.4.refs_6_
  17.5 0.0 collective-permute-done.5.refs_7_
  17.5 0.1 join_rows.5
  17.6 1.6 %collective-permute-start.7 = (bf16[64,3584]{1,0:T(8,128)(2,1)S(1)}, bf16[64,3584]{1,0:T(8,128)(2,1)S(1)}, u32[]{:S(2)}, u32[]{:S(2)}) collective-permute-start(bf16[64,3584]{1,0:T(8,128)(2,1)S(1)} %get-tuple-element.24.refs_0_), channel_id=1, source_target_pairs={{0,2},{1,3},{2,0},{3,1},{4,6},{5,7},{6,4},{7,5},{8,10},{9,11},{10,... | collective-permute-start | bytes 1376264 | tf_op jit(solution)/shard_map/ppermute | solution.py:221
  19.2 4.8 %collective-permute-start.9 = (bf16[64,2048]{1,0:T(8,128)(2,1)S(1)}, bf16[64,2048]{1,0:T(8,128)(2,1)S(1)}, u32[]{:S(2)}, u32[]{:S(2)}) collective-permute-start(bf16[64,2048]{1,0:T(8,128)(2,1)S(1)} %get-tuple-element.25.refs_0_), channel_id=1, source_target_pairs={{0,8},{4,12},{8,0},{12,4},{1,9},{5,13},{9,1},{13,5},{2,10},{6,14},... | collective-permute-start | bytes 786440 | tf_op jit(solution)/shard_map/ppermute | solution.py:221
  23.9 0.0 collective-permute-start.8
  23.9 0.0 collective-permute-start.6
  23.9 11.8 %collective-permute-done.9.refs_2_.refs_1_ = bf16[64,2048]{1,0:T(8,128)(2,1)S(1)} collective-permute-done((bf16[64,2048]{1,0:T(8,128)(2,1)S(1)}, bf16[64,2048]{1,0:T(8,128)(2,1)S(1)}, u32[]{:S(2)}, u32[]{:S(2)}) %collective-permute-start.9) | collective-permute-done | bytes 262176 | tf_op jit(solution)/shard_map/ppermute | solution.py:221
  35.7 0.4 collective-permute-done.8.refs_1_.refs_3_
  36.1 0.0 collective-permute-done.7.refs_0_.refs_2_
  36.1 0.1 collective-permute-start.10
  36.2 1.4 %collective-permute-start.13 = (bf16[64,2048]{1,0:T(8,128)(2,1)S(1)}, bf16[64,2048]{1,0:T(8,128)(2,1)S(1)}, u32[]{:S(2)}, u32[]{:S(2)}) collective-permute-start(bf16[64,2048]{1,0:T(8,128)(2,1)S(1)} %collective-permute-done.9.refs_2_.refs_1_), channel_id=1, source_target_pairs={{0,4},{4,0},{8,12},{12,8},{1,5},{5,1},{9,13},{13,9},{2,6},{6,2},{1... | collective-permute-start | bytes 786440 | tf_op jit(solution)/shard_map/ppermute | solution.py:221
  37.6 0.1 collective-permute-start.11
  37.7 0.0 collective-permute-done.6.refs_1_
  37.7 0.3 collective-permute-done.10.refs_3_
  38.0 2.1 %standardize_a.1.refs_1_.refs_2_.a_ref = bf16[3584,256]{1,0:T(8,128)(2,1)S(1)} custom-call(bf16[64,3584]{1,0:T(8,128)(2,1)S(1)} %get-tuple-element.24.refs_0_, bf16[64,3584]{1,0:T(8,128)(2,1)S(1)} %collective-permute-done.6.refs_1_, bf16[64,3584]{1,0:T(8,128)(2,1)S(1)} %collective-permute-done.7.refs_0_.refs_2_, ...), custom_call_target="tpu_custom_call" | custom-call | flops 9175040 | bytes 3670016 | tf_op jit(solution)/shard_map/standardize_a/pallas_call | solution.py:142
  40.1 9.7 %collective-permute-done.11.refs_0_.refs_4_.refs_2_ = bf16[64,1536]{1,0:T(8,128)(2,1)S(1)} collective-permute-done((bf16[64,1536]{1,0:T(8,128)(2,1)S(1)}, bf16[64,1536]{1,0:T(8,128)(2,1)S(1)}, u32[]{:S(2)}, u32[]{:S(2)}) %collective-permute-start.11) | collective-permute-done | bytes 196640 | tf_op jit(solution)/shard_map/ppermute | solution.py:221
  49.8 0.5 collective-permute-start.12
  50.3 0.0 collective-permute-done.13.refs_1_
  50.3 1.6 %collective-permute-start.14 = (bf16[64,1536]{1,0:T(8,128)(2,1)S(1)}, bf16[64,1536]{1,0:T(8,128)(2,1)S(1)}, u32[]{:S(2)}, u32[]{:S(2)}) collective-permute-start(bf16[64,1536]{1,0:T(8,128)(2,1)S(1)} %join_rows.9), channel_id=1, source_target_pairs={{0,4},{4,0},{8,12},{12,8},{1,5},{5,1},{9,13},{13,9},{2,6},{6,2},{1... | collective-permute-start | bytes 589832 | tf_op jit(solution)/shard_map/ppermute | solution.py:221
  52.0 10.6 %product_chunk.2.refs_4_ = f32[3584,3584]{1,0:T(8,128)} custom-call(bf16[3584,256]{1,0:T(8,128)(2,1)S(1)} %standardize_a.1.refs_1_.refs_2_.a_ref, bf16[64,2048]{1,0:T(8,128)(2,1)S(1)} %get-tuple-element.25.refs_0_, bf16[64,2048]{1,0:T(8,128)(2,1)S(1)} %collective-permute-done.13.refs_1_, bf16[64,2048]{1,0:T(8,128)(2,1)S(1)} %collective-permute-done.9.refs_2_.refs_1_, ...), custom_call_target="tpu_custom_call" | custom-call | flops 3758096384 | bytes 29360128 | tf_op jit(solution)/shard_map/product_chunk/pallas_call | solution.py:201
  62.5 0.0 collective-permute-done.12.refs_1_
  62.6 0.0 collective-permute-done.14.refs_3_
  62.6 8.4 %product_chunk.3 = f32[3584,3584]{1,0:T(8,128)} custom-call(bf16[3584,256]{1,0:T(8,128)(2,1)S(1)} %standardize_a.1.refs_1_.refs_2_.a_ref, bf16[64,1536]{1,0:T(8,128)(2,1)S(1)} %get-tuple-element.26.refs_0_, bf16[64,1536]{1,0:T(8,128)(2,1)S(1)} %collective-permute-done.12.refs_1_, ...), custom_call_target="tpu_custom_call", output_to_operand_aliasing={{}: (5, {})} | custom-call | flops 2818572288 | bytes 22020096 | tf_op jit(solution)/shard_map/product_chunk/pallas_call | solution.py:201
  (4 shorter events, 0.1 us)
Async XLA Ops:
  0.0 1.0 %copy-start = (bf16[16,14336]{1,0:T(8,128)(2,1)S(1)}, bf16[16,14336]{1,0:T(8,128)(2,1)}, u32[]{:S(2)}) copy-start(bf16[16,14336]{1,0:T(8,128)(2,1)} %a_ref.1) | copy-start | bytes 1376260
  1.0 1.0 %copy-start.1 = (bf16[16,14336]{1,0:T(8,128)(2,1)S(1)}, bf16[16,14336]{1,0:T(8,128)(2,1)}, u32[]{:S(2)}) copy-start(bf16[16,14336]{1,0:T(8,128)(2,1)} %b_ref.1) | copy-start | bytes 1376260
  2.7 9.2 %collective-permute-start = (bf16[16,3584]{1,0:T(8,128)(2,1)S(1)}, bf16[16,3584]{1,0:T(8,128)(2,1)S(1)}, u32[]{:S(2)}, u32[]{:S(2)}) collective-permute-start(bf16[16,3584]{1,0:T(8,128)(2,1)S(1)} %get-tuple-element.17), channel_id=1, source_target_pairs={{0,12},{4,8},{8,4},{12,0},{1,13},{5,9},{9,5},{13,1},{2,14},{6,10},... | collective-permute-start | bytes 344072 | tf_op jit(solution)/shard_map/ppermute | solution.py:221
  7.9 9.7 %collective-permute-start.1 = (bf16[16,3584]{1,0:T(8,128)(2,1)S(1)}, bf16[16,3584]{1,0:T(8,128)(2,1)S(1)}, u32[]{:S(2)}, u32[]{:S(2)}) collective-permute-start(bf16[16,3584]{1,0:T(8,128)(2,1)S(1)} %get-tuple-element.18), channel_id=1, source_target_pairs={{0,8},{4,12},{8,0},{12,4},{1,9},{5,13},{9,1},{13,5},{2,10},{6,14},... | collective-permute-start | bytes 344072 | tf_op jit(solution)/shard_map/ppermute | solution.py:221
  7.9 9.7 %collective-permute-start.2 = (bf16[16,3584]{1,0:T(8,128)(2,1)S(1)}, bf16[16,3584]{1,0:T(8,128)(2,1)S(1)}, u32[]{:S(2)}, u32[]{:S(2)}) collective-permute-start(bf16[16,3584]{1,0:T(8,128)(2,1)S(1)} %get-tuple-element.19), channel_id=1, source_target_pairs={{0,4},{4,0},{8,12},{12,8},{1,5},{5,1},{9,13},{13,9},{2,6},{6,2},{1... | collective-permute-start | bytes 344072 | tf_op jit(solution)/shard_map/ppermute | solution.py:221
  8.5 9.0 %collective-permute-start.3 = (bf16[16,3584]{1,0:T(8,128)(2,1)S(1)}, bf16[16,3584]{1,0:T(8,128)(2,1)S(1)}, u32[]{:S(2)}, u32[]{:S(2)}) collective-permute-start(bf16[16,3584]{1,0:T(8,128)(2,1)S(1)} %get-tuple-element.21), channel_id=1, source_target_pairs={{0,1},{1,0},{2,3},{3,2},{4,5},{5,4},{6,7},{7,6},{8,9},{9,8},{10,11... | collective-permute-start | bytes 344072 | tf_op jit(solution)/shard_map/ppermute | solution.py:221
  8.5 9.0 %collective-permute-start.4 = (bf16[16,3584]{1,0:T(8,128)(2,1)S(1)}, bf16[16,3584]{1,0:T(8,128)(2,1)S(1)}, u32[]{:S(2)}, u32[]{:S(2)}) collective-permute-start(bf16[16,3584]{1,0:T(8,128)(2,1)S(1)} %get-tuple-element.22), channel_id=1, source_target_pairs={{0,2},{1,3},{2,0},{3,1},{4,6},{5,7},{6,4},{7,5},{8,10},{9,11},{10,... | collective-permute-start | bytes 344072 | tf_op jit(solution)/shard_map/ppermute | solution.py:221
  11.9 5.6 %collective-permute-start.5 = (bf16[16,3584]{1,0:T(8,128)(2,1)S(1)}, bf16[16,3584]{1,0:T(8,128)(2,1)S(1)}, u32[]{:S(2)}, u32[]{:S(2)}) collective-permute-start(bf16[16,3584]{1,0:T(8,128)(2,1)S(1)} %get-tuple-element.23), channel_id=1, source_target_pairs={{0,3},{1,2},{2,1},{3,0},{4,7},{5,6},{6,5},{7,4},{8,11},{9,10},{10,... | collective-permute-start | bytes 344072 | tf_op jit(solution)/shard_map/ppermute | solution.py:221
  17.6 18.5 %collective-permute-start.7 = (bf16[64,3584]{1,0:T(8,128)(2,1)S(1)}, bf16[64,3584]{1,0:T(8,128)(2,1)S(1)}, u32[]{:S(2)}, u32[]{:S(2)}) collective-permute-start(bf16[64,3584]{1,0:T(8,128)(2,1)S(1)} %get-tuple-element.24.refs_0_), channel_id=1, source_target_pairs={{0,2},{1,3},{2,0},{3,1},{4,6},{5,7},{6,4},{7,5},{8,10},{9,11},{10,... | collective-permute-start | bytes 1376264 | tf_op jit(solution)/shard_map/ppermute | solution.py:221
  19.2 16.5 %collective-permute-start.9 = (bf16[64,2048]{1,0:T(8,128)(2,1)S(1)}, bf16[64,2048]{1,0:T(8,128)(2,1)S(1)}, u32[]{:S(2)}, u32[]{:S(2)}) collective-permute-start(bf16[64,2048]{1,0:T(8,128)(2,1)S(1)} %get-tuple-element.25.refs_0_), channel_id=1, source_target_pairs={{0,8},{4,12},{8,0},{12,4},{1,9},{5,13},{9,1},{13,5},{2,10},{6,14},... | collective-permute-start | bytes 786440 | tf_op jit(solution)/shard_map/ppermute | solution.py:221
  23.9 12.1 %collective-permute-start.8 = (bf16[64,2048]{1,0:T(8,128)(2,1)S(1)}, bf16[64,2048]{1,0:T(8,128)(2,1)S(1)}, u32[]{:S(2)}, u32[]{:S(2)}) collective-permute-start(bf16[64,2048]{1,0:T(8,128)(2,1)S(1)} %get-tuple-element.25.refs_0_), channel_id=1, source_target_pairs={{0,4},{4,0},{8,12},{12,8},{1,5},{5,1},{9,13},{13,9},{2,6},{6,2},{1... | collective-permute-start | bytes 786440 | tf_op jit(solution)/shard_map/ppermute | solution.py:221
  23.9 13.7 %collective-permute-start.6 = (bf16[64,3584]{1,0:T(8,128)(2,1)S(1)}, bf16[64,3584]{1,0:T(8,128)(2,1)S(1)}, u32[]{:S(2)}, u32[]{:S(2)}) collective-permute-start(bf16[64,3584]{1,0:T(8,128)(2,1)S(1)} %get-tuple-element.24.refs_0_), channel_id=1, source_target_pairs={{0,1},{1,0},{2,3},{3,2},{4,5},{5,4},{6,7},{7,6},{8,9},{9,8},{10,11... | collective-permute-start | bytes 1376264 | tf_op jit(solution)/shard_map/ppermute | solution.py:221
  36.1 1.9 %collective-permute-start.10 = (bf16[64,3584]{1,0:T(8,128)(2,1)S(1)}, bf16[64,3584]{1,0:T(8,128)(2,1)S(1)}, u32[]{:S(2)}, u32[]{:S(2)}) collective-permute-start(bf16[64,3584]{1,0:T(8,128)(2,1)S(1)} %join_rows.6), channel_id=1, source_target_pairs={{0,1},{1,0},{2,3},{3,2},{4,5},{5,4},{6,7},{7,6},{8,9},{9,8},{10,11... | collective-permute-start | bytes 1376264 | tf_op jit(solution)/shard_map/ppermute | solution.py:221
  36.2 14.1 %collective-permute-start.13 = (bf16[64,2048]{1,0:T(8,128)(2,1)S(1)}, bf16[64,2048]{1,0:T(8,128)(2,1)S(1)}, u32[]{:S(2)}, u32[]{:S(2)}) collective-permute-start(bf16[64,2048]{1,0:T(8,128)(2,1)S(1)} %collective-permute-done.9.refs_2_.refs_1_), channel_id=1, source_target_pairs={{0,4},{4,0},{8,12},{12,8},{1,5},{5,1},{9,13},{13,9},{2,6},{6,2},{1... | collective-permute-start | bytes 786440 | tf_op jit(solution)/shard_map/ppermute | solution.py:221
  37.6 12.2 %collective-permute-start.11 = (bf16[64,1536]{1,0:T(8,128)(2,1)S(1)}, bf16[64,1536]{1,0:T(8,128)(2,1)S(1)}, u32[]{:S(2)}, u32[]{:S(2)}) collective-permute-start(bf16[64,1536]{1,0:T(8,128)(2,1)S(1)} %join_rows.7), channel_id=1, source_target_pairs={{0,8},{4,12},{8,0},{12,4},{1,9},{5,13},{9,1},{13,5},{2,10},{6,14},... | collective-permute-start | bytes 589832 | tf_op jit(solution)/shard_map/ppermute | solution.py:221
  49.8 12.7 %collective-permute-start.12 = (bf16[64,1536]{1,0:T(8,128)(2,1)S(1)}, bf16[64,1536]{1,0:T(8,128)(2,1)S(1)}, u32[]{:S(2)}, u32[]{:S(2)}) collective-permute-start(bf16[64,1536]{1,0:T(8,128)(2,1)S(1)} %join_rows.8), channel_id=1, source_target_pairs={{0,4},{4,0},{8,12},{12,8},{1,5},{5,1},{9,13},{13,9},{2,6},{6,2},{1... | collective-permute-start | bytes 589832 | tf_op jit(solution)/shard_map/ppermute | solution.py:221
  50.3 12.2 %collective-permute-start.14 = (bf16[64,1536]{1,0:T(8,128)(2,1)S(1)}, bf16[64,1536]{1,0:T(8,128)(2,1)S(1)}, u32[]{:S(2)}, u32[]{:S(2)}) collective-permute-start(bf16[64,1536]{1,0:T(8,128)(2,1)S(1)} %join_rows.9), channel_id=1, source_target_pairs={{0,4},{4,0},{8,12},{12,8},{1,5},{5,1},{9,13},{13,9},{2,6},{6,2},{1... | collective-permute-start | bytes 589832 | tf_op jit(solution)/shard_map/ppermute | solution.py:221

commit v10 on v9

--- a/solution.py
+++ b/solution.py
@@ -104,22 +104,31 @@
         ins, outs = ins[len_in:], outs[len_out:]
 
 
-def join_rows(groups, after=()):
+def join_rows(groups, after=(), first=None):
     pieces = [piece for group, _, _ in groups for piece in group]
+    order = list(range(len(pieces)))
+    if first is not None:
+        order.insert(0, order.pop(first))
     shapes = [
         jax.ShapeDtypeStruct((group[0].shape[0] * len(group), width), group[0].dtype)
         for group, widths, _ in groups
         for width in widths
     ]
+    counts = [(len(group), len(widths), column) for group, widths, column in groups]
+
+    def kernel(*refs):
+        ins = [refs[order.index(place)] for place in range(len(pieces))]
+        join_kernel(counts, *ins, *refs[len(pieces) :])
+
     return pl.pallas_call(
-        functools.partial(join_kernel, [(len(group), len(widths), column) for group, widths, column in groups]),
+        kernel,
         out_shape=shapes,
         in_specs=[pl.BlockSpec(memory_space=pltpu.VMEM)] * len(pieces)
         + [pl.BlockSpec(memory_space=pl.ANY)] * len(after),
         out_specs=[pl.BlockSpec(memory_space=pltpu.VMEM)] * len(shapes),
         compiler_params=pltpu.CompilerParams(vmem_limit_bytes=VMEM),
         name="join_rows",
-    )(*pieces, *after)
+    )(*[pieces[place] for place in order], *after)
 
 
 def stacked(pieces, after=()):
@@ -236,8 +245,9 @@
     own_a = [panels_a[0]] + [sent(panels_a[s], "fa", s) for s in reversed(range(1, n_fa))]
     own_b = [panels_b[0]] + [sent(panels_b[s], "fb", s) for s in range(1, n_fb)]
     width_a, full_width = panels_a[0].shape[1], panels_b[0].shape[1]
-    widths = chunk_widths(full_width, (8, 6))
-    group_a, *parts_b = join_rows([(own_a, [width_a], 0), (own_b, widths, 0)])
+    widths = chunk_widths(full_width, (1, 1))
+    stacks = [(own_a, [width_a], 0), (own_b, widths, 0), (own_b, [full_width], 0)]
+    group_a, *parts_b, group_b = join_rows(stacks, first=n_fa + 1)
 
     def forward(groups, hold):
         for step in range(3, n_fa):
@@ -247,21 +257,23 @@
                 groups.append(forwarded(groups[0], "fa", step, groups, hold if step == 3 else ()))
 
     first = parts_b[0]
-    chunks = [[first, sent(first, "fa", 1), sent(first, "fa", 2)]]
-    forward(chunks[0], ())
+    whole = sent(group_b, "fa", 1)
+    chunks = [[first, None, sent(first, "fa", 2)]]
     all_a = [group_a]
     for step in range(1, n_fb):
         if power_of_two(step):
             all_a.append(sent(group_a, "fb", step))
         else:
-            all_a.append(forwarded(group_a, "fb", step, all_a, chunks[0][1:3]))
+            all_a.append(forwarded(group_a, "fb", step, all_a, chunks[0][2:3]))
     std_a = standardize_a(all_a, n_fa, n_fb)
     for part in parts_b[1:]:
         across = sent(stacked([part], chunks[-1][2:3]), "fa", 2)
-        near = sent(stacked([part], [chunks[-1][3], std_a]), "fa", 1)
-        groups = [part, near, across]
+        chunks.append([part, None, across])
+    for groups, near in zip(chunks, join_rows([([whole], widths, 0)])):
+        groups[1] = near
+    forward(chunks[0], ())
+    for groups in chunks[1:]:
         forward(groups, [std_a])
-        chunks.append(groups)
 
     buffer = None
     column = 0

time: 71.1 us -> 67.9 us (0.955)
  starting transfers between devices: 17.4 us -> 14.2 us
    ppermute x15 -> x14, starting transfers between devices: 17.4 us -> 14.2 us  [sent(): lax.ppermute(x, axis, [(i, partner(i, step, size)) for i in range(size)])]
    ppermute x15 -> x14, waiting for transfers between devices: 29.5 us -> 29.5 us  [sent(): lax.ppermute(x, axis, [(i, partner(i, step, size)) for i in range(size)])]
  transfers between devices with their start and end apart: 15 -> 14, of which waited for: 6 -> 6; matrix products, arithmetic and copies ran while one was open for 0% -> 0% of each run, Pallas kernels for 18% -> 17%
where the time goes in v10:
time: 67.9 us; the launch traced here: 67.7 us
  waiting for transfers between devices  29.5 us (43%)
  Pallas kernels  21.9 us (32%)
  starting transfers between devices  14.2 us (21%)
  local copies, waits for them, and re-layouts  2.04 us (3%)
    ppermute x14, waiting for transfers between devices, sent(): lax.ppermute(x, axis, [(i, partner(i, step, size)) for i in range(size)])  29.5 us
    pallas_call x2, Pallas kernels, product_chunk(): pl.pallas_call(functools.partial(product_kernel, len(groups), column), ou...  18.9 us
    ppermute x14, starting transfers between devices, sent(): lax.ppermute(x, axis, [(i, partner(i, step, size)) for i in range(size)])  14.2 us
    pallas_call x1, Pallas kernels, standardize_a(): pl.pallas_call(functools.partial(standardize_a_kernel, n_fa, n_fb), out_s...  2.12 us
    unnamed x4, local copies, waits for them, and re-layouts  2.04 us
  transfers between devices with their start and end apart: 14, of which 6 were waited for; matrix products, arithmetic and copies ran while one was open for 0% of the time, Pallas kernels for 17%

profile of v10, /device:TPU:0, one launch (start us, length us, event | category | flops | bytes accessed | tf_op | source)
XLA Modules:
  0.0 67.7 jit_solution(5113074109840581668)
XLA Ops:
  0.0 0.0 copy-start
  0.0 1.0 %copy-done = bf16[16,14336]{1,0:T(8,128)(2,1)S(1)} copy-done((bf16[16,14336]{1,0:T(8,128)(2,1)S(1)}, bf16[16,14336]{1,0:T(8,128)(2,1)}, u32[]{:S(2)}) %copy-start) | copy-done | bytes 458776
  1.0 0.0 copy-start.1
  1.0 1.0 %copy-done.1 = bf16[16,14336]{1,0:T(8,128)(2,1)S(1)} copy-done((bf16[16,14336]{1,0:T(8,128)(2,1)S(1)}, bf16[16,14336]{1,0:T(8,128)(2,1)}, u32[]{:S(2)}) %copy-start.1) | copy-done | bytes 458776
  2.0 0.7 %cut_panels.1 = (bf16[16,3584]{1,0:T(8,128)(2,1)S(1)}, bf16[16,3584]{1,0:T(8,128)(2,1)S(1)}, bf16[16,3584]{1,0:T(8,128)(2,1)S(1)}, bf16[16,3584]{1,0:T(8,128)(2,...) custom-call(bf16[16,14336]{1,0:T(8,128)(2,1)S(1)} %copy-done, ...), custom_call_target="tpu_custom_call" | custom-call | tf_op jit(solution)/shard_map/cut_panels/pallas_call | solution.py:81
  2.7 0.5 collective-permute-start
  3.3 4.7 %collective-permute-start.1 = (bf16[16,3584]{1,0:T(8,128)(2,1)S(1)}, bf16[16,3584]{1,0:T(8,128)(2,1)S(1)}, u32[]{:S(2)}, u32[]{:S(2)}) collective-permute-start(bf16[16,3584]{1,0:T(8,128)(2,1)S(1)} %get-tuple-element.21), channel_id=1, source_target_pairs={{0,12},{4,8},{8,4},{12,0},{1,13},{5,9},{9,5},{13,1},{2,14},{6,10},... | collective-permute-start | bytes 344072 | tf_op jit(solution)/shard_map/ppermute | solution.py:230
  7.9 0.0 collective-permute-start.2
  7.9 0.6 collective-permute-start.3
  8.6 1.6 %collective-permute-start.4 = (bf16[16,3584]{1,0:T(8,128)(2,1)S(1)}, bf16[16,3584]{1,0:T(8,128)(2,1)S(1)}, u32[]{:S(2)}, u32[]{:S(2)}) collective-permute-start(bf16[16,3584]{1,0:T(8,128)(2,1)S(1)} %get-tuple-element.25), channel_id=1, source_target_pairs={{0,2},{1,3},{2,0},{3,1},{4,6},{5,7},{6,4},{7,5},{8,10},{9,11},{10,... | collective-permute-start | bytes 344072 | tf_op jit(solution)/shard_map/ppermute | solution.py:230
  10.2 0.0 collective-permute-done.refs_0_.refs_9_
  10.2 0.0 collective-permute-start.5
  10.2 1.8 %collective-permute-done.1.refs_2_ = bf16[16,3584]{1,0:T(8,128)(2,1)S(1)} collective-permute-done((bf16[16,3584]{1,0:T(8,128)(2,1)S(1)}, bf16[16,3584]{1,0:T(8,128)(2,1)S(1)}, u32[]{:S(2)}, u32[]{:S(2)}) %collective-permute-start.1) | collective-permute-done | bytes 114720 | tf_op jit(solution)/shard_map/ppermute | solution.py:230
  12.0 6.2 %collective-permute-done.2.refs_3_ = bf16[16,3584]{1,0:T(8,128)(2,1)S(1)} collective-permute-done((bf16[16,3584]{1,0:T(8,128)(2,1)S(1)}, bf16[16,3584]{1,0:T(8,128)(2,1)S(1)}, u32[]{:S(2)}, u32[]{:S(2)}) %collective-permute-start.2) | collective-permute-done | bytes 114720 | tf_op jit(solution)/shard_map/ppermute | solution.py:230
  18.2 0.0 collective-permute-done.3.refs_4_
  18.2 0.0 collective-permute-done.4.refs_6_.refs_10_
  18.2 0.0 collective-permute-done.5.refs_7_.refs_11_
  18.2 0.1 join_rows.5
  18.3 1.6 %collective-permute-start.7 = (bf16[64,3584]{1,0:T(8,128)(2,1)S(1)}, bf16[64,3584]{1,0:T(8,128)(2,1)S(1)}, u32[]{:S(2)}, u32[]{:S(2)}) collective-permute-start(bf16[64,3584]{1,0:T(8,128)(2,1)S(1)} %get-tuple-element.27.refs_0_), channel_id=1, source_target_pairs={{0,2},{1,3},{2,0},{3,1},{4,6},{5,7},{6,4},{7,5},{8,10},{9,11},{10,... | collective-permute-start | bytes 1376264 | tf_op jit(solution)/shard_map/ppermute | solution.py:230
  19.9 0.0 collective-permute-start.8
  19.9 0.0 collective-permute-start.6
  19.9 3.1 %collective-permute-start.12 = (bf16[64,3584]{1,0:T(8,128)(2,1)S(1)}, bf16[64,3584]{1,0:T(8,128)(2,1)S(1)}, u32[]{:S(2)}, u32[]{:S(2)}) collective-permute-start(bf16[64,3584]{1,0:T(8,128)(2,1)S(1)} %get-tuple-element.30), channel_id=1, source_target_pairs={{0,4},{4,0},{8,12},{12,8},{1,5},{5,1},{9,13},{13,9},{2,6},{6,2},{1... | collective-permute-start | bytes 1376264 | tf_op jit(solution)/shard_map/ppermute | solution.py:230
  23.0 9.6 %collective-permute-done.8.refs_1_.refs_2_ = bf16[64,1792]{1,0:T(8,128)(2,1)S(1)} collective-permute-done((bf16[64,1792]{1,0:T(8,128)(2,1)S(1)}, bf16[64,1792]{1,0:T(8,128)(2,1)S(1)}, u32[]{:S(2)}, u32[]{:S(2)}) %collective-permute-start.8) | collective-permute-done | bytes 229408 | tf_op jit(solution)/shard_map/ppermute | solution.py:230
  32.6 0.0 collective-permute-done.7.refs_0_.refs_2_
  32.6 0.1 collective-permute-start.9
  32.7 0.1 collective-permute-start.10
  32.8 1.9 %collective-permute-start.13 = (bf16[64,1792]{1,0:T(8,128)(2,1)S(1)}, bf16[64,1792]{1,0:T(8,128)(2,1)S(1)}, u32[]{:S(2)}, u32[]{:S(2)}) collective-permute-start(bf16[64,1792]{1,0:T(8,128)(2,1)S(1)} %collective-permute-done.8.refs_1_.refs_2_), channel_id=1, source_target_pairs={{0,4},{4,0},{8,12},{12,8},{1,5},{5,1},{9,13},{13,9},{2,6},{6,2},{1... | collective-permute-start | bytes 688136 | tf_op jit(solution)/shard_map/ppermute | solution.py:230
  34.6 5.6 %collective-permute-done.12.refs_0_ = bf16[64,3584]{1,0:T(8,128)(2,1)S(1)} collective-permute-done((bf16[64,3584]{1,0:T(8,128)(2,1)S(1)}, bf16[64,3584]{1,0:T(8,128)(2,1)S(1)}, u32[]{:S(2)}, u32[]{:S(2)}) %collective-permute-start.12) | collective-permute-done | bytes 458784 | tf_op jit(solution)/shard_map/ppermute | solution.py:230
  40.3 0.0 collective-permute-done.6.refs_1_
  40.3 0.0 collective-permute-done.9.refs_3_
  40.3 2.1 %standardize_a.1.refs_1_.a_ref = bf16[3584,256]{1,0:T(8,128)(2,1)S(1)} custom-call(bf16[64,3584]{1,0:T(8,128)(2,1)S(1)} %get-tuple-element.27.refs_0_, bf16[64,3584]{1,0:T(8,128)(2,1)S(1)} %collective-permute-done.6.refs_1_, bf16[64,3584]{1,0:T(8,128)(2,1)S(1)} %collective-permute-done.7.refs_0_.refs_2_, bf16[64,3584]{1,0:T(8,128)(2,1)S(1)} %collective-permute-done.9.refs_3_), custom_call_target="tpu_custom_call" | custom-call | flops 9175040 | bytes 3670016 | tf_op jit(solution)/shard_map/standardize_a/pallas_call | solution.py:151
  42.5 3.9 %collective-permute-done.10.refs_0_.refs_4_.refs_2_ = bf16[64,1792]{1,0:T(8,128)(2,1)S(1)} collective-permute-done((bf16[64,1792]{1,0:T(8,128)(2,1)S(1)}, bf16[64,1792]{1,0:T(8,128)(2,1)S(1)}, u32[]{:S(2)}, u32[]{:S(2)}) %collective-permute-start.10) | collective-permute-done | bytes 229408 | tf_op jit(solution)/shard_map/ppermute | solution.py:230
  46.3 0.1 collective-permute-start.11
  46.4 2.4 %collective-permute-done.13.refs_1_ = bf16[64,1792]{1,0:T(8,128)(2,1)S(1)} collective-permute-done((bf16[64,1792]{1,0:T(8,128)(2,1)S(1)}, bf16[64,1792]{1,0:T(8,128)(2,1)S(1)}, u32[]{:S(2)}, u32[]{:S(2)}) %collective-permute-start.13) | collective-permute-done | bytes 229408 | tf_op jit(solution)/shard_map/ppermute | solution.py:230
  48.8 9.4 %product_chunk.2.refs_4_ = f32[3584,3584]{1,0:T(8,128)} custom-call(bf16[3584,256]{1,0:T(8,128)(2,1)S(1)} %standardize_a.1.refs_1_.a_ref, bf16[64,1792]{1,0:T(8,128)(2,1)S(1)} %get-tuple-element.28.refs_0_, bf16[64,1792]{1,0:T(8,128)(2,1)S(1)} %collective-permute-done.13.refs_1_, bf16[64,1792]{1,0:T(8,128)(2,1)S(1)} %collective-permute-done.8.refs_1_.refs_2_, ...), custom_call_target="tpu_custom_call" | custom-call | flops 3288334336 | bytes 25690112 | tf_op jit(solution)/shard_map/product_chunk/pallas_call | solution.py:210
  58.2 0.0 collective-permute-done.11.refs_1_
  58.2 9.4 %product_chunk.3 = f32[3584,3584]{1,0:T(8,128)} custom-call(bf16[3584,256]{1,0:T(8,128)(2,1)S(1)} %standardize_a.1.refs_1_.a_ref, bf16[64,1792]{1,0:T(8,128)(2,1)S(1)} %get-tuple-element.29.refs_0_, bf16[64,1792]{1,0:T(8,128)(2,1)S(1)} %collective-permute-done.11.refs_1_, ...), custom_call_target="tpu_custom_call", output_to_operand_aliasing={{}: (5, {})} | custom-call | flops 3288334336 | bytes 25690112 | tf_op jit(solution)/shard_map/product_chunk/pallas_call | solution.py:210
  (4 shorter events, 0.1 us)
Async XLA Ops:
  0.0 1.0 %copy-start = (bf16[16,14336]{1,0:T(8,128)(2,1)S(1)}, bf16[16,14336]{1,0:T(8,128)(2,1)}, u32[]{:S(2)}) copy-start(bf16[16,14336]{1,0:T(8,128)(2,1)} %a_ref.1) | copy-start | bytes 1376260
  1.0 1.0 %copy-start.1 = (bf16[16,14336]{1,0:T(8,128)(2,1)S(1)}, bf16[16,14336]{1,0:T(8,128)(2,1)}, u32[]{:S(2)}) copy-start(bf16[16,14336]{1,0:T(8,128)(2,1)} %b_ref.1) | copy-start | bytes 1376260
  2.7 7.5 %collective-permute-start = (bf16[16,3584]{1,0:T(8,128)(2,1)S(1)}, bf16[16,3584]{1,0:T(8,128)(2,1)S(1)}, u32[]{:S(2)}, u32[]{:S(2)}) collective-permute-start(bf16[16,3584]{1,0:T(8,128)(2,1)S(1)} %get-tuple-element.19), channel_id=1, source_target_pairs={{0,1},{1,0},{2,3},{3,2},{4,5},{5,4},{6,7},{7,6},{8,9},{9,8},{10,11... | collective-permute-start | bytes 344072 | tf_op jit(solution)/shard_map/ppermute | solution.py:230
  3.3 8.8 %collective-permute-start.1 = (bf16[16,3584]{1,0:T(8,128)(2,1)S(1)}, bf16[16,3584]{1,0:T(8,128)(2,1)S(1)}, u32[]{:S(2)}, u32[]{:S(2)}) collective-permute-start(bf16[16,3584]{1,0:T(8,128)(2,1)S(1)} %get-tuple-element.21), channel_id=1, source_target_pairs={{0,12},{4,8},{8,4},{12,0},{1,13},{5,9},{9,5},{13,1},{2,14},{6,10},... | collective-permute-start | bytes 344072 | tf_op jit(solution)/shard_map/ppermute | solution.py:230
  7.9 10.3 %collective-permute-start.2 = (bf16[16,3584]{1,0:T(8,128)(2,1)S(1)}, bf16[16,3584]{1,0:T(8,128)(2,1)S(1)}, u32[]{:S(2)}, u32[]{:S(2)}) collective-permute-start(bf16[16,3584]{1,0:T(8,128)(2,1)S(1)} %get-tuple-element.22), channel_id=1, source_target_pairs={{0,8},{4,12},{8,0},{12,4},{1,9},{5,13},{9,1},{13,5},{2,10},{6,14},... | collective-permute-start | bytes 344072 | tf_op jit(solution)/shard_map/ppermute | solution.py:230
  7.9 10.3 %collective-permute-start.3 = (bf16[16,3584]{1,0:T(8,128)(2,1)S(1)}, bf16[16,3584]{1,0:T(8,128)(2,1)S(1)}, u32[]{:S(2)}, u32[]{:S(2)}) collective-permute-start(bf16[16,3584]{1,0:T(8,128)(2,1)S(1)} %get-tuple-element.23), channel_id=1, source_target_pairs={{0,4},{4,0},{8,12},{12,8},{1,5},{5,1},{9,13},{13,9},{2,6},{6,2},{1... | collective-permute-start | bytes 344072 | tf_op jit(solution)/shard_map/ppermute | solution.py:230
  8.6 9.6 %collective-permute-start.4 = (bf16[16,3584]{1,0:T(8,128)(2,1)S(1)}, bf16[16,3584]{1,0:T(8,128)(2,1)S(1)}, u32[]{:S(2)}, u32[]{:S(2)}) collective-permute-start(bf16[16,3584]{1,0:T(8,128)(2,1)S(1)} %get-tuple-element.25), channel_id=1, source_target_pairs={{0,2},{1,3},{2,0},{3,1},{4,6},{5,7},{6,4},{7,5},{8,10},{9,11},{10,... | collective-permute-start | bytes 344072 | tf_op jit(solution)/shard_map/ppermute | solution.py:230
  10.2 8.0 %collective-permute-start.5 = (bf16[16,3584]{1,0:T(8,128)(2,1)S(1)}, bf16[16,3584]{1,0:T(8,128)(2,1)S(1)}, u32[]{:S(2)}, u32[]{:S(2)}) collective-permute-start(bf16[16,3584]{1,0:T(8,128)(2,1)S(1)} %get-tuple-element.26), channel_id=1, source_target_pairs={{0,3},{1,2},{2,1},{3,0},{4,7},{5,6},{6,5},{7,4},{8,11},{9,10},{10,... | collective-permute-start | bytes 344072 | tf_op jit(solution)/shard_map/ppermute | solution.py:230
  18.3 14.2 %collective-permute-start.7 = (bf16[64,3584]{1,0:T(8,128)(2,1)S(1)}, bf16[64,3584]{1,0:T(8,128)(2,1)S(1)}, u32[]{:S(2)}, u32[]{:S(2)}) collective-permute-start(bf16[64,3584]{1,0:T(8,128)(2,1)S(1)} %get-tuple-element.27.refs_0_), channel_id=1, source_target_pairs={{0,2},{1,3},{2,0},{3,1},{4,6},{5,7},{6,4},{7,5},{8,10},{9,11},{10,... | collective-permute-start | bytes 1376264 | tf_op jit(solution)/shard_map/ppermute | solution.py:230
  19.9 12.7 %collective-permute-start.8 = (bf16[64,1792]{1,0:T(8,128)(2,1)S(1)}, bf16[64,1792]{1,0:T(8,128)(2,1)S(1)}, u32[]{:S(2)}, u32[]{:S(2)}) collective-permute-start(bf16[64,1792]{1,0:T(8,128)(2,1)S(1)} %get-tuple-element.28.refs_0_), channel_id=1, source_target_pairs={{0,8},{4,12},{8,0},{12,4},{1,9},{5,13},{9,1},{13,5},{2,10},{6,14},... | collective-permute-start | bytes 688136 | tf_op jit(solution)/shard_map/ppermute | solution.py:230
  19.9 20.4 %collective-permute-start.6 = (bf16[64,3584]{1,0:T(8,128)(2,1)S(1)}, bf16[64,3584]{1,0:T(8,128)(2,1)S(1)}, u32[]{:S(2)}, u32[]{:S(2)}) collective-permute-start(bf16[64,3584]{1,0:T(8,128)(2,1)S(1)} %get-tuple-element.27.refs_0_), channel_id=1, source_target_pairs={{0,1},{1,0},{2,3},{3,2},{4,5},{5,4},{6,7},{7,6},{8,9},{9,8},{10,11... | collective-permute-start | bytes 1376264 | tf_op jit(solution)/shard_map/ppermute | solution.py:230
  19.9 20.4 %collective-permute-start.12 = (bf16[64,3584]{1,0:T(8,128)(2,1)S(1)}, bf16[64,3584]{1,0:T(8,128)(2,1)S(1)}, u32[]{:S(2)}, u32[]{:S(2)}) collective-permute-start(bf16[64,3584]{1,0:T(8,128)(2,1)S(1)} %get-tuple-element.30), channel_id=1, source_target_pairs={{0,4},{4,0},{8,12},{12,8},{1,5},{5,1},{9,13},{13,9},{2,6},{6,2},{1... | collective-permute-start | bytes 1376264 | tf_op jit(solution)/shard_map/ppermute | solution.py:230
  32.6 7.7 %collective-permute-start.9 = (bf16[64,3584]{1,0:T(8,128)(2,1)S(1)}, bf16[64,3584]{1,0:T(8,128)(2,1)S(1)}, u32[]{:S(2)}, u32[]{:S(2)}) collective-permute-start(bf16[64,3584]{1,0:T(8,128)(2,1)S(1)} %join_rows.6), channel_id=1, source_target_pairs={{0,1},{1,0},{2,3},{3,2},{4,5},{5,4},{6,7},{7,6},{8,9},{9,8},{10,11... | collective-permute-start | bytes 1376264 | tf_op jit(solution)/shard_map/ppermute | solution.py:230
  32.7 13.6 %collective-permute-start.10 = (bf16[64,1792]{1,0:T(8,128)(2,1)S(1)}, bf16[64,1792]{1,0:T(8,128)(2,1)S(1)}, u32[]{:S(2)}, u32[]{:S(2)}) collective-permute-start(bf16[64,1792]{1,0:T(8,128)(2,1)S(1)} %join_rows.7), channel_id=1, source_target_pairs={{0,8},{4,12},{8,0},{12,4},{1,9},{5,13},{9,1},{13,5},{2,10},{6,14},... | collective-permute-start | bytes 688136 | tf_op jit(solution)/shard_map/ppermute | solution.py:230
  32.8 16.0 %collective-permute-start.13 = (bf16[64,1792]{1,0:T(8,128)(2,1)S(1)}, bf16[64,1792]{1,0:T(8,128)(2,1)S(1)}, u32[]{:S(2)}, u32[]{:S(2)}) collective-permute-start(bf16[64,1792]{1,0:T(8,128)(2,1)S(1)} %collective-permute-done.8.refs_1_.refs_2_), channel_id=1, source_target_pairs={{0,4},{4,0},{8,12},{12,8},{1,5},{5,1},{9,13},{13,9},{2,6},{6,2},{1... | collective-permute-start | bytes 688136 | tf_op jit(solution)/shard_map/ppermute | solution.py:230
  46.3 11.9 %collective-permute-start.11 = (bf16[64,1792]{1,0:T(8,128)(2,1)S(1)}, bf16[64,1792]{1,0:T(8,128)(2,1)S(1)}, u32[]{:S(2)}, u32[]{:S(2)}) collective-permute-start(bf16[64,1792]{1,0:T(8,128)(2,1)S(1)} %join_rows.8), channel_id=1, source_target_pairs={{0,4},{4,0},{8,12},{12,8},{1,5},{5,1},{9,13},{13,9},{2,6},{6,2},{1... | collective-permute-start | bytes 688136 | tf_op jit(solution)/shard_map/ppermute | solution.py:230

commit v11 on v10

--- a/solution.py
+++ b/solution.py
@@ -52,42 +52,32 @@
     return (place + step) % size
 
 
-def cut_kernel(n_fa, n_fb, a_ref, b_ref, *refs):
+def cut_kernel(axis, size, ref, *refs):
     outs, sems = refs[:-1], refs[-1]
-    width_a = a_ref.shape[1] // n_fa
-    width_b = b_ref.shape[1] // n_fb
-    fa = lax.axis_index("fa")
-    fb = lax.axis_index("fb")
-    copies = []
-    for step in range(n_fa):
-        start = pl.multiple_of(partner(fa, step, n_fa) * width_a, 128)
-        copies.append((a_ref.at[:, pl.ds(start, width_a)], outs[step]))
-    for step in range(n_fb):
-        start = pl.multiple_of(partner(fb, step, n_fb) * width_b, 128)
-        copies.append((b_ref.at[:, pl.ds(start, width_b)], outs[n_fa + step]))
+    width = ref.shape[1] // size
+    place = lax.axis_index(axis)
     started = []
-    for place, (src, dst) in enumerate(copies):
-        copy = pltpu.make_async_copy(src, dst, sems.at[place])
+    for step in range(size):
+        start = pl.multiple_of(partner(place, step, size) * width, 128)
+        copy = pltpu.make_async_copy(ref.at[:, pl.ds(start, width)], outs[step], sems.at[step])
         copy.start()
         started.append(copy)
     for copy in started:
         copy.wait()
 
 
-def cut_panels(a_acts, b_acts, n_fa, n_fb):
-    tok, width = a_acts.shape
-    shapes = [jax.ShapeDtypeStruct((tok, width // n_fa), a_acts.dtype)] * n_fa
-    shapes += [jax.ShapeDtypeStruct((tok, width // n_fb), b_acts.dtype)] * n_fb
-    outs = pl.pallas_call(
-        functools.partial(cut_kernel, n_fa, n_fb),
-        out_shape=shapes,
-        in_specs=[pl.BlockSpec(memory_space=pltpu.HBM)] * 2,
-        out_specs=[pl.BlockSpec(memory_space=pltpu.VMEM)] * len(shapes),
-        scratch_shapes=[pltpu.SemaphoreType.DMA((len(shapes),))],
+def cut_panels(acts, axis):
+    size = lax.axis_size(axis)
+    tok, width = acts.shape
+    return pl.pallas_call(
+        functools.partial(cut_kernel, axis, size),
+        out_shape=[jax.ShapeDtypeStruct((tok, width // size), acts.dtype)] * size,
+        in_specs=[pl.BlockSpec(memory_space=pl.ANY)],
+        out_specs=[pl.BlockSpec(memory_space=pltpu.VMEM)] * size,
+        scratch_shapes=[pltpu.SemaphoreType.DMA((size,))],
         compiler_params=pltpu.CompilerParams(vmem_limit_bytes=VMEM),
         name="cut_panels",
-    )(a_acts, b_acts)
-    return outs[:n_fa], outs[n_fa:]
+    )(acts)
 
 
 def join_kernel(shapes, *refs):
@@ -167,31 +157,40 @@
     out, slots, sems = refs[-3:]
     total, width = a_ref.shape[1], groups[0].shape[1]
     n_slots, height, strip = slots.shape
-
-    def copy_of(step):
+    n_parts = sems.shape[1]
+    block = height // n_parts
+
+    def copies_of(step, part):
         slot = lax.rem(step, n_slots)
         place = pl.multiple_of(column + step * strip, 128)
-        return pltpu.make_async_copy(slots.at[slot], out.at[:, pl.ds(place, strip)], sems.at[slot])
+        rows = pl.ds(part * block, block)
+        return pltpu.make_async_copy(
+            slots.at[slot, rows], out.at[rows, pl.ds(place, strip)], sems.at[slot, part]
+        )
 
     @pl.loop(0, width // strip)
     def _(step):
-        @pl.when(step >= n_slots)
-        def _():
-            copy_of(step - n_slots).wait()
-
         parts = []
         for part in range(strip // 128):
             columns = pl.ds(pl.multiple_of(step * strip + part * 128, 128), 128)
             pieces = [ref[:, columns].astype(jnp.float32) for ref in groups]
             parts.append(standardize(jnp.concatenate(pieces, axis=0)))
         std = jnp.concatenate(parts, axis=1)
-        product = jnp.dot(a_ref[...], std, preferred_element_type=jnp.float32)
-        slots[lax.rem(step, n_slots)] = over_count(product, total)
-        copy_of(step).start()
+        for part in range(n_parts):
+            rows = pl.ds(part * block, block)
+
+            @pl.when(step >= n_slots)
+            def _():
+                copies_of(step - n_slots, part).wait()
+
+            product = jnp.dot(a_ref[rows, :], std, preferred_element_type=jnp.float32)
+            slots[lax.rem(step, n_slots), rows] = over_count(product, total)
+            copies_of(step, part).start()
 
     @pl.loop(max(width // strip - n_slots, 0), width // strip)
     def _(step):
-        copy_of(step).wait()
+        for part in range(n_parts):
+            copies_of(step, part).wait()
 
 
 def product_chunk(std_a, groups, column, full_width, buffer, after=()):
@@ -214,7 +213,7 @@
         out_specs=pl.BlockSpec(memory_space=pl.ANY),
         scratch_shapes=[
             pltpu.VMEM((n_slots, height, strip), jnp.float32),
-            pltpu.SemaphoreType.DMA((n_slots,)),
+            pltpu.SemaphoreType.DMA((n_slots, height // block_of(height, 1024))),
         ],
         input_output_aliases=aliases,
         compiler_params=pltpu.CompilerParams(vmem_limit_bytes=VMEM),
@@ -241,13 +240,15 @@
 def per_device(a_acts, b_acts):
     n_fa = lax.axis_size("fa")
     n_fb = lax.axis_size("fb")
-    panels_a, panels_b = cut_panels(a_acts, b_acts, n_fa, n_fb)
-    own_a = [panels_a[0]] + [sent(panels_a[s], "fa", s) for s in reversed(range(1, n_fa))]
+    panels_a = cut_panels(a_acts, "fa")
+    panels_b = cut_panels(b_acts, "fb")
+    order = [0, 1, *reversed(range(2, n_fa))]
+    own_a = [sent(panels_a[s], "fa", s) if s else panels_a[0] for s in order]
     own_b = [panels_b[0]] + [sent(panels_b[s], "fb", s) for s in range(1, n_fb)]
     width_a, full_width = panels_a[0].shape[1], panels_b[0].shape[1]
     widths = chunk_widths(full_width, (1, 1))
     stacks = [(own_a, [width_a], 0), (own_b, widths, 0), (own_b, [full_width], 0)]
-    group_a, *parts_b, group_b = join_rows(stacks, first=n_fa + 1)
+    group_a, *parts_b, group_b = join_rows(stacks)
 
     def forward(groups, hold):
         for step in range(3, n_fa):
@@ -279,7 +280,7 @@
     column = 0
     for place, groups in enumerate(chunks):
         after = [later[2] for later in chunks[place + 1 : place + 2]]
-        ordered = groups[:1] + groups[:0:-1]
+        ordered = [groups[s] for s in order]
         buffer = product_chunk(std_a, ordered, column, full_width, buffer, after)
         column += groups[0].shape[1]
     return buffer

time: 67.9 us -> 72.8 us (1.072)
  Pallas kernels: 21.9 us -> 28.3 us
  waiting for transfers between devices: 29.5 us -> 26.1 us
  starting transfers between devices: 14.2 us -> 16 us
    pallas_call x2, Pallas kernels: 18.9 us -> 25.4 us  [product_chunk(): pl.pallas_call(functools.partial(product_kernel, len(groups), column), ou...]
    ppermute x14, waiting for transfers between devices: 29.5 us -> 26.1 us  [sent(): lax.ppermute(x, axis, [(i, partner(i, step, size)) for i in range(size)])]
    ppermute x14, starting transfers between devices: 14.2 us -> 16 us  [sent(): lax.ppermute(x, axis, [(i, partner(i, step, size)) for i in range(size)])]
  transfers between devices with their start and end apart: 14 -> 14, of which waited for: 6 -> 6; matrix products, arithmetic and copies ran while one was open for 0% -> 0% of each run, Pallas kernels for 17% -> 21%
where the time goes in v11:
time: 72.8 us; the launch traced here: 72.6 us
  Pallas kernels  28.3 us (39%)
  waiting for transfers between devices  26.1 us (36%)
  starting transfers between devices  16 us (22%)
  local copies, waits for them, and re-layouts  2.04 us (3%)
    ppermute x14, waiting for transfers between devices, sent(): lax.ppermute(x, axis, [(i, partner(i, step, size)) for i in range(size)])  26.1 us
    pallas_call x2, Pallas kernels, product_chunk(): pl.pallas_call(functools.partial(product_kernel, len(groups), column), ou...  25.4 us
    ppermute x14, starting transfers between devices, sent(): lax.ppermute(x, axis, [(i, partner(i, step, size)) for i in range(size)])  16 us
    pallas_call x1, Pallas kernels, standardize_a(): pl.pallas_call(functools.partial(standardize_a_kernel, n_fa, n_fb), out_s...  2.12 us
    unnamed x4, local copies, waits for them, and re-layouts  2.04 us
  transfers between devices with their start and end apart: 14, of which 6 were waited for; matrix products, arithmetic and copies ran while one was open for 0% of the time, Pallas kernels for 21%

profile of v11, /device:TPU:0, one launch (start us, length us, event | category | flops | bytes accessed | tf_op | source)
XLA Modules:
  0.0 72.6 jit_solution(2462784065861328101)
XLA Ops:
  0.0 0.0 copy-start
  0.0 1.0 %copy-done = bf16[16,14336]{1,0:T(8,128)(2,1)S(1)} copy-done((bf16[16,14336]{1,0:T(8,128)(2,1)S(1)}, bf16[16,14336]{1,0:T(8,128)(2,1)}, u32[]{:S(2)}) %copy-start) | copy-done | bytes 458776
  1.0 0.3 cut_panels.2
  1.4 3.1 %collective-permute-start = (bf16[16,3584]{1,0:T(8,128)(2,1)S(1)}, bf16[16,3584]{1,0:T(8,128)(2,1)S(1)}, u32[]{:S(2)}, u32[]{:S(2)}) collective-permute-start(bf16[16,3584]{1,0:T(8,128)(2,1)S(1)} %get-tuple-element.20), channel_id=1, source_target_pairs={{0,4},{4,0},{8,12},{12,8},{1,5},{5,1},{9,13},{13,9},{2,6},{6,2},{1... | collective-permute-start | bytes 344072 | tf_op jit(solution)/shard_map/ppermute | solution.py:229
  4.4 2.5 %collective-permute-start.1 = (bf16[16,3584]{1,0:T(8,128)(2,1)S(1)}, bf16[16,3584]{1,0:T(8,128)(2,1)S(1)}, u32[]{:S(2)}, u32[]{:S(2)}) collective-permute-start(bf16[16,3584]{1,0:T(8,128)(2,1)S(1)} %get-tuple-element.21), channel_id=1, source_target_pairs={{0,12},{4,8},{8,4},{12,0},{1,13},{5,9},{9,5},{13,1},{2,14},{6,10},... | collective-permute-start | bytes 344072 | tf_op jit(solution)/shard_map/ppermute | solution.py:229
  6.9 0.1 collective-permute-start.2
  7.0 0.0 copy-start.1
  7.0 1.0 %copy-done.1 = bf16[16,14336]{1,0:T(8,128)(2,1)S(1)} copy-done((bf16[16,14336]{1,0:T(8,128)(2,1)S(1)}, bf16[16,14336]{1,0:T(8,128)(2,1)}, u32[]{:S(2)}) %copy-start.1) | copy-done | bytes 458776
  8.1 0.3 cut_panels.3
  8.4 0.1 collective-permute-start.3
  8.5 1.6 %collective-permute-start.4 = (bf16[16,3584]{1,0:T(8,128)(2,1)S(1)}, bf16[16,3584]{1,0:T(8,128)(2,1)S(1)}, u32[]{:S(2)}, u32[]{:S(2)}) collective-permute-start(bf16[16,3584]{1,0:T(8,128)(2,1)S(1)} %get-tuple-element.25), channel_id=1, source_target_pairs={{0,2},{1,3},{2,0},{3,1},{4,6},{5,7},{6,4},{7,5},{8,10},{9,11},{10,... | collective-permute-start | bytes 344072 | tf_op jit(solution)/shard_map/ppermute | solution.py:229
  10.0 0.0 collective-permute-done.refs_1_
  10.0 0.3 collective-permute-start.5
  10.3 3.2 %collective-permute-done.1.refs_2_ = bf16[16,3584]{1,0:T(8,128)(2,1)S(1)} collective-permute-done((bf16[16,3584]{1,0:T(8,128)(2,1)S(1)}, bf16[16,3584]{1,0:T(8,128)(2,1)S(1)}, u32[]{:S(2)}, u32[]{:S(2)}) %collective-permute-start.1) | collective-permute-done | bytes 114720 | tf_op jit(solution)/shard_map/ppermute | solution.py:229
  13.5 3.8 %collective-permute-done.2.refs_3_ = bf16[16,3584]{1,0:T(8,128)(2,1)S(1)} collective-permute-done((bf16[16,3584]{1,0:T(8,128)(2,1)S(1)}, bf16[16,3584]{1,0:T(8,128)(2,1)S(1)}, u32[]{:S(2)}, u32[]{:S(2)}) %collective-permute-start.2) | collective-permute-done | bytes 114720 | tf_op jit(solution)/shard_map/ppermute | solution.py:229
  17.3 0.0 collective-permute-done.3.refs_5_.refs_9_
  17.3 0.0 collective-permute-done.4.refs_6_.refs_10_
  17.3 0.0 collective-permute-done.5.refs_7_.refs_11_
  17.3 0.1 join_rows.5
  17.4 1.6 %collective-permute-start.7 = (bf16[64,3584]{1,0:T(8,128)(2,1)S(1)}, bf16[64,3584]{1,0:T(8,128)(2,1)S(1)}, u32[]{:S(2)}, u32[]{:S(2)}) collective-permute-start(bf16[64,3584]{1,0:T(8,128)(2,1)S(1)} %get-tuple-element.27.refs_0_), channel_id=1, source_target_pairs={{0,2},{1,3},{2,0},{3,1},{4,6},{5,7},{6,4},{7,5},{8,10},{9,11},{10,... | collective-permute-start | bytes 1376264 | tf_op jit(solution)/shard_map/ppermute | solution.py:229
  18.9 1.5 %collective-permute-start.8 = (bf16[64,1792]{1,0:T(8,128)(2,1)S(1)}, bf16[64,1792]{1,0:T(8,128)(2,1)S(1)}, u32[]{:S(2)}, u32[]{:S(2)}) collective-permute-start(bf16[64,1792]{1,0:T(8,128)(2,1)S(1)} %get-tuple-element.28.refs_0_), channel_id=1, source_target_pairs={{0,8},{4,12},{8,0},{12,4},{1,9},{5,13},{9,1},{13,5},{2,10},{6,14},... | collective-permute-start | bytes 688136 | tf_op jit(solution)/shard_map/ppermute | solution.py:229
  20.5 0.0 collective-permute-start.6
  20.5 1.7 %collective-permute-start.10 = (bf16[64,3584]{1,0:T(8,128)(2,1)S(1)}, bf16[64,3584]{1,0:T(8,128)(2,1)S(1)}, u32[]{:S(2)}, u32[]{:S(2)}) collective-permute-start(bf16[64,3584]{1,0:T(8,128)(2,1)S(1)} %get-tuple-element.30), channel_id=1, source_target_pairs={{0,4},{4,0},{8,12},{12,8},{1,5},{5,1},{9,13},{13,9},{2,6},{6,2},{1... | collective-permute-start | bytes 1376264 | tf_op jit(solution)/shard_map/ppermute | solution.py:229
  22.1 9.3 %collective-permute-done.8.refs_1_.refs_3_ = bf16[64,1792]{1,0:T(8,128)(2,1)S(1)} collective-permute-done((bf16[64,1792]{1,0:T(8,128)(2,1)S(1)}, bf16[64,1792]{1,0:T(8,128)(2,1)S(1)}, u32[]{:S(2)}, u32[]{:S(2)}) %collective-permute-start.8) | collective-permute-done | bytes 229408 | tf_op jit(solution)/shard_map/ppermute | solution.py:229
  31.5 0.0 collective-permute-done.7.refs_0_.refs_2_
  31.5 0.1 collective-permute-start.9
  31.6 0.3 collective-permute-start.11
  31.9 3.2 %collective-permute-start.13 = (bf16[64,1792]{1,0:T(8,128)(2,1)S(1)}, bf16[64,1792]{1,0:T(8,128)(2,1)S(1)}, u32[]{:S(2)}, u32[]{:S(2)}) collective-permute-start(bf16[64,1792]{1,0:T(8,128)(2,1)S(1)} %collective-permute-done.8.refs_1_.refs_3_), channel_id=1, source_target_pairs={{0,4},{4,0},{8,12},{12,8},{1,5},{5,1},{9,13},{13,9},{2,6},{6,2},{1... | collective-permute-start | bytes 688136 | tf_op jit(solution)/shard_map/ppermute | solution.py:229
  35.1 4.3 %collective-permute-done.10.refs_0_ = bf16[64,3584]{1,0:T(8,128)(2,1)S(1)} collective-permute-done((bf16[64,3584]{1,0:T(8,128)(2,1)S(1)}, bf16[64,3584]{1,0:T(8,128)(2,1)S(1)}, u32[]{:S(2)}, u32[]{:S(2)}) %collective-permute-start.10) | collective-permute-done | bytes 458784 | tf_op jit(solution)/shard_map/ppermute | solution.py:229
  39.4 0.0 collective-permute-done.6.refs_1_
  39.4 0.0 collective-permute-done.9.refs_3_
  39.4 2.1 %standardize_a.1.refs_1_.a_ref = bf16[3584,256]{1,0:T(8,128)(2,1)S(1)} custom-call(bf16[64,3584]{1,0:T(8,128)(2,1)S(1)} %get-tuple-element.27.refs_0_, bf16[64,3584]{1,0:T(8,128)(2,1)S(1)} %collective-permute-done.6.refs_1_, bf16[64,3584]{1,0:T(8,128)(2,1)S(1)} %collective-permute-done.7.refs_0_.refs_2_, bf16[64,3584]{1,0:T(8,128)(2,1)S(1)} %collective-permute-done.9.refs_3_), custom_call_target="tpu_custom_call" | custom-call | flops 9175040 | bytes 3670016 | tf_op jit(solution)/shard_map/standardize_a/pallas_call | solution.py:141
  41.6 4.0 %collective-permute-done.11.refs_0_.refs_4_.refs_3_ = bf16[64,1792]{1,0:T(8,128)(2,1)S(1)} collective-permute-done((bf16[64,1792]{1,0:T(8,128)(2,1)S(1)}, bf16[64,1792]{1,0:T(8,128)(2,1)S(1)}, u32[]{:S(2)}, u32[]{:S(2)}) %collective-permute-start.11) | collective-permute-done | bytes 229408 | tf_op jit(solution)/shard_map/ppermute | solution.py:229
  45.6 0.1 collective-permute-start.12
  45.7 1.5 %collective-permute-done.13.refs_2_ = bf16[64,1792]{1,0:T(8,128)(2,1)S(1)} collective-permute-done((bf16[64,1792]{1,0:T(8,128)(2,1)S(1)}, bf16[64,1792]{1,0:T(8,128)(2,1)S(1)}, u32[]{:S(2)}, u32[]{:S(2)}) %collective-permute-start.13) | collective-permute-done | bytes 229408 | tf_op jit(solution)/shard_map/ppermute | solution.py:229
  47.2 12.7 %product_chunk.2.refs_4_ = f32[3584,3584]{1,0:T(8,128)} custom-call(bf16[3584,256]{1,0:T(8,128)(2,1)S(1)} %standardize_a.1.refs_1_.a_ref, bf16[64,1792]{1,0:T(8,128)(2,1)S(1)} %get-tuple-element.28.refs_0_, bf16[64,1792]{1,0:T(8,128)(2,1)S(1)} %get-tuple-element.32.refs_1_, bf16[64,1792]{1,0:T(8,128)(2,1)S(1)} %collective-permute-done.13.refs_2_, ...), custom_call_target="tpu_custom_call" | custom-call | flops 3288334336 | bytes 25690112 | tf_op jit(solution)/shard_map/product_chunk/pallas_call | solution.py:209
  59.9 0.0 collective-permute-done.12.refs_2_
  59.9 12.7 %product_chunk.3 = f32[3584,3584]{1,0:T(8,128)} custom-call(bf16[3584,256]{1,0:T(8,128)(2,1)S(1)} %standardize_a.1.refs_1_.a_ref, bf16[64,1792]{1,0:T(8,128)(2,1)S(1)} %get-tuple-element.29.refs_0_, bf16[64,1792]{1,0:T(8,128)(2,1)S(1)} %get-tuple-element.31.refs_1_, ...), custom_call_target="tpu_custom_call", output_to_operand_aliasing={{}: (5, {})} | custom-call | flops 3288334336 | bytes 25690112 | tf_op jit(solution)/shard_map/product_chunk/pallas_call | solution.py:209
  (4 shorter events, 0.1 us)
Async XLA Ops:
  0.0 1.0 %copy-start = (bf16[16,14336]{1,0:T(8,128)(2,1)S(1)}, bf16[16,14336]{1,0:T(8,128)(2,1)}, u32[]{:S(2)}) copy-start(bf16[16,14336]{1,0:T(8,128)(2,1)} %ref.2) | copy-start | bytes 1376260
  1.4 8.7 %collective-permute-start = (bf16[16,3584]{1,0:T(8,128)(2,1)S(1)}, bf16[16,3584]{1,0:T(8,128)(2,1)S(1)}, u32[]{:S(2)}, u32[]{:S(2)}) collective-permute-start(bf16[16,3584]{1,0:T(8,128)(2,1)S(1)} %get-tuple-element.20), channel_id=1, source_target_pairs={{0,4},{4,0},{8,12},{12,8},{1,5},{5,1},{9,13},{13,9},{2,6},{6,2},{1... | collective-permute-start | bytes 344072 | tf_op jit(solution)/shard_map/ppermute | solution.py:229
  4.4 9.0 %collective-permute-start.1 = (bf16[16,3584]{1,0:T(8,128)(2,1)S(1)}, bf16[16,3584]{1,0:T(8,128)(2,1)S(1)}, u32[]{:S(2)}, u32[]{:S(2)}) collective-permute-start(bf16[16,3584]{1,0:T(8,128)(2,1)S(1)} %get-tuple-element.21), channel_id=1, source_target_pairs={{0,12},{4,8},{8,4},{12,0},{1,13},{5,9},{9,5},{13,1},{2,14},{6,10},... | collective-permute-start | bytes 344072 | tf_op jit(solution)/shard_map/ppermute | solution.py:229
  6.9 10.3 %collective-permute-start.2 = (bf16[16,3584]{1,0:T(8,128)(2,1)S(1)}, bf16[16,3584]{1,0:T(8,128)(2,1)S(1)}, u32[]{:S(2)}, u32[]{:S(2)}) collective-permute-start(bf16[16,3584]{1,0:T(8,128)(2,1)S(1)} %get-tuple-element.22), channel_id=1, source_target_pairs={{0,8},{4,12},{8,0},{12,4},{1,9},{5,13},{9,1},{13,5},{2,10},{6,14},... | collective-permute-start | bytes 344072 | tf_op jit(solution)/shard_map/ppermute | solution.py:229
  7.0 1.0 %copy-start.1 = (bf16[16,14336]{1,0:T(8,128)(2,1)S(1)}, bf16[16,14336]{1,0:T(8,128)(2,1)}, u32[]{:S(2)}) copy-start(bf16[16,14336]{1,0:T(8,128)(2,1)} %ref.3) | copy-start | bytes 1376260
  8.4 8.9 %collective-permute-start.3 = (bf16[16,3584]{1,0:T(8,128)(2,1)S(1)}, bf16[16,3584]{1,0:T(8,128)(2,1)S(1)}, u32[]{:S(2)}, u32[]{:S(2)}) collective-permute-start(bf16[16,3584]{1,0:T(8,128)(2,1)S(1)} %get-tuple-element.24), channel_id=1, source_target_pairs={{0,1},{1,0},{2,3},{3,2},{4,5},{5,4},{6,7},{7,6},{8,9},{9,8},{10,11... | collective-permute-start | bytes 344072 | tf_op jit(solution)/shard_map/ppermute | solution.py:229
  8.5 8.8 %collective-permute-start.4 = (bf16[16,3584]{1,0:T(8,128)(2,1)S(1)}, bf16[16,3584]{1,0:T(8,128)(2,1)S(1)}, u32[]{:S(2)}, u32[]{:S(2)}) collective-permute-start(bf16[16,3584]{1,0:T(8,128)(2,1)S(1)} %get-tuple-element.25), channel_id=1, source_target_pairs={{0,2},{1,3},{2,0},{3,1},{4,6},{5,7},{6,4},{7,5},{8,10},{9,11},{10,... | collective-permute-start | bytes 344072 | tf_op jit(solution)/shard_map/ppermute | solution.py:229
  10.0 7.3 %collective-permute-start.5 = (bf16[16,3584]{1,0:T(8,128)(2,1)S(1)}, bf16[16,3584]{1,0:T(8,128)(2,1)S(1)}, u32[]{:S(2)}, u32[]{:S(2)}) collective-permute-start(bf16[16,3584]{1,0:T(8,128)(2,1)S(1)} %get-tuple-element.26), channel_id=1, source_target_pairs={{0,3},{1,2},{2,1},{3,0},{4,7},{5,6},{6,5},{7,4},{8,11},{9,10},{10,... | collective-permute-start | bytes 344072 | tf_op jit(solution)/shard_map/ppermute | solution.py:229
  17.4 14.1 %collective-permute-start.7 = (bf16[64,3584]{1,0:T(8,128)(2,1)S(1)}, bf16[64,3584]{1,0:T(8,128)(2,1)S(1)}, u32[]{:S(2)}, u32[]{:S(2)}) collective-permute-start(bf16[64,3584]{1,0:T(8,128)(2,1)S(1)} %get-tuple-element.27.refs_0_), channel_id=1, source_target_pairs={{0,2},{1,3},{2,0},{3,1},{4,6},{5,7},{6,4},{7,5},{8,10},{9,11},{10,... | collective-permute-start | bytes 1376264 | tf_op jit(solution)/shard_map/ppermute | solution.py:229
  18.9 12.5 %collective-permute-start.8 = (bf16[64,1792]{1,0:T(8,128)(2,1)S(1)}, bf16[64,1792]{1,0:T(8,128)(2,1)S(1)}, u32[]{:S(2)}, u32[]{:S(2)}) collective-permute-start(bf16[64,1792]{1,0:T(8,128)(2,1)S(1)} %get-tuple-element.28.refs_0_), channel_id=1, source_target_pairs={{0,8},{4,12},{8,0},{12,4},{1,9},{5,13},{9,1},{13,5},{2,10},{6,14},... | collective-permute-start | bytes 688136 | tf_op jit(solution)/shard_map/ppermute | solution.py:229
  20.5 18.9 %collective-permute-start.6 = (bf16[64,3584]{1,0:T(8,128)(2,1)S(1)}, bf16[64,3584]{1,0:T(8,128)(2,1)S(1)}, u32[]{:S(2)}, u32[]{:S(2)}) collective-permute-start(bf16[64,3584]{1,0:T(8,128)(2,1)S(1)} %get-tuple-element.27.refs_0_), channel_id=1, source_target_pairs={{0,1},{1,0},{2,3},{3,2},{4,5},{5,4},{6,7},{7,6},{8,9},{9,8},{10,11... | collective-permute-start | bytes 1376264 | tf_op jit(solution)/shard_map/ppermute | solution.py:229
  20.5 18.9 %collective-permute-start.10 = (bf16[64,3584]{1,0:T(8,128)(2,1)S(1)}, bf16[64,3584]{1,0:T(8,128)(2,1)S(1)}, u32[]{:S(2)}, u32[]{:S(2)}) collective-permute-start(bf16[64,3584]{1,0:T(8,128)(2,1)S(1)} %get-tuple-element.30), channel_id=1, source_target_pairs={{0,4},{4,0},{8,12},{12,8},{1,5},{5,1},{9,13},{13,9},{2,6},{6,2},{1... | collective-permute-start | bytes 1376264 | tf_op jit(solution)/shard_map/ppermute | solution.py:229
  31.5 7.9 %collective-permute-start.9 = (bf16[64,3584]{1,0:T(8,128)(2,1)S(1)}, bf16[64,3584]{1,0:T(8,128)(2,1)S(1)}, u32[]{:S(2)}, u32[]{:S(2)}) collective-permute-start(bf16[64,3584]{1,0:T(8,128)(2,1)S(1)} %join_rows.6), channel_id=1, source_target_pairs={{0,1},{1,0},{2,3},{3,2},{4,5},{5,4},{6,7},{7,6},{8,9},{9,8},{10,11... | collective-permute-start | bytes 1376264 | tf_op jit(solution)/shard_map/ppermute | solution.py:229
  31.6 14.0 %collective-permute-start.11 = (bf16[64,1792]{1,0:T(8,128)(2,1)S(1)}, bf16[64,1792]{1,0:T(8,128)(2,1)S(1)}, u32[]{:S(2)}, u32[]{:S(2)}) collective-permute-start(bf16[64,1792]{1,0:T(8,128)(2,1)S(1)} %join_rows.8), channel_id=1, source_target_pairs={{0,8},{4,12},{8,0},{12,4},{1,9},{5,13},{9,1},{13,5},{2,10},{6,14},... | collective-permute-start | bytes 688136 | tf_op jit(solution)/shard_map/ppermute | solution.py:229
  31.9 15.3 %collective-permute-start.13 = (bf16[64,1792]{1,0:T(8,128)(2,1)S(1)}, bf16[64,1792]{1,0:T(8,128)(2,1)S(1)}, u32[]{:S(2)}, u32[]{:S(2)}) collective-permute-start(bf16[64,1792]{1,0:T(8,128)(2,1)S(1)} %collective-permute-done.8.refs_1_.refs_3_), channel_id=1, source_target_pairs={{0,4},{4,0},{8,12},{12,8},{1,5},{5,1},{9,13},{13,9},{2,6},{6,2},{1... | collective-permute-start | bytes 688136 | tf_op jit(solution)/shard_map/ppermute | solution.py:229
  45.6 14.3 %collective-permute-start.12 = (bf16[64,1792]{1,0:T(8,128)(2,1)S(1)}, bf16[64,1792]{1,0:T(8,128)(2,1)S(1)}, u32[]{:S(2)}, u32[]{:S(2)}) collective-permute-start(bf16[64,1792]{1,0:T(8,128)(2,1)S(1)} %join_rows.9), channel_id=1, source_target_pairs={{0,4},{4,0},{8,12},{12,8},{1,5},{5,1},{9,13},{13,9},{2,6},{6,2},{1... | collective-permute-start | bytes 688136 | tf_op jit(solution)/shard_map/ppermute | solution.py:229

commit v12 on v11

--- a/solution.py
+++ b/solution.py
@@ -157,40 +157,31 @@
     out, slots, sems = refs[-3:]
     total, width = a_ref.shape[1], groups[0].shape[1]
     n_slots, height, strip = slots.shape
-    n_parts = sems.shape[1]
-    block = height // n_parts
-
-    def copies_of(step, part):
+
+    def copy_of(step):
         slot = lax.rem(step, n_slots)
         place = pl.multiple_of(column + step * strip, 128)
-        rows = pl.ds(part * block, block)
-        return pltpu.make_async_copy(
-            slots.at[slot, rows], out.at[rows, pl.ds(place, strip)], sems.at[slot, part]
-        )
+        return pltpu.make_async_copy(slots.at[slot], out.at[:, pl.ds(place, strip)], sems.at[slot])
 
     @pl.loop(0, width // strip)
     def _(step):
+        @pl.when(step >= n_slots)
+        def _():
+            copy_of(step - n_slots).wait()
+
         parts = []
         for part in range(strip // 128):
             columns = pl.ds(pl.multiple_of(step * strip + part * 128, 128), 128)
             pieces = [ref[:, columns].astype(jnp.float32) for ref in groups]
             parts.append(standardize(jnp.concatenate(pieces, axis=0)))
         std = jnp.concatenate(parts, axis=1)
-        for part in range(n_parts):
-            rows = pl.ds(part * block, block)
-
-            @pl.when(step >= n_slots)
-            def _():
-                copies_of(step - n_slots, part).wait()
-
-            product = jnp.dot(a_ref[rows, :], std, preferred_element_type=jnp.float32)
-            slots[lax.rem(step, n_slots), rows] = over_count(product, total)
-            copies_of(step, part).start()
+        product = jnp.dot(a_ref[...], std, preferred_element_type=jnp.float32)
+        slots[lax.rem(step, n_slots)] = over_count(product, total)
+        copy_of(step).start()
 
     @pl.loop(max(width // strip - n_slots, 0), width // strip)
     def _(step):
-        for part in range(n_parts):
-            copies_of(step, part).wait()
+        copy_of(step).wait()
 
 
 def product_chunk(std_a, groups, column, full_width, buffer, after=()):
@@ -213,7 +204,7 @@
         out_specs=pl.BlockSpec(memory_space=pl.ANY),
         scratch_shapes=[
             pltpu.VMEM((n_slots, height, strip), jnp.float32),
-            pltpu.SemaphoreType.DMA((n_slots, height // block_of(height, 1024))),
+            pltpu.SemaphoreType.DMA((n_slots,)),
         ],
         input_output_aliases=aliases,
         compiler_params=pltpu.CompilerParams(vmem_limit_bytes=VMEM),

time: 72.8 us -> 66.3 us (0.911)
  Pallas kernels: 28.3 us -> 21.9 us
    pallas_call x2, Pallas kernels: 25.4 us -> 18.9 us  [product_chunk(): pl.pallas_call(functools.partial(product_kernel, len(groups), column), ou...]
  transfers between devices with their start and end apart: 14 -> 14, of which waited for: 6 -> 6; matrix products, arithmetic and copies ran while one was open for 0% -> 0% of each run, Pallas kernels for 21% -> 18%
where the time goes in v12:
time: 66.3 us; the launch traced here: 66.1 us
  waiting for transfers between devices  26.1 us (39%)
  Pallas kernels  21.9 us (33%)
  starting transfers between devices  16 us (24%)
  local copies, waits for them, and re-layouts  2.04 us (3%)
    ppermute x14, waiting for transfers between devices, sent(): lax.ppermute(x, axis, [(i, partner(i, step, size)) for i in range(size)])  26.1 us
    pallas_call x2, Pallas kernels, product_chunk(): pl.pallas_call(functools.partial(product_kernel, len(groups), column), ou...  18.9 us
    ppermute x14, starting transfers between devices, sent(): lax.ppermute(x, axis, [(i, partner(i, step, size)) for i in range(size)])  16 us
    pallas_call x1, Pallas kernels, standardize_a(): pl.pallas_call(functools.partial(standardize_a_kernel, n_fa, n_fb), out_s...  2.12 us
    unnamed x4, local copies, waits for them, and re-layouts  2.04 us
  transfers between devices with their start and end apart: 14, of which 6 were waited for; matrix products, arithmetic and copies ran while one was open for 0% of the time, Pallas kernels for 18%

profile of v12, /device:TPU:0, one launch (start us, length us, event | category | flops | bytes accessed | tf_op | source)
XLA Modules:
  0.0 66.1 jit_solution(12990140448235397859)
XLA Ops:
  0.0 0.0 copy-start
  0.0 1.0 %copy-done = bf16[16,14336]{1,0:T(8,128)(2,1)S(1)} copy-done((bf16[16,14336]{1,0:T(8,128)(2,1)S(1)}, bf16[16,14336]{1,0:T(8,128)(2,1)}, u32[]{:S(2)}) %copy-start) | copy-done | bytes 458776
  1.0 0.3 cut_panels.2
  1.4 3.1 %collective-permute-start = (bf16[16,3584]{1,0:T(8,128)(2,1)S(1)}, bf16[16,3584]{1,0:T(8,128)(2,1)S(1)}, u32[]{:S(2)}, u32[]{:S(2)}) collective-permute-start(bf16[16,3584]{1,0:T(8,128)(2,1)S(1)} %get-tuple-element.20), channel_id=1, source_target_pairs={{0,4},{4,0},{8,12},{12,8},{1,5},{5,1},{9,13},{13,9},{2,6},{6,2},{1... | collective-permute-start | bytes 344072 | tf_op jit(solution)/shard_map/ppermute | solution.py:220
  4.4 2.5 %collective-permute-start.1 = (bf16[16,3584]{1,0:T(8,128)(2,1)S(1)}, bf16[16,3584]{1,0:T(8,128)(2,1)S(1)}, u32[]{:S(2)}, u32[]{:S(2)}) collective-permute-start(bf16[16,3584]{1,0:T(8,128)(2,1)S(1)} %get-tuple-element.21), channel_id=1, source_target_pairs={{0,12},{4,8},{8,4},{12,0},{1,13},{5,9},{9,5},{13,1},{2,14},{6,10},... | collective-permute-start | bytes 344072 | tf_op jit(solution)/shard_map/ppermute | solution.py:220
  6.9 0.1 collective-permute-start.2
  7.0 0.0 copy-start.1
  7.0 1.0 %copy-done.1 = bf16[16,14336]{1,0:T(8,128)(2,1)S(1)} copy-done((bf16[16,14336]{1,0:T(8,128)(2,1)S(1)}, bf16[16,14336]{1,0:T(8,128)(2,1)}, u32[]{:S(2)}) %copy-start.1) | copy-done | bytes 458776
  8.1 0.3 cut_panels.3
  8.4 0.1 collective-permute-start.3
  8.5 1.6 %collective-permute-start.4 = (bf16[16,3584]{1,0:T(8,128)(2,1)S(1)}, bf16[16,3584]{1,0:T(8,128)(2,1)S(1)}, u32[]{:S(2)}, u32[]{:S(2)}) collective-permute-start(bf16[16,3584]{1,0:T(8,128)(2,1)S(1)} %get-tuple-element.25), channel_id=1, source_target_pairs={{0,2},{1,3},{2,0},{3,1},{4,6},{5,7},{6,4},{7,5},{8,10},{9,11},{10,... | collective-permute-start | bytes 344072 | tf_op jit(solution)/shard_map/ppermute | solution.py:220
  10.0 0.0 collective-permute-done.refs_1_
  10.0 0.3 collective-permute-start.5
  10.3 3.2 %collective-permute-done.1.refs_2_ = bf16[16,3584]{1,0:T(8,128)(2,1)S(1)} collective-permute-done((bf16[16,3584]{1,0:T(8,128)(2,1)S(1)}, bf16[16,3584]{1,0:T(8,128)(2,1)S(1)}, u32[]{:S(2)}, u32[]{:S(2)}) %collective-permute-start.1) | collective-permute-done | bytes 114720 | tf_op jit(solution)/shard_map/ppermute | solution.py:220
  13.5 3.8 %collective-permute-done.2.refs_3_ = bf16[16,3584]{1,0:T(8,128)(2,1)S(1)} collective-permute-done((bf16[16,3584]{1,0:T(8,128)(2,1)S(1)}, bf16[16,3584]{1,0:T(8,128)(2,1)S(1)}, u32[]{:S(2)}, u32[]{:S(2)}) %collective-permute-start.2) | collective-permute-done | bytes 114720 | tf_op jit(solution)/shard_map/ppermute | solution.py:220
  17.3 0.0 collective-permute-done.3.refs_5_.refs_9_
  17.3 0.0 collective-permute-done.4.refs_6_.refs_10_
  17.3 0.0 collective-permute-done.5.refs_7_.refs_11_
  17.3 0.1 join_rows.5
  17.4 1.6 %collective-permute-start.7 = (bf16[64,3584]{1,0:T(8,128)(2,1)S(1)}, bf16[64,3584]{1,0:T(8,128)(2,1)S(1)}, u32[]{:S(2)}, u32[]{:S(2)}) collective-permute-start(bf16[64,3584]{1,0:T(8,128)(2,1)S(1)} %get-tuple-element.27.refs_0_), channel_id=1, source_target_pairs={{0,2},{1,3},{2,0},{3,1},{4,6},{5,7},{6,4},{7,5},{8,10},{9,11},{10,... | collective-permute-start | bytes 1376264 | tf_op jit(solution)/shard_map/ppermute | solution.py:220
  18.9 1.5 %collective-permute-start.8 = (bf16[64,1792]{1,0:T(8,128)(2,1)S(1)}, bf16[64,1792]{1,0:T(8,128)(2,1)S(1)}, u32[]{:S(2)}, u32[]{:S(2)}) collective-permute-start(bf16[64,1792]{1,0:T(8,128)(2,1)S(1)} %get-tuple-element.28.refs_0_), channel_id=1, source_target_pairs={{0,8},{4,12},{8,0},{12,4},{1,9},{5,13},{9,1},{13,5},{2,10},{6,14},... | collective-permute-start | bytes 688136 | tf_op jit(solution)/shard_map/ppermute | solution.py:220
  20.5 0.0 collective-permute-start.6
  20.5 1.7 %collective-permute-start.10 = (bf16[64,3584]{1,0:T(8,128)(2,1)S(1)}, bf16[64,3584]{1,0:T(8,128)(2,1)S(1)}, u32[]{:S(2)}, u32[]{:S(2)}) collective-permute-start(bf16[64,3584]{1,0:T(8,128)(2,1)S(1)} %get-tuple-element.30), channel_id=1, source_target_pairs={{0,4},{4,0},{8,12},{12,8},{1,5},{5,1},{9,13},{13,9},{2,6},{6,2},{1... | collective-permute-start | bytes 1376264 | tf_op jit(solution)/shard_map/ppermute | solution.py:220
  22.1 9.3 %collective-permute-done.8.refs_1_.refs_3_ = bf16[64,1792]{1,0:T(8,128)(2,1)S(1)} collective-permute-done((bf16[64,1792]{1,0:T(8,128)(2,1)S(1)}, bf16[64,1792]{1,0:T(8,128)(2,1)S(1)}, u32[]{:S(2)}, u32[]{:S(2)}) %collective-permute-start.8) | collective-permute-done | bytes 229408 | tf_op jit(solution)/shard_map/ppermute | solution.py:220
  31.5 0.0 collective-permute-done.7.refs_0_.refs_2_
  31.5 0.1 collective-permute-start.9
  31.6 0.3 collective-permute-start.11
  31.9 3.2 %collective-permute-start.13 = (bf16[64,1792]{1,0:T(8,128)(2,1)S(1)}, bf16[64,1792]{1,0:T(8,128)(2,1)S(1)}, u32[]{:S(2)}, u32[]{:S(2)}) collective-permute-start(bf16[64,1792]{1,0:T(8,128)(2,1)S(1)} %collective-permute-done.8.refs_1_.refs_3_), channel_id=1, source_target_pairs={{0,4},{4,0},{8,12},{12,8},{1,5},{5,1},{9,13},{13,9},{2,6},{6,2},{1... | collective-permute-start | bytes 688136 | tf_op jit(solution)/shard_map/ppermute | solution.py:220
  35.1 4.3 %collective-permute-done.10.refs_0_ = bf16[64,3584]{1,0:T(8,128)(2,1)S(1)} collective-permute-done((bf16[64,3584]{1,0:T(8,128)(2,1)S(1)}, bf16[64,3584]{1,0:T(8,128)(2,1)S(1)}, u32[]{:S(2)}, u32[]{:S(2)}) %collective-permute-start.10) | collective-permute-done | bytes 458784 | tf_op jit(solution)/shard_map/ppermute | solution.py:220
  39.4 0.0 collective-permute-done.6.refs_1_
  39.4 0.0 collective-permute-done.9.refs_3_
  39.4 2.1 %standardize_a.1.refs_1_.a_ref = bf16[3584,256]{1,0:T(8,128)(2,1)S(1)} custom-call(bf16[64,3584]{1,0:T(8,128)(2,1)S(1)} %get-tuple-element.27.refs_0_, bf16[64,3584]{1,0:T(8,128)(2,1)S(1)} %collective-permute-done.6.refs_1_, bf16[64,3584]{1,0:T(8,128)(2,1)S(1)} %collective-permute-done.7.refs_0_.refs_2_, bf16[64,3584]{1,0:T(8,128)(2,1)S(1)} %collective-permute-done.9.refs_3_), custom_call_target="tpu_custom_call" | custom-call | flops 9175040 | bytes 3670016 | tf_op jit(solution)/shard_map/standardize_a/pallas_call | solution.py:141
  41.6 4.0 %collective-permute-done.11.refs_0_.refs_4_.refs_3_ = bf16[64,1792]{1,0:T(8,128)(2,1)S(1)} collective-permute-done((bf16[64,1792]{1,0:T(8,128)(2,1)S(1)}, bf16[64,1792]{1,0:T(8,128)(2,1)S(1)}, u32[]{:S(2)}, u32[]{:S(2)}) %collective-permute-start.11) | collective-permute-done | bytes 229408 | tf_op jit(solution)/shard_map/ppermute | solution.py:220
  45.6 0.1 collective-permute-start.12
  45.7 1.5 %collective-permute-done.13.refs_2_ = bf16[64,1792]{1,0:T(8,128)(2,1)S(1)} collective-permute-done((bf16[64,1792]{1,0:T(8,128)(2,1)S(1)}, bf16[64,1792]{1,0:T(8,128)(2,1)S(1)}, u32[]{:S(2)}, u32[]{:S(2)}) %collective-permute-start.13) | collective-permute-done | bytes 229408 | tf_op jit(solution)/shard_map/ppermute | solution.py:220
  47.2 9.4 %product_chunk.2.refs_4_ = f32[3584,3584]{1,0:T(8,128)} custom-call(bf16[3584,256]{1,0:T(8,128)(2,1)S(1)} %standardize_a.1.refs_1_.a_ref, bf16[64,1792]{1,0:T(8,128)(2,1)S(1)} %get-tuple-element.28.refs_0_, bf16[64,1792]{1,0:T(8,128)(2,1)S(1)} %get-tuple-element.32.refs_1_, bf16[64,1792]{1,0:T(8,128)(2,1)S(1)} %collective-permute-done.13.refs_2_, ...), custom_call_target="tpu_custom_call" | custom-call | flops 3288334336 | bytes 25690112 | tf_op jit(solution)/shard_map/product_chunk/pallas_call | solution.py:200
  56.7 0.0 collective-permute-done.12.refs_2_
  56.7 9.5 %product_chunk.3 = f32[3584,3584]{1,0:T(8,128)} custom-call(bf16[3584,256]{1,0:T(8,128)(2,1)S(1)} %standardize_a.1.refs_1_.a_ref, bf16[64,1792]{1,0:T(8,128)(2,1)S(1)} %get-tuple-element.29.refs_0_, bf16[64,1792]{1,0:T(8,128)(2,1)S(1)} %get-tuple-element.31.refs_1_, ...), custom_call_target="tpu_custom_call", output_to_operand_aliasing={{}: (5, {})} | custom-call | flops 3288334336 | bytes 25690112 | tf_op jit(solution)/shard_map/product_chunk/pallas_call | solution.py:200
  (4 shorter events, 0.1 us)
Async XLA Ops:
  0.0 1.0 %copy-start = (bf16[16,14336]{1,0:T(8,128)(2,1)S(1)}, bf16[16,14336]{1,0:T(8,128)(2,1)}, u32[]{:S(2)}) copy-start(bf16[16,14336]{1,0:T(8,128)(2,1)} %ref.2) | copy-start | bytes 1376260
  1.4 8.7 %collective-permute-start = (bf16[16,3584]{1,0:T(8,128)(2,1)S(1)}, bf16[16,3584]{1,0:T(8,128)(2,1)S(1)}, u32[]{:S(2)}, u32[]{:S(2)}) collective-permute-start(bf16[16,3584]{1,0:T(8,128)(2,1)S(1)} %get-tuple-element.20), channel_id=1, source_target_pairs={{0,4},{4,0},{8,12},{12,8},{1,5},{5,1},{9,13},{13,9},{2,6},{6,2},{1... | collective-permute-start | bytes 344072 | tf_op jit(solution)/shard_map/ppermute | solution.py:220
  4.4 9.0 %collective-permute-start.1 = (bf16[16,3584]{1,0:T(8,128)(2,1)S(1)}, bf16[16,3584]{1,0:T(8,128)(2,1)S(1)}, u32[]{:S(2)}, u32[]{:S(2)}) collective-permute-start(bf16[16,3584]{1,0:T(8,128)(2,1)S(1)} %get-tuple-element.21), channel_id=1, source_target_pairs={{0,12},{4,8},{8,4},{12,0},{1,13},{5,9},{9,5},{13,1},{2,14},{6,10},... | collective-permute-start | bytes 344072 | tf_op jit(solution)/shard_map/ppermute | solution.py:220
  6.9 10.3 %collective-permute-start.2 = (bf16[16,3584]{1,0:T(8,128)(2,1)S(1)}, bf16[16,3584]{1,0:T(8,128)(2,1)S(1)}, u32[]{:S(2)}, u32[]{:S(2)}) collective-permute-start(bf16[16,3584]{1,0:T(8,128)(2,1)S(1)} %get-tuple-element.22), channel_id=1, source_target_pairs={{0,8},{4,12},{8,0},{12,4},{1,9},{5,13},{9,1},{13,5},{2,10},{6,14},... | collective-permute-start | bytes 344072 | tf_op jit(solution)/shard_map/ppermute | solution.py:220
  7.0 1.0 %copy-start.1 = (bf16[16,14336]{1,0:T(8,128)(2,1)S(1)}, bf16[16,14336]{1,0:T(8,128)(2,1)}, u32[]{:S(2)}) copy-start(bf16[16,14336]{1,0:T(8,128)(2,1)} %ref.3) | copy-start | bytes 1376260
  8.4 8.9 %collective-permute-start.3 = (bf16[16,3584]{1,0:T(8,128)(2,1)S(1)}, bf16[16,3584]{1,0:T(8,128)(2,1)S(1)}, u32[]{:S(2)}, u32[]{:S(2)}) collective-permute-start(bf16[16,3584]{1,0:T(8,128)(2,1)S(1)} %get-tuple-element.24), channel_id=1, source_target_pairs={{0,1},{1,0},{2,3},{3,2},{4,5},{5,4},{6,7},{7,6},{8,9},{9,8},{10,11... | collective-permute-start | bytes 344072 | tf_op jit(solution)/shard_map/ppermute | solution.py:220
  8.5 8.8 %collective-permute-start.4 = (bf16[16,3584]{1,0:T(8,128)(2,1)S(1)}, bf16[16,3584]{1,0:T(8,128)(2,1)S(1)}, u32[]{:S(2)}, u32[]{:S(2)}) collective-permute-start(bf16[16,3584]{1,0:T(8,128)(2,1)S(1)} %get-tuple-element.25), channel_id=1, source_target_pairs={{0,2},{1,3},{2,0},{3,1},{4,6},{5,7},{6,4},{7,5},{8,10},{9,11},{10,... | collective-permute-start | bytes 344072 | tf_op jit(solution)/shard_map/ppermute | solution.py:220
  10.0 7.3 %collective-permute-start.5 = (bf16[16,3584]{1,0:T(8,128)(2,1)S(1)}, bf16[16,3584]{1,0:T(8,128)(2,1)S(1)}, u32[]{:S(2)}, u32[]{:S(2)}) collective-permute-start(bf16[16,3584]{1,0:T(8,128)(2,1)S(1)} %get-tuple-element.26), channel_id=1, source_target_pairs={{0,3},{1,2},{2,1},{3,0},{4,7},{5,6},{6,5},{7,4},{8,11},{9,10},{10,... | collective-permute-start | bytes 344072 | tf_op jit(solution)/shard_map/ppermute | solution.py:220
  17.4 14.1 %collective-permute-start.7 = (bf16[64,3584]{1,0:T(8,128)(2,1)S(1)}, bf16[64,3584]{1,0:T(8,128)(2,1)S(1)}, u32[]{:S(2)}, u32[]{:S(2)}) collective-permute-start(bf16[64,3584]{1,0:T(8,128)(2,1)S(1)} %get-tuple-element.27.refs_0_), channel_id=1, source_target_pairs={{0,2},{1,3},{2,0},{3,1},{4,6},{5,7},{6,4},{7,5},{8,10},{9,11},{10,... | collective-permute-start | bytes 1376264 | tf_op jit(solution)/shard_map/ppermute | solution.py:220
  18.9 12.5 %collective-permute-start.8 = (bf16[64,1792]{1,0:T(8,128)(2,1)S(1)}, bf16[64,1792]{1,0:T(8,128)(2,1)S(1)}, u32[]{:S(2)}, u32[]{:S(2)}) collective-permute-start(bf16[64,1792]{1,0:T(8,128)(2,1)S(1)} %get-tuple-element.28.refs_0_), channel_id=1, source_target_pairs={{0,8},{4,12},{8,0},{12,4},{1,9},{5,13},{9,1},{13,5},{2,10},{6,14},... | collective-permute-start | bytes 688136 | tf_op jit(solution)/shard_map/ppermute | solution.py:220
  20.5 18.9 %collective-permute-start.6 = (bf16[64,3584]{1,0:T(8,128)(2,1)S(1)}, bf16[64,3584]{1,0:T(8,128)(2,1)S(1)}, u32[]{:S(2)}, u32[]{:S(2)}) collective-permute-start(bf16[64,3584]{1,0:T(8,128)(2,1)S(1)} %get-tuple-element.27.refs_0_), channel_id=1, source_target_pairs={{0,1},{1,0},{2,3},{3,2},{4,5},{5,4},{6,7},{7,6},{8,9},{9,8},{10,11... | collective-permute-start | bytes 1376264 | tf_op jit(solution)/shard_map/ppermute | solution.py:220
  20.5 18.9 %collective-permute-start.10 = (bf16[64,3584]{1,0:T(8,128)(2,1)S(1)}, bf16[64,3584]{1,0:T(8,128)(2,1)S(1)}, u32[]{:S(2)}, u32[]{:S(2)}) collective-permute-start(bf16[64,3584]{1,0:T(8,128)(2,1)S(1)} %get-tuple-element.30), channel_id=1, source_target_pairs={{0,4},{4,0},{8,12},{12,8},{1,5},{5,1},{9,13},{13,9},{2,6},{6,2},{1... | collective-permute-start | bytes 1376264 | tf_op jit(solution)/shard_map/ppermute | solution.py:220
  31.5 7.9 %collective-permute-start.9 = (bf16[64,3584]{1,0:T(8,128)(2,1)S(1)}, bf16[64,3584]{1,0:T(8,128)(2,1)S(1)}, u32[]{:S(2)}, u32[]{:S(2)}) collective-permute-start(bf16[64,3584]{1,0:T(8,128)(2,1)S(1)} %join_rows.6), channel_id=1, source_target_pairs={{0,1},{1,0},{2,3},{3,2},{4,5},{5,4},{6,7},{7,6},{8,9},{9,8},{10,11... | collective-permute-start | bytes 1376264 | tf_op jit(solution)/shard_map/ppermute | solution.py:220
  31.6 14.0 %collective-permute-start.11 = (bf16[64,1792]{1,0:T(8,128)(2,1)S(1)}, bf16[64,1792]{1,0:T(8,128)(2,1)S(1)}, u32[]{:S(2)}, u32[]{:S(2)}) collective-permute-start(bf16[64,1792]{1,0:T(8,128)(2,1)S(1)} %join_rows.8), channel_id=1, source_target_pairs={{0,8},{4,12},{8,0},{12,4},{1,9},{5,13},{9,1},{13,5},{2,10},{6,14},... | collective-permute-start | bytes 688136 | tf_op jit(solution)/shard_map/ppermute | solution.py:220
  31.9 15.3 %collective-permute-start.13 = (bf16[64,1792]{1,0:T(8,128)(2,1)S(1)}, bf16[64,1792]{1,0:T(8,128)(2,1)S(1)}, u32[]{:S(2)}, u32[]{:S(2)}) collective-permute-start(bf16[64,1792]{1,0:T(8,128)(2,1)S(1)} %collective-permute-done.8.refs_1_.refs_3_), channel_id=1, source_target_pairs={{0,4},{4,0},{8,12},{12,8},{1,5},{5,1},{9,13},{13,9},{2,6},{6,2},{1... | collective-permute-start | bytes 688136 | tf_op jit(solution)/shard_map/ppermute | solution.py:220
  45.6 11.0 %collective-permute-start.12 = (bf16[64,1792]{1,0:T(8,128)(2,1)S(1)}, bf16[64,1792]{1,0:T(8,128)(2,1)S(1)}, u32[]{:S(2)}, u32[]{:S(2)}) collective-permute-start(bf16[64,1792]{1,0:T(8,128)(2,1)S(1)} %join_rows.9), channel_id=1, source_target_pairs={{0,4},{4,0},{8,12},{12,8},{1,5},{5,1},{9,13},{13,9},{2,6},{6,2},{1... | collective-permute-start | bytes 688136 | tf_op jit(solution)/shard_map/ppermute | solution.py:220

commit v13 on v12

--- a/solution.py
+++ b/solution.py
@@ -154,34 +154,52 @@
 
 def product_kernel(n_groups, column, a_ref, *refs):
     groups = refs[:n_groups]
-    out, slots, sems = refs[-3:]
+    out, slots, edges, sems, edge_sems = refs[-5:]
     total, width = a_ref.shape[1], groups[0].shape[1]
     n_slots, height, strip = slots.shape
+    edge = edges.shape[2]
+    steps = (width - 2 * edge) // strip
+
+    def product_of(start, size):
+        parts = []
+        for part in range(size // 128):
+            columns = pl.ds(pl.multiple_of(start + part * 128, 128), 128)
+            pieces = [ref[:, columns].astype(jnp.float32) for ref in groups]
+            parts.append(standardize(jnp.concatenate(pieces, axis=0)))
+        std = parts[0] if len(parts) == 1 else jnp.concatenate(parts, axis=1)
+        product = jnp.dot(a_ref[...], std, preferred_element_type=jnp.float32)
+        return over_count(product, total)
 
     def copy_of(step):
         slot = lax.rem(step, n_slots)
-        place = pl.multiple_of(column + step * strip, 128)
+        place = pl.multiple_of(column + edge + step * strip, 128)
         return pltpu.make_async_copy(slots.at[slot], out.at[:, pl.ds(place, strip)], sems.at[slot])
 
-    @pl.loop(0, width // strip)
+    def edge_copy(side):
+        place = column + side * (width - edge)
+        return pltpu.make_async_copy(edges.at[side], out.at[:, pl.ds(place, edge)], edge_sems.at[side])
+
+    edges[0] = product_of(0, edge)
+    edge_copy(0).start()
+
+    @pl.loop(0, steps)
     def _(step):
         @pl.when(step >= n_slots)
         def _():
             copy_of(step - n_slots).wait()
 
-        parts = []
-        for part in range(strip // 128):
-            columns = pl.ds(pl.multiple_of(step * strip + part * 128, 128), 128)
-            pieces = [ref[:, columns].astype(jnp.float32) for ref in groups]
-            parts.append(standardize(jnp.concatenate(pieces, axis=0)))
-        std = jnp.concatenate(parts, axis=1)
-        product = jnp.dot(a_ref[...], std, preferred_element_type=jnp.float32)
-        slots[lax.rem(step, n_slots)] = over_count(product, total)
+        slots[lax.rem(step, n_slots)] = product_of(edge + step * strip, strip)
         copy_of(step).start()
 
-    @pl.loop(max(width // strip - n_slots, 0), width // strip)
+    edges[1] = product_of(width - edge, edge)
+    edge_copy(1).start()
+
+    @pl.loop(max(steps - n_slots, 0), steps)
     def _(step):
         copy_of(step).wait()
+
+    edge_copy(0).wait()
+    edge_copy(1).wait()
 
 
 def product_chunk(std_a, groups, column, full_width, buffer, after=()):
@@ -204,7 +222,9 @@
         out_specs=pl.BlockSpec(memory_space=pl.ANY),
         scratch_shapes=[
             pltpu.VMEM((n_slots, height, strip), jnp.float32),
+            pltpu.VMEM((2, height, 128), jnp.float32),
             pltpu.SemaphoreType.DMA((n_slots,)),
+            pltpu.SemaphoreType.DMA((2,)),
         ],
         input_output_aliases=aliases,
         compiler_params=pltpu.CompilerParams(vmem_limit_bytes=VMEM),

time: 66.3 us -> 66.4 us (level)
  no operation moved by 1% of the time
where the time goes in v13:
time: 66.4 us; the launch traced here: 66.2 us
  waiting for transfers between devices  26.1 us (39%)
  Pallas kernels  21.9 us (33%)
  starting transfers between devices  16 us (24%)
  local copies, waits for them, and re-layouts  2.04 us (3%)
    ppermute x14, waiting for transfers between devices, sent(): lax.ppermute(x, axis, [(i, partner(i, step, size)) for i in range(size)])  26.1 us
    pallas_call x2, Pallas kernels, product_chunk(): pl.pallas_call(functools.partial(product_kernel, len(groups), column), ou...  19 us
    ppermute x14, starting transfers between devices, sent(): lax.ppermute(x, axis, [(i, partner(i, step, size)) for i in range(size)])  16 us
    pallas_call x1, Pallas kernels, standardize_a(): pl.pallas_call(functools.partial(standardize_a_kernel, n_fa, n_fb), out_s...  2.12 us
    unnamed x4, local copies, waits for them, and re-layouts  2.04 us
  transfers between devices with their start and end apart: 14, of which 6 were waited for; matrix products, arithmetic and copies ran while one was open for 0% of the time, Pallas kernels for 18%

profile of v13, /device:TPU:0, one launch (start us, length us, event | category | flops | bytes accessed | tf_op | source)
XLA Modules:
  0.0 66.2 jit_solution(4839324436596049961)
XLA Ops:
  0.0 0.0 copy-start
  0.0 1.0 %copy-done = bf16[16,14336]{1,0:T(8,128)(2,1)S(1)} copy-done((bf16[16,14336]{1,0:T(8,128)(2,1)S(1)}, bf16[16,14336]{1,0:T(8,128)(2,1)}, u32[]{:S(2)}) %copy-start) | copy-done | bytes 458776
  1.0 0.3 cut_panels.2
  1.4 3.1 %collective-permute-start = (bf16[16,3584]{1,0:T(8,128)(2,1)S(1)}, bf16[16,3584]{1,0:T(8,128)(2,1)S(1)}, u32[]{:S(2)}, u32[]{:S(2)}) collective-permute-start(bf16[16,3584]{1,0:T(8,128)(2,1)S(1)} %get-tuple-element.20), channel_id=1, source_target_pairs={{0,4},{4,0},{8,12},{12,8},{1,5},{5,1},{9,13},{13,9},{2,6},{6,2},{1... | collective-permute-start | bytes 344072 | tf_op jit(solution)/shard_map/ppermute | solution.py:240
  4.4 2.5 %collective-permute-start.1 = (bf16[16,3584]{1,0:T(8,128)(2,1)S(1)}, bf16[16,3584]{1,0:T(8,128)(2,1)S(1)}, u32[]{:S(2)}, u32[]{:S(2)}) collective-permute-start(bf16[16,3584]{1,0:T(8,128)(2,1)S(1)} %get-tuple-element.21), channel_id=1, source_target_pairs={{0,12},{4,8},{8,4},{12,0},{1,13},{5,9},{9,5},{13,1},{2,14},{6,10},... | collective-permute-start | bytes 344072 | tf_op jit(solution)/shard_map/ppermute | solution.py:240
  6.9 0.1 collective-permute-start.2
  7.0 0.0 copy-start.1
  7.0 1.0 %copy-done.1 = bf16[16,14336]{1,0:T(8,128)(2,1)S(1)} copy-done((bf16[16,14336]{1,0:T(8,128)(2,1)S(1)}, bf16[16,14336]{1,0:T(8,128)(2,1)}, u32[]{:S(2)}) %copy-start.1) | copy-done | bytes 458776
  8.1 0.3 cut_panels.3
  8.4 0.1 collective-permute-start.3
  8.5 1.6 %collective-permute-start.4 = (bf16[16,3584]{1,0:T(8,128)(2,1)S(1)}, bf16[16,3584]{1,0:T(8,128)(2,1)S(1)}, u32[]{:S(2)}, u32[]{:S(2)}) collective-permute-start(bf16[16,3584]{1,0:T(8,128)(2,1)S(1)} %get-tuple-element.25), channel_id=1, source_target_pairs={{0,2},{1,3},{2,0},{3,1},{4,6},{5,7},{6,4},{7,5},{8,10},{9,11},{10,... | collective-permute-start | bytes 344072 | tf_op jit(solution)/shard_map/ppermute | solution.py:240
  10.0 0.0 collective-permute-done.refs_1_
  10.0 0.3 collective-permute-start.5
  10.3 3.2 %collective-permute-done.1.refs_2_ = bf16[16,3584]{1,0:T(8,128)(2,1)S(1)} collective-permute-done((bf16[16,3584]{1,0:T(8,128)(2,1)S(1)}, bf16[16,3584]{1,0:T(8,128)(2,1)S(1)}, u32[]{:S(2)}, u32[]{:S(2)}) %collective-permute-start.1) | collective-permute-done | bytes 114720 | tf_op jit(solution)/shard_map/ppermute | solution.py:240
  13.5 3.8 %collective-permute-done.2.refs_3_ = bf16[16,3584]{1,0:T(8,128)(2,1)S(1)} collective-permute-done((bf16[16,3584]{1,0:T(8,128)(2,1)S(1)}, bf16[16,3584]{1,0:T(8,128)(2,1)S(1)}, u32[]{:S(2)}, u32[]{:S(2)}) %collective-permute-start.2) | collective-permute-done | bytes 114720 | tf_op jit(solution)/shard_map/ppermute | solution.py:240
  17.3 0.0 collective-permute-done.3.refs_5_.refs_9_
  17.3 0.0 collective-permute-done.4.refs_6_.refs_10_
  17.3 0.0 collective-permute-done.5.refs_7_.refs_11_
  17.3 0.1 join_rows.5
  17.4 1.6 %collective-permute-start.7 = (bf16[64,3584]{1,0:T(8,128)(2,1)S(1)}, bf16[64,3584]{1,0:T(8,128)(2,1)S(1)}, u32[]{:S(2)}, u32[]{:S(2)}) collective-permute-start(bf16[64,3584]{1,0:T(8,128)(2,1)S(1)} %get-tuple-element.27.refs_0_), channel_id=1, source_target_pairs={{0,2},{1,3},{2,0},{3,1},{4,6},{5,7},{6,4},{7,5},{8,10},{9,11},{10,... | collective-permute-start | bytes 1376264 | tf_op jit(solution)/shard_map/ppermute | solution.py:240
  18.9 1.5 %collective-permute-start.8 = (bf16[64,1792]{1,0:T(8,128)(2,1)S(1)}, bf16[64,1792]{1,0:T(8,128)(2,1)S(1)}, u32[]{:S(2)}, u32[]{:S(2)}) collective-permute-start(bf16[64,1792]{1,0:T(8,128)(2,1)S(1)} %get-tuple-element.28.refs_0_), channel_id=1, source_target_pairs={{0,8},{4,12},{8,0},{12,4},{1,9},{5,13},{9,1},{13,5},{2,10},{6,14},... | collective-permute-start | bytes 688136 | tf_op jit(solution)/shard_map/ppermute | solution.py:240
  20.5 0.0 collective-permute-start.6
  20.5 1.7 %collective-permute-start.10 = (bf16[64,3584]{1,0:T(8,128)(2,1)S(1)}, bf16[64,3584]{1,0:T(8,128)(2,1)S(1)}, u32[]{:S(2)}, u32[]{:S(2)}) collective-permute-start(bf16[64,3584]{1,0:T(8,128)(2,1)S(1)} %get-tuple-element.30), channel_id=1, source_target_pairs={{0,4},{4,0},{8,12},{12,8},{1,5},{5,1},{9,13},{13,9},{2,6},{6,2},{1... | collective-permute-start | bytes 1376264 | tf_op jit(solution)/shard_map/ppermute | solution.py:240
  22.1 9.3 %collective-permute-done.8.refs_1_.refs_3_ = bf16[64,1792]{1,0:T(8,128)(2,1)S(1)} collective-permute-done((bf16[64,1792]{1,0:T(8,128)(2,1)S(1)}, bf16[64,1792]{1,0:T(8,128)(2,1)S(1)}, u32[]{:S(2)}, u32[]{:S(2)}) %collective-permute-start.8) | collective-permute-done | bytes 229408 | tf_op jit(solution)/shard_map/ppermute | solution.py:240
  31.5 0.0 collective-permute-done.7.refs_0_.refs_2_
  31.5 0.1 collective-permute-start.9
  31.6 0.3 collective-permute-start.11
  31.9 3.2 %collective-permute-start.13 = (bf16[64,1792]{1,0:T(8,128)(2,1)S(1)}, bf16[64,1792]{1,0:T(8,128)(2,1)S(1)}, u32[]{:S(2)}, u32[]{:S(2)}) collective-permute-start(bf16[64,1792]{1,0:T(8,128)(2,1)S(1)} %collective-permute-done.8.refs_1_.refs_3_), channel_id=1, source_target_pairs={{0,4},{4,0},{8,12},{12,8},{1,5},{5,1},{9,13},{13,9},{2,6},{6,2},{1... | collective-permute-start | bytes 688136 | tf_op jit(solution)/shard_map/ppermute | solution.py:240
  35.1 4.3 %collective-permute-done.10.refs_0_ = bf16[64,3584]{1,0:T(8,128)(2,1)S(1)} collective-permute-done((bf16[64,3584]{1,0:T(8,128)(2,1)S(1)}, bf16[64,3584]{1,0:T(8,128)(2,1)S(1)}, u32[]{:S(2)}, u32[]{:S(2)}) %collective-permute-start.10) | collective-permute-done | bytes 458784 | tf_op jit(solution)/shard_map/ppermute | solution.py:240
  39.4 0.0 collective-permute-done.6.refs_1_
  39.4 0.0 collective-permute-done.9.refs_3_
  39.4 2.1 %standardize_a.1.refs_1_.a_ref = bf16[3584,256]{1,0:T(8,128)(2,1)S(1)} custom-call(bf16[64,3584]{1,0:T(8,128)(2,1)S(1)} %get-tuple-element.27.refs_0_, bf16[64,3584]{1,0:T(8,128)(2,1)S(1)} %collective-permute-done.6.refs_1_, bf16[64,3584]{1,0:T(8,128)(2,1)S(1)} %collective-permute-done.7.refs_0_.refs_2_, bf16[64,3584]{1,0:T(8,128)(2,1)S(1)} %collective-permute-done.9.refs_3_), custom_call_target="tpu_custom_call" | custom-call | flops 9175040 | bytes 3670016 | tf_op jit(solution)/shard_map/standardize_a/pallas_call | solution.py:141
  41.6 4.0 %collective-permute-done.11.refs_0_.refs_4_.refs_3_ = bf16[64,1792]{1,0:T(8,128)(2,1)S(1)} collective-permute-done((bf16[64,1792]{1,0:T(8,128)(2,1)S(1)}, bf16[64,1792]{1,0:T(8,128)(2,1)S(1)}, u32[]{:S(2)}, u32[]{:S(2)}) %collective-permute-start.11) | collective-permute-done | bytes 229408 | tf_op jit(solution)/shard_map/ppermute | solution.py:240
  45.6 0.1 collective-permute-start.12
  45.7 1.5 %collective-permute-done.13.refs_2_ = bf16[64,1792]{1,0:T(8,128)(2,1)S(1)} collective-permute-done((bf16[64,1792]{1,0:T(8,128)(2,1)S(1)}, bf16[64,1792]{1,0:T(8,128)(2,1)S(1)}, u32[]{:S(2)}, u32[]{:S(2)}) %collective-permute-start.13) | collective-permute-done | bytes 229408 | tf_op jit(solution)/shard_map/ppermute | solution.py:240
  47.2 9.5 %product_chunk.2.refs_4_ = f32[3584,3584]{1,0:T(8,128)} custom-call(bf16[3584,256]{1,0:T(8,128)(2,1)S(1)} %standardize_a.1.refs_1_.a_ref, bf16[64,1792]{1,0:T(8,128)(2,1)S(1)} %get-tuple-element.28.refs_0_, bf16[64,1792]{1,0:T(8,128)(2,1)S(1)} %get-tuple-element.32.refs_1_, bf16[64,1792]{1,0:T(8,128)(2,1)S(1)} %collective-permute-done.13.refs_2_, ...), custom_call_target="tpu_custom_call" | custom-call | flops 3288334336 | bytes 25690112 | tf_op jit(solution)/shard_map/product_chunk/pallas_call | solution.py:218
  56.7 0.0 collective-permute-done.12.refs_2_
  56.7 9.5 %product_chunk.3 = f32[3584,3584]{1,0:T(8,128)} custom-call(bf16[3584,256]{1,0:T(8,128)(2,1)S(1)} %standardize_a.1.refs_1_.a_ref, bf16[64,1792]{1,0:T(8,128)(2,1)S(1)} %get-tuple-element.29.refs_0_, bf16[64,1792]{1,0:T(8,128)(2,1)S(1)} %get-tuple-element.31.refs_1_, ...), custom_call_target="tpu_custom_call", output_to_operand_aliasing={{}: (5, {})} | custom-call | flops 3288334336 | bytes 25690112 | tf_op jit(solution)/shard_map/product_chunk/pallas_call | solution.py:218
  (4 shorter events, 0.1 us)
Async XLA Ops:
  0.0 1.0 %copy-start = (bf16[16,14336]{1,0:T(8,128)(2,1)S(1)}, bf16[16,14336]{1,0:T(8,128)(2,1)}, u32[]{:S(2)}) copy-start(bf16[16,14336]{1,0:T(8,128)(2,1)} %ref.2) | copy-start | bytes 1376260
  1.4 8.7 %collective-permute-start = (bf16[16,3584]{1,0:T(8,128)(2,1)S(1)}, bf16[16,3584]{1,0:T(8,128)(2,1)S(1)}, u32[]{:S(2)}, u32[]{:S(2)}) collective-permute-start(bf16[16,3584]{1,0:T(8,128)(2,1)S(1)} %get-tuple-element.20), channel_id=1, source_target_pairs={{0,4},{4,0},{8,12},{12,8},{1,5},{5,1},{9,13},{13,9},{2,6},{6,2},{1... | collective-permute-start | bytes 344072 | tf_op jit(solution)/shard_map/ppermute | solution.py:240
  4.4 9.0 %collective-permute-start.1 = (bf16[16,3584]{1,0:T(8,128)(2,1)S(1)}, bf16[16,3584]{1,0:T(8,128)(2,1)S(1)}, u32[]{:S(2)}, u32[]{:S(2)}) collective-permute-start(bf16[16,3584]{1,0:T(8,128)(2,1)S(1)} %get-tuple-element.21), channel_id=1, source_target_pairs={{0,12},{4,8},{8,4},{12,0},{1,13},{5,9},{9,5},{13,1},{2,14},{6,10},... | collective-permute-start | bytes 344072 | tf_op jit(solution)/shard_map/ppermute | solution.py:240
  6.9 10.3 %collective-permute-start.2 = (bf16[16,3584]{1,0:T(8,128)(2,1)S(1)}, bf16[16,3584]{1,0:T(8,128)(2,1)S(1)}, u32[]{:S(2)}, u32[]{:S(2)}) collective-permute-start(bf16[16,3584]{1,0:T(8,128)(2,1)S(1)} %get-tuple-element.22), channel_id=1, source_target_pairs={{0,8},{4,12},{8,0},{12,4},{1,9},{5,13},{9,1},{13,5},{2,10},{6,14},... | collective-permute-start | bytes 344072 | tf_op jit(solution)/shard_map/ppermute | solution.py:240
  7.0 1.0 %copy-start.1 = (bf16[16,14336]{1,0:T(8,128)(2,1)S(1)}, bf16[16,14336]{1,0:T(8,128)(2,1)}, u32[]{:S(2)}) copy-start(bf16[16,14336]{1,0:T(8,128)(2,1)} %ref.3) | copy-start | bytes 1376260
  8.4 8.9 %collective-permute-start.3 = (bf16[16,3584]{1,0:T(8,128)(2,1)S(1)}, bf16[16,3584]{1,0:T(8,128)(2,1)S(1)}, u32[]{:S(2)}, u32[]{:S(2)}) collective-permute-start(bf16[16,3584]{1,0:T(8,128)(2,1)S(1)} %get-tuple-element.24), channel_id=1, source_target_pairs={{0,1},{1,0},{2,3},{3,2},{4,5},{5,4},{6,7},{7,6},{8,9},{9,8},{10,11... | collective-permute-start | bytes 344072 | tf_op jit(solution)/shard_map/ppermute | solution.py:240
  8.5 8.8 %collective-permute-start.4 = (bf16[16,3584]{1,0:T(8,128)(2,1)S(1)}, bf16[16,3584]{1,0:T(8,128)(2,1)S(1)}, u32[]{:S(2)}, u32[]{:S(2)}) collective-permute-start(bf16[16,3584]{1,0:T(8,128)(2,1)S(1)} %get-tuple-element.25), channel_id=1, source_target_pairs={{0,2},{1,3},{2,0},{3,1},{4,6},{5,7},{6,4},{7,5},{8,10},{9,11},{10,... | collective-permute-start | bytes 344072 | tf_op jit(solution)/shard_map/ppermute | solution.py:240
  10.0 7.3 %collective-permute-start.5 = (bf16[16,3584]{1,0:T(8,128)(2,1)S(1)}, bf16[16,3584]{1,0:T(8,128)(2,1)S(1)}, u32[]{:S(2)}, u32[]{:S(2)}) collective-permute-start(bf16[16,3584]{1,0:T(8,128)(2,1)S(1)} %get-tuple-element.26), channel_id=1, source_target_pairs={{0,3},{1,2},{2,1},{3,0},{4,7},{5,6},{6,5},{7,4},{8,11},{9,10},{10,... | collective-permute-start | bytes 344072 | tf_op jit(solution)/shard_map/ppermute | solution.py:240
  17.4 14.1 %collective-permute-start.7 = (bf16[64,3584]{1,0:T(8,128)(2,1)S(1)}, bf16[64,3584]{1,0:T(8,128)(2,1)S(1)}, u32[]{:S(2)}, u32[]{:S(2)}) collective-permute-start(bf16[64,3584]{1,0:T(8,128)(2,1)S(1)} %get-tuple-element.27.refs_0_), channel_id=1, source_target_pairs={{0,2},{1,3},{2,0},{3,1},{4,6},{5,7},{6,4},{7,5},{8,10},{9,11},{10,... | collective-permute-start | bytes 1376264 | tf_op jit(solution)/shard_map/ppermute | solution.py:240
  18.9 12.5 %collective-permute-start.8 = (bf16[64,1792]{1,0:T(8,128)(2,1)S(1)}, bf16[64,1792]{1,0:T(8,128)(2,1)S(1)}, u32[]{:S(2)}, u32[]{:S(2)}) collective-permute-start(bf16[64,1792]{1,0:T(8,128)(2,1)S(1)} %get-tuple-element.28.refs_0_), channel_id=1, source_target_pairs={{0,8},{4,12},{8,0},{12,4},{1,9},{5,13},{9,1},{13,5},{2,10},{6,14},... | collective-permute-start | bytes 688136 | tf_op jit(solution)/shard_map/ppermute | solution.py:240
  20.5 18.9 %collective-permute-start.6 = (bf16[64,3584]{1,0:T(8,128)(2,1)S(1)}, bf16[64,3584]{1,0:T(8,128)(2,1)S(1)}, u32[]{:S(2)}, u32[]{:S(2)}) collective-permute-start(bf16[64,3584]{1,0:T(8,128)(2,1)S(1)} %get-tuple-element.27.refs_0_), channel_id=1, source_target_pairs={{0,1},{1,0},{2,3},{3,2},{4,5},{5,4},{6,7},{7,6},{8,9},{9,8},{10,11... | collective-permute-start | bytes 1376264 | tf_op jit(solution)/shard_map/ppermute | solution.py:240
  20.5 18.9 %collective-permute-start.10 = (bf16[64,3584]{1,0:T(8,128)(2,1)S(1)}, bf16[64,3584]{1,0:T(8,128)(2,1)S(1)}, u32[]{:S(2)}, u32[]{:S(2)}) collective-permute-start(bf16[64,3584]{1,0:T(8,128)(2,1)S(1)} %get-tuple-element.30), channel_id=1, source_target_pairs={{0,4},{4,0},{8,12},{12,8},{1,5},{5,1},{9,13},{13,9},{2,6},{6,2},{1... | collective-permute-start | bytes 1376264 | tf_op jit(solution)/shard_map/ppermute | solution.py:240
  31.5 7.9 %collective-permute-start.9 = (bf16[64,3584]{1,0:T(8,128)(2,1)S(1)}, bf16[64,3584]{1,0:T(8,128)(2,1)S(1)}, u32[]{:S(2)}, u32[]{:S(2)}) collective-permute-start(bf16[64,3584]{1,0:T(8,128)(2,1)S(1)} %join_rows.6), channel_id=1, source_target_pairs={{0,1},{1,0},{2,3},{3,2},{4,5},{5,4},{6,7},{7,6},{8,9},{9,8},{10,11... | collective-permute-start | bytes 1376264 | tf_op jit(solution)/shard_map/ppermute | solution.py:240
  31.6 14.0 %collective-permute-start.11 = (bf16[64,1792]{1,0:T(8,128)(2,1)S(1)}, bf16[64,1792]{1,0:T(8,128)(2,1)S(1)}, u32[]{:S(2)}, u32[]{:S(2)}) collective-permute-start(bf16[64,1792]{1,0:T(8,128)(2,1)S(1)} %join_rows.8), channel_id=1, source_target_pairs={{0,8},{4,12},{8,0},{12,4},{1,9},{5,13},{9,1},{13,5},{2,10},{6,14},... | collective-permute-start | bytes 688136 | tf_op jit(solution)/shard_map/ppermute | solution.py:240
  31.9 15.3 %collective-permute-start.13 = (bf16[64,1792]{1,0:T(8,128)(2,1)S(1)}, bf16[64,1792]{1,0:T(8,128)(2,1)S(1)}, u32[]{:S(2)}, u32[]{:S(2)}) collective-permute-start(bf16[64,1792]{1,0:T(8,128)(2,1)S(1)} %collective-permute-done.8.refs_1_.refs_3_), channel_id=1, source_target_pairs={{0,4},{4,0},{8,12},{12,8},{1,5},{5,1},{9,13},{13,9},{2,6},{6,2},{1... | collective-permute-start | bytes 688136 | tf_op jit(solution)/shard_map/ppermute | solution.py:240
  45.6 11.1 %collective-permute-start.12 = (bf16[64,1792]{1,0:T(8,128)(2,1)S(1)}, bf16[64,1792]{1,0:T(8,128)(2,1)S(1)}, u32[]{:S(2)}, u32[]{:S(2)}) collective-permute-start(bf16[64,1792]{1,0:T(8,128)(2,1)S(1)} %join_rows.9), channel_id=1, source_target_pairs={{0,4},{4,0},{8,12},{12,8},{1,5},{5,1},{9,13},{13,9},{2,6},{6,2},{1... | collective-permute-start | bytes 688136 | tf_op jit(solution)/shard_map/ppermute | solution.py:240

commit v14 on v12

--- a/solution.py
+++ b/solution.py
@@ -34,12 +34,12 @@
     return values / count
 
 
-def standardize(values):
+def standardize(values, scale=1.0):
     count = values.shape[0]
     mean = over_count(jnp.sum(values, axis=0, keepdims=True), count)
     centred = values - mean
     var = over_count(jnp.sum(centred * centred, axis=0, keepdims=True), count)
-    return (centred * lax.rsqrt(var + EPS)).astype(jnp.bfloat16)
+    return (centred * (lax.rsqrt(var + EPS) * scale)).astype(jnp.bfloat16)
 
 
 def power_of_two(count):
@@ -131,7 +131,9 @@
     pieces = [
         group[pl.ds(i * tok, tok), :].astype(jnp.float32) for i in range(n_fa) for group in groups
     ]
-    out[...] = standardize(jnp.concatenate(pieces, axis=0)).T
+    values = jnp.concatenate(pieces, axis=0)
+    total = values.shape[0]
+    out[...] = standardize(values, 1.0 / total if power_of_two(total) else 1.0).T
 
 
 def standardize_a(groups, n_fa, n_fb):
@@ -176,7 +178,7 @@
             parts.append(standardize(jnp.concatenate(pieces, axis=0)))
         std = jnp.concatenate(parts, axis=1)
         product = jnp.dot(a_ref[...], std, preferred_element_type=jnp.float32)
-        slots[lax.rem(step, n_slots)] = over_count(product, total)
+        slots[lax.rem(step, n_slots)] = product if power_of_two(total) else product / total
         copy_of(step).start()
 
     @pl.loop(max(width // strip - n_slots, 0), width // strip)

time: 66.3 us -> 66.3 us (level)
  no operation moved by 1% of the time
where the time goes in v14:
time: 66.3 us; the launch traced here: 66.1 us
  waiting for transfers between devices  26.1 us (39%)
  Pallas kernels  21.9 us (33%)
  starting transfers between devices  16 us (24%)
  local copies, waits for them, and re-layouts  2.04 us (3%)
    ppermute x14, waiting for transfers between devices, sent(): lax.ppermute(x, axis, [(i, partner(i, step, size)) for i in range(size)])  26.1 us
    pallas_call x2, Pallas kernels, product_chunk(): pl.pallas_call(functools.partial(product_kernel, len(groups), column), ou...  18.9 us
    ppermute x14, starting transfers between devices, sent(): lax.ppermute(x, axis, [(i, partner(i, step, size)) for i in range(size)])  16 us
    pallas_call x1, Pallas kernels, standardize_a(): pl.pallas_call(functools.partial(standardize_a_kernel, n_fa, n_fb), out_s...  2.14 us
    unnamed x4, local copies, waits for them, and re-layouts  2.04 us
  transfers between devices with their start and end apart: 14, of which 6 were waited for; matrix products, arithmetic and copies ran while one was open for 0% of the time, Pallas kernels for 18%

profile of v14, /device:TPU:0, one launch (start us, length us, event | category | flops | bytes accessed | tf_op | source)
XLA Modules:
  0.0 66.1 jit_solution(5786608830521525666)
XLA Ops:
  0.0 0.0 copy-start
  0.0 1.0 %copy-done = bf16[16,14336]{1,0:T(8,128)(2,1)S(1)} copy-done((bf16[16,14336]{1,0:T(8,128)(2,1)S(1)}, bf16[16,14336]{1,0:T(8,128)(2,1)}, u32[]{:S(2)}) %copy-start) | copy-done | bytes 458776
  1.0 0.3 cut_panels.2
  1.4 3.1 %collective-permute-start = (bf16[16,3584]{1,0:T(8,128)(2,1)S(1)}, bf16[16,3584]{1,0:T(8,128)(2,1)S(1)}, u32[]{:S(2)}, u32[]{:S(2)}) collective-permute-start(bf16[16,3584]{1,0:T(8,128)(2,1)S(1)} %get-tuple-element.20), channel_id=1, source_target_pairs={{0,4},{4,0},{8,12},{12,8},{1,5},{5,1},{9,13},{13,9},{2,6},{6,2},{1... | collective-permute-start | bytes 344072 | tf_op jit(solution)/shard_map/ppermute | solution.py:222
  4.4 2.5 %collective-permute-start.1 = (bf16[16,3584]{1,0:T(8,128)(2,1)S(1)}, bf16[16,3584]{1,0:T(8,128)(2,1)S(1)}, u32[]{:S(2)}, u32[]{:S(2)}) collective-permute-start(bf16[16,3584]{1,0:T(8,128)(2,1)S(1)} %get-tuple-element.21), channel_id=1, source_target_pairs={{0,12},{4,8},{8,4},{12,0},{1,13},{5,9},{9,5},{13,1},{2,14},{6,10},... | collective-permute-start | bytes 344072 | tf_op jit(solution)/shard_map/ppermute | solution.py:222
  6.9 0.1 collective-permute-start.2
  7.0 0.0 copy-start.1
  7.0 1.0 %copy-done.1 = bf16[16,14336]{1,0:T(8,128)(2,1)S(1)} copy-done((bf16[16,14336]{1,0:T(8,128)(2,1)S(1)}, bf16[16,14336]{1,0:T(8,128)(2,1)}, u32[]{:S(2)}) %copy-start.1) | copy-done | bytes 458776
  8.1 0.3 cut_panels.3
  8.4 0.1 collective-permute-start.3
  8.5 1.6 %collective-permute-start.4 = (bf16[16,3584]{1,0:T(8,128)(2,1)S(1)}, bf16[16,3584]{1,0:T(8,128)(2,1)S(1)}, u32[]{:S(2)}, u32[]{:S(2)}) collective-permute-start(bf16[16,3584]{1,0:T(8,128)(2,1)S(1)} %get-tuple-element.25), channel_id=1, source_target_pairs={{0,2},{1,3},{2,0},{3,1},{4,6},{5,7},{6,4},{7,5},{8,10},{9,11},{10,... | collective-permute-start | bytes 344072 | tf_op jit(solution)/shard_map/ppermute | solution.py:222
  10.0 0.0 collective-permute-done.refs_1_
  10.0 0.3 collective-permute-start.5
  10.3 3.2 %collective-permute-done.1.refs_2_ = bf16[16,3584]{1,0:T(8,128)(2,1)S(1)} collective-permute-done((bf16[16,3584]{1,0:T(8,128)(2,1)S(1)}, bf16[16,3584]{1,0:T(8,128)(2,1)S(1)}, u32[]{:S(2)}, u32[]{:S(2)}) %collective-permute-start.1) | collective-permute-done | bytes 114720 | tf_op jit(solution)/shard_map/ppermute | solution.py:222
  13.5 3.8 %collective-permute-done.2.refs_3_ = bf16[16,3584]{1,0:T(8,128)(2,1)S(1)} collective-permute-done((bf16[16,3584]{1,0:T(8,128)(2,1)S(1)}, bf16[16,3584]{1,0:T(8,128)(2,1)S(1)}, u32[]{:S(2)}, u32[]{:S(2)}) %collective-permute-start.2) | collective-permute-done | bytes 114720 | tf_op jit(solution)/shard_map/ppermute | solution.py:222
  17.3 0.0 collective-permute-done.3.refs_5_.refs_9_
  17.3 0.0 collective-permute-done.4.refs_6_.refs_10_
  17.3 0.0 collective-permute-done.5.refs_7_.refs_11_
  17.3 0.1 join_rows.5
  17.4 1.6 %collective-permute-start.7 = (bf16[64,3584]{1,0:T(8,128)(2,1)S(1)}, bf16[64,3584]{1,0:T(8,128)(2,1)S(1)}, u32[]{:S(2)}, u32[]{:S(2)}) collective-permute-start(bf16[64,3584]{1,0:T(8,128)(2,1)S(1)} %get-tuple-element.27.refs_0_), channel_id=1, source_target_pairs={{0,2},{1,3},{2,0},{3,1},{4,6},{5,7},{6,4},{7,5},{8,10},{9,11},{10,... | collective-permute-start | bytes 1376264 | tf_op jit(solution)/shard_map/ppermute | solution.py:222
  18.9 1.5 %collective-permute-start.8 = (bf16[64,1792]{1,0:T(8,128)(2,1)S(1)}, bf16[64,1792]{1,0:T(8,128)(2,1)S(1)}, u32[]{:S(2)}, u32[]{:S(2)}) collective-permute-start(bf16[64,1792]{1,0:T(8,128)(2,1)S(1)} %get-tuple-element.28.refs_0_), channel_id=1, source_target_pairs={{0,8},{4,12},{8,0},{12,4},{1,9},{5,13},{9,1},{13,5},{2,10},{6,14},... | collective-permute-start | bytes 688136 | tf_op jit(solution)/shard_map/ppermute | solution.py:222
  20.5 0.0 collective-permute-start.6
  20.5 1.7 %collective-permute-start.10 = (bf16[64,3584]{1,0:T(8,128)(2,1)S(1)}, bf16[64,3584]{1,0:T(8,128)(2,1)S(1)}, u32[]{:S(2)}, u32[]{:S(2)}) collective-permute-start(bf16[64,3584]{1,0:T(8,128)(2,1)S(1)} %get-tuple-element.30), channel_id=1, source_target_pairs={{0,4},{4,0},{8,12},{12,8},{1,5},{5,1},{9,13},{13,9},{2,6},{6,2},{1... | collective-permute-start | bytes 1376264 | tf_op jit(solution)/shard_map/ppermute | solution.py:222
  22.1 9.3 %collective-permute-done.8.refs_1_.refs_3_ = bf16[64,1792]{1,0:T(8,128)(2,1)S(1)} collective-permute-done((bf16[64,1792]{1,0:T(8,128)(2,1)S(1)}, bf16[64,1792]{1,0:T(8,128)(2,1)S(1)}, u32[]{:S(2)}, u32[]{:S(2)}) %collective-permute-start.8) | collective-permute-done | bytes 229408 | tf_op jit(solution)/shard_map/ppermute | solution.py:222
  31.5 0.0 collective-permute-done.7.refs_0_.refs_2_
  31.5 0.1 collective-permute-start.9
  31.6 0.3 collective-permute-start.11
  31.9 3.2 %collective-permute-start.13 = (bf16[64,1792]{1,0:T(8,128)(2,1)S(1)}, bf16[64,1792]{1,0:T(8,128)(2,1)S(1)}, u32[]{:S(2)}, u32[]{:S(2)}) collective-permute-start(bf16[64,1792]{1,0:T(8,128)(2,1)S(1)} %collective-permute-done.8.refs_1_.refs_3_), channel_id=1, source_target_pairs={{0,4},{4,0},{8,12},{12,8},{1,5},{5,1},{9,13},{13,9},{2,6},{6,2},{1... | collective-permute-start | bytes 688136 | tf_op jit(solution)/shard_map/ppermute | solution.py:222
  35.1 4.3 %collective-permute-done.10.refs_0_ = bf16[64,3584]{1,0:T(8,128)(2,1)S(1)} collective-permute-done((bf16[64,3584]{1,0:T(8,128)(2,1)S(1)}, bf16[64,3584]{1,0:T(8,128)(2,1)S(1)}, u32[]{:S(2)}, u32[]{:S(2)}) %collective-permute-start.10) | collective-permute-done | bytes 458784 | tf_op jit(solution)/shard_map/ppermute | solution.py:222
  39.4 0.0 collective-permute-done.6.refs_1_
  39.4 0.0 collective-permute-done.9.refs_3_
  39.4 2.1 %standardize_a.1.refs_1_.a_ref = bf16[3584,256]{1,0:T(8,128)(2,1)S(1)} custom-call(bf16[64,3584]{1,0:T(8,128)(2,1)S(1)} %get-tuple-element.27.refs_0_, bf16[64,3584]{1,0:T(8,128)(2,1)S(1)} %collective-permute-done.6.refs_1_, bf16[64,3584]{1,0:T(8,128)(2,1)S(1)} %collective-permute-done.7.refs_0_.refs_2_, bf16[64,3584]{1,0:T(8,128)(2,1)S(1)} %collective-permute-done.9.refs_3_), custom_call_target="tpu_custom_call" | custom-call | flops 9175040 | bytes 3670016 | tf_op jit(solution)/shard_map/standardize_a/pallas_call | solution.py:143
  41.6 4.0 %collective-permute-done.11.refs_0_.refs_4_.refs_3_ = bf16[64,1792]{1,0:T(8,128)(2,1)S(1)} collective-permute-done((bf16[64,1792]{1,0:T(8,128)(2,1)S(1)}, bf16[64,1792]{1,0:T(8,128)(2,1)S(1)}, u32[]{:S(2)}, u32[]{:S(2)}) %collective-permute-start.11) | collective-permute-done | bytes 229408 | tf_op jit(solution)/shard_map/ppermute | solution.py:222
  45.6 0.1 collective-permute-start.12
  45.7 1.5 %collective-permute-done.13.refs_2_ = bf16[64,1792]{1,0:T(8,128)(2,1)S(1)} collective-permute-done((bf16[64,1792]{1,0:T(8,128)(2,1)S(1)}, bf16[64,1792]{1,0:T(8,128)(2,1)S(1)}, u32[]{:S(2)}, u32[]{:S(2)}) %collective-permute-start.13) | collective-permute-done | bytes 229408 | tf_op jit(solution)/shard_map/ppermute | solution.py:222
  47.2 9.4 %product_chunk.2.refs_4_ = f32[3584,3584]{1,0:T(8,128)} custom-call(bf16[3584,256]{1,0:T(8,128)(2,1)S(1)} %standardize_a.1.refs_1_.a_ref, bf16[64,1792]{1,0:T(8,128)(2,1)S(1)} %get-tuple-element.28.refs_0_, bf16[64,1792]{1,0:T(8,128)(2,1)S(1)} %get-tuple-element.32.refs_1_, bf16[64,1792]{1,0:T(8,128)(2,1)S(1)} %collective-permute-done.13.refs_2_, ...), custom_call_target="tpu_custom_call" | custom-call | flops 3288334336 | bytes 25690112 | tf_op jit(solution)/shard_map/product_chunk/pallas_call | solution.py:202
  56.7 0.0 collective-permute-done.12.refs_2_
  56.7 9.5 %product_chunk.3 = f32[3584,3584]{1,0:T(8,128)} custom-call(bf16[3584,256]{1,0:T(8,128)(2,1)S(1)} %standardize_a.1.refs_1_.a_ref, bf16[64,1792]{1,0:T(8,128)(2,1)S(1)} %get-tuple-element.29.refs_0_, bf16[64,1792]{1,0:T(8,128)(2,1)S(1)} %get-tuple-element.31.refs_1_, ...), custom_call_target="tpu_custom_call", output_to_operand_aliasing={{}: (5, {})} | custom-call | flops 3288334336 | bytes 25690112 | tf_op jit(solution)/shard_map/product_chunk/pallas_call | solution.py:202
  (4 shorter events, 0.1 us)
Async XLA Ops:
  0.0 1.0 %copy-start = (bf16[16,14336]{1,0:T(8,128)(2,1)S(1)}, bf16[16,14336]{1,0:T(8,128)(2,1)}, u32[]{:S(2)}) copy-start(bf16[16,14336]{1,0:T(8,128)(2,1)} %ref.2) | copy-start | bytes 1376260
  1.4 8.7 %collective-permute-start = (bf16[16,3584]{1,0:T(8,128)(2,1)S(1)}, bf16[16,3584]{1,0:T(8,128)(2,1)S(1)}, u32[]{:S(2)}, u32[]{:S(2)}) collective-permute-start(bf16[16,3584]{1,0:T(8,128)(2,1)S(1)} %get-tuple-element.20), channel_id=1, source_target_pairs={{0,4},{4,0},{8,12},{12,8},{1,5},{5,1},{9,13},{13,9},{2,6},{6,2},{1... | collective-permute-start | bytes 344072 | tf_op jit(solution)/shard_map/ppermute | solution.py:222
  4.4 9.0 %collective-permute-start.1 = (bf16[16,3584]{1,0:T(8,128)(2,1)S(1)}, bf16[16,3584]{1,0:T(8,128)(2,1)S(1)}, u32[]{:S(2)}, u32[]{:S(2)}) collective-permute-start(bf16[16,3584]{1,0:T(8,128)(2,1)S(1)} %get-tuple-element.21), channel_id=1, source_target_pairs={{0,12},{4,8},{8,4},{12,0},{1,13},{5,9},{9,5},{13,1},{2,14},{6,10},... | collective-permute-start | bytes 344072 | tf_op jit(solution)/shard_map/ppermute | solution.py:222
  6.9 10.3 %collective-permute-start.2 = (bf16[16,3584]{1,0:T(8,128)(2,1)S(1)}, bf16[16,3584]{1,0:T(8,128)(2,1)S(1)}, u32[]{:S(2)}, u32[]{:S(2)}) collective-permute-start(bf16[16,3584]{1,0:T(8,128)(2,1)S(1)} %get-tuple-element.22), channel_id=1, source_target_pairs={{0,8},{4,12},{8,0},{12,4},{1,9},{5,13},{9,1},{13,5},{2,10},{6,14},... | collective-permute-start | bytes 344072 | tf_op jit(solution)/shard_map/ppermute | solution.py:222
  7.0 1.0 %copy-start.1 = (bf16[16,14336]{1,0:T(8,128)(2,1)S(1)}, bf16[16,14336]{1,0:T(8,128)(2,1)}, u32[]{:S(2)}) copy-start(bf16[16,14336]{1,0:T(8,128)(2,1)} %ref.3) | copy-start | bytes 1376260
  8.4 8.9 %collective-permute-start.3 = (bf16[16,3584]{1,0:T(8,128)(2,1)S(1)}, bf16[16,3584]{1,0:T(8,128)(2,1)S(1)}, u32[]{:S(2)}, u32[]{:S(2)}) collective-permute-start(bf16[16,3584]{1,0:T(8,128)(2,1)S(1)} %get-tuple-element.24), channel_id=1, source_target_pairs={{0,1},{1,0},{2,3},{3,2},{4,5},{5,4},{6,7},{7,6},{8,9},{9,8},{10,11... | collective-permute-start | bytes 344072 | tf_op jit(solution)/shard_map/ppermute | solution.py:222
  8.5 8.8 %collective-permute-start.4 = (bf16[16,3584]{1,0:T(8,128)(2,1)S(1)}, bf16[16,3584]{1,0:T(8,128)(2,1)S(1)}, u32[]{:S(2)}, u32[]{:S(2)}) collective-permute-start(bf16[16,3584]{1,0:T(8,128)(2,1)S(1)} %get-tuple-element.25), channel_id=1, source_target_pairs={{0,2},{1,3},{2,0},{3,1},{4,6},{5,7},{6,4},{7,5},{8,10},{9,11},{10,... | collective-permute-start | bytes 344072 | tf_op jit(solution)/shard_map/ppermute | solution.py:222
  10.0 7.3 %collective-permute-start.5 = (bf16[16,3584]{1,0:T(8,128)(2,1)S(1)}, bf16[16,3584]{1,0:T(8,128)(2,1)S(1)}, u32[]{:S(2)}, u32[]{:S(2)}) collective-permute-start(bf16[16,3584]{1,0:T(8,128)(2,1)S(1)} %get-tuple-element.26), channel_id=1, source_target_pairs={{0,3},{1,2},{2,1},{3,0},{4,7},{5,6},{6,5},{7,4},{8,11},{9,10},{10,... | collective-permute-start | bytes 344072 | tf_op jit(solution)/shard_map/ppermute | solution.py:222
  17.4 14.1 %collective-permute-start.7 = (bf16[64,3584]{1,0:T(8,128)(2,1)S(1)}, bf16[64,3584]{1,0:T(8,128)(2,1)S(1)}, u32[]{:S(2)}, u32[]{:S(2)}) collective-permute-start(bf16[64,3584]{1,0:T(8,128)(2,1)S(1)} %get-tuple-element.27.refs_0_), channel_id=1, source_target_pairs={{0,2},{1,3},{2,0},{3,1},{4,6},{5,7},{6,4},{7,5},{8,10},{9,11},{10,... | collective-permute-start | bytes 1376264 | tf_op jit(solution)/shard_map/ppermute | solution.py:222
  18.9 12.5 %collective-permute-start.8 = (bf16[64,1792]{1,0:T(8,128)(2,1)S(1)}, bf16[64,1792]{1,0:T(8,128)(2,1)S(1)}, u32[]{:S(2)}, u32[]{:S(2)}) collective-permute-start(bf16[64,1792]{1,0:T(8,128)(2,1)S(1)} %get-tuple-element.28.refs_0_), channel_id=1, source_target_pairs={{0,8},{4,12},{8,0},{12,4},{1,9},{5,13},{9,1},{13,5},{2,10},{6,14},... | collective-permute-start | bytes 688136 | tf_op jit(solution)/shard_map/ppermute | solution.py:222
  20.5 18.9 %collective-permute-start.6 = (bf16[64,3584]{1,0:T(8,128)(2,1)S(1)}, bf16[64,3584]{1,0:T(8,128)(2,1)S(1)}, u32[]{:S(2)}, u32[]{:S(2)}) collective-permute-start(bf16[64,3584]{1,0:T(8,128)(2,1)S(1)} %get-tuple-element.27.refs_0_), channel_id=1, source_target_pairs={{0,1},{1,0},{2,3},{3,2},{4,5},{5,4},{6,7},{7,6},{8,9},{9,8},{10,11... | collective-permute-start | bytes 1376264 | tf_op jit(solution)/shard_map/ppermute | solution.py:222
  20.5 18.9 %collective-permute-start.10 = (bf16[64,3584]{1,0:T(8,128)(2,1)S(1)}, bf16[64,3584]{1,0:T(8,128)(2,1)S(1)}, u32[]{:S(2)}, u32[]{:S(2)}) collective-permute-start(bf16[64,3584]{1,0:T(8,128)(2,1)S(1)} %get-tuple-element.30), channel_id=1, source_target_pairs={{0,4},{4,0},{8,12},{12,8},{1,5},{5,1},{9,13},{13,9},{2,6},{6,2},{1... | collective-permute-start | bytes 1376264 | tf_op jit(solution)/shard_map/ppermute | solution.py:222
  31.5 7.9 %collective-permute-start.9 = (bf16[64,3584]{1,0:T(8,128)(2,1)S(1)}, bf16[64,3584]{1,0:T(8,128)(2,1)S(1)}, u32[]{:S(2)}, u32[]{:S(2)}) collective-permute-start(bf16[64,3584]{1,0:T(8,128)(2,1)S(1)} %join_rows.6), channel_id=1, source_target_pairs={{0,1},{1,0},{2,3},{3,2},{4,5},{5,4},{6,7},{7,6},{8,9},{9,8},{10,11... | collective-permute-start | bytes 1376264 | tf_op jit(solution)/shard_map/ppermute | solution.py:222
  31.6 14.0 %collective-permute-start.11 = (bf16[64,1792]{1,0:T(8,128)(2,1)S(1)}, bf16[64,1792]{1,0:T(8,128)(2,1)S(1)}, u32[]{:S(2)}, u32[]{:S(2)}) collective-permute-start(bf16[64,1792]{1,0:T(8,128)(2,1)S(1)} %join_rows.8), channel_id=1, source_target_pairs={{0,8},{4,12},{8,0},{12,4},{1,9},{5,13},{9,1},{13,5},{2,10},{6,14},... | collective-permute-start | bytes 688136 | tf_op jit(solution)/shard_map/ppermute | solution.py:222
  31.9 15.3 %collective-permute-start.13 = (bf16[64,1792]{1,0:T(8,128)(2,1)S(1)}, bf16[64,1792]{1,0:T(8,128)(2,1)S(1)}, u32[]{:S(2)}, u32[]{:S(2)}) collective-permute-start(bf16[64,1792]{1,0:T(8,128)(2,1)S(1)} %collective-permute-done.8.refs_1_.refs_3_), channel_id=1, source_target_pairs={{0,4},{4,0},{8,12},{12,8},{1,5},{5,1},{9,13},{13,9},{2,6},{6,2},{1... | collective-permute-start | bytes 688136 | tf_op jit(solution)/shard_map/ppermute | solution.py:222
  45.6 11.0 %collective-permute-start.12 = (bf16[64,1792]{1,0:T(8,128)(2,1)S(1)}, bf16[64,1792]{1,0:T(8,128)(2,1)S(1)}, u32[]{:S(2)}, u32[]{:S(2)}) collective-permute-start(bf16[64,1792]{1,0:T(8,128)(2,1)S(1)} %join_rows.9), channel_id=1, source_target_pairs={{0,4},{4,0},{8,12},{12,8},{1,5},{5,1},{9,13},{13,9},{2,6},{6,2},{1... | collective-permute-start | bytes 688136 | tf_op jit(solution)/shard_map/ppermute | solution.py:222
